TPU v7x, 32 devices: a whole 2x2x4 slice. The times are simulated.
32 devices in a mesh: rep: 4 (over y, x), seq: 8 (over z, core).
Axes of the slice: x: 2, y: 2, z: 4, core: 2. Of those that a mesh axis runs over, the one named last changes fastest.
Arguments:
- queries: bfloat16 [4, 1024, 3072], P('rep', 'seq'), may hold values from -6 to 6
- keys: bfloat16 [4, 1024, 128], P('rep', 'seq'), may hold values from -6 to 6
- values: bfloat16 [4, 1024, 128], P('rep', 'seq'), may hold values from -6 to 6
- outputs: bfloat16 [4, 1024, 3072], P('rep', 'seq'), may hold values from -6 to 6
- out_grad: bfloat16 [4, 1024, 3072], P('rep', 'seq'), may hold values from -24 to 24
- log_norm: float32 [4, 24, 1024], P('rep', None, 'seq'), may hold values from 7 to 8.5
- inputs: bfloat16 [4, 1024, 6144], P('rep', 'seq'), may hold values from -0.29882812 to 0.29882812
- mlp_weight: bfloat16 [4, 12288, 6144], P('rep', 'seq'), may hold values from -0.0546875 to 0.0546875
- initial_right_factor: bfloat16 [8, 4, 6144], P('seq'), may hold values from -6 to 6
Outputs:
- query_grad: float32 [4, 1024, 3072], P('rep', 'seq')
- kv_grad: float32 [4, 1024, 256], P('rep', 'seq')
- proj_grad: float32 [4, 6144, 256], P('rep', 'seq')
- left_factor: float32 [4, 2, 4, 12288], P('rep', None, None, 'seq')
- right_factor: float32 [4, 8, 2, 4, 6144], P('rep', 'seq')
All inputs are finite; a program needn't handle non-finite values.
Results may differ from a plain program's by a relative error of at most 0.004.
Values may be sent and summed in bfloat16 or wider, within the bound.
No kernel may reach another device: no remote copies, remote signals or barrier semaphores. Data moves between devices by JAX's collectives and lax.ppermute only.
A program may use at most 128 MiB of HBM per device.

v0:
```python
import jax
import jax.numpy as jnp
from jax import lax
from jax.sharding import PartitionSpec as P

WINDOW = 2048


epsilon = 1e-06


def shifted(block, axis, distance):
    devices = range(lax.axis_size(axis))
    route = [(i - distance, i) for i in devices if i - distance in devices]
    return lax.ppermute(block, axis, route)


def extended(block, sides, width):
    for axis, dim in sides:
        count = lax.axis_size(axis)
        forward = [(i, i + 1) for i in range(count - 1)]
        forward.append((count - 1, 0))
        backward = [(target, source) for source, target in forward]
        low = lax.ppermute(
            lax.slice_in_dim(block, block.shape[dim] - width, None, axis=dim), axis, forward
        )
        high = lax.ppermute(lax.slice_in_dim(block, 0, width, axis=dim), axis, backward)
        block = jnp.concatenate([low, block, high], axis=dim)
    return block


def window_mask(first_query, row_count, span):
    query_pos = first_query + jnp.arange(row_count, dtype=jnp.int32)
    key_pos = first_query - span + jnp.arange(span + row_count, dtype=jnp.int32)
    lower_ok = key_pos[None, :] > query_pos[:, None] - span
    upper_ok = key_pos[None, :] <= query_pos[:, None]
    return (key_pos[None, :] >= 0) & lower_ok & upper_ok


def attend(query_blk, gradient_block, out_blk, norm_block, window_kv, visible, scale):
    row_count, model_cols = query_blk.shape
    head_count = norm_block.shape[0]
    width = model_cols // head_count
    group = 8
    groups = head_count // group

    def head_rows(source):
        return (
            source.reshape(row_count, head_count, width)
            .transpose(1, 0, 2)
            .reshape(groups, group * row_count, width)
        )

    query_rows = head_rows(query_blk)
    grad_rows = head_rows(gradient_block)
    delta_all = jnp.sum(
        gradient_block.astype(jnp.float32).reshape(row_count, head_count, width)
        * out_blk.astype(jnp.float32).reshape(row_count, head_count, width),
        axis=-1,
    )
    delta_rows = delta_all.T.reshape(groups, group * row_count)
    norm_rows = norm_block.reshape(groups, group, row_count)
    key_mat = window_kv[:, :width]
    value_mat = window_kv[:, width:]

    def per_group(accum, items):
        query_grp, grad_grp, norm_grp, delta_grp = items
        scores = jnp.dot(query_grp, key_mat.T, preferred_element_type=jnp.float32) * scale
        scores = scores.reshape(group, row_count, -1)
        probs = jnp.where(visible[None], jnp.exp(scores - norm_grp[:, :, None]), 0.0)
        probs = probs.reshape(group * row_count, -1)
        probs_b = probs.astype(jnp.bfloat16)
        value_grad = jnp.dot(probs_b.T, grad_grp, preferred_element_type=jnp.float32)
        prob_grad = jnp.dot(grad_grp, value_mat.T, preferred_element_type=jnp.float32)
        score_grad = (scale * probs * (prob_grad - delta_grp[:, None])).astype(jnp.bfloat16)
        query_grad = jnp.dot(score_grad, key_mat, preferred_element_type=jnp.float32)
        key_grad = jnp.dot(score_grad.T, query_grp, preferred_element_type=jnp.float32)
        return (accum + jnp.concatenate([key_grad, value_grad], axis=-1), query_grad)

    start_accum = jnp.zeros((window_kv.shape[0], 2 * width), jnp.float32)
    accum, query_grads = lax.scan(
        per_group, start_accum, (query_rows, grad_rows, norm_rows, delta_rows)
    )
    query_grad = (
        query_grads.reshape(head_count, row_count, width)
        .transpose(1, 0, 2)
        .reshape(row_count, model_cols)
    )
    return (query_grad, accum)


def orthonormal(diffs):
    columns = []
    for index in range(diffs.shape[-2]):
        source = diffs[..., index, :]
        vector = source
        for previous in columns:
            vector = vector - jnp.mean(source * previous, axis=-1, keepdims=True) * previous
        columns.append(
            vector * lax.rsqrt(jnp.mean(vector * vector, axis=-1, keepdims=True) + epsilon)
        )
    return jnp.stack(columns, axis=-2)


def on_device(
    queries, keys, values, outputs, out_grad, log_norm, inputs, mlp_weight, initial_right_factor
):
    tok_rows = queries.shape[1]
    head_dim = keys.shape[2]
    own_kv = jnp.concatenate([keys[0], values[0]], axis=-1)
    span_blocks = WINDOW // tok_rows
    level_count = span_blocks.bit_length() - 1
    earlier_kv = own_kv
    for level_index in range(level_count + 1):
        payload = own_kv if level_index == 0 else earlier_kv
        distance = 1 if level_index == 0 else earlier_kv.shape[0] // tok_rows
        arrived = shifted(payload, "seq", distance)
        earlier_kv = arrived if level_index == 0 else jnp.concatenate([arrived, earlier_kv], axis=0)
    window_kv = jnp.concatenate([earlier_kv, own_kv], axis=0)
    first_query = lax.axis_index("seq") * tok_rows
    visible = window_mask(first_query, tok_rows, WINDOW)
    query_grad, window_grads = attend(
        queries[0], out_grad[0], outputs[0], log_norm[0], window_kv, visible, head_dim ** (-0.5)
    )
    remaining = window_grads[:WINDOW]
    own_grad = window_grads[WINDOW:]
    for level_index in range(level_count + 1):
        if level_index < level_count:
            half_rows = remaining.shape[0] // 2
            send_part = remaining[:half_rows]
            kept_part = remaining[half_rows:]
            distance = half_rows // tok_rows
        else:
            send_part = remaining
            kept_part = remaining
            distance = 1
        returned = shifted(send_part, "seq", -distance)
        if level_index < level_count:
            remaining = kept_part + returned
        else:
            own_grad = own_grad + returned
    kv_grad_b = own_grad.astype(jnp.bfloat16)
    input_local = inputs[0]
    input_cols = lax.all_to_all(input_local, "seq", split_axis=1, concat_axis=0, tiled=True)
    proj_grad = jnp.dot(
        input_cols.T,
        lax.all_gather(kv_grad_b, "seq", axis=0, tiled=True),
        preferred_element_type=jnp.float32,
    )
    weight_block = mlp_weight[0]
    acts = jnp.einsum(
        "kd,rd->kr", initial_right_factor[0], weight_block, preferred_element_type=jnp.float32
    )
    cycle_acts = extended(acts[None], (("rep", 0),), 1)
    diffs = jnp.stack([acts - cycle_acts[0], acts - cycle_acts[2]], axis=0)
    basis = orthonormal(diffs)
    contrib = jnp.einsum(
        "ekr,rd->ekd", basis.astype(jnp.bfloat16), weight_block, preferred_element_type=jnp.float32
    )
    cycle_contrib = extended(contrib, (("rep", 0),), 1)
    right_factor = jnp.stack([contrib[0] + cycle_contrib[0], contrib[1] + cycle_contrib[3]], axis=0)
    return (
        query_grad[None],
        own_grad[None],
        proj_grad[None],
        basis[None],
        right_factor[None, None],
    )


def solution(mesh):
    return jax.shard_map(
        on_device,
        mesh=mesh,
        in_specs=(
            P("rep", "seq", None),
            P("rep", "seq", None),
            P("rep", "seq", None),
            P("rep", "seq", None),
            P("rep", "seq", None),
            P("rep", None, "seq"),
            P("rep", "seq", None),
            P("rep", "seq", None),
            P("seq", None, None),
        ),
        out_specs=(
            P("rep", "seq", None),
            P("rep", "seq", None),
            P("rep", "seq", None),
            P("rep", None, None, "seq"),
            P("rep", "seq", None, None, None),
        ),
        check_vma=False,
    )
```

profile of v0, /device:TPU:0, one launch (start us, length us, event | category | flops | bytes accessed | tf_op | source)
XLA Modules:
  0.0 187.5 jit_solution(15382292193114890918)
XLA Ops:
  0.7 0.8 copy-done
  1.4 8.9 %fusion.20 = f32[4,1536]{1,0:T(4,128)S(1)} fusion(bf16[1,1536,6144]{2,1,0:T(8,128)(2,1)} %param.18, bf16[1,4,6144]{2,1,0:T(4,128)(2,1)S(1)} %copy-done), kind=kOutput, calls=%fused_computation.26 | convolution fusion | flops 75497472 | bytes 18948096 | tf_op jit(solution)/shard_map/kd,rd->kr/dot_general | solution.py:151
  10.3 3.0 %collective-permute-start.10 = (f32[1,4,1536]{2,1,0:T(4,128)S(1)}, f32[1,4,1536]{2,1,0:T(4,128)S(1)}, u32[]{:S(2)}, u32[]{:S(2)}) collective-permute-start(f32[1,4,1536]{2,1,0:T(4,128)S(1)} %bitcast.179), channel_id=1, source_target_pairs={{0,8},{8,16},{16,24},{24,0},{1,9},{9,17},{17,25},{25,1},{2,10},{10... | collective-permute-start | bytes 73736 | tf_op jit(solution)/shard_map/ppermute | solution.py:24
  13.3 1.0 collective-permute-start.11
  14.3 1.5 collective-permute-start
  15.8 1.6 copy.83
  17.4 6.2 %all-to-all-start = ((bf16[128,8,768]{0,2,1:T(8,128)(2,1)}), bf16[128,8,768]{0,2,1:T(8,128)(2,1)}, u32[]{:S(2)}, u32[]{:S(2)}) async-start(bf16[128,8,768]{0,2,1:T(8,128)(2,1)} %bitcast.11), calls=%async_computation | async-start | bytes 3145728 | tf_op jit(solution)/shard_map/all_to_all | solution.py:144
  24.0 0.3 copy.91
  24.2 0.5 multiply_reduce_fusion
  24.8 0.3 copy-done.11
  26.2 2.7 %collective-permute-start.1 = (bf16[128,256]{1,0:T(8,128)(2,1)S(1)}, bf16[128,256]{1,0:T(8,128)(2,1)S(1)}, u32[]{:S(2)}, u32[]{:S(2)}) collective-permute-start(bf16[128,256]{1,0:T(8,128)(2,1)S(1)} %collective-permute-done), channel_id=1, source_target_pairs={{0,1},{1,2},{2,3},{3,4},{4,5},{5,6},{6,7},{8,9},{9,10},{10,11},{11... | collective-permute-start | bytes 196616 | tf_op jit(solution)/shard_map/ppermute | solution.py:15
  29.1 0.7 collective-permute-done.1
  29.8 25.5 %collective-permute-start.2 = (bf16[256,256]{1,0:T(8,128)(2,1)S(1)}, bf16[256,256]{1,0:T(8,128)(2,1)S(1)}, u32[]{:S(2)}, u32[]{:S(2)}) collective-permute-start(bf16[256,256]{1,0:T(8,128)(2,1)S(1)} %pad_maximum_fusion.2), channel_id=1, source_target_pairs={{0,2},{1,3},{2,4},{3,5},{4,6},{5,7},{8,10},{9,11},{10,12},{11,13},... | collective-permute-start | bytes 393224 | tf_op jit(solution)/shard_map/ppermute | solution.py:15
  55.5 2.3 %collective-permute-done.2 = bf16[256,256]{1,0:T(8,128)(2,1)S(1)} collective-permute-done((bf16[256,256]{1,0:T(8,128)(2,1)S(1)}, bf16[256,256]{1,0:T(8,128)(2,1)S(1)}, u32[]{:S(2)}, u32[]{:S(2)}) %collective-permute-start.2) | collective-permute-done | bytes 131104 | tf_op jit(solution)/shard_map/ppermute | solution.py:15
  57.8 13.6 %collective-permute-start.3 = (bf16[512,256]{1,0:T(8,128)(2,1)S(1)}, bf16[512,256]{1,0:T(8,128)(2,1)S(1)}, u32[]{:S(2)}, u32[]{:S(2)}) collective-permute-start(bf16[512,256]{1,0:T(8,128)(2,1)S(1)} %pad_maximum_fusion.1), channel_id=1, source_target_pairs={{0,4},{1,5},{2,6},{3,7},{8,12},{9,13},{10,14},{11,15},{16,20},{17,... | collective-permute-start | bytes 786440 | tf_op jit(solution)/shard_map/ppermute | solution.py:15
  71.5 3.9 %collective-permute-done.3 = bf16[512,256]{1,0:T(8,128)(2,1)S(1)} collective-permute-done((bf16[512,256]{1,0:T(8,128)(2,1)S(1)}, bf16[512,256]{1,0:T(8,128)(2,1)S(1)}, u32[]{:S(2)}, u32[]{:S(2)}) %collective-permute-start.3) | collective-permute-done | bytes 262176 | tf_op jit(solution)/shard_map/ppermute | solution.py:15
  75.4 0.9 collective-permute-start.4
  77.0 39.6 %while.13 = (s32[]{:T(128)}, f32[2176,256]{0,1:T(8,128)}, f32[3,1024,128]{2,1,0:T(8,128)}, bf16[3,1024,128]{2,1,0:T(8,128)(2,1)S(1)}, bf16[2176,128]{1,0:T(8,128...) while((s32[]{:T(128)}, f32[2176,256]{0,1:T(8,128)}, ...), condition=%wide.region_2.3_spmd.clone, body=%wide.region_1.2_spmd.clone.sunk | while | flops 2872737792 | bytes 101093352 | solution.py:81
  77.0 0.7 dynamic-slice_bitcast_fusion.2
  77.7 0.4 compare_and_fusion.2
  78.1 2.2 %exponential_select_fusion.2 = f32[1024,2176]{1,0:T(8,128)S(1)} fusion(bf16[2176,128]{1,0:T(8,128)(2,1)S(1)} %get-tuple-element.311, f32[1024]{0:T(1024)S(1)} %dynamic-slice_bitcast_fusion.2, pred[128,2176]{1,0:T(8,128)(4,1)S(1)} %compare_and_fusion.2, bf16[3,1024,128]{2,1,0:T(8,128)(2,1)S(1)} %get-tuple-element.310, s32[]{:T(128)S(6)} %copy.105), kind=kOutput, calls=%fused_computation.2.clone.1 | convolution fusion | flops 577110016 | bytes 10014724 | tf_op jit(solution)/shard_map/while/body/eval_jaxpr/dot_general | solution.py:68
  80.3 0.9 fusion.80
  81.2 1.5 multiply_convert_fusion.2
  82.7 2.0 %fusion.81 = f32[2176,128]{0,1:T(8,128)S(1)} fusion(bf16[1024,2176]{1,0:T(8,128)(2,1)S(1)} %multiply_convert_fusion.2, bf16[3,1024,128]{2,1,0:T(8,128)(2,1)} %copy-done.6, s32[]{:T(128)S(6)} %copy.105), kind=kOutput, calls=%fused_computation.11.clone.1 | convolution fusion | flops 570425344 | bytes 5832708 | tf_op jit(solution)/shard_map/while/body/eval_jaxpr/dot_general | solution.py:77
  84.7 1.6 maximum_add_fusion.2
  86.4 1.4 copy-done.3
  87.8 2.1 %fusion.82 = f32[3,1024,128]{2,1,0:T(8,128)} fusion(f32[3,1024,128]{2,1,0:T(8,128)} %get-tuple-element.294, s32[]{:T(128)S(6)} %copy.105, bf16[1024,2176]{1,0:T(8,128)(2,1)S(1)} %copy-done.3, bf16[2176,128]{1,0:T(8,128)(2,1)S(1)} %get-tuple-element.311), kind=kOutput, calls=%fused_computation.7.clone.1 | convolution fusion | flops 570425344 | bytes 5537796 | tf_op jit(solution)/shard_map/while/body/eval_jaxpr/dot_general | solution.py:76
  89.9 0.7 dynamic-slice_bitcast_fusion.2
  90.7 0.4 compare_and_fusion.2
  91.0 2.2 %exponential_select_fusion.2 = f32[1024,2176]{1,0:T(8,128)S(1)} fusion(bf16[2176,128]{1,0:T(8,128)(2,1)S(1)} %get-tuple-element.311, f32[1024]{0:T(1024)S(1)} %dynamic-slice_bitcast_fusion.2, pred[128,2176]{1,0:T(8,128)(4,1)S(1)} %compare_and_fusion.2, bf16[3,1024,128]{2,1,0:T(8,128)(2,1)S(1)} %get-tuple-element.310, s32[]{:T(128)S(6)} %copy.105), kind=kOutput, calls=%fused_computation.2.clone.1 | convolution fusion | flops 577110016 | bytes 10014724 | tf_op jit(solution)/shard_map/while/body/eval_jaxpr/dot_general | solution.py:68
  93.2 0.9 fusion.80
  94.1 1.5 multiply_convert_fusion.2
  95.7 2.0 %fusion.81 = f32[2176,128]{0,1:T(8,128)S(1)} fusion(bf16[1024,2176]{1,0:T(8,128)(2,1)S(1)} %multiply_convert_fusion.2, bf16[3,1024,128]{2,1,0:T(8,128)(2,1)} %copy-done.6, s32[]{:T(128)S(6)} %copy.105), kind=kOutput, calls=%fused_computation.11.clone.1 | convolution fusion | flops 570425344 | bytes 5832708 | tf_op jit(solution)/shard_map/while/body/eval_jaxpr/dot_general | solution.py:77
  97.7 3.4 %maximum_add_fusion.2 = f32[2176,256]{0,1:T(8,128)} fusion(f32[2176,128]{0,1:T(8,128)S(1)} %fusion.80, f32[2176,128]{0,1:T(8,128)S(1)} %fusion.81, f32[2176,256]{0,1:T(8,128)} %get-tuple-element.293, pred[]{:T(512)S(6)} %compare.3), kind=kLoop, calls=%fused_computation.5.clone.1 | loop fusion | flops 1671168 | bytes 6684673 | tf_op jit(solution)/shard_map/while/body/eval_jaxpr/add | solution.py:78
  101.1 2.1 %fusion.82 = f32[3,1024,128]{2,1,0:T(8,128)} fusion(f32[3,1024,128]{2,1,0:T(8,128)} %get-tuple-element.294, s32[]{:T(128)S(6)} %copy.105, bf16[1024,2176]{1,0:T(8,128)(2,1)S(1)} %copy-done.3, bf16[2176,128]{1,0:T(8,128)(2,1)S(1)} %get-tuple-element.311), kind=kOutput, calls=%fused_computation.7.clone.1 | convolution fusion | flops 570425344 | bytes 5537796 | tf_op jit(solution)/shard_map/while/body/eval_jaxpr/dot_general | solution.py:76
  103.2 0.7 dynamic-slice_bitcast_fusion.2
  104.0 0.4 compare_and_fusion.2
  104.3 2.2 %exponential_select_fusion.2 = f32[1024,2176]{1,0:T(8,128)S(1)} fusion(bf16[2176,128]{1,0:T(8,128)(2,1)S(1)} %get-tuple-element.311, f32[1024]{0:T(1024)S(1)} %dynamic-slice_bitcast_fusion.2, pred[128,2176]{1,0:T(8,128)(4,1)S(1)} %compare_and_fusion.2, bf16[3,1024,128]{2,1,0:T(8,128)(2,1)S(1)} %get-tuple-element.310, s32[]{:T(128)S(6)} %copy.105), kind=kOutput, calls=%fused_computation.2.clone.1 | convolution fusion | flops 577110016 | bytes 10014724 | tf_op jit(solution)/shard_map/while/body/eval_jaxpr/dot_general | solution.py:68
  106.5 0.9 fusion.80
  107.4 1.5 multiply_convert_fusion.2
  108.9 2.0 %fusion.81 = f32[2176,128]{0,1:T(8,128)S(1)} fusion(bf16[1024,2176]{1,0:T(8,128)(2,1)S(1)} %multiply_convert_fusion.2, bf16[3,1024,128]{2,1,0:T(8,128)(2,1)} %copy-done.6, s32[]{:T(128)S(6)} %copy.105), kind=kOutput, calls=%fused_computation.11.clone.1 | convolution fusion | flops 570425344 | bytes 5832708 | tf_op jit(solution)/shard_map/while/body/eval_jaxpr/dot_general | solution.py:77
  111.0 3.4 %maximum_add_fusion.2 = f32[2176,256]{0,1:T(8,128)} fusion(f32[2176,128]{0,1:T(8,128)S(1)} %fusion.80, f32[2176,128]{0,1:T(8,128)S(1)} %fusion.81, f32[2176,256]{0,1:T(8,128)} %get-tuple-element.293, pred[]{:T(512)S(6)} %compare.3), kind=kLoop, calls=%fused_computation.5.clone.1 | loop fusion | flops 1671168 | bytes 6684673 | tf_op jit(solution)/shard_map/while/body/eval_jaxpr/add | solution.py:78
  114.4 2.1 %fusion.82 = f32[3,1024,128]{2,1,0:T(8,128)} fusion(f32[3,1024,128]{2,1,0:T(8,128)} %get-tuple-element.294, s32[]{:T(128)S(6)} %copy.105, bf16[1024,2176]{1,0:T(8,128)(2,1)S(1)} %copy-done.3, bf16[2176,128]{1,0:T(8,128)(2,1)S(1)} %get-tuple-element.311), kind=kOutput, calls=%fused_computation.7.clone.1 | convolution fusion | flops 570425344 | bytes 5537796 | tf_op jit(solution)/shard_map/while/body/eval_jaxpr/dot_general | solution.py:76
  116.5 2.0 %copy.80 = f32[2176,256]{1,0:T(8,128)S(1)} copy(f32[2176,256]{0,1:T(8,128)} %get-tuple-element.59) | data formatting | bytes 4456448 | tf_op jit(solution)/shard_map/while | solution.py:81
  118.6 0.7 collective-permute-start.5
  119.9 1.3 collective-permute-start.6
  121.2 9.0 %fusion.18 = f32[2,4,6144]{2,1,0:T(4,128)S(1)} fusion(bf16[1,1536,6144]{2,1,0:T(8,128)(2,1)} %param.18, bf16[2,4,1536]{2,0,1:T(2,128)(2,1)S(1)} %fusion.42), kind=kOutput, calls=%fused_computation.24 | convolution fusion | flops 150994944 | bytes 19095552 | tf_op jit(solution)/shard_map/ekr,rd->ekd/dot_general | solution.py:157
  130.3 16.1 %collective-permute-done.6 = f32[512,256]{1,0:T(8,128)S(1)} collective-permute-done((f32[512,256]{1,0:T(8,128)S(1)}, f32[512,256]{1,0:T(8,128)S(1)}, u32[]{:S(2)}, u32[]{:S(2)}) %collective-permute-start.6) | collective-permute-done | bytes 524320 | tf_op jit(solution)/shard_map/ppermute | solution.py:15
  146.5 1.3 collective-permute-start.7
  147.8 0.6 copy.88
  148.5 0.6 collective-permute-start.12
  149.1 2.3 %collective-permute-start.13 = (f32[1,4,6144]{2,1,0:T(4,128)S(1)}, f32[1,4,6144]{2,1,0:T(4,128)S(1)}, u32[]{:S(2)}, u32[]{:S(2)}) collective-permute-start(f32[1,4,6144]{2,1,0:T(4,128)S(1)} %get-tuple-element.189), channel_id=1, source_target_pairs={{8,0},{16,8},{24,16},{0,24},{9,1},{17,9},{25,17},{1,25},{10,2},{18... | collective-permute-start | bytes 294920 | tf_op jit(solution)/shard_map/ppermute | solution.py:27
  151.4 3.3 %collective-permute-done.7 = f32[256,256]{1,0:T(8,128)S(1)} collective-permute-done((f32[256,256]{1,0:T(8,128)S(1)}, f32[256,256]{1,0:T(8,128)S(1)}, u32[]{:S(2)}, u32[]{:S(2)}) %collective-permute-start.7) | collective-permute-done | bytes 262176 | tf_op jit(solution)/shard_map/ppermute | solution.py:15
  154.8 1.3 collective-permute-start.8
  156.2 1.9 collective-permute-done.8
  158.1 1.5 collective-permute-start.9
  159.6 0.7 maximum_bitcast_fusion
  160.3 2.1 %copy.95 = f32[24,128,128]{2,0,1:T(8,128)} copy(f32[24,128,128]{2,1,0:T(8,128)S(1)} %bitcast.170) | data formatting | bytes 3145728 | tf_op jit(solution)/shard_map/reshape | solution.py:85
  162.4 2.5 %broadcast_in_dim_reshape.3 = f32[1,128,3072]{2,1,0:T(8,128)} reshape(f32[128,24,128]{2,1,0:T(8,128)} %bitcast.167) | data formatting | bytes 3145728 | tf_op jit(solution)/shard_map/broadcast_in_dim;reshape | solution.py:163
  164.9 2.6 %copy.84 = bf16[8,128,768]{2,1,0:T(8,128)(2,1)} copy(bf16[8,128,768]{1,2,0:T(8,128)(2,1)} %bitcast.12) | data formatting | bytes 3145728 | tf_op jit(solution)/shard_map/all_to_all | solution.py:144
  167.6 0.7 fusion.22
  168.2 16.1 %all_gather.3 = bf16[1024,256]{1,0:T(8,128)(2,1)S(1)} all-gather(bf16[128,256]{1,0:T(8,128)(2,1)S(1)} %get-tuple-element.182), channel_id=1, replica_groups=mesh['rep'=4,'seq'=8] {'seq'}, dimensions={0}, use_global_device_ids=true | all-gather | bytes 589824 | tf_op jit(solution)/shard_map/all_gather | solution.py:147
  184.4 2.0 %convolution_bitcast_fusion.1 = f32[1,768,256]{1,2,0:T(8,128)S(1)} fusion(bf16[1024,256]{1,0:T(8,128)(2,1)S(1)} %all_gather.3, bf16[1024,768]{1,0:T(8,128)(2,1)} %bitcast.168), kind=kOutput, calls=%fused_computation.31 | convolution fusion | flops 402653184 | bytes 2883584 | tf_op jit(solution)/shard_map/dot_general | solution.py:145
  186.4 1.2 copy.87
  (117 shorter events, 3.5 us)
Async XLA Ops:
  0.6 0.8 copy-start
  0.6 13.7 %copy-start.13 = (bf16[1,128,128]{2,1,0:T(8,128)(2,1)S(1)}, bf16[1,128,128]{2,1,0:T(8,128)(2,1)}, u32[]{:S(2)}) copy-start(bf16[1,128,128]{2,1,0:T(8,128)(2,1)} %param.13) | copy-start | bytes 98308
  0.7 13.7 %copy-start.14 = (bf16[1,128,128]{2,1,0:T(8,128)(2,1)S(1)}, bf16[1,128,128]{2,1,0:T(8,128)(2,1)}, u32[]{:S(2)}) copy-start(bf16[1,128,128]{2,1,0:T(8,128)(2,1)} %param.12) | copy-start | bytes 98308
  0.7 15.1 %copy-start.8 = (bf16[1,128,6144]{2,1,0:T(8,128)(2,1)S(1)}, bf16[1,128,6144]{2,1,0:T(8,128)(2,1)}, u32[]{:S(2)}) copy-start(bf16[1,128,6144]{2,1,0:T(8,128)(2,1)} %param.17) | copy-start | bytes 4718596
  10.3 15.3 %collective-permute-start.10 = (f32[1,4,1536]{2,1,0:T(4,128)S(1)}, f32[1,4,1536]{2,1,0:T(4,128)S(1)}, u32[]{:S(2)}, u32[]{:S(2)}) collective-permute-start(f32[1,4,1536]{2,1,0:T(4,128)S(1)} %bitcast.179), channel_id=1, source_target_pairs={{0,8},{8,16},{16,24},{24,0},{1,9},{9,17},{17,25},{25,1},{2,10},{10... | collective-permute-start | bytes 73736 | tf_op jit(solution)/shard_map/ppermute | solution.py:24
  13.3 12.4 %collective-permute-start.11 = (f32[1,4,1536]{2,1,0:T(4,128)S(1)}, f32[1,4,1536]{2,1,0:T(4,128)S(1)}, u32[]{:S(2)}, u32[]{:S(2)}) collective-permute-start(f32[1,4,1536]{2,1,0:T(4,128)S(1)} %bitcast.180), channel_id=1, source_target_pairs={{8,0},{16,8},{24,16},{0,24},{9,1},{17,9},{25,17},{1,25},{10,2},{18... | collective-permute-start | bytes 73736 | tf_op jit(solution)/shard_map/ppermute | solution.py:27
  14.3 11.8 %collective-permute-start = (bf16[128,256]{1,0:T(8,128)(2,1)S(1)}, bf16[128,256]{1,0:T(8,128)(2,1)S(1)}, u32[]{:S(2)}, u32[]{:S(2)}) collective-permute-start(bf16[128,256]{1,0:T(8,128)(2,1)S(1)} %pad_maximum_fusion.3), channel_id=1, source_target_pairs={{0,1},{1,2},{2,3},{3,4},{4,5},{5,6},{6,7},{8,9},{9,10},{10,11},{11... | collective-permute-start | bytes 196616 | tf_op jit(solution)/shard_map/ppermute | solution.py:15
  17.4 6.2 %copy-start.10 = (bf16[1,128,3072]{2,1,0:T(8,128)(2,1)S(1)}, bf16[1,128,3072]{2,1,0:T(8,128)(2,1)}, u32[]{:S(2)}) copy-start(bf16[1,128,3072]{2,1,0:T(8,128)(2,1)} %param.15) | copy-start | bytes 2359300
  17.4 6.4 %copy-start.12 = (bf16[1,128,3072]{2,1,0:T(8,128)(2,1)S(1)}, bf16[1,128,3072]{2,1,0:T(8,128)(2,1)}, u32[]{:S(2)}) copy-start(bf16[1,128,3072]{2,1,0:T(8,128)(2,1)} %param.14) | copy-start | bytes 2359300
  17.4 147.5 %all-to-all-start = ((bf16[128,8,768]{0,2,1:T(8,128)(2,1)}), bf16[128,8,768]{0,2,1:T(8,128)(2,1)}, u32[]{:S(2)}, u32[]{:S(2)}) async-start(bf16[128,8,768]{0,2,1:T(8,128)(2,1)} %bitcast.11), calls=%async_computation | async-start | bytes 3145728 | tf_op jit(solution)/shard_map/all_to_all | solution.py:144
  24.0 1.1 copy-start.11
  26.2 3.6 %collective-permute-start.1 = (bf16[128,256]{1,0:T(8,128)(2,1)S(1)}, bf16[128,256]{1,0:T(8,128)(2,1)S(1)}, u32[]{:S(2)}, u32[]{:S(2)}) collective-permute-start(bf16[128,256]{1,0:T(8,128)(2,1)S(1)} %collective-permute-done), channel_id=1, source_target_pairs={{0,1},{1,2},{2,3},{3,4},{4,5},{5,6},{6,7},{8,9},{9,10},{10,11},{11... | collective-permute-start | bytes 196616 | tf_op jit(solution)/shard_map/ppermute | solution.py:15
  29.8 28.0 %collective-permute-start.2 = (bf16[256,256]{1,0:T(8,128)(2,1)S(1)}, bf16[256,256]{1,0:T(8,128)(2,1)S(1)}, u32[]{:S(2)}, u32[]{:S(2)}) collective-permute-start(bf16[256,256]{1,0:T(8,128)(2,1)S(1)} %pad_maximum_fusion.2), channel_id=1, source_target_pairs={{0,2},{1,3},{2,4},{3,5},{4,6},{5,7},{8,10},{9,11},{10,12},{11,13},... | collective-permute-start | bytes 393224 | tf_op jit(solution)/shard_map/ppermute | solution.py:15
  57.8 17.6 %collective-permute-start.3 = (bf16[512,256]{1,0:T(8,128)(2,1)S(1)}, bf16[512,256]{1,0:T(8,128)(2,1)S(1)}, u32[]{:S(2)}, u32[]{:S(2)}) collective-permute-start(bf16[512,256]{1,0:T(8,128)(2,1)S(1)} %pad_maximum_fusion.1), channel_id=1, source_target_pairs={{0,4},{1,5},{2,6},{3,7},{8,12},{9,13},{10,14},{11,15},{16,20},{17,... | collective-permute-start | bytes 786440 | tf_op jit(solution)/shard_map/ppermute | solution.py:15
  75.4 1.3 collective-permute-start.4
  77.0 3.3 %copy-start.6 = (bf16[3,1024,128]{2,1,0:T(8,128)(2,1)}, bf16[3,1024,128]{2,1,0:T(8,128)(2,1)S(1)}, u32[]{:S(2)}) copy-start(bf16[3,1024,128]{2,1,0:T(8,128)(2,1)S(1)} %get-tuple-element.310) | copy-start | bytes 2359300 | tf_op jit(solution)/shard_map/while
  77.0 4.2 %copy-start.4 = (bf16[3,1024,128]{2,1,0:T(8,128)(2,1)}, bf16[3,1024,128]{2,1,0:T(8,128)(2,1)S(1)}, u32[]{:S(2)}) copy-start(bf16[3,1024,128]{2,1,0:T(8,128)(2,1)S(1)} %get-tuple-element.313) | copy-start | bytes 2359300 | tf_op jit(solution)/shard_map/while
  82.7 2.0 %copy-start.2 = (bf16[1024,2176]{1,0:T(8,128)(2,1)}, bf16[1024,2176]{1,0:T(8,128)(2,1)S(1)}, u32[]{:S(2)}) copy-start(bf16[1024,2176]{1,0:T(8,128)(2,1)S(1)} %multiply_convert_fusion.2) | copy-start | bytes 13369348 | tf_op jit(solution)/shard_map/while
  84.7 3.1 %copy-start.3 = (bf16[1024,2176]{1,0:T(8,128)(2,1)S(1)}, bf16[1024,2176]{1,0:T(8,128)(2,1)}, u32[]{:S(2)}) copy-start(bf16[1024,2176]{1,0:T(8,128)(2,1)} %copy-done.2) | copy-start | bytes 13369348 | tf_op jit(solution)/shard_map/while
  87.8 2.1 %copy-start.5 = (bf16[3,1024,128]{2,1,0:T(8,128)(2,1)S(1)}, bf16[3,1024,128]{2,1,0:T(8,128)(2,1)}, u32[]{:S(2)}) copy-start(bf16[3,1024,128]{2,1,0:T(8,128)(2,1)} %copy-done.4) | copy-start | bytes 2359300 | tf_op jit(solution)/shard_map/while
  87.8 2.1 %copy-start.7 = (bf16[3,1024,128]{2,1,0:T(8,128)(2,1)S(1)}, bf16[3,1024,128]{2,1,0:T(8,128)(2,1)}, u32[]{:S(2)}) copy-start(bf16[3,1024,128]{2,1,0:T(8,128)(2,1)} %copy-done.6) | copy-start | bytes 2359300 | tf_op jit(solution)/shard_map/while
  89.9 3.3 %copy-start.6 = (bf16[3,1024,128]{2,1,0:T(8,128)(2,1)}, bf16[3,1024,128]{2,1,0:T(8,128)(2,1)S(1)}, u32[]{:S(2)}) copy-start(bf16[3,1024,128]{2,1,0:T(8,128)(2,1)S(1)} %get-tuple-element.310) | copy-start | bytes 2359300 | tf_op jit(solution)/shard_map/while
  89.9 4.2 %copy-start.4 = (bf16[3,1024,128]{2,1,0:T(8,128)(2,1)}, bf16[3,1024,128]{2,1,0:T(8,128)(2,1)S(1)}, u32[]{:S(2)}) copy-start(bf16[3,1024,128]{2,1,0:T(8,128)(2,1)S(1)} %get-tuple-element.313) | copy-start | bytes 2359300 | tf_op jit(solution)/shard_map/while
  95.6 2.0 %copy-start.2 = (bf16[1024,2176]{1,0:T(8,128)(2,1)}, bf16[1024,2176]{1,0:T(8,128)(2,1)S(1)}, u32[]{:S(2)}) copy-start(bf16[1024,2176]{1,0:T(8,128)(2,1)S(1)} %multiply_convert_fusion.2) | copy-start | bytes 13369348 | tf_op jit(solution)/shard_map/while
  97.7 3.4 %copy-start.3 = (bf16[1024,2176]{1,0:T(8,128)(2,1)S(1)}, bf16[1024,2176]{1,0:T(8,128)(2,1)}, u32[]{:S(2)}) copy-start(bf16[1024,2176]{1,0:T(8,128)(2,1)} %copy-done.2) | copy-start | bytes 13369348 | tf_op jit(solution)/shard_map/while
  101.1 2.1 %copy-start.5 = (bf16[3,1024,128]{2,1,0:T(8,128)(2,1)S(1)}, bf16[3,1024,128]{2,1,0:T(8,128)(2,1)}, u32[]{:S(2)}) copy-start(bf16[3,1024,128]{2,1,0:T(8,128)(2,1)} %copy-done.4) | copy-start | bytes 2359300 | tf_op jit(solution)/shard_map/while
  101.1 2.1 %copy-start.7 = (bf16[3,1024,128]{2,1,0:T(8,128)(2,1)S(1)}, bf16[3,1024,128]{2,1,0:T(8,128)(2,1)}, u32[]{:S(2)}) copy-start(bf16[3,1024,128]{2,1,0:T(8,128)(2,1)} %copy-done.6) | copy-start | bytes 2359300 | tf_op jit(solution)/shard_map/while
  103.2 3.3 %copy-start.6 = (bf16[3,1024,128]{2,1,0:T(8,128)(2,1)}, bf16[3,1024,128]{2,1,0:T(8,128)(2,1)S(1)}, u32[]{:S(2)}) copy-start(bf16[3,1024,128]{2,1,0:T(8,128)(2,1)S(1)} %get-tuple-element.310) | copy-start | bytes 2359300 | tf_op jit(solution)/shard_map/while
  103.2 4.2 %copy-start.4 = (bf16[3,1024,128]{2,1,0:T(8,128)(2,1)}, bf16[3,1024,128]{2,1,0:T(8,128)(2,1)S(1)}, u32[]{:S(2)}) copy-start(bf16[3,1024,128]{2,1,0:T(8,128)(2,1)S(1)} %get-tuple-element.313) | copy-start | bytes 2359300 | tf_op jit(solution)/shard_map/while
  108.9 2.0 %copy-start.2 = (bf16[1024,2176]{1,0:T(8,128)(2,1)}, bf16[1024,2176]{1,0:T(8,128)(2,1)S(1)}, u32[]{:S(2)}) copy-start(bf16[1024,2176]{1,0:T(8,128)(2,1)S(1)} %multiply_convert_fusion.2) | copy-start | bytes 13369348 | tf_op jit(solution)/shard_map/while
  111.0 3.4 %copy-start.3 = (bf16[1024,2176]{1,0:T(8,128)(2,1)S(1)}, bf16[1024,2176]{1,0:T(8,128)(2,1)}, u32[]{:S(2)}) copy-start(bf16[1024,2176]{1,0:T(8,128)(2,1)} %copy-done.2) | copy-start | bytes 13369348 | tf_op jit(solution)/shard_map/while
  114.4 2.1 %copy-start.5 = (bf16[3,1024,128]{2,1,0:T(8,128)(2,1)S(1)}, bf16[3,1024,128]{2,1,0:T(8,128)(2,1)}, u32[]{:S(2)}) copy-start(bf16[3,1024,128]{2,1,0:T(8,128)(2,1)} %copy-done.4) | copy-start | bytes 2359300 | tf_op jit(solution)/shard_map/while
  114.4 2.1 %copy-start.7 = (bf16[3,1024,128]{2,1,0:T(8,128)(2,1)S(1)}, bf16[3,1024,128]{2,1,0:T(8,128)(2,1)}, u32[]{:S(2)}) copy-start(bf16[3,1024,128]{2,1,0:T(8,128)(2,1)} %copy-done.6) | copy-start | bytes 2359300 | tf_op jit(solution)/shard_map/while
  118.6 1.1 collective-permute-start.5
  119.9 26.5 %collective-permute-start.6 = (f32[512,256]{1,0:T(8,128)S(1)}, f32[512,256]{1,0:T(8,128)S(1)}, u32[]{:S(2)}, u32[]{:S(2)}) collective-permute-start(f32[512,256]{1,0:T(8,128)S(1)} %slice.79), channel_id=1, source_target_pairs={{4,0},{5,1},{6,2},{7,3},{12,8},{13,9},{14,10},{15,11},{20,16},{21,... | collective-permute-start | bytes 1572872 | tf_op jit(solution)/shard_map/ppermute | solution.py:15
  130.3 30.1 %copy-start.9 = (f32[3,1024,128]{2,1,0:T(8,128)S(1)}, f32[3,1024,128]{2,1,0:T(8,128)}, u32[]{:S(2)}) copy-start(f32[3,1024,128]{2,1,0:T(8,128)} %get-tuple-element.58) | copy-start | bytes 4718596
  146.5 8.3 %collective-permute-start.7 = (f32[256,256]{1,0:T(8,128)S(1)}, f32[256,256]{1,0:T(8,128)S(1)}, u32[]{:S(2)}, u32[]{:S(2)}) collective-permute-start(f32[256,256]{1,0:T(8,128)S(1)} %slice.81), channel_id=1, source_target_pairs={{2,0},{3,1},{4,2},{5,3},{6,4},{7,5},{10,8},{11,9},{12,10},{13,11},... | collective-permute-start | bytes 786440 | tf_op jit(solution)/shard_map/ppermute | solution.py:15
  148.5 7.6 %collective-permute-start.12 = (f32[1,4,6144]{2,1,0:T(4,128)S(1)}, f32[1,4,6144]{2,1,0:T(4,128)S(1)}, u32[]{:S(2)}, u32[]{:S(2)}) collective-permute-start(f32[1,4,6144]{2,1,0:T(4,128)S(1)} %get-tuple-element.188), channel_id=1, source_target_pairs={{0,8},{8,16},{16,24},{24,0},{1,9},{9,17},{17,25},{25,1},{2,10},{10... | collective-permute-start | bytes 294920 | tf_op jit(solution)/shard_map/ppermute | solution.py:24
  149.1 7.0 %collective-permute-start.13 = (f32[1,4,6144]{2,1,0:T(4,128)S(1)}, f32[1,4,6144]{2,1,0:T(4,128)S(1)}, u32[]{:S(2)}, u32[]{:S(2)}) collective-permute-start(f32[1,4,6144]{2,1,0:T(4,128)S(1)} %get-tuple-element.189), channel_id=1, source_target_pairs={{8,0},{16,8},{24,16},{0,24},{9,1},{17,9},{25,17},{1,25},{10,2},{18... | collective-permute-start | bytes 294920 | tf_op jit(solution)/shard_map/ppermute | solution.py:27
  154.8 3.2 %collective-permute-start.8 = (f32[128,256]{1,0:T(8,128)S(1)}, f32[128,256]{1,0:T(8,128)S(1)}, u32[]{:S(2)}, u32[]{:S(2)}) collective-permute-start(f32[128,256]{1,0:T(8,128)S(1)} %slice.83), channel_id=1, source_target_pairs={{1,0},{2,1},{3,2},{4,3},{5,4},{6,5},{7,6},{9,8},{10,9},{11,10},{12... | collective-permute-start | bytes 393224 | tf_op jit(solution)/shard_map/ppermute | solution.py:15
  158.1 9.5 %collective-permute-start.9 = (f32[128,256]{1,0:T(8,128)S(1)}, f32[128,256]{1,0:T(8,128)S(1)}, u32[]{:S(2)}, u32[]{:S(2)}) collective-permute-start(f32[128,256]{1,0:T(8,128)S(1)} %slice_add_fusion.3), channel_id=1, source_target_pairs={{1,0},{2,1},{3,2},{4,3},{5,4},{6,5},{7,6},{9,8},{10,9},{11,10},{12... | collective-permute-start | bytes 393224 | tf_op jit(solution)/shard_map/ppermute | solution.py:15
  184.4 3.2 %copy-start.1 = (bf16[1,4,6144]{2,1,0:T(4,128)(2,1)S(1)}, bf16[1,4,6144]{2,1,0:T(4,128)(2,1)}, u32[]{:S(2)}) copy-start(bf16[1,4,6144]{2,1,0:T(4,128)(2,1)} %param.19) | copy-start | bytes 147460
where the time goes:
time: 188 us
  starting transfers between devices  63.4 us (34%)
  matrix products  45.9 us (24%)
  waiting for transfers between devices  28.2 us (15%)
  local copies, waits for them, and re-layouts  18.9 us (10%)
  blocking collectives  16.1 us (9%)
  other arithmetic  13.6 us (7%)
    ppermute x10, starting transfers between devices, shifted(): return lax.ppermute(block, axis, route)  50.3 us
    ppermute x10, waiting for transfers between devices, shifted(): return lax.ppermute(block, axis, route)  28.2 us
    all_gather x1, blocking collectives, on_device(): lax.all_gather(kv_grad_b, 'seq', axis=0, tiled=True)  16.1 us
    dot_general x1, matrix products, on_device(): jnp.einsum('ekr,rd->ekd', basis.astype(jnp.bfloat16), weight_block, prefe...  9.03 us
    dot_general x1, matrix products, on_device(): jnp.einsum('kd,rd->kr', initial_right_factor[0], weight_block, preferred_...  8.9 us
    add x3, other arithmetic, per_group(): accum + jnp.concatenate([key_grad, value_grad], axis=-1)  8.49 us
    dot_general x3, matrix products, per_group(): jnp.dot(query_grp, key_mat.T, preferred_element_type=jnp.float32) * scale  6.55 us
    dot_general x3, matrix products, per_group(): jnp.dot(score_grad, key_mat, preferred_element_type=jnp.float32)  6.36 us
  transfers between devices with their start and end apart: 15, of which 6 were waited for; matrix products, arithmetic and copies ran while one was open for 34% of the time, Pallas kernels for 0%

commit v1 on v0

v1 whole, which is shorter than its diff:
```python
import functools
import math

import jax
import jax.numpy as jnp
from jax import lax
from jax.experimental import pallas as pl
from jax.experimental.pallas import tpu as pltpu
from jax.sharding import PartitionSpec as P

WINDOW = 2048
EPSILON = 1e-06
LOG2E = math.log2(math.e)
F32 = jnp.float32
BF16 = jnp.bfloat16
VMEM_LIMIT = 48 * 1024 * 1024


def dot_nt(a, b):
    return lax.dot_general(a, b, (((1,), (1,)), ((), ())), preferred_element_type=F32)


def dot_tn(a, b):
    return lax.dot_general(a, b, (((0,), (0,)), ((), ())), preferred_element_type=F32)


def vmem_specs(count):
    return [pl.BlockSpec(memory_space=pltpu.VMEM)] * count


def delta_kernel(head_dim, grad_ref, out_ref, delta_ref):
    for head in range(delta_ref.shape[0]):
        cols = slice(head * head_dim, (head + 1) * head_dim)
        prod = grad_ref[:, cols].astype(F32) * out_ref[:, cols].astype(F32)
        delta_ref[head : head + 1, :] = jnp.sum(prod.T, axis=0, keepdims=True)


def head_delta(out_grad, outputs, heads):
    rows, cols = out_grad.shape
    return pl.pallas_call(
        functools.partial(delta_kernel, cols // heads),
        out_shape=jax.ShapeDtypeStruct((heads, rows), F32),
        in_specs=vmem_specs(2),
        out_specs=pl.BlockSpec(memory_space=pltpu.VMEM),
        compiler_params=pltpu.CompilerParams(vmem_limit_bytes=VMEM_LIMIT),
        cost_estimate=pl.CostEstimate(
            flops=2 * rows * cols, bytes_accessed=4 * rows * cols, transcendentals=0
        ),
    )(out_grad, outputs)


def attention_kernel(blocks, group, scale, me_ref, q_ref, do_ref, norm_ref, delta_ref, *refs):
    kv_refs = refs[:blocks]
    qg_ref = refs[blocks]
    grad_refs = refs[blocks + 1 : 2 * blocks + 1]
    acc_ref, kt_ref, qgt_ref = refs[2 * blocks + 1 :]
    tok = q_ref.shape[0]
    span, hd = kv_refs[0].shape[0], kv_refs[0].shape[1] // 2
    heads = norm_ref.shape[0]
    me = me_ref[0]
    acc_ref[...] = jnp.zeros_like(acc_ref)
    for k in range(blocks):
        kt_ref[k] = kv_refs[k][:, :hd].T

    def step(index, carry):
        def stacked(ref):
            parts = []
            for i in range(group):
                first = pl.multiple_of((index * group + i) * hd, hd)
                parts.append(ref[:, pl.ds(first, hd)])
            return jnp.concatenate(parts, axis=0)

        def row(ref):
            return jnp.concatenate(
                [ref[pl.ds(index * group + i, 1), :] for i in range(group)], axis=1
            )

        q = stacked(q_ref)
        do = stacked(do_ref)
        norm = row(norm_ref) * LOG2E
        delta = row(delta_ref)
        qgt = None
        for k in range(blocks):
            key = kv_refs[k][:, :hd]
            value = kv_refs[k][:, hd:]
            probs = jnp.exp2(dot_nt(key, q) * (scale * LOG2E) - norm)
            if k == 0 or (k + 1) * span > WINDOW:
                shape = probs.shape
                key_pos = (me // 2 - k) * span + lax.broadcasted_iota(jnp.int32, shape, 0)
                query = lax.broadcasted_iota(jnp.int32, shape, 1)
                query_pos = me * tok + lax.rem(query, tok)
                visible = (key_pos <= query_pos) & (key_pos > query_pos - WINDOW)
                probs = jnp.where(visible, probs, 0.0)
            prob_grad = dot_nt(value, do)
            score_grad = (scale * probs * (prob_grad - delta)).astype(BF16)
            acc_ref[k, :, hd:] += jnp.dot(probs.astype(BF16), do, preferred_element_type=F32)
            acc_ref[k, :, :hd] += jnp.dot(score_grad, q, preferred_element_type=F32)
            part = jnp.dot(kt_ref[k], score_grad, preferred_element_type=F32)
            qgt = part if qgt is None else qgt + part
        qgt_ref[...] = qgt
        for i in range(group):
            first = pl.multiple_of((index * group + i) * hd, hd)
            qg_ref[:, pl.ds(first, hd)] = qgt_ref[:, i * tok : (i + 1) * tok].T
        return carry

    lax.fori_loop(0, heads // group, step, 0)
    for k in range(blocks):
        grad_refs[k][...] = acc_ref[k].astype(grad_refs[k].dtype)


def attend(me, queries, out_grad, norm, delta, kvs):
    tok, cols = queries.shape
    heads = norm.shape[0]
    hd = cols // heads
    span = kvs[0].shape[0]
    blocks = len(kvs)
    group = next(g for g in (4, 3, 2, 1) if heads % g == 0)
    outs = [jax.ShapeDtypeStruct((tok, cols), F32), jax.ShapeDtypeStruct((span, 2 * hd), F32)]
    outs += [jax.ShapeDtypeStruct((span, 2 * hd), BF16)] * (blocks - 1)
    work = heads * tok * span * blocks
    return pl.pallas_call(
        functools.partial(attention_kernel, blocks, group, hd ** (-0.5)),
        out_shape=outs,
        in_specs=[pl.BlockSpec(memory_space=pltpu.SMEM)] + vmem_specs(4 + blocks),
        out_specs=vmem_specs(len(outs)),
        scratch_shapes=[
            pltpu.VMEM((blocks, span, 2 * hd), F32),
            pltpu.VMEM((blocks, hd, span), BF16),
            pltpu.VMEM((hd, group * tok), F32),
        ],
        compiler_params=pltpu.CompilerParams(vmem_limit_bytes=VMEM_LIMIT),
        cost_estimate=pl.CostEstimate(
            flops=20 * work * hd, bytes_accessed=8 * tok * cols, transcendentals=work
        ),
    )(me[None], queries, out_grad, norm, delta, *kvs)


def project_kernel(chips, me_ref, x_ref, *refs):
    grad_refs, out_ref = refs[:chips], refs[chips]
    tok, width = x_ref.shape[1:]
    chip = me_ref[0] // 2
    total = None
    for k in range(chips):
        source = lax.rem(chip - k + chips, chips)
        x = x_ref[pl.ds(2 * source, 2)].reshape(2 * tok, width)
        part = dot_tn(x, grad_refs[k][...])
        total = part if total is None else total + part
    out_ref[...] = total


def project(me, blocks, grads):
    count, tok, width = blocks.shape
    cols = grads[0].shape[1]
    return pl.pallas_call(
        functools.partial(project_kernel, len(grads)),
        out_shape=jax.ShapeDtypeStruct((width, cols), F32),
        in_specs=[pl.BlockSpec(memory_space=pltpu.SMEM)] + vmem_specs(1 + len(grads)),
        out_specs=pl.BlockSpec(memory_space=pltpu.VMEM),
        compiler_params=pltpu.CompilerParams(vmem_limit_bytes=VMEM_LIMIT),
        cost_estimate=pl.CostEstimate(
            flops=2 * count * tok * width * cols,
            bytes_accessed=2 * count * tok * width,
            transcendentals=0,
        ),
    )(me[None], blocks, *grads)


def orthonormal(diffs):
    columns = []
    for index in range(diffs.shape[-2]):
        source = diffs[..., index, :]
        vector = source
        for previous in columns:
            vector = vector - jnp.mean(source * previous, axis=-1, keepdims=True) * previous
        columns.append(
            vector * lax.rsqrt(jnp.mean(vector * vector, axis=-1, keepdims=True) + EPSILON)
        )
    return jnp.stack(columns, axis=-2)


def from_cycle(block, axis, distance):
    count = lax.axis_size(axis)
    return lax.ppermute(block, axis, [(i, (i + distance) % count) for i in range(count)])


def from_line(block, axis, distance):
    count = lax.axis_size(axis)
    route = [(i, i + distance) for i in range(count) if 0 <= i + distance < count]
    return lax.ppermute(block, axis, route)


def from_partner(block, axis):
    count = lax.axis_size(axis)
    return lax.ppermute(block, axis, [(i, i ^ 1) for i in range(count)])


def on_device(
    queries, keys, values, outputs, out_grad, log_norm, inputs, mlp_weight, initial_right_factor
):
    tok = queries.shape[1]
    heads = log_norm.shape[1]
    count = lax.axis_size("seq")
    chips = count // 2
    me = lax.axis_index("seq")
    odd = lax.rem(me, 2) == 1
    reach = min(chips - 1, -(-WINDOW // (2 * tok)))

    own_kv = jnp.concatenate([keys[0], values[0]], axis=-1)
    other_kv = from_partner(own_kv, "seq")
    chip_kv = jnp.concatenate(
        [jnp.where(odd, other_kv, own_kv), jnp.where(odd, own_kv, other_kv)], axis=0
    )
    kvs = [chip_kv] + [from_line(chip_kv, "seq", 2 * k) for k in range(1, reach + 1)]

    width = inputs.shape[2] // count
    split_inputs = inputs[0].reshape(tok, count, width).transpose(1, 0, 2)
    split_inputs, kvs = lax.optimization_barrier((split_inputs, kvs))
    feature_blocks = lax.all_to_all(
        split_inputs, "seq", split_axis=0, concat_axis=0, tiled=True
    )

    delta = head_delta(out_grad[0], outputs[0], heads)
    query_grad, chip_grad, *sent = attend(me, queries[0], out_grad[0], log_norm[0], delta, kvs)
    for k, part in enumerate(sent, 1):
        chip_grad = chip_grad + from_line(part, "seq", -2 * k).astype(F32)
    chip_grad = chip_grad + from_partner(chip_grad, "seq")
    own_grad = jnp.where(odd, chip_grad[tok:], chip_grad[:tok])
    chip_grad_b = chip_grad.astype(BF16)
    grads = [chip_grad_b] + [from_cycle(chip_grad_b, "seq", 2 * k) for k in range(1, chips)]
    proj_grad = project(me, feature_blocks, grads)

    weight_block = mlp_weight[0]
    acts = jnp.einsum(
        "kd,rd->kr", initial_right_factor[0], weight_block, preferred_element_type=F32
    )
    lower_acts = from_cycle(acts, "rep", 1)
    higher_acts = from_cycle(acts, "rep", -1)
    basis = orthonormal(jnp.stack([acts - lower_acts, acts - higher_acts], axis=0))
    contrib = jnp.einsum(
        "ekr,rd->ekd", basis.astype(BF16), weight_block, preferred_element_type=F32
    )
    lower_half = from_cycle(contrib[1], "rep", 1)
    higher_half = from_cycle(contrib[0], "rep", -1)
    right_factor = jnp.stack([contrib[0] + lower_half, contrib[1] + higher_half], axis=0)
    return (
        query_grad[None],
        own_grad[None],
        proj_grad[None],
        basis[None],
        right_factor[None, None],
    )


def solution(mesh):
    return jax.shard_map(
        on_device,
        mesh=mesh,
        in_specs=(
            P("rep", "seq", None),
            P("rep", "seq", None),
            P("rep", "seq", None),
            P("rep", "seq", None),
            P("rep", "seq", None),
            P("rep", None, "seq"),
            P("rep", "seq", None),
            P("rep", "seq", None),
            P("seq", None, None),
        ),
        out_specs=(
            P("rep", "seq", None),
            P("rep", "seq", None),
            P("rep", "seq", None),
            P("rep", None, None, "seq"),
            P("rep", "seq", None, None, None),
        ),
        check_vma=False,
    )
```

time: 188 us -> 119 us (0.63)
  starting transfers between devices: 63.4 us -> 29.7 us
  matrix products: 45.9 us -> 17.9 us
  blocking collectives: 16.1 us -> 0 us
  waiting for transfers between devices: 28.2 us -> 42.4 us
  Pallas kernels: 0 us -> 13.2 us
  other arithmetic: 13.6 us -> 4.14 us
  local copies, waits for them, and re-layouts: 18.9 us -> 10.5 us
    ppermute x14 -> x15, starting transfers between devices: 57.2 us -> 22.2 us  [the longest x6 13.1 us: from_line(): return lax.ppermute(block, axis, route)]
    dot_general x17 -> x1, matrix products: 37 us -> 9.04 us  [on_device(): jnp.einsum('ekr,rd->ekd', basis.astype(BF16), weight_block, preferred_ele...]
    all_gather x1 -> x0, blocking collectives: 16.1 us -> none  [on_device(): lax.all_gather(kv_grad_b, 'seq', axis=0, tiled=True)]
    ppermute x14 -> x15, waiting for transfers between devices: 28.2 us -> 42.4 us  [the longest x6 32.1 us: from_line(): return lax.ppermute(block, axis, route)]
    pallas_call x0 -> x3, Pallas kernels: none -> 13.2 us  [the longest x1 11.2 us: attend(): pl.pallas_call(functools.partial(attention_kernel, blocks, group, hd ** (...]
    add x10 -> x1, other arithmetic: 8.81 us -> 0.06 us  [on_device(): chip_grad = chip_grad + from_line(part, 'seq', -2 * k).astype(F32)]
    while x37 -> x0, local copies, waits for them, and re-layouts: 3.59 us -> none  [the longest x1 2 us: attend(): lax.scan(per_group, start_accum, (query_rows, grad_rows, norm_rows, delta...]
    all_to_all x1 -> x0, local copies, waits for them, and re-layouts: 2.61 us -> none  [on_device(): lax.all_to_all(input_local, 'seq', split_axis=1, concat_axis=0, tiled=True)]
  transfers between devices with their start and end apart: 15 -> 16, of which waited for: 6 -> 6; matrix products, arithmetic and copies ran while one was open for 34% -> 17% of each run, Pallas kernels for 0% -> 10%
where the time goes in v1:
time: 119 us
  waiting for transfers between devices  42.4 us (36%)
  starting transfers between devices  29.7 us (25%)
  matrix products  17.9 us (15%)
  Pallas kernels  13.2 us (11%)
  local copies, waits for them, and re-layouts  10.5 us (9%)
  other arithmetic  4.14 us (3%)
    ppermute x6, waiting for transfers between devices, from_line(): return lax.ppermute(block, axis, route)  32.1 us
    ppermute x6, starting transfers between devices, from_line(): return lax.ppermute(block, axis, route)  13.1 us
    pallas_call x1, Pallas kernels, attend(): pl.pallas_call(functools.partial(attention_kernel, blocks, group, hd ** (...  11.2 us
    ppermute x7, waiting for transfers between devices, from_cycle(): lax.ppermute(block, axis, [(i, (i + distance) % count) for i in range(cou...  9.49 us
    dot_general x1, matrix products, on_device(): jnp.einsum('ekr,rd->ekd', basis.astype(BF16), weight_block, preferred_ele...  9.04 us
    ppermute x7, starting transfers between devices, from_cycle(): lax.ppermute(block, axis, [(i, (i + distance) % count) for i in range(cou...  8.94 us
    dot_general x1, matrix products, on_device(): jnp.einsum('kd,rd->kr', initial_right_factor[0], weight_block, preferred_...  8.9 us
    all_to_all x1, starting transfers between devices, on_device(): lax.all_to_all(split_inputs, 'seq', split_axis=0, concat_axis=0, tiled=True)  7.42 us
  transfers between devices with their start and end apart: 16, of which 6 were waited for; matrix products, arithmetic and copies ran while one was open for 17% of the time, Pallas kernels for 10%

profile of v1, /device:TPU:0, one launch (start us, length us, event | category | flops | bytes accessed | tf_op | source)
XLA Modules:
  0.0 118.9 jit_solution(14490882925004875428)
XLA Ops:
  0.6 0.0 copy-start
  0.7 0.7 copy-done
  1.4 8.9 %fusion.2 = f32[4,1536]{1,0:T(4,128)S(1)} fusion(bf16[1,1536,6144]{2,1,0:T(8,128)(2,1)} %param.16, bf16[1,4,6144]{2,1,0:T(4,128)(2,1)S(1)} %copy-done), kind=kOutput, calls=%fused_computation.2 | convolution fusion | flops 75497472 | bytes 18948096 | tf_op jit(solution)/shard_map/kd,rd->kr/dot_general | solution.py:233
  10.3 0.0 copy-start.8
  10.4 3.9 %collective-permute-start.12 = (f32[4,1536]{1,0:T(4,128)S(1)}, f32[4,1536]{1,0:T(4,128)S(1)}, u32[]{:S(2)}, u32[]{:S(2)}) collective-permute-start(f32[4,1536]{1,0:T(4,128)S(1)} %fusion.2), channel_id=1, source_target_pairs={{0,24},{8,0},{16,8},{24,16},{1,25},{9,1},{17,9},{25,17},{2,26},{10... | collective-permute-start | bytes 73736 | tf_op jit(solution)/shard_map/ppermute | solution.py:183
  14.3 0.0 collective-permute-start.11
  14.3 0.0 copy-done.12
  14.3 0.1 collective-permute-start
  14.4 2.6 %copy.24 = bf16[1,128,6144]{1,2,0:T(8,128)(2,1)} copy(bf16[1,128,6144]{2,1,0:T(8,128)(2,1)} %param.15) | data formatting | bytes 3145728 | tf_op args[6]
  17.0 2.6 %copy.25 = bf16[128,8,768]{2,0,1:T(8,128)(2,1)} copy(bf16[128,8,768]{0,2,1:T(8,128)(2,1)} %bitcast.99) | data formatting | bytes 3145728 | tf_op jit(solution)/shard_map/reshape;squeeze | solution.py:216
  19.6 0.5 shard_map.128.delta_ref
  20.1 0.0 collective-permute-done.12
  20.1 0.0 collective-permute-done.11
  20.2 0.1 fusion.20
  20.3 0.2 fusion.10
  20.6 0.2 multiply_reduce_fusion.1
  20.8 0.2 fusion.11
  21.0 0.2 multiply_reduce_fusion
  21.2 0.2 fusion.12
  21.4 0.2 fusion.21
  21.7 0.1 subtract_multiply_fusion
  21.8 9.0 %fusion = f32[2,4,6144]{2,1,0:T(4,128)S(1)} fusion(bf16[1,1536,6144]{2,1,0:T(8,128)(2,1)} %param.16, bf16[2,4,1536]{2,0,1:T(2,128)(2,1)S(1)} %fusion.22), kind=kOutput, calls=%fused_computation | convolution fusion | flops 150994944 | bytes 19095552 | tf_op jit(solution)/shard_map/ekr,rd->ekd/dot_general | solution.py:239
  30.9 0.0 copy-start.9
  30.9 0.7 slice_bitcast_fusion
  31.6 0.0 collective-permute-done
  31.7 5.5 %collective-permute-start.3 = (bf16[256,256]{1,0:T(8,128)(2,1)S(1)}, bf16[256,256]{1,0:T(8,128)(2,1)S(1)}, u32[]{:S(2)}, u32[]{:S(2)}) collective-permute-start(bf16[256,256]{1,0:T(8,128)(2,1)S(1)} %pad_maximum_fusion.refs_0_), channel_id=1, source_target_pairs={{0,6},{1,7},{8,14},{9,15},{16,22},{17,23},{24,30},{25,31}} | collective-permute-start | bytes 393224 | tf_op jit(solution)/shard_map/ppermute | solution.py:189
  37.2 1.3 %collective-permute-start.2 = (bf16[256,256]{1,0:T(8,128)(2,1)S(1)}, bf16[256,256]{1,0:T(8,128)(2,1)S(1)}, u32[]{:S(2)}, u32[]{:S(2)}) collective-permute-start(bf16[256,256]{1,0:T(8,128)(2,1)S(1)} %pad_maximum_fusion.refs_0_), channel_id=1, source_target_pairs={{0,4},{1,5},{2,6},{3,7},{8,12},{9,13},{10,14},{11,15},{16,20},{17,... | collective-permute-start | bytes 393224 | tf_op jit(solution)/shard_map/ppermute | solution.py:189
  38.5 2.5 %collective-permute-start.1 = (bf16[256,256]{1,0:T(8,128)(2,1)S(1)}, bf16[256,256]{1,0:T(8,128)(2,1)S(1)}, u32[]{:S(2)}, u32[]{:S(2)}) collective-permute-start(bf16[256,256]{1,0:T(8,128)(2,1)S(1)} %pad_maximum_fusion.refs_0_), channel_id=1, source_target_pairs={{0,2},{1,3},{2,4},{3,5},{4,6},{5,7},{8,10},{9,11},{10,12},{11,13},... | collective-permute-start | bytes 393224 | tf_op jit(solution)/shard_map/ppermute | solution.py:189
  41.0 0.6 copy.27
  41.6 2.0 %collective-permute-start.13 = (f32[4,6144]{1,0:T(4,128)}, f32[4,6144]{1,0:T(4,128)}, u32[]{:S(2)}, u32[]{:S(2)}) collective-permute-start(f32[4,6144]{1,0:T(4,128)} %get-tuple-element.52), channel_id=1, source_target_pairs={{0,8},{8,16},{16,24},{24,0},{1,9},{9,17},{17,25},{25,1},{2,10},{10... | collective-permute-start | bytes 294920 | tf_op jit(solution)/shard_map/ppermute | solution.py:183
  43.6 1.0 collective-permute-start.14
  44.6 0.0 collective-permute-done.3.refs_3_
  44.6 0.0 collective-permute-done.2.refs_2_
  44.6 0.7 copy-done.4
  45.2 1.0 collective-permute-done.1.refs_1_
  46.3 0.0 copy-done.9
  46.3 0.7 copy-done.6
  46.9 7.4 %all-to-all-start = ((bf16[8,128,768]{2,1,0:T(8,128)(2,1)}), bf16[8,128,768]{2,1,0:T(8,128)(2,1)S(1)}, u32[]{:S(2)}, u32[]{:S(2)}) async-start(bf16[8,128,768]{2,1,0:T(8,128)(2,1)} %bitcast.98), calls=%async_computation | async-start | bytes 3145728 | tf_op jit(solution)/shard_map/all_to_all | solution.py:218
  54.4 0.0 copy-start.5
  54.4 0.9 copy-done.5
  55.3 0.9 copy-done.7
  56.2 11.2 %shard_map.129 = (f32[128,3072]{1,0:T(8,128)}, f32[256,256]{1,0:T(8,128)S(1)}, bf16[256,256]{1,0:T(8,128)(2,1)S(1)}, bf16[256,256]{1,0:T(8,128)(2,1)S(1)}, bf16[256,256]{1,0:T(8,128)(2,1)S(1)}) custom-call(s32[1]{0:T(128)} %bitcast.me_ref, bf16[128,3072]{1,0:T(8,128)(2,1)S(1)} %bitcast.96, bf16[128,3072]{1,0:T(8,128)(2,1)S(1)} %bitcast.95, ...), custom_call_target="tpu_custom_call" | custom-call | flops 8053063680 | bytes 3145728 | tf_op jit(solution)/shard_map/pallas_call | solution.py:121
  67.4 1.3 %collective-permute-start.4 = (bf16[256,256]{1,0:T(8,128)(2,1)S(1)}, bf16[256,256]{1,0:T(8,128)(2,1)S(1)}, u32[]{:S(2)}, u32[]{:S(2)}) collective-permute-start(bf16[256,256]{1,0:T(8,128)(2,1)S(1)} %get-tuple-element.21), channel_id=1, source_target_pairs={{2,0},{3,1},{4,2},{5,3},{6,4},{7,5},{10,8},{11,9},{12,10},{13,11},... | collective-permute-start | bytes 393224 | tf_op jit(solution)/shard_map/ppermute | solution.py:189
  68.7 1.3 %collective-permute-start.5 = (bf16[256,256]{1,0:T(8,128)(2,1)S(1)}, bf16[256,256]{1,0:T(8,128)(2,1)S(1)}, u32[]{:S(2)}, u32[]{:S(2)}) collective-permute-start(bf16[256,256]{1,0:T(8,128)(2,1)S(1)} %get-tuple-element.22), channel_id=1, source_target_pairs={{4,0},{5,1},{6,2},{7,3},{12,8},{13,9},{14,10},{15,11},{20,16},{21,... | collective-permute-start | bytes 393224 | tf_op jit(solution)/shard_map/ppermute | solution.py:189
  70.0 1.3 %collective-permute-start.6 = (bf16[256,256]{1,0:T(8,128)(2,1)S(1)}, bf16[256,256]{1,0:T(8,128)(2,1)S(1)}, u32[]{:S(2)}, u32[]{:S(2)}) collective-permute-start(bf16[256,256]{1,0:T(8,128)(2,1)S(1)} %get-tuple-element.23), channel_id=1, source_target_pairs={{6,0},{7,1},{14,8},{15,9},{22,16},{23,17},{30,24},{31,25}} | collective-permute-start | bytes 393224 | tf_op jit(solution)/shard_map/ppermute | solution.py:189
  71.3 0.0 collective-permute-done.13
  71.3 0.0 collective-permute-done.14
  71.3 1.0 add_bitcast_fusion.1
  72.3 6.9 %collective-permute-done.4 = bf16[256,256]{1,0:T(8,128)(2,1)S(1)} collective-permute-done((bf16[256,256]{1,0:T(8,128)(2,1)S(1)}, bf16[256,256]{1,0:T(8,128)(2,1)S(1)}, u32[]{:S(2)}, u32[]{:S(2)}) %collective-permute-start.4) | collective-permute-done | bytes 131104 | tf_op jit(solution)/shard_map/ppermute | solution.py:189
  79.2 24.2 %collective-permute-done.5 = bf16[256,256]{1,0:T(8,128)(2,1)S(1)} collective-permute-done((bf16[256,256]{1,0:T(8,128)(2,1)S(1)}, bf16[256,256]{1,0:T(8,128)(2,1)S(1)}, u32[]{:S(2)}, u32[]{:S(2)}) %collective-permute-start.5) | collective-permute-done | bytes 131104 | tf_op jit(solution)/shard_map/ppermute | solution.py:189
  103.4 0.0 collective-permute-done.6
  103.4 0.1 convert_add_fusion
  103.5 0.1 collective-permute-start.7
  103.5 0.7 maximum_bitcast_fusion
  104.3 0.8 collective-permute-done.7
  105.1 0.1 collective-permute-start.10
  105.2 0.1 collective-permute-start.9
  105.2 1.9 %collective-permute-start.8 = (bf16[256,256]{1,0:T(8,128)(2,1)S(1)}, bf16[256,256]{1,0:T(8,128)(2,1)S(1)}, u32[]{:S(2)}, u32[]{:S(2)}) collective-permute-start(bf16[256,256]{1,0:T(8,128)(2,1)S(1)} %get-tuple-element.48.refs_0_), channel_id=1, source_target_pairs={{0,2},{1,3},{2,4},{3,5},{4,6},{5,7},{6,0},{7,1},{8,10},{9,11},{10,... | collective-permute-start | bytes 393224 | tf_op jit(solution)/shard_map/ppermute | solution.py:183
  107.2 0.7 fusion.4
  107.9 4.0 %collective-permute-done.10.refs_3_ = bf16[256,256]{1,0:T(8,128)(2,1)S(1)} collective-permute-done((bf16[256,256]{1,0:T(8,128)(2,1)S(1)}, bf16[256,256]{1,0:T(8,128)(2,1)S(1)}, u32[]{:S(2)}, u32[]{:S(2)}) %collective-permute-start.10) | collective-permute-done | bytes 131104 | tf_op jit(solution)/shard_map/ppermute | solution.py:183
  111.9 5.4 %collective-permute-done.9.refs_2_ = bf16[256,256]{1,0:T(8,128)(2,1)S(1)} collective-permute-done((bf16[256,256]{1,0:T(8,128)(2,1)S(1)}, bf16[256,256]{1,0:T(8,128)(2,1)S(1)}, u32[]{:S(2)}, u32[]{:S(2)}) %collective-permute-start.9) | collective-permute-done | bytes 131104 | tf_op jit(solution)/shard_map/ppermute | solution.py:183
  117.3 0.0 collective-permute-done.8.refs_1_
  117.3 0.0 all-to-all-done.x_ref
  117.3 1.5 %shard_map.130 = f32[768,256]{1,0:T(8,128)} custom-call(s32[1]{0:T(128)} %bitcast.me_ref, bf16[8,128,768]{2,1,0:T(8,128)(2,1)S(1)} %all-to-all-done.x_ref, bf16[256,256]{1,0:T(8,128)(2,1)S(1)} %get-tuple-element.48.refs_0_, bf16[256,256]{1,0:T(8,128)(2,1)S(1)} %collective-permute-done.8.refs_1_, bf16[256,256]{1,0:T(8,128)(2,1)S(1)} %collective-permute-done.9.refs_2_, ...), custom_call_target="tpu_custom_call" | custom-call | flops 402653184 | bytes 1572864 | tf_op jit(solution)/shard_map/pallas_call | solution.py:154
  (32 shorter events, 0.3 us)
Async XLA Ops:
  0.6 0.8 copy-start
  0.6 13.7 %copy-start.11 = (bf16[1,128,128]{2,1,0:T(8,128)(2,1)S(1)}, bf16[1,128,128]{2,1,0:T(8,128)(2,1)}, u32[]{:S(2)}) copy-start(bf16[1,128,128]{2,1,0:T(8,128)(2,1)} %param.11) | copy-start | bytes 98308
  0.7 13.7 %copy-start.12 = (bf16[1,128,128]{2,1,0:T(8,128)(2,1)S(1)}, bf16[1,128,128]{2,1,0:T(8,128)(2,1)}, u32[]{:S(2)}) copy-start(bf16[1,128,128]{2,1,0:T(8,128)(2,1)} %param.10) | copy-start | bytes 98308
  0.7 19.0 %copy-start.2 = (bf16[1,128,3072]{2,1,0:T(8,128)(2,1)S(1)}, bf16[1,128,3072]{2,1,0:T(8,128)(2,1)}, u32[]{:S(2)}) copy-start(bf16[1,128,3072]{2,1,0:T(8,128)(2,1)} %param.13) | copy-start | bytes 2359300
  0.7 19.0 %copy-start.1 = (bf16[1,128,3072]{2,1,0:T(8,128)(2,1)S(1)}, bf16[1,128,3072]{2,1,0:T(8,128)(2,1)}, u32[]{:S(2)}) copy-start(bf16[1,128,3072]{2,1,0:T(8,128)(2,1)} %param.12) | copy-start | bytes 2359300
  10.3 44.0 %copy-start.3 = (bf16[1,128,3072]{2,1,0:T(8,128)(2,1)S(1)}, bf16[1,128,3072]{2,1,0:T(8,128)(2,1)}, u32[]{:S(2)}) copy-start(bf16[1,128,3072]{2,1,0:T(8,128)(2,1)} %param.9) | copy-start | bytes 2359300
  10.3 44.0 %copy-start.8 = (f32[1,24,128]{2,1,0:T(8,128)S(1)}, f32[1,24,128]{2,1,0:T(8,128)}, u32[]{:S(2)}) copy-start(f32[1,24,128]{2,1,0:T(8,128)} %param.14) | copy-start | bytes 36868
  10.4 9.8 %collective-permute-start.12 = (f32[4,1536]{1,0:T(4,128)S(1)}, f32[4,1536]{1,0:T(4,128)S(1)}, u32[]{:S(2)}, u32[]{:S(2)}) collective-permute-start(f32[4,1536]{1,0:T(4,128)S(1)} %fusion.2), channel_id=1, source_target_pairs={{0,24},{8,0},{16,8},{24,16},{1,25},{9,1},{17,9},{25,17},{2,26},{10... | collective-permute-start | bytes 73736 | tf_op jit(solution)/shard_map/ppermute | solution.py:183
  14.3 5.8 %collective-permute-start.11 = (f32[4,1536]{1,0:T(4,128)S(1)}, f32[4,1536]{1,0:T(4,128)S(1)}, u32[]{:S(2)}, u32[]{:S(2)}) collective-permute-start(f32[4,1536]{1,0:T(4,128)S(1)} %fusion.2), channel_id=1, source_target_pairs={{0,8},{8,16},{16,24},{24,0},{1,9},{9,17},{17,25},{25,1},{2,10},{10... | collective-permute-start | bytes 73736 | tf_op jit(solution)/shard_map/ppermute | solution.py:183
  14.3 17.3 %collective-permute-start = (bf16[128,256]{1,0:T(8,128)(2,1)S(1)}, bf16[128,256]{1,0:T(8,128)(2,1)S(1)}, u32[]{:S(2)}, u32[]{:S(2)}) collective-permute-start(bf16[128,256]{1,0:T(8,128)(2,1)S(1)} %pad_maximum_fusion.1), channel_id=1, source_target_pairs={{0,1},{1,0},{2,3},{3,2},{4,5},{5,4},{6,7},{7,6},{8,9},{9,8},{10,11... | collective-permute-start | bytes 196616 | tf_op jit(solution)/shard_map/ppermute | solution.py:194
  30.9 15.4 %copy-start.9 = (f32[2,4,6144]{2,1,0:T(4,128)}, f32[2,4,6144]{2,1,0:T(4,128)S(1)}, u32[]{:S(2)}) copy-start(f32[2,4,6144]{2,1,0:T(4,128)S(1)} %fusion) | copy-start | bytes 589828
  31.7 12.9 %collective-permute-start.3 = (bf16[256,256]{1,0:T(8,128)(2,1)S(1)}, bf16[256,256]{1,0:T(8,128)(2,1)S(1)}, u32[]{:S(2)}, u32[]{:S(2)}) collective-permute-start(bf16[256,256]{1,0:T(8,128)(2,1)S(1)} %pad_maximum_fusion.refs_0_), channel_id=1, source_target_pairs={{0,6},{1,7},{8,14},{9,15},{16,22},{17,23},{24,30},{25,31}} | collective-permute-start | bytes 393224 | tf_op jit(solution)/shard_map/ppermute | solution.py:189
  37.2 7.4 %collective-permute-start.2 = (bf16[256,256]{1,0:T(8,128)(2,1)S(1)}, bf16[256,256]{1,0:T(8,128)(2,1)S(1)}, u32[]{:S(2)}, u32[]{:S(2)}) collective-permute-start(bf16[256,256]{1,0:T(8,128)(2,1)S(1)} %pad_maximum_fusion.refs_0_), channel_id=1, source_target_pairs={{0,4},{1,5},{2,6},{3,7},{8,12},{9,13},{10,14},{11,15},{16,20},{17,... | collective-permute-start | bytes 393224 | tf_op jit(solution)/shard_map/ppermute | solution.py:189
  38.5 7.8 %collective-permute-start.1 = (bf16[256,256]{1,0:T(8,128)(2,1)S(1)}, bf16[256,256]{1,0:T(8,128)(2,1)S(1)}, u32[]{:S(2)}, u32[]{:S(2)}) collective-permute-start(bf16[256,256]{1,0:T(8,128)(2,1)S(1)} %pad_maximum_fusion.refs_0_), channel_id=1, source_target_pairs={{0,2},{1,3},{2,4},{3,5},{4,6},{5,7},{8,10},{9,11},{10,12},{11,13},... | collective-permute-start | bytes 393224 | tf_op jit(solution)/shard_map/ppermute | solution.py:189
  41.6 29.6 %collective-permute-start.13 = (f32[4,6144]{1,0:T(4,128)}, f32[4,6144]{1,0:T(4,128)}, u32[]{:S(2)}, u32[]{:S(2)}) collective-permute-start(f32[4,6144]{1,0:T(4,128)} %get-tuple-element.52), channel_id=1, source_target_pairs={{0,8},{8,16},{16,24},{24,0},{1,9},{9,17},{17,25},{25,1},{2,10},{10... | collective-permute-start | bytes 294920 | tf_op jit(solution)/shard_map/ppermute | solution.py:183
  43.6 27.7 %collective-permute-start.14 = (f32[4,6144]{1,0:T(4,128)}, f32[4,6144]{1,0:T(4,128)}, u32[]{:S(2)}, u32[]{:S(2)}) collective-permute-start(f32[4,6144]{1,0:T(4,128)} %get-tuple-element.53), channel_id=1, source_target_pairs={{0,24},{8,0},{16,8},{24,16},{1,25},{9,1},{17,9},{25,17},{2,26},{10... | collective-permute-start | bytes 294920 | tf_op jit(solution)/shard_map/ppermute | solution.py:183
  44.6 0.7 copy-start.4
  46.3 0.7 copy-start.6
  46.9 70.4 %all-to-all-start = ((bf16[8,128,768]{2,1,0:T(8,128)(2,1)}), bf16[8,128,768]{2,1,0:T(8,128)(2,1)S(1)}, u32[]{:S(2)}, u32[]{:S(2)}) async-start(bf16[8,128,768]{2,1,0:T(8,128)(2,1)} %bitcast.98), calls=%async_computation | async-start | bytes 3145728 | tf_op jit(solution)/shard_map/all_to_all | solution.py:218
  54.4 0.9 copy-start.5
  55.3 0.9 copy-start.7
  56.2 15.1 %copy-start.10 = (f32[2,4,6144]{2,1,0:T(4,128)S(1)}, f32[2,4,6144]{2,1,0:T(4,128)}, u32[]{:S(2)}) copy-start(f32[2,4,6144]{2,1,0:T(4,128)} %copy-done.9) | copy-start | bytes 589828
  67.4 11.8 %collective-permute-start.4 = (bf16[256,256]{1,0:T(8,128)(2,1)S(1)}, bf16[256,256]{1,0:T(8,128)(2,1)S(1)}, u32[]{:S(2)}, u32[]{:S(2)}) collective-permute-start(bf16[256,256]{1,0:T(8,128)(2,1)S(1)} %get-tuple-element.21), channel_id=1, source_target_pairs={{2,0},{3,1},{4,2},{5,3},{6,4},{7,5},{10,8},{11,9},{12,10},{13,11},... | collective-permute-start | bytes 393224 | tf_op jit(solution)/shard_map/ppermute | solution.py:189
  68.7 34.7 %collective-permute-start.5 = (bf16[256,256]{1,0:T(8,128)(2,1)S(1)}, bf16[256,256]{1,0:T(8,128)(2,1)S(1)}, u32[]{:S(2)}, u32[]{:S(2)}) collective-permute-start(bf16[256,256]{1,0:T(8,128)(2,1)S(1)} %get-tuple-element.22), channel_id=1, source_target_pairs={{4,0},{5,1},{6,2},{7,3},{12,8},{13,9},{14,10},{15,11},{20,16},{21,... | collective-permute-start | bytes 393224 | tf_op jit(solution)/shard_map/ppermute | solution.py:189
  70.0 33.4 %collective-permute-start.6 = (bf16[256,256]{1,0:T(8,128)(2,1)S(1)}, bf16[256,256]{1,0:T(8,128)(2,1)S(1)}, u32[]{:S(2)}, u32[]{:S(2)}) collective-permute-start(bf16[256,256]{1,0:T(8,128)(2,1)S(1)} %get-tuple-element.23), channel_id=1, source_target_pairs={{6,0},{7,1},{14,8},{15,9},{22,16},{23,17},{30,24},{31,25}} | collective-permute-start | bytes 393224 | tf_op jit(solution)/shard_map/ppermute | solution.py:189
  103.5 1.6 %collective-permute-start.7 = (f32[256,256]{1,0:T(8,128)S(1)}, f32[256,256]{1,0:T(8,128)S(1)}, u32[]{:S(2)}, u32[]{:S(2)}) collective-permute-start(f32[256,256]{1,0:T(8,128)S(1)} %convert_add_fusion), channel_id=1, source_target_pairs={{0,1},{1,0},{2,3},{3,2},{4,5},{5,4},{6,7},{7,6},{8,9},{9,8},{10,11... | collective-permute-start | bytes 786440 | tf_op jit(solution)/shard_map/ppermute | solution.py:194
  105.1 6.8 %collective-permute-start.10 = (bf16[256,256]{1,0:T(8,128)(2,1)S(1)}, bf16[256,256]{1,0:T(8,128)(2,1)S(1)}, u32[]{:S(2)}, u32[]{:S(2)}) collective-permute-start(bf16[256,256]{1,0:T(8,128)(2,1)S(1)} %get-tuple-element.48.refs_0_), channel_id=1, source_target_pairs={{0,6},{1,7},{2,0},{3,1},{4,2},{5,3},{6,4},{7,5},{8,14},{9,15},{10,... | collective-permute-start | bytes 393224 | tf_op jit(solution)/shard_map/ppermute | solution.py:183
  105.2 12.2 %collective-permute-start.9 = (bf16[256,256]{1,0:T(8,128)(2,1)S(1)}, bf16[256,256]{1,0:T(8,128)(2,1)S(1)}, u32[]{:S(2)}, u32[]{:S(2)}) collective-permute-start(bf16[256,256]{1,0:T(8,128)(2,1)S(1)} %get-tuple-element.48.refs_0_), channel_id=1, source_target_pairs={{0,4},{1,5},{2,6},{3,7},{4,0},{5,1},{6,2},{7,3},{8,12},{9,13},{10,... | collective-permute-start | bytes 393224 | tf_op jit(solution)/shard_map/ppermute | solution.py:183
  105.2 12.1 %collective-permute-start.8 = (bf16[256,256]{1,0:T(8,128)(2,1)S(1)}, bf16[256,256]{1,0:T(8,128)(2,1)S(1)}, u32[]{:S(2)}, u32[]{:S(2)}) collective-permute-start(bf16[256,256]{1,0:T(8,128)(2,1)S(1)} %get-tuple-element.48.refs_0_), channel_id=1, source_target_pairs={{0,2},{1,3},{2,4},{3,5},{4,6},{5,7},{6,0},{7,1},{8,10},{9,11},{10,... | collective-permute-start | bytes 393224 | tf_op jit(solution)/shard_map/ppermute | solution.py:183

commit v2 on v1

v2 whole, which is shorter than its diff:
```python
import functools
import math

import jax
import jax.numpy as jnp
from jax import lax
from jax.experimental import pallas as pl
from jax.experimental.pallas import tpu as pltpu
from jax.sharding import PartitionSpec as P

WINDOW = 2048
EPSILON = 1e-06
LOG2E = math.log2(math.e)
F32 = jnp.float32
BF16 = jnp.bfloat16
VMEM_LIMIT = 48 * 1024 * 1024
PARTS = 3
PARTS = 3
COST = pl.CostEstimate(flops=1, bytes_accessed=1, transcendentals=0)


def dot_nt(a, b):
    return lax.dot_general(a, b, (((1,), (1,)), ((), ())), preferred_element_type=F32)


def dot_tn(a, b):
    return lax.dot_general(a, b, (((0,), (0,)), ((), ())), preferred_element_type=F32)


def vmem_specs(count):
    return [pl.BlockSpec(memory_space=pltpu.VMEM)] * count


def delta_kernel(head_dim, grad_ref, out_ref, delta_ref):
    for head in range(delta_ref.shape[0]):
        cols = slice(head * head_dim, (head + 1) * head_dim)
        prod = grad_ref[:, cols].astype(F32) * out_ref[:, cols].astype(F32)
        delta_ref[head : head + 1, :] = jnp.sum(prod.T, axis=0, keepdims=True)


def head_delta(out_grad, outputs, heads):
    rows, cols = out_grad.shape
    return pl.pallas_call(
        functools.partial(delta_kernel, cols // heads),
        out_shape=jax.ShapeDtypeStruct((heads, rows), F32),
        in_specs=vmem_specs(2),
        out_specs=pl.BlockSpec(memory_space=pltpu.VMEM),
        compiler_params=pltpu.CompilerParams(vmem_limit_bytes=VMEM_LIMIT),
        cost_estimate=COST,
    )(out_grad, outputs)


def swap(block, axis, bit, only_up=None):
    count = lax.axis_size(axis)
    route = [
        (i, i ^ bit) for i in range(count) if only_up is None or (i < i ^ bit) == only_up
    ]
    return lax.ppermute(block, axis, route)


def gather_bits(count):
    return [1 << b for b in reversed(range(count.bit_length() - 1))]


def gather_order(count):
    order = [0]
    for bit in gather_bits(count):
        order = order + [x ^ bit for x in order]
    return order


def swap(block, axis, bit, only_up=None):
    count = lax.axis_size(axis)
    route = [
        (i, i ^ bit) for i in range(count) if only_up is None or (i < i ^ bit) == only_up
    ]
    return lax.ppermute(block, axis, route)


def gather_bits(count):
    return [1 << b for b in reversed(range(count.bit_length() - 1))]


def gather_order(count):
    order = [0]
    for bit in gather_bits(count):
        order = order + [x ^ bit for x in order]
    return order


def attention_kernel(
    order, group, join, scale, me_ref, q_ref, do_ref, norm_ref, delta_ref, near_ref, far_ref,
    qg_ref, near_grad_ref, far_grad_ref, near_t_ref, far_t_ref, qgt_ref,
):
    tok = q_ref.shape[0]
    hd = near_ref.shape[1] // 2
    heads = norm_ref.shape[0]
    half = near_ref.shape[0]
    rows = join * tok
    me = me_ref[0]
    windowed = len(order) * tok > WINDOW
    chunks = [(s, first) for s in range(2) for first in range(0, half, rows)]
    kv_refs = (near_ref, far_ref)
    grad_refs = (near_grad_ref, far_grad_ref)
    t_refs = (near_t_ref, far_t_ref)
    for s, first in chunks:
        t_refs[s][:, first : first + rows] = kv_refs[s][first : first + rows, :hd].T
        grad_refs[s][first : first + rows, :] = jnp.zeros((rows, 2 * hd), F32)

    def step(index, carry):
        def stacked(ref):
            parts = []
            for i in range(group):
                first = pl.multiple_of((index * group + i) * hd, hd)
                parts.append(ref[:, pl.ds(first, hd)])
            return jnp.concatenate(parts, axis=0)

        def row(ref):
            return jnp.concatenate(
                [ref[pl.ds(index * group + i, 1), :] for i in range(group)], axis=1
            )

        q = stacked(q_ref)
        do = stacked(do_ref)
        norm = row(norm_ref) * LOG2E
        delta = row(delta_ref)
        qgt = None
        for s, first in chunks:
            area = slice(first, first + rows)
            key = kv_refs[s][area, :hd]
            value = kv_refs[s][area, hd:]
            logits = dot_nt(key, q) * (scale * LOG2E)
            parts = []
            for j in range(join):
                x = order[(s * half + first) // tok + j]
                source = me ^ x
                part = logits[j * tok : (j + 1) * tok]
                if x == 0 or windowed:
                    key_pos = source * tok + lax.broadcasted_iota(jnp.int32, part.shape, 0)
                    query = lax.broadcasted_iota(jnp.int32, part.shape, 1)
                    query_pos = me * tok + lax.rem(query, tok)
                    visible = (key_pos <= query_pos) & (key_pos > query_pos - WINDOW)
                    parts.append(jnp.where(visible, jnp.exp2(part - norm), 0.0))
                else:
                    hidden = jnp.where(source < me, 0.0, 1e30).astype(F32)
                    parts.append(jnp.exp2(part - (norm + hidden)))
            probs = jnp.concatenate(parts, axis=0)
            prob_grad = dot_nt(value, do)
            score_grad = (scale * probs * (prob_grad - delta)).astype(BF16)
            grad_refs[s][area, hd:] += jnp.dot(
                probs.astype(BF16), do, preferred_element_type=F32
            )
            grad_refs[s][area, :hd] += jnp.dot(score_grad, q, preferred_element_type=F32)
            part = jnp.dot(t_refs[s][:, area], score_grad, preferred_element_type=F32)
            qgt = part if qgt is None else qgt + part
        qgt_ref[...] = qgt
        for i in range(group):
            first = pl.multiple_of((index * group + i) * hd, hd)
            qg_ref[:, pl.ds(first, hd)] = qgt_ref[:, i * tok : (i + 1) * tok].T
        return carry

    lax.fori_loop(0, heads // group, step, 0)


def attend(me, queries, out_grad, norm, delta, near, far):
    tok, cols = queries.shape
    heads = norm.shape[0]
    hd = cols // heads
    half = near.shape[0]
    order = gather_order(2 * half // tok)
    group = next(g for g in (4, 3, 2, 1) if heads % g == 0)
    join = 2 if half % (2 * tok) == 0 else 1
    work = heads * tok * half * 2
    return pl.pallas_call(
        functools.partial(attention_kernel, order, group, join, hd ** (-0.5)),
        out_shape=[
            jax.ShapeDtypeStruct((tok, cols), F32),
            jax.ShapeDtypeStruct((half, 2 * hd), F32),
            jax.ShapeDtypeStruct((half, 2 * hd), F32),
        ],
        in_specs=[pl.BlockSpec(memory_space=pltpu.SMEM)] + vmem_specs(6),
        out_specs=vmem_specs(3),
        scratch_shapes=[
            pltpu.VMEM((hd, half), BF16),
            pltpu.VMEM((hd, half), BF16),
            pltpu.VMEM((hd, group * tok), F32),
        ],
        compiler_params=pltpu.CompilerParams(vmem_limit_bytes=VMEM_LIMIT),
        cost_estimate=pl.CostEstimate(
            flops=20 * work * hd, bytes_accessed=8 * tok * cols, transcendentals=work
        ),
    )(me[None], queries, out_grad, norm, delta, near, far)


def pack_kernel(x_ref, out_ref):
    width = out_ref.shape[2]
    for j in range(out_ref.shape[0]):
        out_ref[j] = x_ref[:, j * width : (j + 1) * width]


def pack(inputs, count):
    tok, cols = inputs.shape
    width = cols // count
    if width % 128:
        return inputs.reshape(tok, count, width).transpose(1, 0, 2)
    return pl.pallas_call(
        pack_kernel,
        out_shape=jax.ShapeDtypeStruct((count, tok, width), inputs.dtype),
        in_specs=vmem_specs(1),
        out_specs=pl.BlockSpec(memory_space=pltpu.VMEM),
        compiler_params=pltpu.CompilerParams(vmem_limit_bytes=VMEM_LIMIT),
        cost_estimate=pl.CostEstimate(
            flops=0, bytes_accessed=4 * tok * cols, transcendentals=0
        ),
    )(inputs)


def project_kernel(order, me_ref, x_ref, near_ref, far_ref, out_ref):
    me = me_ref[0]
    x = jnp.concatenate([x_ref[me ^ part] for part in order], axis=0)
    grads = jnp.concatenate([near_ref[...], far_ref[...]], axis=0)
    out_ref[...] = dot_tn(x, grads)


def project(me, blocks, near, far):
    count, tok, width = blocks.shape
    cols = near.shape[1]
    return pl.pallas_call(
        functools.partial(project_kernel, gather_order(count)),
        out_shape=jax.ShapeDtypeStruct((width, cols), F32),
        in_specs=[pl.BlockSpec(memory_space=pltpu.SMEM)] + vmem_specs(3),
        out_specs=pl.BlockSpec(memory_space=pltpu.VMEM),
        compiler_params=pltpu.CompilerParams(vmem_limit_bytes=VMEM_LIMIT),
        cost_estimate=pl.CostEstimate(
            flops=2 * count * tok * width * cols,
            bytes_accessed=2 * count * tok * width,
            transcendentals=0,
        ),
    )(me[None], blocks, near, far)


def acts_kernel(factor_ref, w_ref, out_ref):
    rank, rows = out_ref.shape
    part = dot_nt(w_ref[...], factor_ref[...])
    wide = jnp.concatenate([part, jnp.zeros((rows, 128 - rank), F32)], axis=1)
    out_ref[...] = wide.T[:rank]


def acts_part(factor, weight, index, parts):
    rank, cols = factor.shape
    rows = weight.shape[0] // parts
    tile = 256 if rows % 256 == 0 else rows
    steps = rows // tile
    return pl.pallas_call(
        acts_kernel,
        grid=(steps,),
        out_shape=jax.ShapeDtypeStruct((rank, rows), F32),
        in_specs=[
            pl.BlockSpec((rank, cols), lambda i: (0, 0)),
            pl.BlockSpec((tile, cols), lambda i: (index * steps + i, 0)),
        ],
        out_specs=pl.BlockSpec((rank, tile), lambda i: (0, i)),
        compiler_params=pltpu.CompilerParams(vmem_limit_bytes=VMEM_LIMIT),
        cost_estimate=pl.CostEstimate(
            flops=2 * rank * rows * cols, bytes_accessed=2 * rows * cols, transcendentals=0
        ),
    )(factor, weight)


def orthonormal(diffs):
    columns = []
    for index in range(diffs.shape[0]):
        source = diffs[index : index + 1]
        vector = source
        for previous in columns:
            vector = vector - jnp.mean(source * previous, axis=-1, keepdims=True) * previous
        columns.append(
            vector * lax.rsqrt(jnp.mean(vector * vector, axis=-1, keepdims=True) + EPSILON)
        )
    return jnp.concatenate(columns, axis=0)


def basis_kernel(acts_ref, lower_ref, higher_ref, basis_ref, both_ref):
    acts = acts_ref[...]
    edges = [orthonormal(acts - ref[...]) for ref in (lower_ref, higher_ref)]
    for e, edge in enumerate(edges):
        basis_ref[e] = edge
    both_ref[...] = jnp.concatenate(edges, axis=0).astype(BF16)


def make_basis(acts, lower, higher):
    rank, rows = acts.shape
    return pl.pallas_call(
        basis_kernel,
        out_shape=[
            jax.ShapeDtypeStruct((2, rank, rows), F32),
            jax.ShapeDtypeStruct((2 * rank, rows), BF16),
        ],
        in_specs=vmem_specs(3),
        out_specs=vmem_specs(2),
        cost_estimate=pl.CostEstimate(
            flops=60 * rank * rows, bytes_accessed=40 * rank * rows, transcendentals=0
        ),
    )(acts, lower, higher)


def contrib_kernel(both_ref, w_ref, out_ref):
    rank = out_ref.shape[1]
    part = jnp.dot(both_ref[...], w_ref[...], preferred_element_type=F32)
    for e in range(2):
        out_ref[e] = part[e * rank : (e + 1) * rank]


def contrib_part(both, weight, index, parts):
    count, rows = both.shape
    cols = weight.shape[1] // parts
    tile = 512 if cols % 512 == 0 else cols
    steps = cols // tile
    return pl.pallas_call(
        contrib_kernel,
        grid=(steps,),
        out_shape=jax.ShapeDtypeStruct((2, count // 2, cols), F32),
        in_specs=[
            pl.BlockSpec((count, rows), lambda i: (0, 0)),
            pl.BlockSpec((rows, tile), lambda i: (0, index * steps + i)),
        ],
        out_specs=pl.BlockSpec((2, count // 2, tile), lambda i: (0, 0, i)),
        compiler_params=pltpu.CompilerParams(vmem_limit_bytes=VMEM_LIMIT),
        cost_estimate=pl.CostEstimate(
            flops=2 * count * rows * cols, bytes_accessed=2 * rows * cols, transcendentals=0
        ),
    )(both, weight)


def from_cycle(block, axis, distance):
    count = lax.axis_size(axis)
    return lax.ppermute(block, axis, [(i, (i + distance) % count) for i in range(count)])


def on_device(
    queries, keys, values, outputs, out_grad, log_norm, inputs, mlp_weight, initial_right_factor
):
    tok = queries.shape[1]
    heads = log_norm.shape[1]
    count = lax.axis_size("seq")
    me = lax.axis_index("seq")
    bits = gather_bits(count)
    factor = initial_right_factor[0]
    weight = mlp_weight[0]

    near = jnp.concatenate([keys[0], values[0]], axis=-1)
    packed = pack(inputs[0], count)
    acts_parts = []
    for index, bit in enumerate(bits):
        far = swap(near, "seq", bit, True if index == 0 else None)
        if index < PARTS:
            acts_parts.append(acts_part(factor, weight, index, PARTS))
        factor, near, far, packed, acts_parts = lax.optimization_barrier(
            (factor, near, far, packed, acts_parts)
        )
        if bit > 1:
            near = jnp.concatenate([near, far], axis=0)
    acts = jnp.concatenate(acts_parts, axis=1)

    feature_blocks = lax.all_to_all(packed, "seq", split_axis=0, concat_axis=0, tiled=True)
    lower_acts = from_cycle(acts, "rep", 1)
    higher_acts = from_cycle(acts, "rep", -1)

    delta = head_delta(out_grad[0], outputs[0], heads)
    query_grad, grads, sent = attend(me, queries[0], out_grad[0], log_norm[0], delta, near, far)
    lower_acts, higher_acts, sent = lax.optimization_barrier((lower_acts, higher_acts, sent))

    basis, both = make_basis(acts, lower_acts, higher_acts)
    contrib_parts = []
    for index, bit in enumerate(reversed(bits)):
        arrived = swap(sent, "seq", bit, False if bit == bits[0] else None)
        if index < PARTS:
            contrib_parts.append(contrib_part(both, weight, index, PARTS))
        both, grads, arrived, contrib_parts = lax.optimization_barrier(
            (both, grads, arrived, contrib_parts)
        )
        grads = grads + arrived.astype(F32)
        if bit < bits[0]:
            keep = grads.shape[0] // 2
            sent = grads[keep:].astype(BF16)
            grads = grads[:keep]
    contrib = jnp.concatenate(contrib_parts, axis=2)
    lower_half = from_cycle(contrib[1], "rep", 1)
    higher_half = from_cycle(contrib[0], "rep", -1)
    right_factor = jnp.stack([contrib[0] + lower_half, contrib[1] + higher_half], axis=0)

    near_b = grads.astype(BF16)
    for bit in bits:
        far_b = swap(near_b, "seq", bit)
        if bit > 1:
            near_b = jnp.concatenate([near_b, far_b], axis=0)
    proj_grad = project(me, feature_blocks, near_b, far_b)
    return (
        query_grad[None],
        grads[None],
        proj_grad[None],
        basis[None],
        right_factor[None, None],
    )


def solution(mesh):
    return jax.shard_map(
        on_device,
        mesh=mesh,
        in_specs=(
            P("rep", "seq", None),
            P("rep", "seq", None),
            P("rep", "seq", None),
            P("rep", "seq", None),
            P("rep", "seq", None),
            P("rep", None, "seq"),
            P("rep", "seq", None),
            P("rep", "seq", None),
            P("seq", None, None),
        ),
        out_specs=(
            P("rep", "seq", None),
            P("rep", "seq", None),
            P("rep", "seq", None),
            P("rep", None, None, "seq"),
            P("rep", "seq", None, None, None),
        ),
        check_vma=False,
    )
```

time: 119 us -> 107 us (0.90)
  Pallas kernels: 13.2 us -> 40 us
  matrix products: 17.9 us -> 0 us
  local copies, waits for them, and re-layouts: 10.5 us -> 2.69 us
  waiting for transfers between devices: 42.4 us -> 36.1 us
  starting transfers between devices: 29.7 us -> 24.4 us
  other arithmetic: 4.14 us -> 2.38 us
    pallas_call x2 -> x10, Pallas kernels: 12.7 us -> 39.5 us  [the longest x3 12.2 us: contrib_part(): pl.pallas_call(contrib_kernel, grid=(steps,), out_shape=jax.ShapeDtypeStr...]
    dot_general x2 -> x0, matrix products: 17.9 us -> none  [the longest x1 9.04 us: on_device(): jnp.einsum('ekr,rd->ekd', basis.astype(BF16), weight_block, preferred_ele...]
    ppermute x7 -> x4, waiting for transfers between devices: 9.49 us -> 0.01 us  [from_cycle(): lax.ppermute(block, axis, [(i, (i + distance) % count) for i in range(cou...]
    unnamed x28 -> x30, local copies, waits for them, and re-layouts: 7.12 us -> 2.58 us
    ppermute x7 -> x4, starting transfers between devices: 8.94 us -> 5.48 us  [from_cycle(): lax.ppermute(block, axis, [(i, (i + distance) % count) for i in range(cou...]
    ppermute x8 -> x9, waiting for transfers between devices: 32.9 us -> 36.1 us  [swap(): return lax.ppermute(block, axis, route)]
    another operation x3 -> x0, local copies, waits for them, and re-layouts: 2.66 us -> none  [the longest x1 2.63 us: on_device(): split_inputs = inputs[0].reshape(tok, count, width).transpose(1, 0, 2)]
    all_to_all x1, starting transfers between devices: 7.42 us -> 5.38 us  [on_device(): lax.all_to_all(packed, 'seq', split_axis=0, concat_axis=0, tiled=True)]
  transfers between devices with their start and end apart: 16 -> 14, of which waited for: 6 -> 4; matrix products, arithmetic and copies ran while one was open for 17% -> 1% of each run, Pallas kernels for 10% -> 36%
where the time goes in v2:
time: 107 us
  Pallas kernels  40 us (37%)
  waiting for transfers between devices  36.1 us (34%)
  starting transfers between devices  24.4 us (23%)
  local copies, waits for them, and re-layouts  2.69 us (3%)
  other arithmetic  2.38 us (2%)
    ppermute x9, waiting for transfers between devices, swap(): return lax.ppermute(block, axis, route)  36.1 us
    ppermute x9, starting transfers between devices, swap(): return lax.ppermute(block, axis, route)  13.5 us
    pallas_call x3, Pallas kernels, contrib_part(): pl.pallas_call(contrib_kernel, grid=(steps,), out_shape=jax.ShapeDtypeStr...  12.2 us
    pallas_call x3, Pallas kernels, acts_part(): pl.pallas_call(acts_kernel, grid=(steps,), out_shape=jax.ShapeDtypeStruct...  11.7 us
    pallas_call x1, Pallas kernels, attend(): pl.pallas_call(functools.partial(attention_kernel, order, group, join, hd...  10.8 us
    ppermute x4, starting transfers between devices, from_cycle(): lax.ppermute(block, axis, [(i, (i + distance) % count) for i in range(cou...  5.48 us
    all_to_all x1, starting transfers between devices, on_device(): lax.all_to_all(packed, 'seq', split_axis=0, concat_axis=0, tiled=True)  5.38 us
    unnamed x30, local copies, waits for them, and re-layouts  2.58 us
  transfers between devices with their start and end apart: 14, of which 4 were waited for; matrix products, arithmetic and copies ran while one was open for 1% of the time, Pallas kernels for 36%

profile of v2, /device:TPU:0, one launch (start us, length us, event | category | flops | bytes accessed | tf_op | source)
XLA Modules:
  0.0 106.5 jit_solution(15411587678661182690)
XLA Ops:
  0.6 0.8 pad_maximum_fusion.2
  1.4 5.9 %collective-permute-start = (bf16[128,256]{1,0:T(8,128)(2,1)S(1)}, bf16[128,256]{1,0:T(8,128)(2,1)S(1)}, u32[]{:S(2)}, u32[]{:S(2)}) collective-permute-start(bf16[128,256]{1,0:T(8,128)(2,1)S(1)} %pad_maximum_fusion.2), channel_id=1, source_target_pairs={{0,4},{1,5},{2,6},{3,7},{8,12},{9,13},{10,14},{11,15},{16,20},{17,... | collective-permute-start | bytes 196616 | tf_op jit(solution)/shard_map/ppermute | solution.py:77
  7.4 0.0 copy-start
  7.4 1.4 %copy-done = bf16[1,128,6144]{2,1,0:T(8,128)(2,1)S(1)} copy-done((bf16[1,128,6144]{2,1,0:T(8,128)(2,1)S(1)}, bf16[1,128,6144]{2,1,0:T(8,128)(2,1)}, u32[]{:S(2)}) %copy-start) | copy-done | bytes 1572888
  8.8 1.3 %shard_map.129 = bf16[8,128,768]{2,1,0:T(8,128)(2,1)} custom-call(bf16[128,6144]{1,0:T(8,128)(2,1)S(1)} %bitcast.29), custom_call_target="tpu_custom_call" | custom-call | bytes 3145728 | tf_op jit(solution)/shard_map/pallas_call | solution.py:206
  10.1 0.0 copy-done.3
  10.1 3.9 %shard_map.130 = f32[4,512]{1,0:T(4,128)S(1)} custom-call(bf16[4,6144]{1,0:T(4,128)(2,1)S(1)} %bitcast.33, bf16[1536,6144]{1,0:T(8,128)(2,1)} %bitcast.38), custom_call_target="tpu_custom_call" | custom-call | flops 25165824 | bytes 6291456 | tf_op jit(solution)/shard_map/pallas_call | solution.py:254
  13.9 0.0 collective-permute-done
  14.0 0.0 copy-start.1
  14.0 0.0 copy-start.2
  14.0 1.6 %collective-permute-start.1 = (bf16[256,256]{1,0:T(8,128)(2,1)S(1)}, bf16[256,256]{1,0:T(8,128)(2,1)S(1)}, u32[]{:S(2)}, u32[]{:S(2)}) collective-permute-start(bf16[256,256]{1,0:T(8,128)(2,1)S(1)} %constant_dynamic-update-slice_fusion), channel_id=1, source_target_pairs={{0,2},{1,3},{2,0},{3,1},{4,6},{5,7},{6,4},{7,5},{8,10},{9,11},{10,... | collective-permute-start | bytes 393224 | tf_op jit(solution)/shard_map/ppermute | solution.py:77
  15.6 3.9 %shard_map.131 = f32[4,512]{1,0:T(4,128)S(1)} custom-call(bf16[4,6144]{1,0:T(4,128)(2,1)S(1)} %bitcast.34, bf16[1536,6144]{1,0:T(8,128)(2,1)} %bitcast.39), custom_call_target="tpu_custom_call" | custom-call | flops 25165824 | bytes 6291456 | tf_op jit(solution)/shard_map/pallas_call | solution.py:254
  19.5 0.0 collective-permute-done.1
  19.5 0.1 collective-permute-start.2
  19.6 0.0 copy-done.1
  19.6 0.0 copy-done.2
  19.6 0.5 shard_map.128.delta_ref
  20.1 0.0 copy-start.6
  20.1 0.0 copy-start.7
  20.1 3.9 %shard_map.132 = f32[4,512]{1,0:T(4,128)S(1)} custom-call(bf16[4,6144]{1,0:T(4,128)(2,1)S(1)} %bitcast.35, bf16[1536,6144]{1,0:T(8,128)(2,1)} %bitcast.40), custom_call_target="tpu_custom_call" | custom-call | flops 25165824 | bytes 6291456 | tf_op jit(solution)/shard_map/pallas_call | solution.py:254
  24.1 0.0 collective-permute-done.2.far_ref
  24.1 0.0 copy-start.9
  24.1 2.5 %collective-permute-start.4 = (f32[4,1536]{1,0:T(4,128)S(1)}, f32[4,1536]{1,0:T(4,128)S(1)}, u32[]{:S(2)}, u32[]{:S(2)}) collective-permute-start(f32[4,1536]{1,0:T(4,128)S(1)} %constant_dynamic-update-slice_fusion.4.acts_ref), channel_id=1, source_target_pairs={{0,24},{8,0},{16,8},{24,16},{1,25},{9,1},{17,9},{25,17},{2,26},{10... | collective-permute-start | bytes 73736 | tf_op jit(solution)/shard_map/ppermute | solution.py:337
  26.6 0.0 collective-permute-start.3
  26.6 0.0 copy-done.6
  26.6 10.8 %shard_map.133 = (f32[128,3072]{1,0:T(8,128)}, f32[512,256]{1,0:T(8,128)S(1)}, f32[512,256]{1,0:T(8,128)S(1)}) custom-call(s32[1]{0:T(128)} %bitcast.me_ref, bf16[128,3072]{1,0:T(8,128)(2,1)S(1)} %bitcast.36, bf16[128,3072]{1,0:T(8,128)(2,1)S(1)} %bitcast.32, f32[24,128]{1,0:T(8,128)S(1)} %bitcast.37, f32[24,128]{1,0:T(8,128)S(1)} %shard_map.128.delta_ref, ...), custom_call_target="tpu_custom_call" | custom-call | flops 8053063680 | bytes 3145728 | tf_op jit(solution)/shard_map/pallas_call | solution.py:174
  37.5 0.0 collective-permute-done.4.higher_ref
  37.5 0.0 collective-permute-done.3.lower_ref
  37.5 0.0 copy-start.11
  37.5 0.3 collective-permute-start.5
  37.8 0.3 copy-done.10
  38.1 0.0 copy-done.11
  38.1 2.1 %shard_map.134 = (f32[2,4,1536]{2,1,0:T(4,128)}, bf16[8,1536]{1,0:T(8,128)(2,1)}) custom-call(f32[4,1536]{1,0:T(4,128)} %copy-done.9, f32[4,1536]{1,0:T(4,128)} %copy-done.11, f32[4,1536]{1,0:T(4,128)} %copy-done.10), custom_call_target="tpu_custom_call" | custom-call | flops 368640 | bytes 245760 | tf_op jit(solution)/shard_map/pallas_call | solution.py:293
  40.2 0.7 copy-done.4
  40.9 4.0 %shard_map.135 = f32[2,4,2048]{2,1,0:T(4,128)S(1)} custom-call(bf16[8,1536]{1,0:T(8,128)(2,1)S(1)} %copy-done.4, bf16[1536,6144]{1,0:T(8,128)(2,1)} %bitcast.41), custom_call_target="tpu_custom_call" | custom-call | flops 50331648 | bytes 6291456 | tf_op jit(solution)/shard_map/pallas_call | solution.py:319
  45.0 0.0 collective-permute-done.5
  45.0 0.1 add.15
  45.1 1.1 %collective-permute-start.6 = (bf16[256,256]{1,0:T(8,128)(2,1)S(1)}, bf16[256,256]{1,0:T(8,128)(2,1)S(1)}, u32[]{:S(2)}, u32[]{:S(2)}) collective-permute-start(bf16[256,256]{1,0:T(8,128)(2,1)S(1)} %slice.42), channel_id=1, source_target_pairs={{0,2},{1,3},{2,0},{3,1},{4,6},{5,7},{6,4},{7,5},{8,10},{9,11},{10,... | collective-permute-start | bytes 393224 | tf_op jit(solution)/shard_map/ppermute | solution.py:77
  46.2 4.1 %shard_map.136 = f32[2,4,2048]{2,1,0:T(4,128)S(1)} custom-call(bf16[8,1536]{1,0:T(8,128)(2,1)S(1)} %copy-done.4, bf16[1536,6144]{1,0:T(8,128)(2,1)} %bitcast.42), custom_call_target="tpu_custom_call" | custom-call | flops 50331648 | bytes 6291456 | tf_op jit(solution)/shard_map/pallas_call | solution.py:319
  50.3 0.4 collective-permute-done.6
  50.8 0.0 copy-start.8
  50.8 1.4 %collective-permute-start.7 = (bf16[128,256]{1,0:T(8,128)(2,1)S(1)}, bf16[128,256]{1,0:T(8,128)(2,1)S(1)}, u32[]{:S(2)}, u32[]{:S(2)}) collective-permute-start(bf16[128,256]{1,0:T(8,128)(2,1)S(1)} %slice.43), channel_id=1, source_target_pairs={{4,0},{5,1},{6,2},{7,3},{12,8},{13,9},{14,10},{15,11},{20,16},{21,... | collective-permute-start | bytes 196616 | tf_op jit(solution)/shard_map/ppermute | solution.py:77
  52.2 5.4 %all-to-all-start = ((bf16[8,128,768]{2,1,0:T(8,128)(2,1)}), bf16[8,128,768]{2,1,0:T(8,128)(2,1)S(1)}, u32[]{:S(2)}, u32[]{:S(2)}) async-start(bf16[8,128,768]{2,1,0:T(8,128)(2,1)} %shard_map.129), calls=%async_computation | async-start | bytes 3145728 | tf_op jit(solution)/shard_map/all_to_all | solution.py:365
  57.6 0.0 copy-done.8
  57.6 0.0 copy-done.5
  57.6 0.0 slice-start
  57.7 4.1 %shard_map.137 = f32[2,4,2048]{2,1,0:T(4,128)S(1)} custom-call(bf16[8,1536]{1,0:T(8,128)(2,1)S(1)} %copy-done.5, bf16[1536,6144]{1,0:T(8,128)(2,1)} %bitcast.43), custom_call_target="tpu_custom_call" | custom-call | flops 50331648 | bytes 6291456 | tf_op jit(solution)/shard_map/pallas_call | solution.py:319
  61.7 0.0 collective-permute-done.7
  61.7 0.0 slice-done
  61.8 0.7 fusion
  62.4 2.9 %collective-permute-start.8 = (bf16[128,256]{1,0:T(8,128)(2,1)S(1)}, bf16[128,256]{1,0:T(8,128)(2,1)S(1)}, u32[]{:S(2)}, u32[]{:S(2)}) collective-permute-start(bf16[128,256]{1,0:T(8,128)(2,1)S(1)} %get-tuple-element.87), channel_id=1, source_target_pairs={{0,4},{1,5},{2,6},{3,7},{4,0},{5,1},{6,2},{7,3},{8,12},{9,13},{10,... | collective-permute-start | bytes 196616 | tf_op jit(solution)/shard_map/ppermute | solution.py:77
  65.4 1.8 %collective-permute-start.11 = (f32[4,6144]{1,0:T(4,128)S(1)}, f32[4,6144]{1,0:T(4,128)S(1)}, u32[]{:S(2)}, u32[]{:S(2)}) collective-permute-start(f32[4,6144]{1,0:T(4,128)S(1)} %get-tuple-element.85), channel_id=1, source_target_pairs={{0,8},{8,16},{16,24},{24,0},{1,9},{9,17},{17,25},{25,1},{2,10},{10... | collective-permute-start | bytes 294920 | tf_op jit(solution)/shard_map/ppermute | solution.py:337
  67.2 1.2 %collective-permute-start.12 = (f32[4,6144]{1,0:T(4,128)S(1)}, f32[4,6144]{1,0:T(4,128)S(1)}, u32[]{:S(2)}, u32[]{:S(2)}) collective-permute-start(f32[4,6144]{1,0:T(4,128)S(1)} %get-tuple-element.86), channel_id=1, source_target_pairs={{0,24},{8,0},{16,8},{24,16},{1,25},{9,1},{17,9},{25,17},{2,26},{10... | collective-permute-start | bytes 294920 | tf_op jit(solution)/shard_map/ppermute | solution.py:337
  68.4 29.9 %collective-permute-done.8 = bf16[128,256]{1,0:T(8,128)(2,1)S(1)} collective-permute-done((bf16[128,256]{1,0:T(8,128)(2,1)S(1)}, bf16[128,256]{1,0:T(8,128)(2,1)S(1)}, u32[]{:S(2)}, u32[]{:S(2)}) %collective-permute-start.8) | collective-permute-done | bytes 65568 | tf_op jit(solution)/shard_map/ppermute | solution.py:77
  98.3 0.1 collective-permute-start.9
  98.4 0.0 collective-permute-done.11
  98.4 0.0 collective-permute-done.12
  98.4 0.1 add_bitcast_fusion.1
  98.4 4.9 %collective-permute-done.9 = bf16[256,256]{1,0:T(8,128)(2,1)S(1)} collective-permute-done((bf16[256,256]{1,0:T(8,128)(2,1)S(1)}, bf16[256,256]{1,0:T(8,128)(2,1)S(1)}, u32[]{:S(2)}, u32[]{:S(2)}) %collective-permute-start.9) | collective-permute-done | bytes 131104 | tf_op jit(solution)/shard_map/ppermute | solution.py:77
  103.4 0.1 collective-permute-start.10
  103.5 0.7 maximum_bitcast_fusion
  104.2 0.8 collective-permute-done.10.far_ref
  105.0 0.0 all-to-all-done.x_ref
  105.0 1.5 %shard_map.138 = f32[768,256]{1,0:T(8,128)} custom-call(s32[1]{0:T(128)} %bitcast.me_ref, bf16[8,128,768]{2,1,0:T(8,128)(2,1)S(1)} %all-to-all-done.x_ref, bf16[512,256]{1,0:T(8,128)(2,1)S(1)} %pad_maximum_fusion.near_ref, bf16[512,256]{1,0:T(8,128)(2,1)S(1)} %collective-permute-done.10.far_ref), custom_call_target="tpu_custom_call" | custom-call | flops 402653184 | bytes 1572864 | tf_op jit(solution)/shard_map/pallas_call | solution.py:228
  (23 shorter events, 0.2 us)
Async XLA Ops:
  1.4 12.5 %collective-permute-start = (bf16[128,256]{1,0:T(8,128)(2,1)S(1)}, bf16[128,256]{1,0:T(8,128)(2,1)S(1)}, u32[]{:S(2)}, u32[]{:S(2)}) collective-permute-start(bf16[128,256]{1,0:T(8,128)(2,1)S(1)} %pad_maximum_fusion.2), channel_id=1, source_target_pairs={{0,4},{1,5},{2,6},{3,7},{8,12},{9,13},{10,14},{11,15},{16,20},{17,... | collective-permute-start | bytes 196616 | tf_op jit(solution)/shard_map/ppermute | solution.py:77
  7.4 1.4 %copy-start = (bf16[1,128,6144]{2,1,0:T(8,128)(2,1)S(1)}, bf16[1,128,6144]{2,1,0:T(8,128)(2,1)}, u32[]{:S(2)}) copy-start(bf16[1,128,6144]{2,1,0:T(8,128)(2,1)} %param.15) | copy-start | bytes 4718596
  8.8 1.3 %copy-start.3 = (bf16[1,4,6144]{2,1,0:T(4,128)(2,1)S(1)}, bf16[1,4,6144]{2,1,0:T(4,128)(2,1)}, u32[]{:S(2)}) copy-start(bf16[1,4,6144]{2,1,0:T(4,128)(2,1)} %param.17) | copy-start | bytes 147460
  14.0 5.7 %copy-start.1 = (bf16[1,128,3072]{2,1,0:T(8,128)(2,1)S(1)}, bf16[1,128,3072]{2,1,0:T(8,128)(2,1)}, u32[]{:S(2)}) copy-start(bf16[1,128,3072]{2,1,0:T(8,128)(2,1)} %param.12) | copy-start | bytes 2359300
  14.0 5.7 %copy-start.2 = (bf16[1,128,3072]{2,1,0:T(8,128)(2,1)S(1)}, bf16[1,128,3072]{2,1,0:T(8,128)(2,1)}, u32[]{:S(2)}) copy-start(bf16[1,128,3072]{2,1,0:T(8,128)(2,1)} %param.13) | copy-start | bytes 2359300
  14.0 5.5 %collective-permute-start.1 = (bf16[256,256]{1,0:T(8,128)(2,1)S(1)}, bf16[256,256]{1,0:T(8,128)(2,1)S(1)}, u32[]{:S(2)}, u32[]{:S(2)}) collective-permute-start(bf16[256,256]{1,0:T(8,128)(2,1)S(1)} %constant_dynamic-update-slice_fusion), channel_id=1, source_target_pairs={{0,2},{1,3},{2,0},{3,1},{4,6},{5,7},{6,4},{7,5},{8,10},{9,11},{10,... | collective-permute-start | bytes 393224 | tf_op jit(solution)/shard_map/ppermute | solution.py:77
  19.5 4.5 %collective-permute-start.2 = (bf16[512,256]{1,0:T(8,128)(2,1)S(1)}, bf16[512,256]{1,0:T(8,128)(2,1)S(1)}, u32[]{:S(2)}, u32[]{:S(2)}) collective-permute-start(bf16[512,256]{1,0:T(8,128)(2,1)S(1)} %constant_dynamic-update-slice_fusion.2.near_ref), channel_id=1, source_target_pairs={{0,1},{1,0},{2,3},{3,2},{4,5},{5,4},{6,7},{7,6},{8,9},{9,8},{10,11... | collective-permute-start | bytes 786440 | tf_op jit(solution)/shard_map/ppermute | solution.py:77
  20.1 6.5 %copy-start.6 = (bf16[1,128,3072]{2,1,0:T(8,128)(2,1)S(1)}, bf16[1,128,3072]{2,1,0:T(8,128)(2,1)}, u32[]{:S(2)}) copy-start(bf16[1,128,3072]{2,1,0:T(8,128)(2,1)} %param.9) | copy-start | bytes 2359300
  20.1 6.5 %copy-start.7 = (f32[1,24,128]{2,1,0:T(8,128)S(1)}, f32[1,24,128]{2,1,0:T(8,128)}, u32[]{:S(2)}) copy-start(f32[1,24,128]{2,1,0:T(8,128)} %param.14) | copy-start | bytes 36868
  24.1 13.3 %copy-start.9 = (f32[4,1536]{1,0:T(4,128)}, f32[4,1536]{1,0:T(4,128)S(1)}, u32[]{:S(2)}) copy-start(f32[4,1536]{1,0:T(4,128)S(1)} %constant_dynamic-update-slice_fusion.4.acts_ref) | copy-start | bytes 73732
  24.1 13.3 %collective-permute-start.4 = (f32[4,1536]{1,0:T(4,128)S(1)}, f32[4,1536]{1,0:T(4,128)S(1)}, u32[]{:S(2)}, u32[]{:S(2)}) collective-permute-start(f32[4,1536]{1,0:T(4,128)S(1)} %constant_dynamic-update-slice_fusion.4.acts_ref), channel_id=1, source_target_pairs={{0,24},{8,0},{16,8},{24,16},{1,25},{9,1},{17,9},{25,17},{2,26},{10... | collective-permute-start | bytes 73736 | tf_op jit(solution)/shard_map/ppermute | solution.py:337
  26.6 10.8 %collective-permute-start.3 = (f32[4,1536]{1,0:T(4,128)S(1)}, f32[4,1536]{1,0:T(4,128)S(1)}, u32[]{:S(2)}, u32[]{:S(2)}) collective-permute-start(f32[4,1536]{1,0:T(4,128)S(1)} %constant_dynamic-update-slice_fusion.4.acts_ref), channel_id=1, source_target_pairs={{0,8},{8,16},{16,24},{24,0},{1,9},{9,17},{17,25},{25,1},{2,10},{10... | collective-permute-start | bytes 73736 | tf_op jit(solution)/shard_map/ppermute | solution.py:337
  37.5 0.6 copy-start.10
  37.5 0.6 copy-start.11
  37.5 7.5 %collective-permute-start.5 = (f32[512,256]{1,0:T(8,128)S(1)}, f32[512,256]{1,0:T(8,128)S(1)}, u32[]{:S(2)}, u32[]{:S(2)}) collective-permute-start(f32[512,256]{1,0:T(8,128)S(1)} %get-tuple-element.66), channel_id=1, source_target_pairs={{0,1},{1,0},{2,3},{3,2},{4,5},{5,4},{6,7},{7,6},{8,9},{9,8},{10,11... | collective-permute-start | bytes 1572872 | tf_op jit(solution)/shard_map/ppermute | solution.py:77
  40.2 0.7 copy-start.4
  45.1 5.7 %collective-permute-start.6 = (bf16[256,256]{1,0:T(8,128)(2,1)S(1)}, bf16[256,256]{1,0:T(8,128)(2,1)S(1)}, u32[]{:S(2)}, u32[]{:S(2)}) collective-permute-start(bf16[256,256]{1,0:T(8,128)(2,1)S(1)} %slice.42), channel_id=1, source_target_pairs={{0,2},{1,3},{2,0},{3,1},{4,6},{5,7},{6,4},{7,5},{8,10},{9,11},{10,... | collective-permute-start | bytes 393224 | tf_op jit(solution)/shard_map/ppermute | solution.py:77
  50.8 6.9 %copy-start.8 = (f32[256,256]{1,0:T(8,128)}, f32[256,256]{1,0:T(8,128)S(1)}, u32[]{:S(2)}) copy-start(f32[256,256]{1,0:T(8,128)S(1)} %convert_add_fusion) | copy-start | bytes 786436
  50.8 6.8 %copy-start.5 = (bf16[8,1536]{1,0:T(8,128)(2,1)S(1)}, bf16[8,1536]{1,0:T(8,128)(2,1)}, u32[]{:S(2)}) copy-start(bf16[8,1536]{1,0:T(8,128)(2,1)} %get-tuple-element.71.both_ref) | copy-start | bytes 73732
  50.8 10.9 %collective-permute-start.7 = (bf16[128,256]{1,0:T(8,128)(2,1)S(1)}, bf16[128,256]{1,0:T(8,128)(2,1)S(1)}, u32[]{:S(2)}, u32[]{:S(2)}) collective-permute-start(bf16[128,256]{1,0:T(8,128)(2,1)S(1)} %slice.43), channel_id=1, source_target_pairs={{4,0},{5,1},{6,2},{7,3},{12,8},{13,9},{14,10},{15,11},{20,16},{21,... | collective-permute-start | bytes 196616 | tf_op jit(solution)/shard_map/ppermute | solution.py:77
  52.2 52.8 %all-to-all-start = ((bf16[8,128,768]{2,1,0:T(8,128)(2,1)}), bf16[8,128,768]{2,1,0:T(8,128)(2,1)S(1)}, u32[]{:S(2)}, u32[]{:S(2)}) async-start(bf16[8,128,768]{2,1,0:T(8,128)(2,1)} %shard_map.129), calls=%async_computation | async-start | bytes 3145728 | tf_op jit(solution)/shard_map/all_to_all | solution.py:365
  57.6 4.1 %slice-start = ((f32[256,256]{1,0:T(8,128)}), f32[128,256]{1,0:T(8,128)S(1)}, s32[]{:S(2)}) async-start(f32[256,256]{1,0:T(8,128)} %copy-done.8), calls=%async_computation.1 | async-start | bytes 262144 | tf_op jit(solution)/shard_map/slice | solution.py:386
  62.4 35.8 %collective-permute-start.8 = (bf16[128,256]{1,0:T(8,128)(2,1)S(1)}, bf16[128,256]{1,0:T(8,128)(2,1)S(1)}, u32[]{:S(2)}, u32[]{:S(2)}) collective-permute-start(bf16[128,256]{1,0:T(8,128)(2,1)S(1)} %get-tuple-element.87), channel_id=1, source_target_pairs={{0,4},{1,5},{2,6},{3,7},{4,0},{5,1},{6,2},{7,3},{8,12},{9,13},{10,... | collective-permute-start | bytes 196616 | tf_op jit(solution)/shard_map/ppermute | solution.py:77
  65.4 33.0 %collective-permute-start.11 = (f32[4,6144]{1,0:T(4,128)S(1)}, f32[4,6144]{1,0:T(4,128)S(1)}, u32[]{:S(2)}, u32[]{:S(2)}) collective-permute-start(f32[4,6144]{1,0:T(4,128)S(1)} %get-tuple-element.85), channel_id=1, source_target_pairs={{0,8},{8,16},{16,24},{24,0},{1,9},{9,17},{17,25},{25,1},{2,10},{10... | collective-permute-start | bytes 294920 | tf_op jit(solution)/shard_map/ppermute | solution.py:337
  67.2 31.2 %collective-permute-start.12 = (f32[4,6144]{1,0:T(4,128)S(1)}, f32[4,6144]{1,0:T(4,128)S(1)}, u32[]{:S(2)}, u32[]{:S(2)}) collective-permute-start(f32[4,6144]{1,0:T(4,128)S(1)} %get-tuple-element.86), channel_id=1, source_target_pairs={{0,24},{8,0},{16,8},{24,16},{1,25},{9,1},{17,9},{25,17},{2,26},{10... | collective-permute-start | bytes 294920 | tf_op jit(solution)/shard_map/ppermute | solution.py:337
  98.3 5.1 %collective-permute-start.9 = (bf16[256,256]{1,0:T(8,128)(2,1)S(1)}, bf16[256,256]{1,0:T(8,128)(2,1)S(1)}, u32[]{:S(2)}, u32[]{:S(2)}) collective-permute-start(bf16[256,256]{1,0:T(8,128)(2,1)S(1)} %pad_maximum_fusion.1), channel_id=1, source_target_pairs={{0,2},{1,3},{2,0},{3,1},{4,6},{5,7},{6,4},{7,5},{8,10},{9,11},{10,... | collective-permute-start | bytes 393224 | tf_op jit(solution)/shard_map/ppermute | solution.py:77
  103.4 1.6 %collective-permute-start.10 = (bf16[512,256]{1,0:T(8,128)(2,1)S(1)}, bf16[512,256]{1,0:T(8,128)(2,1)S(1)}, u32[]{:S(2)}, u32[]{:S(2)}) collective-permute-start(bf16[512,256]{1,0:T(8,128)(2,1)S(1)} %pad_maximum_fusion.near_ref), channel_id=1, source_target_pairs={{0,1},{1,0},{2,3},{3,2},{4,5},{5,4},{6,7},{7,6},{8,9},{9,8},{10,11... | collective-permute-start | bytes 786440 | tf_op jit(solution)/shard_map/ppermute | solution.py:77

commit v3 on v2

--- a/solution.py
+++ b/solution.py
@@ -15,7 +15,9 @@
 BF16 = jnp.bfloat16
 VMEM_LIMIT = 48 * 1024 * 1024
 PARTS = 3
+STREAMS = 4
 PARTS = 3
+STREAMS = 4
 COST = pl.CostEstimate(flops=1, bytes_accessed=1, transcendentals=0)
 
 
@@ -192,56 +194,63 @@
     )(me[None], queries, out_grad, norm, delta, near, far)
 
 
-def pack_kernel(x_ref, out_ref):
-    width = out_ref.shape[2]
-    for j in range(out_ref.shape[0]):
-        out_ref[j] = x_ref[:, j * width : (j + 1) * width]
-
-
-def pack(inputs, count):
+def pack_kernel(width, me_ref, x_ref, *out_refs):
+    me = me_ref[0]
+    for x, out_ref in enumerate(out_refs):
+        first = pl.multiple_of((me ^ x) * width, width)
+        out_ref[...] = x_ref[:, pl.ds(first, width)]
+
+
+def pack(me, inputs, count):
     tok, cols = inputs.shape
     width = cols // count
     if width % 128:
-        return inputs.reshape(tok, count, width).transpose(1, 0, 2)
-    return pl.pallas_call(
-        pack_kernel,
-        out_shape=jax.ShapeDtypeStruct((count, tok, width), inputs.dtype),
-        in_specs=vmem_specs(1),
-        out_specs=pl.BlockSpec(memory_space=pltpu.VMEM),
+        return [
+            lax.dynamic_slice_in_dim(inputs, (me ^ x) * width, width, axis=1)
+            for x in range(count)
+        ]
+    return pl.pallas_call(
+        functools.partial(pack_kernel, width),
+        out_shape=[jax.ShapeDtypeStruct((tok, width), inputs.dtype)] * count,
+        in_specs=[pl.BlockSpec(memory_space=pltpu.SMEM)] + vmem_specs(1),
+        out_specs=vmem_specs(count),
         compiler_params=pltpu.CompilerParams(vmem_limit_bytes=VMEM_LIMIT),
         cost_estimate=pl.CostEstimate(
             flops=0, bytes_accessed=4 * tok * cols, transcendentals=0
         ),
-    )(inputs)
-
-
-def project_kernel(order, me_ref, x_ref, near_ref, far_ref, out_ref):
-    me = me_ref[0]
-    x = jnp.concatenate([x_ref[me ^ part] for part in order], axis=0)
+    )(me[None], inputs)
+
+
+def project_kernel(*refs):
+    *x_refs, near_ref, far_ref, out_ref = refs
+    x = jnp.concatenate([ref[...] for ref in x_refs], axis=0)
     grads = jnp.concatenate([near_ref[...], far_ref[...]], axis=0)
     out_ref[...] = dot_tn(x, grads)
 
 
-def project(me, blocks, near, far):
-    count, tok, width = blocks.shape
+def project(parts, near, far):
+    tok, width = parts[0].shape
     cols = near.shape[1]
     return pl.pallas_call(
-        functools.partial(project_kernel, gather_order(count)),
+        project_kernel,
         out_shape=jax.ShapeDtypeStruct((width, cols), F32),
-        in_specs=[pl.BlockSpec(memory_space=pltpu.SMEM)] + vmem_specs(3),
+        in_specs=vmem_specs(len(parts) + 2),
         out_specs=pl.BlockSpec(memory_space=pltpu.VMEM),
         compiler_params=pltpu.CompilerParams(vmem_limit_bytes=VMEM_LIMIT),
         cost_estimate=pl.CostEstimate(
-            flops=2 * count * tok * width * cols,
-            bytes_accessed=2 * count * tok * width,
+            flops=2 * len(parts) * tok * width * cols,
+            bytes_accessed=2 * len(parts) * tok * width,
             transcendentals=0,
         ),
-    )(me[None], blocks, near, far)
-
-
-def acts_kernel(factor_ref, w_ref, out_ref):
+    )(*parts, near, far)
+
+
+def acts_kernel(factor_ref, *refs):
+    *w_refs, out_ref = refs
     rank, rows = out_ref.shape
-    part = dot_nt(w_ref[...], factor_ref[...])
+    factor = factor_ref[...]
+    parts = [dot_nt(ref[...], factor) for ref in w_refs]
+    part = jnp.concatenate(parts, axis=0)
     wide = jnp.concatenate([part, jnp.zeros((rows, 128 - rank), F32)], axis=1)
     out_ref[...] = wide.T[:rank]
 
@@ -249,22 +258,24 @@
 def acts_part(factor, weight, index, parts):
     rank, cols = factor.shape
     rows = weight.shape[0] // parts
-    tile = 256 if rows % 256 == 0 else rows
+    tile = 128 if rows % 128 == 0 else rows
     steps = rows // tile
+    block = tile // STREAMS
+    specs = [
+        pl.BlockSpec((block, cols), lambda i, s=s: ((index * steps + i) * STREAMS + s, 0))
+        for s in range(STREAMS)
+    ]
     return pl.pallas_call(
         acts_kernel,
         grid=(steps,),
         out_shape=jax.ShapeDtypeStruct((rank, rows), F32),
-        in_specs=[
-            pl.BlockSpec((rank, cols), lambda i: (0, 0)),
-            pl.BlockSpec((tile, cols), lambda i: (index * steps + i, 0)),
-        ],
+        in_specs=[pl.BlockSpec((rank, cols), lambda i: (0, 0))] + specs,
         out_specs=pl.BlockSpec((rank, tile), lambda i: (0, i)),
         compiler_params=pltpu.CompilerParams(vmem_limit_bytes=VMEM_LIMIT),
         cost_estimate=pl.CostEstimate(
             flops=2 * rank * rows * cols, bytes_accessed=2 * rows * cols, transcendentals=0
         ),
-    )(factor, weight)
+    )(factor, *[weight] * STREAMS)
 
 
 def orthonormal(diffs):
@@ -304,9 +315,15 @@
     )(acts, lower, higher)
 
 
-def contrib_kernel(both_ref, w_ref, out_ref):
+def contrib_kernel(both_ref, *refs):
+    *w_refs, out_ref = refs
     rank = out_ref.shape[1]
-    part = jnp.dot(both_ref[...], w_ref[...], preferred_element_type=F32)
+    block = w_refs[0].shape[0]
+    part = None
+    for s, ref in enumerate(w_refs):
+        both = both_ref[:, s * block : (s + 1) * block]
+        more = jnp.dot(both, ref[...], preferred_element_type=F32)
+        part = more if part is None else part + more
     for e in range(2):
         out_ref[e] = part[e * rank : (e + 1) * rank]
 
@@ -316,20 +333,24 @@
     cols = weight.shape[1] // parts
     tile = 512 if cols % 512 == 0 else cols
     steps = cols // tile
+    block = rows // STREAMS
+    specs = [
+        pl.BlockSpec((block, tile), lambda i, s=s: (s, index * steps + i))
+        for s in range(STREAMS)
+    ]
+    if block % 16:
+        specs = [pl.BlockSpec((rows, tile), lambda i: (0, index * steps + i))]
     return pl.pallas_call(
         contrib_kernel,
         grid=(steps,),
         out_shape=jax.ShapeDtypeStruct((2, count // 2, cols), F32),
-        in_specs=[
-            pl.BlockSpec((count, rows), lambda i: (0, 0)),
-            pl.BlockSpec((rows, tile), lambda i: (0, index * steps + i)),
-        ],
+        in_specs=[pl.BlockSpec((count, rows), lambda i: (0, 0))] + specs,
         out_specs=pl.BlockSpec((2, count // 2, tile), lambda i: (0, 0, i)),
         compiler_params=pltpu.CompilerParams(vmem_limit_bytes=VMEM_LIMIT),
         cost_estimate=pl.CostEstimate(
             flops=2 * count * rows * cols, bytes_accessed=2 * rows * cols, transcendentals=0
         ),
-    )(both, weight)
+    )(both, *[weight] * len(specs))
 
 
 def from_cycle(block, axis, distance):
@@ -348,27 +369,51 @@
     factor = initial_right_factor[0]
     weight = mlp_weight[0]
 
+    far_parts = list(range(count // 2, count))
+    near_parts = [x for x in range(1, count // 2) if x > 1] + ([1] if count > 2 else [])
+    quarter = -(-len(far_parts) // 4)
+    due = [far_parts[i * quarter : (i + 1) * quarter] for i in range(4)]
+    packed = pack(me, inputs[0], count)
+    parts = {0: packed[0]}
+
+    def send(group):
+        for x in group:
+            parts[x] = swap(packed[x], "seq", x)
+
+    def tie(group, values):
+        values, held, rest = lax.optimization_barrier(
+            (values, [parts[x] for x in group], [packed[x] for x in range(count)])
+        )
+        parts.update(zip(group, held))
+        packed[:] = rest
+        return values
+
+    packed = list(packed)
     near = jnp.concatenate([keys[0], values[0]], axis=-1)
-    packed = pack(inputs[0], count)
+    near = tie([], near)
+
     acts_parts = []
     for index, bit in enumerate(bits):
         far = swap(near, "seq", bit, True if index == 0 else None)
+        if index < 2:
+            send(due[index])
         if index < PARTS:
             acts_parts.append(acts_part(factor, weight, index, PARTS))
-        factor, near, far, packed, acts_parts = lax.optimization_barrier(
-            (factor, near, far, packed, acts_parts)
+        factor, near, far, acts_parts = tie(
+            due[0] if index == 1 else [], (factor, near, far, acts_parts)
         )
         if bit > 1:
             near = jnp.concatenate([near, far], axis=0)
     acts = jnp.concatenate(acts_parts, axis=1)
-
-    feature_blocks = lax.all_to_all(packed, "seq", split_axis=0, concat_axis=0, tiled=True)
     lower_acts = from_cycle(acts, "rep", 1)
     higher_acts = from_cycle(acts, "rep", -1)
+    send(due[2])
 
     delta = head_delta(out_grad[0], outputs[0], heads)
+    delta, near, far = tie(due[1], (delta, near, far))
     query_grad, grads, sent = attend(me, queries[0], out_grad[0], log_norm[0], delta, near, far)
-    lower_acts, higher_acts, sent = lax.optimization_barrier((lower_acts, higher_acts, sent))
+    lower_acts, higher_acts, sent = tie(due[2], (lower_acts, higher_acts, sent))
+    send(due[3])
 
     basis, both = make_basis(acts, lower_acts, higher_acts)
     contrib_parts = []
@@ -376,8 +421,11 @@
         arrived = swap(sent, "seq", bit, False if bit == bits[0] else None)
         if index < PARTS:
             contrib_parts.append(contrib_part(both, weight, index, PARTS))
-        both, grads, arrived, contrib_parts = lax.optimization_barrier(
-            (both, grads, arrived, contrib_parts)
+        if index == 1:
+            send(near_parts)
+        both, grads, arrived, contrib_parts = tie(
+            due[3] if index == 1 else [],
+            (both, grads, arrived, contrib_parts),
         )
         grads = grads + arrived.astype(F32)
         if bit < bits[0]:
@@ -394,7 +442,7 @@
         far_b = swap(near_b, "seq", bit)
         if bit > 1:
             near_b = jnp.concatenate([near_b, far_b], axis=0)
-    proj_grad = project(me, feature_blocks, near_b, far_b)
+    proj_grad = project([parts[x] for x in gather_order(count)], near_b, far_b)
     return (
         query_grad[None],
         grads[None],

time: 107 us -> 93.7 us (0.88)
  waiting for transfers between devices: 36.1 us -> 6.94 us
  starting transfers between devices: 24.4 us -> 39.2 us
  Pallas kernels: 40 us -> 41.2 us
    ppermute x9 -> x16, waiting for transfers between devices: 36.1 us -> 6.44 us  [swap(): return lax.ppermute(block, axis, route)]
    ppermute x9 -> x16, starting transfers between devices: 13.5 us -> 27.1 us  [swap(): return lax.ppermute(block, axis, route)]
    ppermute x4, starting transfers between devices: 5.48 us -> 12.1 us  [from_cycle(): lax.ppermute(block, axis, [(i, (i + distance) % count) for i in range(cou...]
    all_to_all x1 -> x0, starting transfers between devices: 5.38 us -> none  [on_device(): lax.all_to_all(packed, 'seq', split_axis=0, concat_axis=0, tiled=True)]
    pallas_call x3, Pallas kernels: 11.7 us -> 14.3 us  [acts_part(): pl.pallas_call(acts_kernel, grid=(steps,), out_shape=jax.ShapeDtypeStruct...]
    pallas_call x2, Pallas kernels: 2.79 us -> 1.6 us  [the longest x1 1.5 us: project(): pl.pallas_call(project_kernel, out_shape=jax.ShapeDtypeStruct((width, col...]
    unnamed x30 -> x26, local copies, waits for them, and re-layouts: 2.58 us -> 2.26 us
  transfers between devices with their start and end apart: 14 -> 20, of which waited for: 4 -> 6; matrix products, arithmetic and copies ran while one was open for 1% -> 2% of each run, Pallas kernels for 36% -> 43%
where the time goes in v3:
time: 93.7 us; the launch traced here: 93.1 us
  Pallas kernels  41.2 us (44%)
  starting transfers between devices  39.2 us (42%)
  waiting for transfers between devices  6.94 us (7%)
  local copies, waits for them, and re-layouts  2.37 us (3%)
  other arithmetic  2.36 us (3%)
  between operations  0.95 us (1%)
    ppermute x16, starting transfers between devices, swap(): return lax.ppermute(block, axis, route)  27.1 us
    pallas_call x3, Pallas kernels, acts_part(): pl.pallas_call(acts_kernel, grid=(steps,), out_shape=jax.ShapeDtypeStruct...  14.3 us
    ppermute x4, starting transfers between devices, from_cycle(): lax.ppermute(block, axis, [(i, (i + distance) % count) for i in range(cou...  12.1 us
    pallas_call x3, Pallas kernels, contrib_part(): pl.pallas_call(contrib_kernel, grid=(steps,), out_shape=jax.ShapeDtypeStr...  11.9 us
    pallas_call x1, Pallas kernels, attend(): pl.pallas_call(functools.partial(attention_kernel, order, group, join, hd...  10.8 us
    ppermute x16, waiting for transfers between devices, swap(): return lax.ppermute(block, axis, route)  6.44 us
    unnamed x26, local copies, waits for them, and re-layouts  2.26 us
    pallas_call x1, Pallas kernels, make_basis(): pl.pallas_call(basis_kernel, out_shape=[jax.ShapeDtypeStruct((2, rank, ro...  2.1 us
  transfers between devices with their start and end apart: 20, of which 6 were waited for; matrix products, arithmetic and copies ran while one was open for 2% of the time, Pallas kernels for 43%

profile of v3, /device:TPU:0, one launch (start us, length us, event | category | flops | bytes accessed | tf_op | source)
XLA Modules:
  0.0 93.1 jit_solution(9838206865405012475)
XLA Ops:
  0.6 0.8 pad_maximum_fusion.2
  1.4 1.4 %copy-done = bf16[1,128,6144]{2,1,0:T(8,128)(2,1)S(1)} copy-done((bf16[1,128,6144]{2,1,0:T(8,128)(2,1)S(1)}, bf16[1,128,6144]{2,1,0:T(8,128)(2,1)}, u32[]{:S(2)}) %copy-start) | copy-done | bytes 1572888
  2.8 0.1 shard_map.129
  3.0 5.9 %collective-permute-start = (bf16[128,256]{1,0:T(8,128)(2,1)S(1)}, bf16[128,256]{1,0:T(8,128)(2,1)S(1)}, u32[]{:S(2)}, u32[]{:S(2)}) collective-permute-start(bf16[128,256]{1,0:T(8,128)(2,1)S(1)} %pad_maximum_fusion.2), channel_id=1, source_target_pairs={{0,4},{1,5},{2,6},{3,7},{8,12},{9,13},{10,14},{11,15},{16,20},{17,... | collective-permute-start | bytes 196616 | tf_op jit(solution)/shard_map/ppermute | solution.py:79
  8.9 0.1 collective-permute-start.2
  9.0 4.8 %shard_map.130 = f32[4,512]{1,0:T(4,128)S(1)} custom-call(bf16[4,6144]{1,0:T(4,128)(2,1)S(1)} %bitcast.33, bf16[1536,6144]{1,0:T(8,128)(2,1)} %bitcast.38, bf16[1536,6144]{1,0:T(8,128)(2,1)} %bitcast.39, bf16[1536,6144]{1,0:T(8,128)(2,1)} %bitcast.40, bf16[1536,6144]{1,0:T(8,128)(2,1)} %bitcast.41), custom_call_target="tpu_custom_call" | custom-call | flops 25165824 | bytes 6291456 | tf_op jit(solution)/shard_map/pallas_call | solution.py:268
  13.8 0.0 collective-permute-done
  13.9 0.0 copy-start.1
  13.9 0.0 copy-start.2
  13.9 3.6 %collective-permute-start.1 = (bf16[256,256]{1,0:T(8,128)(2,1)S(1)}, bf16[256,256]{1,0:T(8,128)(2,1)S(1)}, u32[]{:S(2)}, u32[]{:S(2)}) collective-permute-start(bf16[256,256]{1,0:T(8,128)(2,1)S(1)} %constant_dynamic-update-slice_fusion), channel_id=1, source_target_pairs={{0,2},{1,3},{2,0},{3,1},{4,6},{5,7},{6,4},{7,5},{8,10},{9,11},{10,... | collective-permute-start | bytes 393224 | tf_op jit(solution)/shard_map/ppermute | solution.py:79
  17.5 4.8 %shard_map.131 = f32[4,512]{1,0:T(4,128)S(1)} custom-call(bf16[4,6144]{1,0:T(4,128)(2,1)S(1)} %bitcast.34, bf16[1536,6144]{1,0:T(8,128)(2,1)} %bitcast.42, bf16[1536,6144]{1,0:T(8,128)(2,1)} %bitcast.43, bf16[1536,6144]{1,0:T(8,128)(2,1)} %bitcast.44, bf16[1536,6144]{1,0:T(8,128)(2,1)} %bitcast.45), custom_call_target="tpu_custom_call" | custom-call | flops 25165824 | bytes 6291456 | tf_op jit(solution)/shard_map/pallas_call | solution.py:268
  22.3 1.0 %collective-permute-done.1 = bf16[256,256]{1,0:T(8,128)(2,1)S(1)} collective-permute-done((bf16[256,256]{1,0:T(8,128)(2,1)S(1)}, bf16[256,256]{1,0:T(8,128)(2,1)S(1)}, u32[]{:S(2)}, u32[]{:S(2)}) %collective-permute-start.1) | collective-permute-done | bytes 131104 | tf_op jit(solution)/shard_map/ppermute | solution.py:79
  23.3 0.0 collective-permute-done.2.refs_1_
  23.3 0.1 collective-permute-start.3
  23.4 0.5 shard_map.128.delta_ref
  23.9 0.0 copy-start.5
  23.9 0.0 copy-start.6
  23.9 2.6 %collective-permute-start.4 = (bf16[128,768]{1,0:T(8,128)(2,1)S(1)}, bf16[128,768]{1,0:T(8,128)(2,1)S(1)}, u32[]{:S(2)}, u32[]{:S(2)}) collective-permute-start(bf16[128,768]{1,0:T(8,128)(2,1)S(1)} %get-tuple-element.114), channel_id=1, source_target_pairs={{0,5},{1,4},{2,7},{3,6},{4,1},{5,0},{6,3},{7,2},{8,13},{9,12},{10,... | collective-permute-start | bytes 589832 | tf_op jit(solution)/shard_map/ppermute | solution.py:79
  26.5 4.8 %shard_map.132 = f32[4,512]{1,0:T(4,128)S(1)} custom-call(bf16[4,6144]{1,0:T(4,128)(2,1)S(1)} %bitcast.35, bf16[1536,6144]{1,0:T(8,128)(2,1)} %bitcast.49, bf16[1536,6144]{1,0:T(8,128)(2,1)} %bitcast.47, bf16[1536,6144]{1,0:T(8,128)(2,1)} %bitcast.48, bf16[1536,6144]{1,0:T(8,128)(2,1)} %bitcast.46), custom_call_target="tpu_custom_call" | custom-call | flops 25165824 | bytes 6291456 | tf_op jit(solution)/shard_map/pallas_call | solution.py:268
  31.3 0.0 collective-permute-done.3.far_ref
  31.3 0.0 copy-start.7
  31.3 1.5 %collective-permute-start.5 = (f32[4,1536]{1,0:T(4,128)S(1)}, f32[4,1536]{1,0:T(4,128)S(1)}, u32[]{:S(2)}, u32[]{:S(2)}) collective-permute-start(f32[4,1536]{1,0:T(4,128)S(1)} %constant_dynamic-update-slice_fusion.4.acts_ref), channel_id=1, source_target_pairs={{0,8},{8,16},{16,24},{24,0},{1,9},{9,17},{17,25},{25,1},{2,10},{10... | collective-permute-start | bytes 73736 | tf_op jit(solution)/shard_map/ppermute | solution.py:358
  32.9 1.4 %collective-permute-start.6 = (f32[4,1536]{1,0:T(4,128)S(1)}, f32[4,1536]{1,0:T(4,128)S(1)}, u32[]{:S(2)}, u32[]{:S(2)}) collective-permute-start(f32[4,1536]{1,0:T(4,128)S(1)} %constant_dynamic-update-slice_fusion.4.acts_ref), channel_id=1, source_target_pairs={{0,24},{8,0},{16,8},{24,16},{1,25},{9,1},{17,9},{25,17},{2,26},{10... | collective-permute-start | bytes 73736 | tf_op jit(solution)/shard_map/ppermute | solution.py:358
  34.3 1.5 %collective-permute-start.7 = (bf16[128,768]{1,0:T(8,128)(2,1)S(1)}, bf16[128,768]{1,0:T(8,128)(2,1)S(1)}, u32[]{:S(2)}, u32[]{:S(2)}) collective-permute-start(bf16[128,768]{1,0:T(8,128)(2,1)S(1)} %get-tuple-element.132), channel_id=1, source_target_pairs={{0,6},{1,7},{2,4},{3,5},{4,2},{5,3},{6,0},{7,1},{8,14},{9,15},{10,... | collective-permute-start | bytes 589832 | tf_op jit(solution)/shard_map/ppermute | solution.py:79
  35.8 0.0 collective-permute-done.4.refs_5_
  35.8 10.8 %shard_map.133 = (f32[128,3072]{1,0:T(8,128)}, f32[512,256]{1,0:T(8,128)S(1)}, f32[512,256]{1,0:T(8,128)S(1)}) custom-call(s32[1]{0:T(128)} %bitcast.me_ref, bf16[128,3072]{1,0:T(8,128)(2,1)S(1)} %bitcast.36, bf16[128,3072]{1,0:T(8,128)(2,1)S(1)} %bitcast.32, f32[24,128]{1,0:T(8,128)S(1)} %bitcast.37, f32[24,128]{1,0:T(8,128)S(1)} %shard_map.128.delta_ref, ...), custom_call_target="tpu_custom_call" | custom-call | flops 8053063680 | bytes 3145728 | tf_op jit(solution)/shard_map/pallas_call | solution.py:176
  46.6 0.0 collective-permute-done.5.lower_ref
  46.6 0.0 collective-permute-done.6.higher_ref
  46.6 0.0 copy-start.9
  46.6 0.0 collective-permute-done.7.refs_3_
  46.6 0.5 collective-permute-start.8
  47.2 3.4 %collective-permute-start.10 = (bf16[128,768]{1,0:T(8,128)(2,1)S(1)}, bf16[128,768]{1,0:T(8,128)(2,1)S(1)}, u32[]{:S(2)}, u32[]{:S(2)}) collective-permute-start(bf16[128,768]{1,0:T(8,128)(2,1)S(1)} %get-tuple-element.154), channel_id=1, source_target_pairs={{0,7},{1,6},{2,5},{3,4},{4,3},{5,2},{6,1},{7,0},{8,15},{9,14},{10,... | collective-permute-start | bytes 589832 | tf_op jit(solution)/shard_map/ppermute | solution.py:79
  50.6 2.1 %shard_map.134 = (f32[2,4,1536]{2,1,0:T(4,128)}, bf16[8,1536]{1,0:T(8,128)(2,1)}) custom-call(f32[4,1536]{1,0:T(4,128)} %copy-done.7, f32[4,1536]{1,0:T(4,128)} %copy-done.8, f32[4,1536]{1,0:T(4,128)} %copy-done.9), custom_call_target="tpu_custom_call" | custom-call | flops 368640 | bytes 245760 | tf_op jit(solution)/shard_map/pallas_call | solution.py:304
  52.7 0.7 copy-done.4
  53.4 3.9 %shard_map.135 = f32[2,4,2048]{2,1,0:T(4,128)S(1)} custom-call(bf16[8,1536]{1,0:T(8,128)(2,1)S(1)} %copy-done.4, bf16[1536,6144]{1,0:T(8,128)(2,1)} %bitcast.50, bf16[1536,6144]{1,0:T(8,128)(2,1)} %bitcast.51, bf16[1536,6144]{1,0:T(8,128)(2,1)} %bitcast.52, bf16[1536,6144]{1,0:T(8,128)(2,1)} %bitcast.53), custom_call_target="tpu_custom_call" | custom-call | flops 50331648 | bytes 6291456 | tf_op jit(solution)/shard_map/pallas_call | solution.py:343
  57.4 0.0 collective-permute-done.8
  57.4 0.1 add.15
  57.5 0.1 collective-permute-start.9
  57.6 4.0 %shard_map.136 = f32[2,4,2048]{2,1,0:T(4,128)S(1)} custom-call(bf16[8,1536]{1,0:T(8,128)(2,1)S(1)} %copy-done.4, bf16[1536,6144]{1,0:T(8,128)(2,1)} %bitcast.54, bf16[1536,6144]{1,0:T(8,128)(2,1)} %bitcast.55, bf16[1536,6144]{1,0:T(8,128)(2,1)} %bitcast.56, bf16[1536,6144]{1,0:T(8,128)(2,1)} %bitcast.57), custom_call_target="tpu_custom_call" | custom-call | flops 50331648 | bytes 6291456 | tf_op jit(solution)/shard_map/pallas_call | solution.py:343
  61.6 0.0 collective-permute-done.10.refs_7_
  61.6 1.5 %collective-permute-done.9 = bf16[256,256]{1,0:T(8,128)(2,1)S(1)} collective-permute-done((bf16[256,256]{1,0:T(8,128)(2,1)S(1)}, bf16[256,256]{1,0:T(8,128)(2,1)S(1)}, u32[]{:S(2)}, u32[]{:S(2)}) %collective-permute-start.9) | collective-permute-done | bytes 131104 | tf_op jit(solution)/shard_map/ppermute | solution.py:79
  63.2 1.3 %collective-permute-start.11 = (bf16[128,256]{1,0:T(8,128)(2,1)S(1)}, bf16[128,256]{1,0:T(8,128)(2,1)S(1)}, u32[]{:S(2)}, u32[]{:S(2)}) collective-permute-start(bf16[128,256]{1,0:T(8,128)(2,1)S(1)} %slice.43), channel_id=1, source_target_pairs={{4,0},{5,1},{6,2},{7,3},{12,8},{13,9},{14,10},{15,11},{20,16},{21,... | collective-permute-start | bytes 196616 | tf_op jit(solution)/shard_map/ppermute | solution.py:79
  64.5 0.6 collective-permute-start.12
  65.0 0.0 collective-permute-start.13
  65.0 1.6 %collective-permute-start.14 = (bf16[128,768]{1,0:T(8,128)(2,1)S(1)}, bf16[128,768]{1,0:T(8,128)(2,1)S(1)}, u32[]{:S(2)}, u32[]{:S(2)}) collective-permute-start(bf16[128,768]{1,0:T(8,128)(2,1)S(1)} %get-tuple-element.161), channel_id=1, source_target_pairs={{0,3},{1,2},{2,1},{3,0},{4,7},{5,6},{6,5},{7,4},{8,11},{9,10},{10,... | collective-permute-start | bytes 589832 | tf_op jit(solution)/shard_map/ppermute | solution.py:79
  66.7 4.0 %shard_map.137 = f32[2,4,2048]{2,1,0:T(4,128)S(1)} custom-call(bf16[8,1536]{1,0:T(8,128)(2,1)S(1)} %copy-done.4, bf16[1536,6144]{1,0:T(8,128)(2,1)} %bitcast.58, bf16[1536,6144]{1,0:T(8,128)(2,1)} %bitcast.59, bf16[1536,6144]{1,0:T(8,128)(2,1)} %bitcast.60, bf16[1536,6144]{1,0:T(8,128)(2,1)} %bitcast.61), custom_call_target="tpu_custom_call" | custom-call | flops 50331648 | bytes 6291456 | tf_op jit(solution)/shard_map/pallas_call | solution.py:343
  70.7 0.2 collective-permute-done.11
  70.9 0.7 fusion
  71.6 3.3 %collective-permute-start.15 = (bf16[128,256]{1,0:T(8,128)(2,1)S(1)}, bf16[128,256]{1,0:T(8,128)(2,1)S(1)}, u32[]{:S(2)}, u32[]{:S(2)}) collective-permute-start(bf16[128,256]{1,0:T(8,128)(2,1)S(1)} %get-tuple-element.181), channel_id=1, source_target_pairs={{0,4},{1,5},{2,6},{3,7},{4,0},{5,1},{6,2},{7,3},{8,12},{9,13},{10,... | collective-permute-start | bytes 196616 | tf_op jit(solution)/shard_map/ppermute | solution.py:79
  75.0 5.7 %collective-permute-start.18 = (f32[4,6144]{1,0:T(4,128)S(1)}, f32[4,6144]{1,0:T(4,128)S(1)}, u32[]{:S(2)}, u32[]{:S(2)}) collective-permute-start(f32[4,6144]{1,0:T(4,128)S(1)} %get-tuple-element.179), channel_id=1, source_target_pairs={{0,8},{8,16},{16,24},{24,0},{1,9},{9,17},{17,25},{25,1},{2,10},{10... | collective-permute-start | bytes 294920 | tf_op jit(solution)/shard_map/ppermute | solution.py:358
  80.7 0.0 collective-permute-done.15
  80.7 3.4 %collective-permute-start.19 = (f32[4,6144]{1,0:T(4,128)S(1)}, f32[4,6144]{1,0:T(4,128)S(1)}, u32[]{:S(2)}, u32[]{:S(2)}) collective-permute-start(f32[4,6144]{1,0:T(4,128)S(1)} %get-tuple-element.180), channel_id=1, source_target_pairs={{0,24},{8,0},{16,8},{24,16},{1,25},{9,1},{17,9},{25,17},{2,26},{10... | collective-permute-start | bytes 294920 | tf_op jit(solution)/shard_map/ppermute | solution.py:358
  84.1 0.5 collective-permute-done.18
  84.6 2.4 %collective-permute-start.16 = (bf16[256,256]{1,0:T(8,128)(2,1)S(1)}, bf16[256,256]{1,0:T(8,128)(2,1)S(1)}, u32[]{:S(2)}, u32[]{:S(2)}) collective-permute-start(bf16[256,256]{1,0:T(8,128)(2,1)S(1)} %pad_maximum_fusion.1), channel_id=1, source_target_pairs={{0,2},{1,3},{2,0},{3,1},{4,6},{5,7},{6,4},{7,5},{8,10},{9,11},{10,... | collective-permute-start | bytes 393224 | tf_op jit(solution)/shard_map/ppermute | solution.py:79
  87.0 0.0 collective-permute-done.19
  87.0 0.1 add_bitcast_fusion.1
  87.1 2.9 %collective-permute-done.16 = bf16[256,256]{1,0:T(8,128)(2,1)S(1)} collective-permute-done((bf16[256,256]{1,0:T(8,128)(2,1)S(1)}, bf16[256,256]{1,0:T(8,128)(2,1)S(1)}, u32[]{:S(2)}, u32[]{:S(2)}) %collective-permute-start.16) | collective-permute-done | bytes 131104 | tf_op jit(solution)/shard_map/ppermute | solution.py:79
  90.0 0.1 collective-permute-start.17
  90.1 0.7 maximum_bitcast_fusion
  90.8 0.0 collective-permute-done.12.refs_2_
  90.8 0.0 collective-permute-done.13.refs_4_
  90.8 0.0 collective-permute-done.14.refs_6_
  90.8 0.8 collective-permute-done.17.refs_9_
  91.6 1.5 %shard_map.138 = f32[768,256]{1,0:T(8,128)} custom-call(bf16[128,768]{1,0:T(8,128)(2,1)S(1)} %get-tuple-element.91.refs_0_, bf16[128,768]{1,0:T(8,128)(2,1)S(1)} %collective-permute-done.2.refs_1_, bf16[128,768]{1,0:T(8,128)(2,1)S(1)} %collective-permute-done.12.refs_2_, bf16[128,768]{1,0:T(8,128)(2,1)S(1)} %collective-permute-done.7.refs_3_, ...), custom_call_target="tpu_custom_call" | custom-call | flops 402653184 | bytes 1572864 | tf_op jit(solution)/shard_map/pallas_call | solution.py:234
  (30 shorter events, 0.3 us)
Async XLA Ops:
  0.6 8.4 %copy-start.3 = (bf16[1,4,6144]{2,1,0:T(4,128)(2,1)S(1)}, bf16[1,4,6144]{2,1,0:T(4,128)(2,1)}, u32[]{:S(2)}) copy-start(bf16[1,4,6144]{2,1,0:T(4,128)(2,1)} %param.17) | copy-start | bytes 147460
  1.4 1.4 %copy-start = (bf16[1,128,6144]{2,1,0:T(8,128)(2,1)S(1)}, bf16[1,128,6144]{2,1,0:T(8,128)(2,1)}, u32[]{:S(2)}) copy-start(bf16[1,128,6144]{2,1,0:T(8,128)(2,1)} %param.15) | copy-start | bytes 4718596
  3.0 10.8 %collective-permute-start = (bf16[128,256]{1,0:T(8,128)(2,1)S(1)}, bf16[128,256]{1,0:T(8,128)(2,1)S(1)}, u32[]{:S(2)}, u32[]{:S(2)}) collective-permute-start(bf16[128,256]{1,0:T(8,128)(2,1)S(1)} %pad_maximum_fusion.2), channel_id=1, source_target_pairs={{0,4},{1,5},{2,6},{3,7},{8,12},{9,13},{10,14},{11,15},{16,20},{17,... | collective-permute-start | bytes 196616 | tf_op jit(solution)/shard_map/ppermute | solution.py:79
  8.9 14.4 %collective-permute-start.2 = (bf16[128,768]{1,0:T(8,128)(2,1)S(1)}, bf16[128,768]{1,0:T(8,128)(2,1)S(1)}, u32[]{:S(2)}, u32[]{:S(2)}) collective-permute-start(bf16[128,768]{1,0:T(8,128)(2,1)S(1)} %get-tuple-element.103), channel_id=1, source_target_pairs={{0,4},{1,5},{2,6},{3,7},{4,0},{5,1},{6,2},{7,3},{8,12},{9,13},{10,... | collective-permute-start | bytes 589832 | tf_op jit(solution)/shard_map/ppermute | solution.py:79
  13.9 9.5 %copy-start.1 = (bf16[1,128,3072]{2,1,0:T(8,128)(2,1)S(1)}, bf16[1,128,3072]{2,1,0:T(8,128)(2,1)}, u32[]{:S(2)}) copy-start(bf16[1,128,3072]{2,1,0:T(8,128)(2,1)} %param.12) | copy-start | bytes 2359300
  13.9 9.5 %copy-start.2 = (bf16[1,128,3072]{2,1,0:T(8,128)(2,1)S(1)}, bf16[1,128,3072]{2,1,0:T(8,128)(2,1)}, u32[]{:S(2)}) copy-start(bf16[1,128,3072]{2,1,0:T(8,128)(2,1)} %param.13) | copy-start | bytes 2359300
  13.9 9.4 %collective-permute-start.1 = (bf16[256,256]{1,0:T(8,128)(2,1)S(1)}, bf16[256,256]{1,0:T(8,128)(2,1)S(1)}, u32[]{:S(2)}, u32[]{:S(2)}) collective-permute-start(bf16[256,256]{1,0:T(8,128)(2,1)S(1)} %constant_dynamic-update-slice_fusion), channel_id=1, source_target_pairs={{0,2},{1,3},{2,0},{3,1},{4,6},{5,7},{6,4},{7,5},{8,10},{9,11},{10,... | collective-permute-start | bytes 393224 | tf_op jit(solution)/shard_map/ppermute | solution.py:79
  23.3 8.0 %collective-permute-start.3 = (bf16[512,256]{1,0:T(8,128)(2,1)S(1)}, bf16[512,256]{1,0:T(8,128)(2,1)S(1)}, u32[]{:S(2)}, u32[]{:S(2)}) collective-permute-start(bf16[512,256]{1,0:T(8,128)(2,1)S(1)} %constant_dynamic-update-slice_fusion.2.near_ref), channel_id=1, source_target_pairs={{0,1},{1,0},{2,3},{3,2},{4,5},{5,4},{6,7},{7,6},{8,9},{9,8},{10,11... | collective-permute-start | bytes 786440 | tf_op jit(solution)/shard_map/ppermute | solution.py:79
  23.9 11.9 %copy-start.5 = (bf16[1,128,3072]{2,1,0:T(8,128)(2,1)S(1)}, bf16[1,128,3072]{2,1,0:T(8,128)(2,1)}, u32[]{:S(2)}) copy-start(bf16[1,128,3072]{2,1,0:T(8,128)(2,1)} %param.9) | copy-start | bytes 2359300
  23.9 11.9 %copy-start.6 = (f32[1,24,128]{2,1,0:T(8,128)S(1)}, f32[1,24,128]{2,1,0:T(8,128)}, u32[]{:S(2)}) copy-start(f32[1,24,128]{2,1,0:T(8,128)} %param.14) | copy-start | bytes 36868
  23.9 11.9 %collective-permute-start.4 = (bf16[128,768]{1,0:T(8,128)(2,1)S(1)}, bf16[128,768]{1,0:T(8,128)(2,1)S(1)}, u32[]{:S(2)}, u32[]{:S(2)}) collective-permute-start(bf16[128,768]{1,0:T(8,128)(2,1)S(1)} %get-tuple-element.114), channel_id=1, source_target_pairs={{0,5},{1,4},{2,7},{3,6},{4,1},{5,0},{6,3},{7,2},{8,13},{9,12},{10,... | collective-permute-start | bytes 589832 | tf_op jit(solution)/shard_map/ppermute | solution.py:79
  31.3 15.3 %copy-start.7 = (f32[4,1536]{1,0:T(4,128)}, f32[4,1536]{1,0:T(4,128)S(1)}, u32[]{:S(2)}) copy-start(f32[4,1536]{1,0:T(4,128)S(1)} %constant_dynamic-update-slice_fusion.4.acts_ref) | copy-start | bytes 73732
  31.3 15.3 %collective-permute-start.5 = (f32[4,1536]{1,0:T(4,128)S(1)}, f32[4,1536]{1,0:T(4,128)S(1)}, u32[]{:S(2)}, u32[]{:S(2)}) collective-permute-start(f32[4,1536]{1,0:T(4,128)S(1)} %constant_dynamic-update-slice_fusion.4.acts_ref), channel_id=1, source_target_pairs={{0,8},{8,16},{16,24},{24,0},{1,9},{9,17},{17,25},{25,1},{2,10},{10... | collective-permute-start | bytes 73736 | tf_op jit(solution)/shard_map/ppermute | solution.py:358
  32.9 13.7 %collective-permute-start.6 = (f32[4,1536]{1,0:T(4,128)S(1)}, f32[4,1536]{1,0:T(4,128)S(1)}, u32[]{:S(2)}, u32[]{:S(2)}) collective-permute-start(f32[4,1536]{1,0:T(4,128)S(1)} %constant_dynamic-update-slice_fusion.4.acts_ref), channel_id=1, source_target_pairs={{0,24},{8,0},{16,8},{24,16},{1,25},{9,1},{17,9},{25,17},{2,26},{10... | collective-permute-start | bytes 73736 | tf_op jit(solution)/shard_map/ppermute | solution.py:358
  34.3 12.3 %collective-permute-start.7 = (bf16[128,768]{1,0:T(8,128)(2,1)S(1)}, bf16[128,768]{1,0:T(8,128)(2,1)S(1)}, u32[]{:S(2)}, u32[]{:S(2)}) collective-permute-start(bf16[128,768]{1,0:T(8,128)(2,1)S(1)} %get-tuple-element.132), channel_id=1, source_target_pairs={{0,6},{1,7},{2,4},{3,5},{4,2},{5,3},{6,0},{7,1},{8,14},{9,15},{10,... | collective-permute-start | bytes 589832 | tf_op jit(solution)/shard_map/ppermute | solution.py:79
  46.6 4.0 %copy-start.8 = (f32[4,1536]{1,0:T(4,128)}, f32[4,1536]{1,0:T(4,128)S(1)}, u32[]{:S(2)}) copy-start(f32[4,1536]{1,0:T(4,128)S(1)} %collective-permute-done.5.lower_ref) | copy-start | bytes 73732
  46.6 4.0 %copy-start.9 = (f32[4,1536]{1,0:T(4,128)}, f32[4,1536]{1,0:T(4,128)S(1)}, u32[]{:S(2)}) copy-start(f32[4,1536]{1,0:T(4,128)S(1)} %collective-permute-done.6.higher_ref) | copy-start | bytes 73732
  46.6 10.8 %collective-permute-start.8 = (f32[512,256]{1,0:T(8,128)S(1)}, f32[512,256]{1,0:T(8,128)S(1)}, u32[]{:S(2)}, u32[]{:S(2)}) collective-permute-start(f32[512,256]{1,0:T(8,128)S(1)} %get-tuple-element.150), channel_id=1, source_target_pairs={{0,1},{1,0},{2,3},{3,2},{4,5},{5,4},{6,7},{7,6},{8,9},{9,8},{10,11... | collective-permute-start | bytes 1572872 | tf_op jit(solution)/shard_map/ppermute | solution.py:79
  47.2 14.4 %collective-permute-start.10 = (bf16[128,768]{1,0:T(8,128)(2,1)S(1)}, bf16[128,768]{1,0:T(8,128)(2,1)S(1)}, u32[]{:S(2)}, u32[]{:S(2)}) collective-permute-start(bf16[128,768]{1,0:T(8,128)(2,1)S(1)} %get-tuple-element.154), channel_id=1, source_target_pairs={{0,7},{1,6},{2,5},{3,4},{4,3},{5,2},{6,1},{7,0},{8,15},{9,14},{10,... | collective-permute-start | bytes 589832 | tf_op jit(solution)/shard_map/ppermute | solution.py:79
  52.7 0.7 copy-start.4
  57.5 5.6 %collective-permute-start.9 = (bf16[256,256]{1,0:T(8,128)(2,1)S(1)}, bf16[256,256]{1,0:T(8,128)(2,1)S(1)}, u32[]{:S(2)}, u32[]{:S(2)}) collective-permute-start(bf16[256,256]{1,0:T(8,128)(2,1)S(1)} %slice.42), channel_id=1, source_target_pairs={{0,2},{1,3},{2,0},{3,1},{4,6},{5,7},{6,4},{7,5},{8,10},{9,11},{10,... | collective-permute-start | bytes 393224 | tf_op jit(solution)/shard_map/ppermute | solution.py:79
  63.2 7.7 %collective-permute-start.11 = (bf16[128,256]{1,0:T(8,128)(2,1)S(1)}, bf16[128,256]{1,0:T(8,128)(2,1)S(1)}, u32[]{:S(2)}, u32[]{:S(2)}) collective-permute-start(bf16[128,256]{1,0:T(8,128)(2,1)S(1)} %slice.43), channel_id=1, source_target_pairs={{4,0},{5,1},{6,2},{7,3},{12,8},{13,9},{14,10},{15,11},{20,16},{21,... | collective-permute-start | bytes 196616 | tf_op jit(solution)/shard_map/ppermute | solution.py:79
  64.5 26.3 %collective-permute-start.12 = (bf16[128,768]{1,0:T(8,128)(2,1)S(1)}, bf16[128,768]{1,0:T(8,128)(2,1)S(1)}, u32[]{:S(2)}, u32[]{:S(2)}) collective-permute-start(bf16[128,768]{1,0:T(8,128)(2,1)S(1)} %get-tuple-element.160), channel_id=1, source_target_pairs={{0,2},{1,3},{2,0},{3,1},{4,6},{5,7},{6,4},{7,5},{8,10},{9,11},{10,... | collective-permute-start | bytes 589832 | tf_op jit(solution)/shard_map/ppermute | solution.py:79
  65.0 25.7 %collective-permute-start.13 = (bf16[128,768]{1,0:T(8,128)(2,1)S(1)}, bf16[128,768]{1,0:T(8,128)(2,1)S(1)}, u32[]{:S(2)}, u32[]{:S(2)}) collective-permute-start(bf16[128,768]{1,0:T(8,128)(2,1)S(1)} %get-tuple-element.159), channel_id=1, source_target_pairs={{0,1},{1,0},{2,3},{3,2},{4,5},{5,4},{6,7},{7,6},{8,9},{9,8},{10,11... | collective-permute-start | bytes 589832 | tf_op jit(solution)/shard_map/ppermute | solution.py:79
  65.0 25.7 %collective-permute-start.14 = (bf16[128,768]{1,0:T(8,128)(2,1)S(1)}, bf16[128,768]{1,0:T(8,128)(2,1)S(1)}, u32[]{:S(2)}, u32[]{:S(2)}) collective-permute-start(bf16[128,768]{1,0:T(8,128)(2,1)S(1)} %get-tuple-element.161), channel_id=1, source_target_pairs={{0,3},{1,2},{2,1},{3,0},{4,7},{5,6},{6,5},{7,4},{8,11},{9,10},{10,... | collective-permute-start | bytes 589832 | tf_op jit(solution)/shard_map/ppermute | solution.py:79
  71.6 9.1 %collective-permute-start.15 = (bf16[128,256]{1,0:T(8,128)(2,1)S(1)}, bf16[128,256]{1,0:T(8,128)(2,1)S(1)}, u32[]{:S(2)}, u32[]{:S(2)}) collective-permute-start(bf16[128,256]{1,0:T(8,128)(2,1)S(1)} %get-tuple-element.181), channel_id=1, source_target_pairs={{0,4},{1,5},{2,6},{3,7},{4,0},{5,1},{6,2},{7,3},{8,12},{9,13},{10,... | collective-permute-start | bytes 196616 | tf_op jit(solution)/shard_map/ppermute | solution.py:79
  75.0 9.6 %collective-permute-start.18 = (f32[4,6144]{1,0:T(4,128)S(1)}, f32[4,6144]{1,0:T(4,128)S(1)}, u32[]{:S(2)}, u32[]{:S(2)}) collective-permute-start(f32[4,6144]{1,0:T(4,128)S(1)} %get-tuple-element.179), channel_id=1, source_target_pairs={{0,8},{8,16},{16,24},{24,0},{1,9},{9,17},{17,25},{25,1},{2,10},{10... | collective-permute-start | bytes 294920 | tf_op jit(solution)/shard_map/ppermute | solution.py:358
  80.7 6.3 %collective-permute-start.19 = (f32[4,6144]{1,0:T(4,128)S(1)}, f32[4,6144]{1,0:T(4,128)S(1)}, u32[]{:S(2)}, u32[]{:S(2)}) collective-permute-start(f32[4,6144]{1,0:T(4,128)S(1)} %get-tuple-element.180), channel_id=1, source_target_pairs={{0,24},{8,0},{16,8},{24,16},{1,25},{9,1},{17,9},{25,17},{2,26},{10... | collective-permute-start | bytes 294920 | tf_op jit(solution)/shard_map/ppermute | solution.py:358
  84.6 5.4 %collective-permute-start.16 = (bf16[256,256]{1,0:T(8,128)(2,1)S(1)}, bf16[256,256]{1,0:T(8,128)(2,1)S(1)}, u32[]{:S(2)}, u32[]{:S(2)}) collective-permute-start(bf16[256,256]{1,0:T(8,128)(2,1)S(1)} %pad_maximum_fusion.1), channel_id=1, source_target_pairs={{0,2},{1,3},{2,0},{3,1},{4,6},{5,7},{6,4},{7,5},{8,10},{9,11},{10,... | collective-permute-start | bytes 393224 | tf_op jit(solution)/shard_map/ppermute | solution.py:79
  90.0 1.6 %collective-permute-start.17 = (bf16[512,256]{1,0:T(8,128)(2,1)S(1)}, bf16[512,256]{1,0:T(8,128)(2,1)S(1)}, u32[]{:S(2)}, u32[]{:S(2)}) collective-permute-start(bf16[512,256]{1,0:T(8,128)(2,1)S(1)} %pad_maximum_fusion.refs_8_), channel_id=1, source_target_pairs={{0,1},{1,0},{2,3},{3,2},{4,5},{5,4},{6,7},{7,6},{8,9},{9,8},{10,11... | collective-permute-start | bytes 786440 | tf_op jit(solution)/shard_map/ppermute | solution.py:79

commit v4 on v3

--- a/solution.py
+++ b/solution.py
@@ -15,9 +15,9 @@
 BF16 = jnp.bfloat16
 VMEM_LIMIT = 48 * 1024 * 1024
 PARTS = 3
-STREAMS = 4
+COST = pl.CostEstimate(flops=1, bytes_accessed=1, transcendentals=0)
 PARTS = 3
-STREAMS = 4
+COST = pl.CostEstimate(flops=1, bytes_accessed=1, transcendentals=0)
 COST = pl.CostEstimate(flops=1, bytes_accessed=1, transcendentals=0)
 
 
@@ -172,7 +172,6 @@
     order = gather_order(2 * half // tok)
     group = next(g for g in (4, 3, 2, 1) if heads % g == 0)
     join = 2 if half % (2 * tok) == 0 else 1
-    work = heads * tok * half * 2
     return pl.pallas_call(
         functools.partial(attention_kernel, order, group, join, hd ** (-0.5)),
         out_shape=[
@@ -188,9 +187,7 @@
             pltpu.VMEM((hd, group * tok), F32),
         ],
         compiler_params=pltpu.CompilerParams(vmem_limit_bytes=VMEM_LIMIT),
-        cost_estimate=pl.CostEstimate(
-            flops=20 * work * hd, bytes_accessed=8 * tok * cols, transcendentals=work
-        ),
+        cost_estimate=COST,
     )(me[None], queries, out_grad, norm, delta, near, far)
 
 
@@ -215,9 +212,7 @@
         in_specs=[pl.BlockSpec(memory_space=pltpu.SMEM)] + vmem_specs(1),
         out_specs=vmem_specs(count),
         compiler_params=pltpu.CompilerParams(vmem_limit_bytes=VMEM_LIMIT),
-        cost_estimate=pl.CostEstimate(
-            flops=0, bytes_accessed=4 * tok * cols, transcendentals=0
-        ),
+        cost_estimate=COST,
     )(me[None], inputs)
 
 
@@ -237,63 +232,67 @@
         in_specs=vmem_specs(len(parts) + 2),
         out_specs=pl.BlockSpec(memory_space=pltpu.VMEM),
         compiler_params=pltpu.CompilerParams(vmem_limit_bytes=VMEM_LIMIT),
-        cost_estimate=pl.CostEstimate(
-            flops=2 * len(parts) * tok * width * cols,
-            bytes_accessed=2 * len(parts) * tok * width,
-            transcendentals=0,
-        ),
+        cost_estimate=COST,
     )(*parts, near, far)
 
 
-def acts_kernel(factor_ref, *refs):
-    *w_refs, out_ref = refs
+def acts_kernel(factor_ref, w_ref, out_ref, sum_ref):
+    step = pl.program_id(0)
     rank, rows = out_ref.shape
-    factor = factor_ref[...]
-    parts = [dot_nt(ref[...], factor) for ref in w_refs]
-    part = jnp.concatenate(parts, axis=0)
-    wide = jnp.concatenate([part, jnp.zeros((rows, 128 - rank), F32)], axis=1)
-    out_ref[...] = wide.T[:rank]
+    part = dot_nt(w_ref[...], factor_ref[...])
+
+    @pl.when(step == 0)
+    def _():
+        sum_ref[...] = jnp.zeros_like(sum_ref)
+
+    sum_ref[:, :rank] += part
+
+    @pl.when(step == pl.num_programs(0) - 1)
+    def _():
+        out_ref[...] = sum_ref[...].T[:rank]
 
 
 def acts_part(factor, weight, index, parts):
     rank, cols = factor.shape
-    rows = weight.shape[0] // parts
-    tile = 128 if rows % 128 == 0 else rows
-    steps = rows // tile
-    block = tile // STREAMS
-    specs = [
-        pl.BlockSpec((block, cols), lambda i, s=s: ((index * steps + i) * STREAMS + s, 0))
-        for s in range(STREAMS)
-    ]
+    rows = weight.shape[0]
+    tile = 512 if cols % (512 * parts) == 0 else cols // parts
+    steps = cols // parts // tile
     return pl.pallas_call(
         acts_kernel,
         grid=(steps,),
         out_shape=jax.ShapeDtypeStruct((rank, rows), F32),
-        in_specs=[pl.BlockSpec((rank, cols), lambda i: (0, 0))] + specs,
-        out_specs=pl.BlockSpec((rank, tile), lambda i: (0, i)),
-        compiler_params=pltpu.CompilerParams(vmem_limit_bytes=VMEM_LIMIT),
-        cost_estimate=pl.CostEstimate(
-            flops=2 * rank * rows * cols, bytes_accessed=2 * rows * cols, transcendentals=0
-        ),
-    )(factor, *[weight] * STREAMS)
-
-
-def orthonormal(diffs):
+        in_specs=[
+            pl.BlockSpec((rank, tile), lambda i: (0, index * steps + i)),
+            pl.BlockSpec((rows, tile), lambda i: (0, index * steps + i)),
+        ],
+        out_specs=pl.BlockSpec((rank, rows), lambda i: (0, 0)),
+        scratch_shapes=[pltpu.VMEM((rows, 128), F32)],
+        compiler_params=pltpu.CompilerParams(vmem_limit_bytes=VMEM_LIMIT),
+        cost_estimate=COST,
+    )(factor, weight)
+
+
+def orthonormal(rows):
     columns = []
-    for index in range(diffs.shape[0]):
-        source = diffs[index : index + 1]
+    for source in rows:
         vector = source
         for previous in columns:
             vector = vector - jnp.mean(source * previous, axis=-1, keepdims=True) * previous
         columns.append(
             vector * lax.rsqrt(jnp.mean(vector * vector, axis=-1, keepdims=True) + EPSILON)
         )
-    return jnp.concatenate(columns, axis=0)
+    return columns
 
 
 def basis_kernel(acts_ref, lower_ref, higher_ref, basis_ref, both_ref):
-    acts = acts_ref[...]
-    edges = [orthonormal(acts - ref[...]) for ref in (lower_ref, higher_ref)]
+    rank = acts_ref.shape[0]
+    rows = [
+        acts_ref[k : k + 1]
+        - jnp.concatenate([lower_ref[k : k + 1], higher_ref[k : k + 1]], axis=0)
+        for k in range(rank)
+    ]
+    columns = orthonormal(rows)
+    edges = [jnp.concatenate([c[e : e + 1] for c in columns], axis=0) for e in range(2)]
     for e, edge in enumerate(edges):
         basis_ref[e] = edge
     both_ref[...] = jnp.concatenate(edges, axis=0).astype(BF16)
@@ -309,21 +308,13 @@
         ],
         in_specs=vmem_specs(3),
         out_specs=vmem_specs(2),
-        cost_estimate=pl.CostEstimate(
-            flops=60 * rank * rows, bytes_accessed=40 * rank * rows, transcendentals=0
-        ),
+        cost_estimate=COST,
     )(acts, lower, higher)
 
 
-def contrib_kernel(both_ref, *refs):
-    *w_refs, out_ref = refs
+def contrib_kernel(both_ref, w_ref, out_ref):
     rank = out_ref.shape[1]
-    block = w_refs[0].shape[0]
-    part = None
-    for s, ref in enumerate(w_refs):
-        both = both_ref[:, s * block : (s + 1) * block]
-        more = jnp.dot(both, ref[...], preferred_element_type=F32)
-        part = more if part is None else part + more
+    part = jnp.dot(both_ref[...], w_ref[...], preferred_element_type=F32)
     for e in range(2):
         out_ref[e] = part[e * rank : (e + 1) * rank]
 
@@ -333,24 +324,18 @@
     cols = weight.shape[1] // parts
     tile = 512 if cols % 512 == 0 else cols
     steps = cols // tile
-    block = rows // STREAMS
-    specs = [
-        pl.BlockSpec((block, tile), lambda i, s=s: (s, index * steps + i))
-        for s in range(STREAMS)
-    ]
-    if block % 16:
-        specs = [pl.BlockSpec((rows, tile), lambda i: (0, index * steps + i))]
     return pl.pallas_call(
         contrib_kernel,
         grid=(steps,),
         out_shape=jax.ShapeDtypeStruct((2, count // 2, cols), F32),
-        in_specs=[pl.BlockSpec((count, rows), lambda i: (0, 0))] + specs,
+        in_specs=[
+            pl.BlockSpec((count, rows), lambda i: (0, 0)),
+            pl.BlockSpec((rows, tile), lambda i: (0, index * steps + i)),
+        ],
         out_specs=pl.BlockSpec((2, count // 2, tile), lambda i: (0, 0, i)),
         compiler_params=pltpu.CompilerParams(vmem_limit_bytes=VMEM_LIMIT),
-        cost_estimate=pl.CostEstimate(
-            flops=2 * count * rows * cols, bytes_accessed=2 * rows * cols, transcendentals=0
-        ),
-    )(both, *[weight] * len(specs))
+        cost_estimate=COST,
+    )(both, weight)
 
 
 def from_cycle(block, axis, distance):
@@ -369,11 +354,13 @@
     factor = initial_right_factor[0]
     weight = mlp_weight[0]
 
-    far_parts = list(range(count // 2, count))
-    near_parts = [x for x in range(1, count // 2) if x > 1] + ([1] if count > 2 else [])
-    quarter = -(-len(far_parts) // 4)
-    due = [far_parts[i * quarter : (i + 1) * quarter] for i in range(4)]
-    packed = pack(me, inputs[0], count)
+    quarter = -(-(count // 2) // 4)
+    due = [
+        [x for x in range(count // 2 + i * quarter, count // 2 + (i + 1) * quarter) if x < count]
+        for i in range(4)
+    ]
+    rest = list(range(2, count // 2)) + ([1] if count > 2 else [])
+    packed = list(pack(me, inputs[0], count))
     parts = {0: packed[0]}
 
     def send(group):
@@ -381,30 +368,24 @@
             parts[x] = swap(packed[x], "seq", x)
 
     def tie(group, values):
-        values, held, rest = lax.optimization_barrier(
-            (values, [parts[x] for x in group], [packed[x] for x in range(count)])
+        values, held, packed[:] = lax.optimization_barrier(
+            (values, [parts[x] for x in group], list(packed))
         )
         parts.update(zip(group, held))
-        packed[:] = rest
         return values
 
-    packed = list(packed)
-    near = jnp.concatenate([keys[0], values[0]], axis=-1)
-    near = tie([], near)
-
-    acts_parts = []
+    near = tie([], jnp.concatenate([keys[0], values[0]], axis=-1))
+    acts = None
     for index, bit in enumerate(bits):
         far = swap(near, "seq", bit, True if index == 0 else None)
         if index < 2:
             send(due[index])
         if index < PARTS:
-            acts_parts.append(acts_part(factor, weight, index, PARTS))
-        factor, near, far, acts_parts = tie(
-            due[0] if index == 1 else [], (factor, near, far, acts_parts)
-        )
+            part = acts_part(factor, weight, index, PARTS)
+            acts = part if acts is None else acts + part
+        factor, near, far, acts = tie(due[0] if index == 1 else [], (factor, near, far, acts))
         if bit > 1:
             near = jnp.concatenate([near, far], axis=0)
-    acts = jnp.concatenate(acts_parts, axis=1)
     lower_acts = from_cycle(acts, "rep", 1)
     higher_acts = from_cycle(acts, "rep", -1)
     send(due[2])
@@ -417,35 +398,43 @@
 
     basis, both = make_basis(acts, lower_acts, higher_acts)
     contrib_parts = []
-    for index, bit in enumerate(reversed(bits)):
-        arrived = swap(sent, "seq", bit, False if bit == bits[0] else None)
+    last = bits[0]
+    for index, bit in enumerate(b for b in reversed(bits) if b != last):
+        arrived = swap(sent, "seq", bit)
+        share = PARTS - index if bit * 2 == last else 1
         if index < PARTS:
-            contrib_parts.append(contrib_part(both, weight, index, PARTS))
-        if index == 1:
-            send(near_parts)
+            contrib_parts += [
+                contrib_part(both, weight, index + i, PARTS) for i in range(share)
+            ]
+        if bit * 2 == last:
+            send(rest)
         both, grads, arrived, contrib_parts = tie(
-            due[3] if index == 1 else [],
-            (both, grads, arrived, contrib_parts),
+            due[3] if bit * 2 == last else [], (both, grads, arrived, contrib_parts)
         )
         grads = grads + arrived.astype(F32)
-        if bit < bits[0]:
-            keep = grads.shape[0] // 2
+        keep = grads.shape[0] // 2
+        if bit * 2 < last:
             sent = grads[keep:].astype(BF16)
             grads = grads[:keep]
     contrib = jnp.concatenate(contrib_parts, axis=2)
     lower_half = from_cycle(contrib[1], "rep", 1)
     higher_half = from_cycle(contrib[0], "rep", -1)
-    right_factor = jnp.stack([contrib[0] + lower_half, contrib[1] + higher_half], axis=0)
-
-    near_b = grads.astype(BF16)
-    for bit in bits:
+
+    upper = (me & last) != 0
+    arrived = swap(grads.astype(BF16), "seq", last).astype(F32)
+    mine, theirs = grads[:keep], grads[keep:]
+    own = jnp.where(upper, mine, mine + arrived[keep:])
+    other = jnp.where(upper, theirs + arrived[:keep], arrived[:keep])
+    near_b = jnp.concatenate([own, other], axis=0).astype(BF16)
+    for bit in bits[1:]:
         far_b = swap(near_b, "seq", bit)
         if bit > 1:
             near_b = jnp.concatenate([near_b, far_b], axis=0)
     proj_grad = project([parts[x] for x in gather_order(count)], near_b, far_b)
+    right_factor = jnp.stack([contrib[0] + lower_half, contrib[1] + higher_half], axis=0)
     return (
         query_grad[None],
-        grads[None],
+        own[None],
         proj_grad[None],
         basis[None],
         right_factor[None, None],

time: 93.7 us -> 95 us (1.014)
  starting transfers between devices: 39.2 us -> 32.5 us
  waiting for transfers between devices: 6.94 us -> 13.3 us
  Pallas kernels: 41.2 us -> 42.4 us
    ppermute x16 -> x15, waiting for transfers between devices: 6.44 us -> 13.3 us  [swap(): return lax.ppermute(block, axis, route)]
    ppermute x4, starting transfers between devices: 12.1 us -> 6.89 us  [from_cycle(): lax.ppermute(block, axis, [(i, (i + distance) % count) for i in range(cou...]
    ppermute x16 -> x15, starting transfers between devices: 27.1 us -> 25.6 us  [swap(): return lax.ppermute(block, axis, route)]
  transfers between devices with their start and end apart: 20 -> 19, of which waited for: 6 -> 4; matrix products, arithmetic and copies ran while one was open for 2% -> 2% of each run, Pallas kernels for 43% -> 43%
where the time goes in v4:
time: 95 us; the launch traced here: 94.5 us
  Pallas kernels  42.4 us (45%)
  starting transfers between devices  32.5 us (34%)
  waiting for transfers between devices  13.3 us (14%)
  local copies, waits for them, and re-layouts  2.86 us (3%)
  other arithmetic  2.44 us (3%)
    ppermute x15, starting transfers between devices, swap(): return lax.ppermute(block, axis, route)  25.6 us
    pallas_call x3, Pallas kernels, acts_part(): pl.pallas_call(acts_kernel, grid=(steps,), out_shape=jax.ShapeDtypeStruct...  15.2 us
    ppermute x15, waiting for transfers between devices, swap(): return lax.ppermute(block, axis, route)  13.3 us
    pallas_call x3, Pallas kernels, contrib_part(): pl.pallas_call(contrib_kernel, grid=(steps,), out_shape=jax.ShapeDtypeStr...  12.1 us
    pallas_call x1, Pallas kernels, attend(): pl.pallas_call(functools.partial(attention_kernel, order, group, join, hd...  10.9 us
    ppermute x4, starting transfers between devices, from_cycle(): lax.ppermute(block, axis, [(i, (i + distance) % count) for i in range(cou...  6.89 us
    unnamed x26, local copies, waits for them, and re-layouts  2.77 us
    pallas_call x1, Pallas kernels, make_basis(): pl.pallas_call(basis_kernel, out_shape=[jax.ShapeDtypeStruct((2, rank, ro...  2.07 us
  transfers between devices with their start and end apart: 19, of which 4 were waited for; matrix products, arithmetic and copies ran while one was open for 2% of the time, Pallas kernels for 43%

profile of v4, /device:TPU:0, one launch (start us, length us, event | category | flops | bytes accessed | tf_op | source)
XLA Modules:
  0.0 94.5 jit_solution(6361102410497808625)
XLA Ops:
  0.6 0.0 copy-start.4
  0.6 0.8 pad_maximum_fusion.2
  1.4 1.4 %copy-done.1 = bf16[1,128,6144]{2,1,0:T(8,128)(2,1)S(1)} copy-done((bf16[1,128,6144]{2,1,0:T(8,128)(2,1)S(1)}, bf16[1,128,6144]{2,1,0:T(8,128)(2,1)}, u32[]{:S(2)}) %copy-start.1) | copy-done | bytes 1572888
  2.8 0.1 shard_map.129
  3.0 5.9 %collective-permute-start = (bf16[128,256]{1,0:T(8,128)(2,1)S(1)}, bf16[128,256]{1,0:T(8,128)(2,1)S(1)}, u32[]{:S(2)}, u32[]{:S(2)}) collective-permute-start(bf16[128,256]{1,0:T(8,128)(2,1)S(1)} %pad_maximum_fusion.2), channel_id=1, source_target_pairs={{0,4},{1,5},{2,6},{3,7},{8,12},{9,13},{10,14},{11,15},{16,20},{17,... | collective-permute-start | bytes 196616 | tf_op jit(solution)/shard_map/ppermute | solution.py:79
  8.9 0.1 collective-permute-start.2
  9.0 5.1 %shard_map.130 = f32[4,1536]{1,0:T(4,128)S(1)} custom-call(bf16[4,6144]{1,0:T(4,128)(2,1)S(1)} %bitcast.34, bf16[1536,6144]{1,0:T(8,128)(2,1)} %bitcast.38), custom_call_target="tpu_custom_call" | custom-call | flops 1 | bytes 1 | tf_op jit(solution)/shard_map/pallas_call | solution.py:260
  14.1 0.0 collective-permute-done
  14.1 3.4 %collective-permute-start.1 = (bf16[256,256]{1,0:T(8,128)(2,1)S(1)}, bf16[256,256]{1,0:T(8,128)(2,1)S(1)}, u32[]{:S(2)}, u32[]{:S(2)}) collective-permute-start(bf16[256,256]{1,0:T(8,128)(2,1)S(1)} %constant_dynamic-update-slice_fusion), channel_id=1, source_target_pairs={{0,2},{1,3},{2,0},{3,1},{4,6},{5,7},{6,4},{7,5},{8,10},{9,11},{10,... | collective-permute-start | bytes 393224 | tf_op jit(solution)/shard_map/ppermute | solution.py:79
  17.5 5.1 %shard_map.131 = f32[4,1536]{1,0:T(4,128)S(1)} custom-call(bf16[4,6144]{1,0:T(4,128)(2,1)S(1)} %bitcast.35, bf16[1536,6144]{1,0:T(8,128)(2,1)} %bitcast.39), custom_call_target="tpu_custom_call" | custom-call | flops 1 | bytes 1 | tf_op jit(solution)/shard_map/pallas_call | solution.py:260
  22.6 0.7 collective-permute-done.1
  23.3 0.0 collective-permute-done.2.refs_1_
  23.3 0.0 copy-start
  23.3 0.0 copy-start.2
  23.3 0.1 collective-permute-start.3
  23.4 2.8 %collective-permute-start.4 = (bf16[128,768]{1,0:T(8,128)(2,1)S(1)}, bf16[128,768]{1,0:T(8,128)(2,1)S(1)}, u32[]{:S(2)}, u32[]{:S(2)}) collective-permute-start(bf16[128,768]{1,0:T(8,128)(2,1)S(1)} %get-tuple-element.106), channel_id=1, source_target_pairs={{0,5},{1,4},{2,7},{3,6},{4,1},{5,0},{6,3},{7,2},{8,13},{9,12},{10,... | collective-permute-start | bytes 589832 | tf_op jit(solution)/shard_map/ppermute | solution.py:79
  26.2 5.1 %shard_map.132 = f32[4,1536]{1,0:T(4,128)S(1)} custom-call(bf16[4,6144]{1,0:T(4,128)(2,1)S(1)} %bitcast.36, bf16[1536,6144]{1,0:T(8,128)(2,1)} %bitcast.40), custom_call_target="tpu_custom_call" | custom-call | flops 1 | bytes 1 | tf_op jit(solution)/shard_map/pallas_call | solution.py:260
  31.3 0.0 copy-start.3
  31.3 0.0 copy-start.7
  31.4 0.0 copy-start.8
  31.4 0.0 collective-permute-done.3.far_ref
  31.4 1.3 %collective-permute-start.7 = (bf16[128,768]{1,0:T(8,128)(2,1)S(1)}, bf16[128,768]{1,0:T(8,128)(2,1)S(1)}, u32[]{:S(2)}, u32[]{:S(2)}) collective-permute-start(bf16[128,768]{1,0:T(8,128)(2,1)S(1)} %get-tuple-element.123), channel_id=1, source_target_pairs={{0,6},{1,7},{2,4},{3,5},{4,2},{5,3},{6,0},{7,1},{8,14},{9,15},{10,... | collective-permute-start | bytes 589832 | tf_op jit(solution)/shard_map/ppermute | solution.py:79
  32.7 1.5 %collective-permute-start.5 = (f32[4,1536]{1,0:T(4,128)S(1)}, f32[4,1536]{1,0:T(4,128)S(1)}, u32[]{:S(2)}, u32[]{:S(2)}) collective-permute-start(f32[4,1536]{1,0:T(4,128)S(1)} %add.25.acts_ref), channel_id=1, source_target_pairs={{0,8},{8,16},{16,24},{24,0},{1,9},{9,17},{17,25},{25,1},{2,10},{10... | collective-permute-start | bytes 73736 | tf_op jit(solution)/shard_map/ppermute | solution.py:343
  34.2 1.4 %collective-permute-start.6 = (f32[4,1536]{1,0:T(4,128)S(1)}, f32[4,1536]{1,0:T(4,128)S(1)}, u32[]{:S(2)}, u32[]{:S(2)}) collective-permute-start(f32[4,1536]{1,0:T(4,128)S(1)} %add.25.acts_ref), channel_id=1, source_target_pairs={{0,24},{8,0},{16,8},{24,16},{1,25},{9,1},{17,9},{25,17},{2,26},{10... | collective-permute-start | bytes 73736 | tf_op jit(solution)/shard_map/ppermute | solution.py:343
  35.6 0.5 shard_map.128.delta_ref
  36.1 0.0 collective-permute-done.4.refs_5_
  36.1 10.9 %shard_map.133 = (f32[128,3072]{1,0:T(8,128)}, f32[512,256]{1,0:T(8,128)S(1)}, f32[512,256]{1,0:T(8,128)S(1)}) custom-call(s32[1]{0:T(128)} %bitcast.me_ref, bf16[128,3072]{1,0:T(8,128)(2,1)S(1)} %bitcast.33, bf16[128,3072]{1,0:T(8,128)(2,1)S(1)} %bitcast.30, f32[24,128]{1,0:T(8,128)S(1)} %bitcast.37, f32[24,128]{1,0:T(8,128)S(1)} %shard_map.128.delta_ref, ...), custom_call_target="tpu_custom_call" | custom-call | flops 1 | bytes 1 | tf_op jit(solution)/shard_map/pallas_call | solution.py:175
  47.0 0.0 collective-permute-done.5.lower_ref
  47.0 0.0 collective-permute-done.6.higher_ref
  47.0 0.0 copy-start.10
  47.0 0.0 collective-permute-done.7.refs_3_
  47.0 4.3 %collective-permute-start.8 = (f32[512,256]{1,0:T(8,128)S(1)}, f32[512,256]{1,0:T(8,128)S(1)}, u32[]{:S(2)}, u32[]{:S(2)}) collective-permute-start(f32[512,256]{1,0:T(8,128)S(1)} %get-tuple-element.139), channel_id=1, source_target_pairs={{0,1},{1,0},{2,3},{3,2},{4,5},{5,4},{6,7},{7,6},{8,9},{9,8},{10,11... | collective-permute-start | bytes 1572872 | tf_op jit(solution)/shard_map/ppermute | solution.py:79
  51.3 3.3 %collective-permute-start.10 = (bf16[128,768]{1,0:T(8,128)(2,1)S(1)}, bf16[128,768]{1,0:T(8,128)(2,1)S(1)}, u32[]{:S(2)}, u32[]{:S(2)}) collective-permute-start(bf16[128,768]{1,0:T(8,128)(2,1)S(1)} %get-tuple-element.143), channel_id=1, source_target_pairs={{0,7},{1,6},{2,5},{3,4},{4,3},{5,2},{6,1},{7,0},{8,15},{9,14},{10,... | collective-permute-start | bytes 589832 | tf_op jit(solution)/shard_map/ppermute | solution.py:79
  54.7 2.1 %shard_map.134 = (f32[2,4,1536]{2,1,0:T(4,128)}, bf16[8,1536]{1,0:T(8,128)(2,1)}) custom-call(f32[4,1536]{1,0:T(4,128)} %copy-done.8, f32[4,1536]{1,0:T(4,128)} %copy-done.9, f32[4,1536]{1,0:T(4,128)} %copy-done.10), custom_call_target="tpu_custom_call" | custom-call | flops 1 | bytes 1 | tf_op jit(solution)/shard_map/pallas_call | solution.py:303
  56.7 0.7 copy-done.5
  57.5 4.0 %shard_map.135 = f32[2,4,2048]{2,1,0:T(4,128)S(1)} custom-call(bf16[8,1536]{1,0:T(8,128)(2,1)S(1)} %copy-done.5, bf16[1536,6144]{1,0:T(8,128)(2,1)} %bitcast.41), custom_call_target="tpu_custom_call" | custom-call | flops 1 | bytes 1 | tf_op jit(solution)/shard_map/pallas_call | solution.py:327
  61.5 0.0 collective-permute-done.8
  61.5 0.1 add.26
  61.6 0.1 collective-permute-start.9
  61.7 0.5 copy-done.6
  62.3 4.0 %shard_map.136 = f32[2,4,2048]{2,1,0:T(4,128)S(1)} custom-call(bf16[8,1536]{1,0:T(8,128)(2,1)S(1)} %copy-done.6, bf16[1536,6144]{1,0:T(8,128)(2,1)} %bitcast.42), custom_call_target="tpu_custom_call" | custom-call | flops 1 | bytes 1 | tf_op jit(solution)/shard_map/pallas_call | solution.py:327
  66.3 4.1 %shard_map.137 = f32[2,4,2048]{2,1,0:T(4,128)S(1)} custom-call(bf16[8,1536]{1,0:T(8,128)(2,1)S(1)} %copy-done.6, bf16[1536,6144]{1,0:T(8,128)(2,1)} %bitcast.43), custom_call_target="tpu_custom_call" | custom-call | flops 1 | bytes 1 | tf_op jit(solution)/shard_map/pallas_call | solution.py:327
  70.4 1.5 %collective-permute-start.12 = (bf16[128,768]{1,0:T(8,128)(2,1)S(1)}, bf16[128,768]{1,0:T(8,128)(2,1)S(1)}, u32[]{:S(2)}, u32[]{:S(2)}) collective-permute-start(bf16[128,768]{1,0:T(8,128)(2,1)S(1)} %get-tuple-element.149), channel_id=1, source_target_pairs={{0,2},{1,3},{2,0},{3,1},{4,6},{5,7},{6,4},{7,5},{8,10},{9,11},{10,... | collective-permute-start | bytes 589832 | tf_op jit(solution)/shard_map/ppermute | solution.py:79
  71.9 0.0 collective-permute-start.13
  71.9 0.7 collective-permute-start.14
  72.6 0.0 collective-permute-done.10.refs_7_
  72.6 0.0 collective-permute-done.9
  72.7 0.5 collective-permute-start.11
  73.2 1.6 %collective-permute-start.17 = (f32[4,6144]{1,0:T(4,128)S(1)}, f32[4,6144]{1,0:T(4,128)S(1)}, u32[]{:S(2)}, u32[]{:S(2)}) collective-permute-start(f32[4,6144]{1,0:T(4,128)S(1)} %get-tuple-element.168), channel_id=1, source_target_pairs={{0,8},{8,16},{16,24},{24,0},{1,9},{9,17},{17,25},{25,1},{2,10},{10... | collective-permute-start | bytes 294920 | tf_op jit(solution)/shard_map/ppermute | solution.py:343
  74.7 8.4 %collective-permute-done.11 = bf16[256,256]{1,0:T(8,128)(2,1)S(1)} collective-permute-done((bf16[256,256]{1,0:T(8,128)(2,1)S(1)}, bf16[256,256]{1,0:T(8,128)(2,1)S(1)}, u32[]{:S(2)}, u32[]{:S(2)}) %collective-permute-start.11) | collective-permute-done | bytes 131104 | tf_op jit(solution)/shard_map/ppermute | solution.py:79
  83.1 2.4 %collective-permute-start.18 = (f32[4,6144]{1,0:T(4,128)S(1)}, f32[4,6144]{1,0:T(4,128)S(1)}, u32[]{:S(2)}, u32[]{:S(2)}) collective-permute-start(f32[4,6144]{1,0:T(4,128)S(1)} %get-tuple-element.169), channel_id=1, source_target_pairs={{0,24},{8,0},{16,8},{24,16},{1,25},{9,1},{17,9},{25,17},{2,26},{10... | collective-permute-start | bytes 294920 | tf_op jit(solution)/shard_map/ppermute | solution.py:343
  85.6 0.7 fusion.1
  86.3 0.0 collective-permute-done.17
  86.3 1.6 %collective-permute-start.15 = (bf16[256,256]{1,0:T(8,128)(2,1)S(1)}, bf16[256,256]{1,0:T(8,128)(2,1)S(1)}, u32[]{:S(2)}, u32[]{:S(2)}) collective-permute-start(bf16[256,256]{1,0:T(8,128)(2,1)S(1)} %pad_maximum_fusion.1), channel_id=1, source_target_pairs={{0,2},{1,3},{2,0},{3,1},{4,6},{5,7},{6,4},{7,5},{8,10},{9,11},{10,... | collective-permute-start | bytes 393224 | tf_op jit(solution)/shard_map/ppermute | solution.py:79
  87.9 0.0 collective-permute-done.18
  87.9 0.1 add_bitcast_fusion.1
  87.9 3.4 %collective-permute-done.15 = bf16[256,256]{1,0:T(8,128)(2,1)S(1)} collective-permute-done((bf16[256,256]{1,0:T(8,128)(2,1)S(1)}, bf16[256,256]{1,0:T(8,128)(2,1)S(1)}, u32[]{:S(2)}, u32[]{:S(2)}) %collective-permute-start.15) | collective-permute-done | bytes 131104 | tf_op jit(solution)/shard_map/ppermute | solution.py:79
  91.3 0.1 collective-permute-start.16
  91.4 0.7 maximum_bitcast_fusion
  92.1 0.0 collective-permute-done.12.refs_2_
  92.1 0.0 collective-permute-done.13.refs_4_
  92.2 0.0 collective-permute-done.14.refs_6_
  92.2 0.8 collective-permute-done.16.refs_9_
  92.9 1.5 %shard_map.138 = f32[768,256]{1,0:T(8,128)} custom-call(bf16[128,768]{1,0:T(8,128)(2,1)S(1)} %get-tuple-element.83.refs_0_, bf16[128,768]{1,0:T(8,128)(2,1)S(1)} %collective-permute-done.2.refs_1_, bf16[128,768]{1,0:T(8,128)(2,1)S(1)} %collective-permute-done.12.refs_2_, bf16[128,768]{1,0:T(8,128)(2,1)S(1)} %collective-permute-done.7.refs_3_, ...), custom_call_target="tpu_custom_call" | custom-call | flops 1 | bytes 1 | tf_op jit(solution)/shard_map/pallas_call | solution.py:229
  (28 shorter events, 0.3 us)
Async XLA Ops:
  0.6 8.4 %copy-start.4 = (bf16[1,4,6144]{2,1,0:T(4,128)(2,1)S(1)}, bf16[1,4,6144]{2,1,0:T(4,128)(2,1)}, u32[]{:S(2)}) copy-start(bf16[1,4,6144]{2,1,0:T(4,128)(2,1)} %param.17) | copy-start | bytes 147460
  1.4 1.4 %copy-start.1 = (bf16[1,128,6144]{2,1,0:T(8,128)(2,1)S(1)}, bf16[1,128,6144]{2,1,0:T(8,128)(2,1)}, u32[]{:S(2)}) copy-start(bf16[1,128,6144]{2,1,0:T(8,128)(2,1)} %param.15) | copy-start | bytes 4718596
  3.0 11.1 %collective-permute-start = (bf16[128,256]{1,0:T(8,128)(2,1)S(1)}, bf16[128,256]{1,0:T(8,128)(2,1)S(1)}, u32[]{:S(2)}, u32[]{:S(2)}) collective-permute-start(bf16[128,256]{1,0:T(8,128)(2,1)S(1)} %pad_maximum_fusion.2), channel_id=1, source_target_pairs={{0,4},{1,5},{2,6},{3,7},{8,12},{9,13},{10,14},{11,15},{16,20},{17,... | collective-permute-start | bytes 196616 | tf_op jit(solution)/shard_map/ppermute | solution.py:79
  8.9 14.4 %collective-permute-start.2 = (bf16[128,768]{1,0:T(8,128)(2,1)S(1)}, bf16[128,768]{1,0:T(8,128)(2,1)S(1)}, u32[]{:S(2)}, u32[]{:S(2)}) collective-permute-start(bf16[128,768]{1,0:T(8,128)(2,1)S(1)} %get-tuple-element.95), channel_id=1, source_target_pairs={{0,4},{1,5},{2,6},{3,7},{4,0},{5,1},{6,2},{7,3},{8,12},{9,13},{10,... | collective-permute-start | bytes 589832 | tf_op jit(solution)/shard_map/ppermute | solution.py:79
  14.1 9.1 %collective-permute-start.1 = (bf16[256,256]{1,0:T(8,128)(2,1)S(1)}, bf16[256,256]{1,0:T(8,128)(2,1)S(1)}, u32[]{:S(2)}, u32[]{:S(2)}) collective-permute-start(bf16[256,256]{1,0:T(8,128)(2,1)S(1)} %constant_dynamic-update-slice_fusion), channel_id=1, source_target_pairs={{0,2},{1,3},{2,0},{3,1},{4,6},{5,7},{6,4},{7,5},{8,10},{9,11},{10,... | collective-permute-start | bytes 393224 | tf_op jit(solution)/shard_map/ppermute | solution.py:79
  23.3 12.3 %copy-start = (bf16[1,128,3072]{2,1,0:T(8,128)(2,1)S(1)}, bf16[1,128,3072]{2,1,0:T(8,128)(2,1)}, u32[]{:S(2)}) copy-start(bf16[1,128,3072]{2,1,0:T(8,128)(2,1)} %param.13) | copy-start | bytes 2359300
  23.3 12.3 %copy-start.2 = (bf16[1,128,3072]{2,1,0:T(8,128)(2,1)S(1)}, bf16[1,128,3072]{2,1,0:T(8,128)(2,1)}, u32[]{:S(2)}) copy-start(bf16[1,128,3072]{2,1,0:T(8,128)(2,1)} %param.12) | copy-start | bytes 2359300
  23.3 8.1 %collective-permute-start.3 = (bf16[512,256]{1,0:T(8,128)(2,1)S(1)}, bf16[512,256]{1,0:T(8,128)(2,1)S(1)}, u32[]{:S(2)}, u32[]{:S(2)}) collective-permute-start(bf16[512,256]{1,0:T(8,128)(2,1)S(1)} %constant_dynamic-update-slice_fusion.2.near_ref), channel_id=1, source_target_pairs={{0,1},{1,0},{2,3},{3,2},{4,5},{5,4},{6,7},{7,6},{8,9},{9,8},{10,11... | collective-permute-start | bytes 786440 | tf_op jit(solution)/shard_map/ppermute | solution.py:79
  23.4 12.7 %collective-permute-start.4 = (bf16[128,768]{1,0:T(8,128)(2,1)S(1)}, bf16[128,768]{1,0:T(8,128)(2,1)S(1)}, u32[]{:S(2)}, u32[]{:S(2)}) collective-permute-start(bf16[128,768]{1,0:T(8,128)(2,1)S(1)} %get-tuple-element.106), channel_id=1, source_target_pairs={{0,5},{1,4},{2,7},{3,6},{4,1},{5,0},{6,3},{7,2},{8,13},{9,12},{10,... | collective-permute-start | bytes 589832 | tf_op jit(solution)/shard_map/ppermute | solution.py:79
  31.3 4.8 %copy-start.3 = (bf16[1,128,3072]{2,1,0:T(8,128)(2,1)S(1)}, bf16[1,128,3072]{2,1,0:T(8,128)(2,1)}, u32[]{:S(2)}) copy-start(bf16[1,128,3072]{2,1,0:T(8,128)(2,1)} %param.9) | copy-start | bytes 2359300
  31.3 4.8 %copy-start.7 = (f32[1,24,128]{2,1,0:T(8,128)S(1)}, f32[1,24,128]{2,1,0:T(8,128)}, u32[]{:S(2)}) copy-start(f32[1,24,128]{2,1,0:T(8,128)} %param.14) | copy-start | bytes 36868
  31.4 15.6 %copy-start.8 = (f32[4,1536]{1,0:T(4,128)}, f32[4,1536]{1,0:T(4,128)S(1)}, u32[]{:S(2)}) copy-start(f32[4,1536]{1,0:T(4,128)S(1)} %add.25.acts_ref) | copy-start | bytes 73732
  31.4 15.6 %collective-permute-start.7 = (bf16[128,768]{1,0:T(8,128)(2,1)S(1)}, bf16[128,768]{1,0:T(8,128)(2,1)S(1)}, u32[]{:S(2)}, u32[]{:S(2)}) collective-permute-start(bf16[128,768]{1,0:T(8,128)(2,1)S(1)} %get-tuple-element.123), channel_id=1, source_target_pairs={{0,6},{1,7},{2,4},{3,5},{4,2},{5,3},{6,0},{7,1},{8,14},{9,15},{10,... | collective-permute-start | bytes 589832 | tf_op jit(solution)/shard_map/ppermute | solution.py:79
  32.7 14.3 %collective-permute-start.5 = (f32[4,1536]{1,0:T(4,128)S(1)}, f32[4,1536]{1,0:T(4,128)S(1)}, u32[]{:S(2)}, u32[]{:S(2)}) collective-permute-start(f32[4,1536]{1,0:T(4,128)S(1)} %add.25.acts_ref), channel_id=1, source_target_pairs={{0,8},{8,16},{16,24},{24,0},{1,9},{9,17},{17,25},{25,1},{2,10},{10... | collective-permute-start | bytes 73736 | tf_op jit(solution)/shard_map/ppermute | solution.py:343
  34.2 12.8 %collective-permute-start.6 = (f32[4,1536]{1,0:T(4,128)S(1)}, f32[4,1536]{1,0:T(4,128)S(1)}, u32[]{:S(2)}, u32[]{:S(2)}) collective-permute-start(f32[4,1536]{1,0:T(4,128)S(1)} %add.25.acts_ref), channel_id=1, source_target_pairs={{0,24},{8,0},{16,8},{24,16},{1,25},{9,1},{17,9},{25,17},{2,26},{10... | collective-permute-start | bytes 73736 | tf_op jit(solution)/shard_map/ppermute | solution.py:343
  47.0 7.7 %copy-start.9 = (f32[4,1536]{1,0:T(4,128)}, f32[4,1536]{1,0:T(4,128)S(1)}, u32[]{:S(2)}) copy-start(f32[4,1536]{1,0:T(4,128)S(1)} %collective-permute-done.5.lower_ref) | copy-start | bytes 73732
  47.0 7.6 %copy-start.10 = (f32[4,1536]{1,0:T(4,128)}, f32[4,1536]{1,0:T(4,128)S(1)}, u32[]{:S(2)}) copy-start(f32[4,1536]{1,0:T(4,128)S(1)} %collective-permute-done.6.higher_ref) | copy-start | bytes 73732
  47.0 14.5 %collective-permute-start.8 = (f32[512,256]{1,0:T(8,128)S(1)}, f32[512,256]{1,0:T(8,128)S(1)}, u32[]{:S(2)}, u32[]{:S(2)}) collective-permute-start(f32[512,256]{1,0:T(8,128)S(1)} %get-tuple-element.139), channel_id=1, source_target_pairs={{0,1},{1,0},{2,3},{3,2},{4,5},{5,4},{6,7},{7,6},{8,9},{9,8},{10,11... | collective-permute-start | bytes 1572872 | tf_op jit(solution)/shard_map/ppermute | solution.py:79
  51.3 21.3 %collective-permute-start.10 = (bf16[128,768]{1,0:T(8,128)(2,1)S(1)}, bf16[128,768]{1,0:T(8,128)(2,1)S(1)}, u32[]{:S(2)}, u32[]{:S(2)}) collective-permute-start(bf16[128,768]{1,0:T(8,128)(2,1)S(1)} %get-tuple-element.143), channel_id=1, source_target_pairs={{0,7},{1,6},{2,5},{3,4},{4,3},{5,2},{6,1},{7,0},{8,15},{9,14},{10,... | collective-permute-start | bytes 589832 | tf_op jit(solution)/shard_map/ppermute | solution.py:79
  56.7 0.7 copy-start.5
  61.5 0.8 copy-start.6
  61.6 11.0 %collective-permute-start.9 = (bf16[256,256]{1,0:T(8,128)(2,1)S(1)}, bf16[256,256]{1,0:T(8,128)(2,1)S(1)}, u32[]{:S(2)}, u32[]{:S(2)}) collective-permute-start(bf16[256,256]{1,0:T(8,128)(2,1)S(1)} %slice.63), channel_id=1, source_target_pairs={{0,2},{1,3},{2,0},{3,1},{4,6},{5,7},{6,4},{7,5},{8,10},{9,11},{10,... | collective-permute-start | bytes 393224 | tf_op jit(solution)/shard_map/ppermute | solution.py:79
  70.4 21.8 %collective-permute-start.12 = (bf16[128,768]{1,0:T(8,128)(2,1)S(1)}, bf16[128,768]{1,0:T(8,128)(2,1)S(1)}, u32[]{:S(2)}, u32[]{:S(2)}) collective-permute-start(bf16[128,768]{1,0:T(8,128)(2,1)S(1)} %get-tuple-element.149), channel_id=1, source_target_pairs={{0,2},{1,3},{2,0},{3,1},{4,6},{5,7},{6,4},{7,5},{8,10},{9,11},{10,... | collective-permute-start | bytes 589832 | tf_op jit(solution)/shard_map/ppermute | solution.py:79
  71.9 20.2 %collective-permute-start.13 = (bf16[128,768]{1,0:T(8,128)(2,1)S(1)}, bf16[128,768]{1,0:T(8,128)(2,1)S(1)}, u32[]{:S(2)}, u32[]{:S(2)}) collective-permute-start(bf16[128,768]{1,0:T(8,128)(2,1)S(1)} %get-tuple-element.148), channel_id=1, source_target_pairs={{0,1},{1,0},{2,3},{3,2},{4,5},{5,4},{6,7},{7,6},{8,9},{9,8},{10,11... | collective-permute-start | bytes 589832 | tf_op jit(solution)/shard_map/ppermute | solution.py:79
  71.9 20.2 %collective-permute-start.14 = (bf16[128,768]{1,0:T(8,128)(2,1)S(1)}, bf16[128,768]{1,0:T(8,128)(2,1)S(1)}, u32[]{:S(2)}, u32[]{:S(2)}) collective-permute-start(bf16[128,768]{1,0:T(8,128)(2,1)S(1)} %get-tuple-element.150), channel_id=1, source_target_pairs={{0,3},{1,2},{2,1},{3,0},{4,7},{5,6},{6,5},{7,4},{8,11},{9,10},{10,... | collective-permute-start | bytes 589832 | tf_op jit(solution)/shard_map/ppermute | solution.py:79
  72.7 10.5 %collective-permute-start.11 = (bf16[256,256]{1,0:T(8,128)(2,1)S(1)}, bf16[256,256]{1,0:T(8,128)(2,1)S(1)}, u32[]{:S(2)}, u32[]{:S(2)}) collective-permute-start(bf16[256,256]{1,0:T(8,128)(2,1)S(1)} %get-tuple-element.161), channel_id=1, source_target_pairs={{0,4},{1,5},{2,6},{3,7},{4,0},{5,1},{6,2},{7,3},{8,12},{9,13},{10,... | collective-permute-start | bytes 393224 | tf_op jit(solution)/shard_map/ppermute | solution.py:79
  73.2 13.1 %collective-permute-start.17 = (f32[4,6144]{1,0:T(4,128)S(1)}, f32[4,6144]{1,0:T(4,128)S(1)}, u32[]{:S(2)}, u32[]{:S(2)}) collective-permute-start(f32[4,6144]{1,0:T(4,128)S(1)} %get-tuple-element.168), channel_id=1, source_target_pairs={{0,8},{8,16},{16,24},{24,0},{1,9},{9,17},{17,25},{25,1},{2,10},{10... | collective-permute-start | bytes 294920 | tf_op jit(solution)/shard_map/ppermute | solution.py:343
  83.1 4.7 %collective-permute-start.18 = (f32[4,6144]{1,0:T(4,128)S(1)}, f32[4,6144]{1,0:T(4,128)S(1)}, u32[]{:S(2)}, u32[]{:S(2)}) collective-permute-start(f32[4,6144]{1,0:T(4,128)S(1)} %get-tuple-element.169), channel_id=1, source_target_pairs={{0,24},{8,0},{16,8},{24,16},{1,25},{9,1},{17,9},{25,17},{2,26},{10... | collective-permute-start | bytes 294920 | tf_op jit(solution)/shard_map/ppermute | solution.py:343
  86.3 5.0 %collective-permute-start.15 = (bf16[256,256]{1,0:T(8,128)(2,1)S(1)}, bf16[256,256]{1,0:T(8,128)(2,1)S(1)}, u32[]{:S(2)}, u32[]{:S(2)}) collective-permute-start(bf16[256,256]{1,0:T(8,128)(2,1)S(1)} %pad_maximum_fusion.1), channel_id=1, source_target_pairs={{0,2},{1,3},{2,0},{3,1},{4,6},{5,7},{6,4},{7,5},{8,10},{9,11},{10,... | collective-permute-start | bytes 393224 | tf_op jit(solution)/shard_map/ppermute | solution.py:79
  91.3 1.6 %collective-permute-start.16 = (bf16[512,256]{1,0:T(8,128)(2,1)S(1)}, bf16[512,256]{1,0:T(8,128)(2,1)S(1)}, u32[]{:S(2)}, u32[]{:S(2)}) collective-permute-start(bf16[512,256]{1,0:T(8,128)(2,1)S(1)} %pad_maximum_fusion.refs_8_), channel_id=1, source_target_pairs={{0,1},{1,0},{2,3},{3,2},{4,5},{5,4},{6,7},{7,6},{8,9},{9,8},{10,11... | collective-permute-start | bytes 786440 | tf_op jit(solution)/shard_map/ppermute | solution.py:79

commit v5 on v4

--- a/solution.py
+++ b/solution.py
@@ -14,9 +14,9 @@
 F32 = jnp.float32
 BF16 = jnp.bfloat16
 VMEM_LIMIT = 48 * 1024 * 1024
-PARTS = 3
+PARTS = 2
 COST = pl.CostEstimate(flops=1, bytes_accessed=1, transcendentals=0)
-PARTS = 3
+PARTS = 2
 COST = pl.CostEstimate(flops=1, bytes_accessed=1, transcendentals=0)
 COST = pl.CostEstimate(flops=1, bytes_accessed=1, transcendentals=0)
 
@@ -191,85 +191,59 @@
     )(me[None], queries, out_grad, norm, delta, near, far)
 
 
-def pack_kernel(width, me_ref, x_ref, *out_refs):
-    me = me_ref[0]
-    for x, out_ref in enumerate(out_refs):
-        first = pl.multiple_of((me ^ x) * width, width)
-        out_ref[...] = x_ref[:, pl.ds(first, width)]
-
-
-def pack(me, inputs, count):
+def pack_kernel(x_ref, out_ref):
+    width = out_ref.shape[2]
+    for j in range(out_ref.shape[0]):
+        out_ref[j] = x_ref[:, j * width : (j + 1) * width]
+
+
+def pack(inputs, chips):
     tok, cols = inputs.shape
-    width = cols // count
-    if width % 128:
-        return [
-            lax.dynamic_slice_in_dim(inputs, (me ^ x) * width, width, axis=1)
-            for x in range(count)
-        ]
     return pl.pallas_call(
-        functools.partial(pack_kernel, width),
-        out_shape=[jax.ShapeDtypeStruct((tok, width), inputs.dtype)] * count,
-        in_specs=[pl.BlockSpec(memory_space=pltpu.SMEM)] + vmem_specs(1),
-        out_specs=vmem_specs(count),
-        compiler_params=pltpu.CompilerParams(vmem_limit_bytes=VMEM_LIMIT),
-        cost_estimate=COST,
-    )(me[None], inputs)
-
-
-def project_kernel(*refs):
-    *x_refs, near_ref, far_ref, out_ref = refs
-    x = jnp.concatenate([ref[...] for ref in x_refs], axis=0)
-    grads = jnp.concatenate([near_ref[...], far_ref[...]], axis=0)
-    out_ref[...] = dot_tn(x, grads)
-
-
-def project(parts, near, far):
-    tok, width = parts[0].shape
-    cols = near.shape[1]
-    return pl.pallas_call(
-        project_kernel,
-        out_shape=jax.ShapeDtypeStruct((width, cols), F32),
-        in_specs=vmem_specs(len(parts) + 2),
+        pack_kernel,
+        out_shape=jax.ShapeDtypeStruct((chips, tok, cols // chips), inputs.dtype),
+        in_specs=vmem_specs(1),
         out_specs=pl.BlockSpec(memory_space=pltpu.VMEM),
         compiler_params=pltpu.CompilerParams(vmem_limit_bytes=VMEM_LIMIT),
         cost_estimate=COST,
-    )(*parts, near, far)
-
-
-def acts_kernel(factor_ref, w_ref, out_ref, sum_ref):
-    step = pl.program_id(0)
-    rank, rows = out_ref.shape
-    part = dot_nt(w_ref[...], factor_ref[...])
-
-    @pl.when(step == 0)
-    def _():
-        sum_ref[...] = jnp.zeros_like(sum_ref)
-
-    sum_ref[:, :rank] += part
-
-    @pl.when(step == pl.num_programs(0) - 1)
-    def _():
-        out_ref[...] = sum_ref[...].T[:rank]
-
-
-def acts_part(factor, weight, index, parts):
-    rank, cols = factor.shape
-    rows = weight.shape[0]
-    tile = 512 if cols % (512 * parts) == 0 else cols // parts
-    steps = cols // parts // tile
+    )(inputs)
+
+
+def project_kernel(order, me_ref, x_ref, grads_ref, mine_ref, theirs_ref):
+    chip = me_ref[0] // 2
+    x = jnp.concatenate([x_ref[chip ^ part] for part in order], axis=0)
+    width = mine_ref.shape[0]
+    grads = grads_ref[...]
+    odd = lax.rem(me_ref[0], 2) == 1
+    first = dot_tn(x[:, :width], grads)
+    second = dot_tn(x[:, width:], grads)
+    mine_ref[...] = jnp.where(odd, second, first)
+    theirs_ref[...] = jnp.where(odd, first, second)
+
+
+def project(me, blocks, grads, order):
+    width = blocks.shape[2] // 2
     return pl.pallas_call(
-        acts_kernel,
-        grid=(steps,),
-        out_shape=jax.ShapeDtypeStruct((rank, rows), F32),
-        in_specs=[
-            pl.BlockSpec((rank, tile), lambda i: (0, index * steps + i)),
-            pl.BlockSpec((rows, tile), lambda i: (0, index * steps + i)),
-        ],
-        out_specs=pl.BlockSpec((rank, rows), lambda i: (0, 0)),
-        scratch_shapes=[pltpu.VMEM((rows, 128), F32)],
+        functools.partial(project_kernel, order),
+        out_shape=[jax.ShapeDtypeStruct((width, grads.shape[1]), F32)] * 2,
+        in_specs=[pl.BlockSpec(memory_space=pltpu.SMEM)] + vmem_specs(2),
+        out_specs=vmem_specs(2),
         compiler_params=pltpu.CompilerParams(vmem_limit_bytes=VMEM_LIMIT),
         cost_estimate=COST,
-    )(factor, weight)
+    )(me[None], blocks, grads)
+
+
+def acts_part(factor, weight, index, parts):
+    rows = weight.shape[0] // parts
+    some = weight[index * rows : (index + 1) * rows]
+    return dot_nt(factor, some)
+
+
+def contrib_part(both, weight, index, parts):
+    cols = weight.shape[1] // parts
+    some = weight[:, index * cols : (index + 1) * cols]
+    part = jnp.dot(both, some, preferred_element_type=F32)
+    return part.reshape(2, both.shape[0] // 2, cols)
 
 
 def orthonormal(rows):
@@ -312,32 +286,6 @@
     )(acts, lower, higher)
 
 
-def contrib_kernel(both_ref, w_ref, out_ref):
-    rank = out_ref.shape[1]
-    part = jnp.dot(both_ref[...], w_ref[...], preferred_element_type=F32)
-    for e in range(2):
-        out_ref[e] = part[e * rank : (e + 1) * rank]
-
-
-def contrib_part(both, weight, index, parts):
-    count, rows = both.shape
-    cols = weight.shape[1] // parts
-    tile = 512 if cols % 512 == 0 else cols
-    steps = cols // tile
-    return pl.pallas_call(
-        contrib_kernel,
-        grid=(steps,),
-        out_shape=jax.ShapeDtypeStruct((2, count // 2, cols), F32),
-        in_specs=[
-            pl.BlockSpec((count, rows), lambda i: (0, 0)),
-            pl.BlockSpec((rows, tile), lambda i: (0, index * steps + i)),
-        ],
-        out_specs=pl.BlockSpec((2, count // 2, tile), lambda i: (0, 0, i)),
-        compiler_params=pltpu.CompilerParams(vmem_limit_bytes=VMEM_LIMIT),
-        cost_estimate=COST,
-    )(both, weight)
-
-
 def from_cycle(block, axis, distance):
     count = lax.axis_size(axis)
     return lax.ppermute(block, axis, [(i, (i + distance) % count) for i in range(count)])
@@ -354,47 +302,37 @@
     factor = initial_right_factor[0]
     weight = mlp_weight[0]
 
-    quarter = -(-(count // 2) // 4)
-    due = [
-        [x for x in range(count // 2 + i * quarter, count // 2 + (i + 1) * quarter) if x < count]
-        for i in range(4)
-    ]
-    rest = list(range(2, count // 2)) + ([1] if count > 2 else [])
-    packed = list(pack(me, inputs[0], count))
-    parts = {0: packed[0]}
-
-    def send(group):
-        for x in group:
-            parts[x] = swap(packed[x], "seq", x)
-
-    def tie(group, values):
-        values, held, packed[:] = lax.optimization_barrier(
-            (values, [parts[x] for x in group], list(packed))
-        )
-        parts.update(zip(group, held))
-        return values
-
-    near = tie([], jnp.concatenate([keys[0], values[0]], axis=-1))
-    acts = None
+    chips = count // 2
+    packed = pack(inputs[0], chips)
+    near = jnp.concatenate([keys[0], values[0]], axis=-1)
+    near, packed = lax.optimization_barrier((near, packed))
+    blocks = lax.all_to_all(
+        packed,
+        "seq",
+        split_axis=0,
+        concat_axis=0,
+        tiled=True,
+        axis_index_groups=[list(range(core, count, 2)) for core in range(2)],
+    )
+
+    acts_parts = []
     for index, bit in enumerate(bits):
         far = swap(near, "seq", bit, True if index == 0 else None)
-        if index < 2:
-            send(due[index])
         if index < PARTS:
-            part = acts_part(factor, weight, index, PARTS)
-            acts = part if acts is None else acts + part
-        factor, near, far, acts = tie(due[0] if index == 1 else [], (factor, near, far, acts))
+            acts_parts.append(acts_part(factor, weight, index, PARTS))
+        factor, near, far, acts_parts = lax.optimization_barrier(
+            (factor, near, far, acts_parts)
+        )
         if bit > 1:
             near = jnp.concatenate([near, far], axis=0)
+    acts = jnp.concatenate(acts_parts, axis=1)
     lower_acts = from_cycle(acts, "rep", 1)
     higher_acts = from_cycle(acts, "rep", -1)
-    send(due[2])
 
     delta = head_delta(out_grad[0], outputs[0], heads)
-    delta, near, far = tie(due[1], (delta, near, far))
+    delta, near, far = lax.optimization_barrier((delta, near, far))
     query_grad, grads, sent = attend(me, queries[0], out_grad[0], log_norm[0], delta, near, far)
-    lower_acts, higher_acts, sent = tie(due[2], (lower_acts, higher_acts, sent))
-    send(due[3])
+    lower_acts, higher_acts, sent = lax.optimization_barrier((lower_acts, higher_acts, sent))
 
     basis, both = make_basis(acts, lower_acts, higher_acts)
     contrib_parts = []
@@ -406,10 +344,10 @@
             contrib_parts += [
                 contrib_part(both, weight, index + i, PARTS) for i in range(share)
             ]
-        if bit * 2 == last:
-            send(rest)
-        both, grads, arrived, contrib_parts = tie(
-            due[3] if bit * 2 == last else [], (both, grads, arrived, contrib_parts)
+        both, grads, arrived, contrib_parts, blocks = lax.optimization_barrier(
+            (both, grads, arrived, contrib_parts, blocks)
+        ) if bit * 2 == last else (
+            *lax.optimization_barrier((both, grads, arrived, contrib_parts)), blocks
         )
         grads = grads + arrived.astype(F32)
         keep = grads.shape[0] // 2
@@ -426,11 +364,11 @@
     own = jnp.where(upper, mine, mine + arrived[keep:])
     other = jnp.where(upper, theirs + arrived[:keep], arrived[:keep])
     near_b = jnp.concatenate([own, other], axis=0).astype(BF16)
-    for bit in bits[1:]:
-        far_b = swap(near_b, "seq", bit)
-        if bit > 1:
-            near_b = jnp.concatenate([near_b, far_b], axis=0)
-    proj_grad = project([parts[x] for x in gather_order(count)], near_b, far_b)
+    for bit in bits[1:-1]:
+        near_b = jnp.concatenate([near_b, swap(near_b, "seq", bit)], axis=0)
+    order = [x // 2 for x in gather_order(count)[: count // 2]]
+    proj_mine, proj_theirs = project(me, blocks, near_b, order)
+    proj_grad = proj_mine + swap(proj_theirs, "seq", 1)
     right_factor = jnp.stack([contrib[0] + lower_half, contrib[1] + higher_half], axis=0)
     return (
         query_grad[None],

time: 95 us -> 107 us (1.13)
  Pallas kernels: 42.4 us -> 15.3 us
  matrix products: 0 us -> 22.5 us
  waiting for transfers between devices: 13.3 us -> 27.1 us
    pallas_call x8 -> x2, Pallas kernels: 29 us -> 1.91 us  [the longest x1 1.28 us: pack(): pl.pallas_call(pack_kernel, out_shape=jax.ShapeDtypeStruct((chips, tok, c...]
    dot_general x0 -> x4, matrix products: none -> 22.5 us  [the longest x2 12.4 us: dot_nt(): lax.dot_general(a, b, (((1,), (1,)), ((), ())), preferred_element_type=F32)]
    ppermute x15 -> x8, waiting for transfers between devices: 13.3 us -> 24.9 us  [swap(): return lax.ppermute(block, axis, route)]
    all_to_all x0 -> x1, starting transfers between devices: none -> 6.32 us  [on_device(): lax.all_to_all(packed, 'seq', split_axis=0, concat_axis=0, tiled=True, ax...]
    ppermute x15 -> x8, starting transfers between devices: 25.6 us -> 21.1 us  [swap(): return lax.ppermute(block, axis, route)]
    ppermute x4, waiting for transfers between devices: 0.01 us -> 2.25 us  [from_cycle(): lax.ppermute(block, axis, [(i, (i + distance) % count) for i in range(cou...]
    ppermute x4, starting transfers between devices: 6.89 us -> 5.53 us  [from_cycle(): lax.ppermute(block, axis, [(i, (i + distance) % count) for i in range(cou...]
    unnamed x26 -> x32, local copies, waits for them, and re-layouts: 2.77 us -> 3.74 us
  transfers between devices with their start and end apart: 19 -> 13, of which waited for: 4 -> 7; matrix products, arithmetic and copies ran while one was open for 2% -> 22% of each run, Pallas kernels for 43% -> 13%
where the time goes in v5:
time: 107 us; the launch traced here: 106 us
  starting transfers between devices  32.9 us (31%)
  waiting for transfers between devices  27.1 us (25%)
  matrix products  22.5 us (21%)
  Pallas kernels  15.3 us (14%)
  local copies, waits for them, and re-layouts  3.89 us (4%)
  other arithmetic  3.38 us (3%)
    ppermute x8, waiting for transfers between devices, swap(): return lax.ppermute(block, axis, route)  24.9 us
    ppermute x8, starting transfers between devices, swap(): return lax.ppermute(block, axis, route)  21.1 us
    dot_general x2, matrix products, dot_nt(): lax.dot_general(a, b, (((1,), (1,)), ((), ())), preferred_element_type=F32)  12.4 us
    pallas_call x1, Pallas kernels, attend(): pl.pallas_call(functools.partial(attention_kernel, order, group, join, hd...  10.9 us
    dot_general x2, matrix products, contrib_part(): part = jnp.dot(both, some, preferred_element_type=F32)  10 us
    all_to_all x1, starting transfers between devices, on_device(): lax.all_to_all(packed, 'seq', split_axis=0, concat_axis=0, tiled=True, ax...  6.32 us
    ppermute x4, starting transfers between devices, from_cycle(): lax.ppermute(block, axis, [(i, (i + distance) % count) for i in range(cou...  5.53 us
    unnamed x32, local copies, waits for them, and re-layouts  3.74 us
  transfers between devices with their start and end apart: 13, of which 7 were waited for; matrix products, arithmetic and copies ran while one was open for 22% of the time, Pallas kernels for 13%

profile of v5, /device:TPU:0, one launch (start us, length us, event | category | flops | bytes accessed | tf_op | source)
XLA Modules:
  0.0 106.0 jit_solution(1582657789059667782)
XLA Ops:
  0.6 0.0 copy-start
  0.6 0.0 copy-start.2
  0.7 1.4 %copy-done.2 = bf16[1,128,6144]{2,1,0:T(8,128)(2,1)S(1)} copy-done((bf16[1,128,6144]{2,1,0:T(8,128)(2,1)S(1)}, bf16[1,128,6144]{2,1,0:T(8,128)(2,1)}, u32[]{:S(2)}) %copy-start.2) | copy-done | bytes 1572888
  2.1 1.3 %shard_map.129 = bf16[4,128,1536]{2,1,0:T(8,128)(2,1)} custom-call(bf16[128,6144]{1,0:T(8,128)(2,1)S(1)} %bitcast.44), custom_call_target="tpu_custom_call" | custom-call | flops 1 | bytes 1 | tf_op jit(solution)/shard_map/pallas_call | solution.py:202
  3.4 0.8 pad_maximum_fusion.2
  4.1 6.3 %all-to-all-start = ((bf16[4,128,1536]{2,1,0:T(8,128)(2,1)}), bf16[4,128,1536]{2,1,0:T(8,128)(2,1)S(1)}, u32[]{:S(2)}, u32[]{:S(2)}) async-start(bf16[4,128,1536]{2,1,0:T(8,128)(2,1)} %shard_map.129), calls=%async_computation | async-start | bytes 3145728 | tf_op jit(solution)/shard_map/all_to_all | solution.py:309
  10.5 0.0 copy-start.3
  10.5 0.0 copy-start.4
  10.5 0.0 copy-start.9
  10.5 5.0 %collective-permute-start = (bf16[128,256]{1,0:T(8,128)(2,1)S(1)}, bf16[128,256]{1,0:T(8,128)(2,1)S(1)}, u32[]{:S(2)}, u32[]{:S(2)}) collective-permute-start(bf16[128,256]{1,0:T(8,128)(2,1)S(1)} %pad_maximum_fusion.2), channel_id=1, source_target_pairs={{0,4},{1,5},{2,6},{3,7},{8,12},{9,13},{10,14},{11,15},{16,20},{17,... | collective-permute-start | bytes 196616 | tf_op jit(solution)/shard_map/ppermute | solution.py:79
  15.4 0.0 copy-done
  15.5 6.2 %fusion.6 = f32[4,768]{1,0:T(4,128)S(1)} fusion(bf16[1,1536,6144]{2,1,0:T(8,128)(2,1)} %param.16, bf16[1,4,6144]{2,1,0:T(4,128)(2,1)S(1)} %copy-done), kind=kOutput, calls=%fused_computation.6 | convolution fusion | flops 37748736 | bytes 9498624 | tf_op jit(solution)/shard_map/dot_general | solution.py:25
  21.7 15.7 %collective-permute-done = bf16[128,256]{1,0:T(8,128)(2,1)S(1)} collective-permute-done((bf16[128,256]{1,0:T(8,128)(2,1)S(1)}, bf16[128,256]{1,0:T(8,128)(2,1)S(1)}, u32[]{:S(2)}, u32[]{:S(2)}) %collective-permute-start) | collective-permute-done | bytes 65568 | tf_op jit(solution)/shard_map/ppermute | solution.py:79
  37.4 11.6 %collective-permute-start.1 = (bf16[256,256]{1,0:T(8,128)(2,1)S(1)}, bf16[256,256]{1,0:T(8,128)(2,1)S(1)}, u32[]{:S(2)}, u32[]{:S(2)}) collective-permute-start(bf16[256,256]{1,0:T(8,128)(2,1)S(1)} %constant_dynamic-update-slice_fusion), channel_id=1, source_target_pairs={{0,2},{1,3},{2,0},{3,1},{4,6},{5,7},{6,4},{7,5},{8,10},{9,11},{10,... | collective-permute-start | bytes 393224 | tf_op jit(solution)/shard_map/ppermute | solution.py:79
  49.0 6.2 %fusion.4 = f32[4,768]{1,0:T(4,128)S(1)} fusion(bf16[4,6144]{1,0:T(4,128)(2,1)S(1)} %bitcast.41, bf16[1,1536,6144]{2,1,0:T(8,128)(2,1)} %param.16), kind=kOutput, calls=%fused_computation.4 | convolution fusion | flops 37748736 | bytes 9498624 | tf_op jit(solution)/shard_map/dot_general | solution.py:25
  55.2 0.0 collective-permute-done.1
  55.2 0.1 collective-permute-start.2
  55.3 1.5 %collective-permute-done.2.far_ref = bf16[512,256]{1,0:T(8,128)(2,1)S(1)} collective-permute-done((bf16[512,256]{1,0:T(8,128)(2,1)S(1)}, bf16[512,256]{1,0:T(8,128)(2,1)S(1)}, u32[]{:S(2)}, u32[]{:S(2)}) %collective-permute-start.2) | collective-permute-done | bytes 262176 | tf_op jit(solution)/shard_map/ppermute | solution.py:79
  56.8 0.0 copy-start.7
  56.8 0.0 copy-start.11
  56.8 2.5 %collective-permute-start.4 = (f32[4,1536]{1,0:T(4,128)S(1)}, f32[4,1536]{1,0:T(4,128)S(1)}, u32[]{:S(2)}, u32[]{:S(2)}) collective-permute-start(f32[4,1536]{1,0:T(4,128)S(1)} %constant_dynamic-update-slice_fusion.4.acts_ref), channel_id=1, source_target_pairs={{0,24},{8,0},{16,8},{24,16},{1,25},{9,1},{17,9},{25,17},{2,26},{10... | collective-permute-start | bytes 73736 | tf_op jit(solution)/shard_map/ppermute | solution.py:291
  59.3 0.0 collective-permute-start.3
  59.3 0.0 copy-done.1
  59.3 0.0 copy-done.3
  59.3 0.5 shard_map.128.delta_ref
  59.8 0.0 copy-done.7
  59.8 0.0 copy-done.4
  59.9 0.0 copy-done.9
  59.9 0.0 copy-start.8
  59.9 0.9 copy-done.8
  60.8 10.9 %shard_map.130 = (f32[128,3072]{1,0:T(8,128)}, f32[512,256]{1,0:T(8,128)S(1)}, f32[512,256]{1,0:T(8,128)}) custom-call(s32[1]{0:T(128)} %bitcast.me_ref, bf16[128,3072]{1,0:T(8,128)(2,1)S(1)} %bitcast.46, bf16[128,3072]{1,0:T(8,128)(2,1)S(1)} %bitcast.43, f32[24,128]{1,0:T(8,128)S(1)} %bitcast.47, f32[24,128]{1,0:T(8,128)S(1)} %shard_map.128.delta_ref, ...), custom_call_target="tpu_custom_call" | custom-call | flops 1 | bytes 1 | tf_op jit(solution)/shard_map/pallas_call | solution.py:175
  71.7 0.8 copy-done.5
  72.5 0.0 collective-permute-done.4.higher_ref
  72.5 0.0 collective-permute-done.3.lower_ref
  72.5 0.0 copy-start.13
  72.5 0.1 collective-permute-start.5
  72.6 0.0 copy-done.11
  72.6 0.5 copy-done.12
  73.1 0.0 copy-done.13
  73.1 2.1 %shard_map.131 = (f32[2,4,1536]{2,1,0:T(4,128)}, bf16[8,1536]{1,0:T(8,128)(2,1)}) custom-call(f32[4,1536]{1,0:T(4,128)} %copy-done.11, f32[4,1536]{1,0:T(4,128)} %copy-done.13, f32[4,1536]{1,0:T(4,128)} %copy-done.12), custom_call_target="tpu_custom_call" | custom-call | flops 1 | bytes 1 | tf_op jit(solution)/shard_map/pallas_call | solution.py:277
  75.2 5.0 %fusion.2 = f32[8,3072]{1,0:T(8,128)S(1)} fusion(bf16[8,1536]{1,0:T(8,128)(2,1)} %get-tuple-element.64, bf16[1536,6144]{1,0:T(8,128)(2,1)} %bitcast.48), kind=kOutput, calls=%fused_computation.2 | convolution fusion | flops 75497472 | bytes 9560064 | tf_op jit(solution)/shard_map/dot_general | solution.py:245
  80.2 0.0 collective-permute-done.5
  80.3 0.0 copy-done.6
  80.3 0.1 add.21
  80.4 0.1 collective-permute-start.6
  80.4 0.0 copy-done.10
  80.4 5.0 %fusion = f32[8,3072]{1,0:T(8,128)S(1)} fusion(bf16[8,1536]{1,0:T(8,128)(2,1)S(1)} %copy-done.10, bf16[1536,6144]{1,0:T(8,128)(2,1)} %bitcast.49), kind=kOutput, calls=%fused_computation | convolution fusion | flops 75497472 | bytes 9560064 | tf_op jit(solution)/shard_map/dot_general | solution.py:245
  85.5 0.3 collective-permute-done.6
  85.8 0.0 all-to-all-done.x_ref
  85.9 3.4 %collective-permute-start.7 = (bf16[256,256]{1,0:T(8,128)(2,1)S(1)}, bf16[256,256]{1,0:T(8,128)(2,1)S(1)}, u32[]{:S(2)}, u32[]{:S(2)}) collective-permute-start(bf16[256,256]{1,0:T(8,128)(2,1)S(1)} %get-tuple-element.77), channel_id=1, source_target_pairs={{0,4},{1,5},{2,6},{3,7},{4,0},{5,1},{6,2},{7,3},{8,12},{9,13},{10,... | collective-permute-start | bytes 393224 | tf_op jit(solution)/shard_map/ppermute | solution.py:79
  89.3 6.2 %collective-permute-done.7 = bf16[256,256]{1,0:T(8,128)(2,1)S(1)} collective-permute-done((bf16[256,256]{1,0:T(8,128)(2,1)S(1)}, bf16[256,256]{1,0:T(8,128)(2,1)S(1)}, u32[]{:S(2)}, u32[]{:S(2)}) %collective-permute-start.7) | collective-permute-done | bytes 131104 | tf_op jit(solution)/shard_map/ppermute | solution.py:79
  95.5 0.7 fusion.11
  96.2 0.8 collective-permute-start.8
  97.0 2.0 %collective-permute-start.10 = (f32[4,6144]{1,0:T(4,128)S(1)}, f32[4,6144]{1,0:T(4,128)S(1)}, u32[]{:S(2)}, u32[]{:S(2)}) collective-permute-start(f32[4,6144]{1,0:T(4,128)S(1)} %get-tuple-element.84), channel_id=1, source_target_pairs={{0,8},{8,16},{16,24},{24,0},{1,9},{9,17},{17,25},{25,1},{2,10},{10... | collective-permute-start | bytes 294920 | tf_op jit(solution)/shard_map/ppermute | solution.py:291
  99.0 1.0 collective-permute-start.11
  100.1 1.2 %collective-permute-done.8 = bf16[256,256]{1,0:T(8,128)(2,1)S(1)} collective-permute-done((bf16[256,256]{1,0:T(8,128)(2,1)S(1)}, bf16[256,256]{1,0:T(8,128)(2,1)S(1)}, u32[]{:S(2)}, u32[]{:S(2)}) %collective-permute-start.8) | collective-permute-done | bytes 131104 | tf_op jit(solution)/shard_map/ppermute | solution.py:79
  101.3 0.6 shard_map.132
  101.9 0.1 collective-permute-start.9
  102.0 1.4 %collective-permute-done.10 = f32[4,6144]{1,0:T(4,128)S(1)} collective-permute-done((f32[4,6144]{1,0:T(4,128)S(1)}, f32[4,6144]{1,0:T(4,128)S(1)}, u32[]{:S(2)}, u32[]{:S(2)}) %collective-permute-start.10) | collective-permute-done | bytes 98336 | tf_op jit(solution)/shard_map/ppermute | solution.py:291
  103.4 0.8 collective-permute-done.11
  104.2 0.1 add_bitcast_fusion.2
  104.3 0.7 maximum_bitcast_fusion
  105.0 0.0 collective-permute-done.9
  105.0 1.0 add_bitcast_fusion
  (22 shorter events, 0.3 us)
Async XLA Ops:
  0.6 14.8 %copy-start = (bf16[1,4,6144]{2,1,0:T(4,128)(2,1)S(1)}, bf16[1,4,6144]{2,1,0:T(4,128)(2,1)}, u32[]{:S(2)}) copy-start(bf16[1,4,6144]{2,1,0:T(4,128)(2,1)} %param.17) | copy-start | bytes 147460
  0.6 1.4 %copy-start.2 = (bf16[1,128,6144]{2,1,0:T(8,128)(2,1)S(1)}, bf16[1,128,6144]{2,1,0:T(8,128)(2,1)}, u32[]{:S(2)}) copy-start(bf16[1,128,6144]{2,1,0:T(8,128)(2,1)} %param.15) | copy-start | bytes 4718596
  4.1 81.7 %all-to-all-start = ((bf16[4,128,1536]{2,1,0:T(8,128)(2,1)}), bf16[4,128,1536]{2,1,0:T(8,128)(2,1)S(1)}, u32[]{:S(2)}, u32[]{:S(2)}) async-start(bf16[4,128,1536]{2,1,0:T(8,128)(2,1)} %shard_map.129), calls=%async_computation | async-start | bytes 3145728 | tf_op jit(solution)/shard_map/all_to_all | solution.py:309
  10.5 48.9 %copy-start.1 = (bf16[1,128,3072]{2,1,0:T(8,128)(2,1)S(1)}, bf16[1,128,3072]{2,1,0:T(8,128)(2,1)}, u32[]{:S(2)}) copy-start(bf16[1,128,3072]{2,1,0:T(8,128)(2,1)} %param.13) | copy-start | bytes 2359300
  10.5 48.9 %copy-start.3 = (bf16[1,128,3072]{2,1,0:T(8,128)(2,1)S(1)}, bf16[1,128,3072]{2,1,0:T(8,128)(2,1)}, u32[]{:S(2)}) copy-start(bf16[1,128,3072]{2,1,0:T(8,128)(2,1)} %param.12) | copy-start | bytes 2359300
  10.5 49.4 %copy-start.4 = (bf16[1,128,3072]{2,1,0:T(8,128)(2,1)S(1)}, bf16[1,128,3072]{2,1,0:T(8,128)(2,1)}, u32[]{:S(2)}) copy-start(bf16[1,128,3072]{2,1,0:T(8,128)(2,1)} %param.9) | copy-start | bytes 2359300
  10.5 49.4 %copy-start.9 = (f32[1,24,128]{2,1,0:T(8,128)S(1)}, f32[1,24,128]{2,1,0:T(8,128)}, u32[]{:S(2)}) copy-start(f32[1,24,128]{2,1,0:T(8,128)} %param.14) | copy-start | bytes 36868
  10.5 26.9 %collective-permute-start = (bf16[128,256]{1,0:T(8,128)(2,1)S(1)}, bf16[128,256]{1,0:T(8,128)(2,1)S(1)}, u32[]{:S(2)}, u32[]{:S(2)}) collective-permute-start(bf16[128,256]{1,0:T(8,128)(2,1)S(1)} %pad_maximum_fusion.2), channel_id=1, source_target_pairs={{0,4},{1,5},{2,6},{3,7},{8,12},{9,13},{10,14},{11,15},{16,20},{17,... | collective-permute-start | bytes 196616 | tf_op jit(solution)/shard_map/ppermute | solution.py:79
  37.4 17.8 %collective-permute-start.1 = (bf16[256,256]{1,0:T(8,128)(2,1)S(1)}, bf16[256,256]{1,0:T(8,128)(2,1)S(1)}, u32[]{:S(2)}, u32[]{:S(2)}) collective-permute-start(bf16[256,256]{1,0:T(8,128)(2,1)S(1)} %constant_dynamic-update-slice_fusion), channel_id=1, source_target_pairs={{0,2},{1,3},{2,0},{3,1},{4,6},{5,7},{6,4},{7,5},{8,10},{9,11},{10,... | collective-permute-start | bytes 393224 | tf_op jit(solution)/shard_map/ppermute | solution.py:79
  55.2 1.6 %collective-permute-start.2 = (bf16[512,256]{1,0:T(8,128)(2,1)S(1)}, bf16[512,256]{1,0:T(8,128)(2,1)S(1)}, u32[]{:S(2)}, u32[]{:S(2)}) collective-permute-start(bf16[512,256]{1,0:T(8,128)(2,1)S(1)} %constant_dynamic-update-slice_fusion.2.near_ref), channel_id=1, source_target_pairs={{0,1},{1,0},{2,3},{3,2},{4,5},{5,4},{6,7},{7,6},{8,9},{9,8},{10,11... | collective-permute-start | bytes 786440 | tf_op jit(solution)/shard_map/ppermute | solution.py:79
  56.8 3.0 %copy-start.7 = (bf16[512,256]{1,0:T(8,128)(2,1)}, bf16[512,256]{1,0:T(8,128)(2,1)S(1)}, u32[]{:S(2)}) copy-start(bf16[512,256]{1,0:T(8,128)(2,1)S(1)} %collective-permute-done.2.far_ref) | copy-start | bytes 786436
  56.8 15.8 %copy-start.11 = (f32[4,1536]{1,0:T(4,128)}, f32[4,1536]{1,0:T(4,128)S(1)}, u32[]{:S(2)}) copy-start(f32[4,1536]{1,0:T(4,128)S(1)} %constant_dynamic-update-slice_fusion.4.acts_ref) | copy-start | bytes 73732
  56.8 15.6 %collective-permute-start.4 = (f32[4,1536]{1,0:T(4,128)S(1)}, f32[4,1536]{1,0:T(4,128)S(1)}, u32[]{:S(2)}, u32[]{:S(2)}) collective-permute-start(f32[4,1536]{1,0:T(4,128)S(1)} %constant_dynamic-update-slice_fusion.4.acts_ref), channel_id=1, source_target_pairs={{0,24},{8,0},{16,8},{24,16},{1,25},{9,1},{17,9},{25,17},{2,26},{10... | collective-permute-start | bytes 73736 | tf_op jit(solution)/shard_map/ppermute | solution.py:291
  59.3 13.1 %collective-permute-start.3 = (f32[4,1536]{1,0:T(4,128)S(1)}, f32[4,1536]{1,0:T(4,128)S(1)}, u32[]{:S(2)}, u32[]{:S(2)}) collective-permute-start(f32[4,1536]{1,0:T(4,128)S(1)} %constant_dynamic-update-slice_fusion.4.acts_ref), channel_id=1, source_target_pairs={{0,8},{8,16},{16,24},{24,0},{1,9},{9,17},{17,25},{25,1},{2,10},{10... | collective-permute-start | bytes 73736 | tf_op jit(solution)/shard_map/ppermute | solution.py:291
  59.9 1.0 copy-start.8
  71.7 0.8 copy-start.5
  72.5 0.6 copy-start.12
  72.5 7.8 %copy-start.6 = (f32[512,256]{1,0:T(8,128)S(1)}, f32[512,256]{1,0:T(8,128)}, u32[]{:S(2)}) copy-start(f32[512,256]{1,0:T(8,128)} %copy-done.5) | copy-start | bytes 1572868
  72.5 0.6 copy-start.13
  72.5 7.7 %collective-permute-start.5 = (f32[512,256]{1,0:T(8,128)}, f32[512,256]{1,0:T(8,128)S(1)}, u32[]{:S(2)}, u32[]{:S(2)}) collective-permute-start(f32[512,256]{1,0:T(8,128)} %get-tuple-element.63), channel_id=1, source_target_pairs={{0,1},{1,0},{2,3},{3,2},{4,5},{5,4},{6,7},{7,6},{8,9},{9,8},{10,11... | collective-permute-start | bytes 1572872 | tf_op jit(solution)/shard_map/ppermute | solution.py:79
  75.2 5.3 %copy-start.10 = (bf16[8,1536]{1,0:T(8,128)(2,1)S(1)}, bf16[8,1536]{1,0:T(8,128)(2,1)}, u32[]{:S(2)}) copy-start(bf16[8,1536]{1,0:T(8,128)(2,1)} %get-tuple-element.64) | copy-start | bytes 73732
  80.4 5.5 %collective-permute-start.6 = (bf16[256,256]{1,0:T(8,128)(2,1)S(1)}, bf16[256,256]{1,0:T(8,128)(2,1)S(1)}, u32[]{:S(2)}, u32[]{:S(2)}) collective-permute-start(bf16[256,256]{1,0:T(8,128)(2,1)S(1)} %slice.101), channel_id=1, source_target_pairs={{0,2},{1,3},{2,0},{3,1},{4,6},{5,7},{6,4},{7,5},{8,10},{9,11},{10,... | collective-permute-start | bytes 393224 | tf_op jit(solution)/shard_map/ppermute | solution.py:79
  85.9 9.6 %collective-permute-start.7 = (bf16[256,256]{1,0:T(8,128)(2,1)S(1)}, bf16[256,256]{1,0:T(8,128)(2,1)S(1)}, u32[]{:S(2)}, u32[]{:S(2)}) collective-permute-start(bf16[256,256]{1,0:T(8,128)(2,1)S(1)} %get-tuple-element.77), channel_id=1, source_target_pairs={{0,4},{1,5},{2,6},{3,7},{4,0},{5,1},{6,2},{7,3},{8,12},{9,13},{10,... | collective-permute-start | bytes 393224 | tf_op jit(solution)/shard_map/ppermute | solution.py:79
  96.2 5.0 %collective-permute-start.8 = (bf16[256,256]{1,0:T(8,128)(2,1)S(1)}, bf16[256,256]{1,0:T(8,128)(2,1)S(1)}, u32[]{:S(2)}, u32[]{:S(2)}) collective-permute-start(bf16[256,256]{1,0:T(8,128)(2,1)S(1)} %pad_maximum_fusion.1), channel_id=1, source_target_pairs={{0,2},{1,3},{2,0},{3,1},{4,6},{5,7},{6,4},{7,5},{8,10},{9,11},{10,... | collective-permute-start | bytes 393224 | tf_op jit(solution)/shard_map/ppermute | solution.py:79
  97.0 6.4 %collective-permute-start.10 = (f32[4,6144]{1,0:T(4,128)S(1)}, f32[4,6144]{1,0:T(4,128)S(1)}, u32[]{:S(2)}, u32[]{:S(2)}) collective-permute-start(f32[4,6144]{1,0:T(4,128)S(1)} %get-tuple-element.84), channel_id=1, source_target_pairs={{0,8},{8,16},{16,24},{24,0},{1,9},{9,17},{17,25},{25,1},{2,10},{10... | collective-permute-start | bytes 294920 | tf_op jit(solution)/shard_map/ppermute | solution.py:291
  99.0 5.2 %collective-permute-start.11 = (f32[4,6144]{1,0:T(4,128)S(1)}, f32[4,6144]{1,0:T(4,128)S(1)}, u32[]{:S(2)}, u32[]{:S(2)}) collective-permute-start(f32[4,6144]{1,0:T(4,128)S(1)} %get-tuple-element.85), channel_id=1, source_target_pairs={{0,24},{8,0},{16,8},{24,16},{1,25},{9,1},{17,9},{25,17},{2,26},{10... | collective-permute-start | bytes 294920 | tf_op jit(solution)/shard_map/ppermute | solution.py:291
  101.9 3.1 %collective-permute-start.9 = (f32[768,256]{1,0:T(8,128)S(1)}, f32[768,256]{1,0:T(8,128)S(1)}, u32[]{:S(2)}, u32[]{:S(2)}) collective-permute-start(f32[768,256]{1,0:T(8,128)S(1)} %get-tuple-element.73), channel_id=1, source_target_pairs={{0,1},{1,0},{2,3},{3,2},{4,5},{5,4},{6,7},{7,6},{8,9},{9,8},{10,11... | collective-permute-start | bytes 2359304 | tf_op jit(solution)/shard_map/ppermute | solution.py:79

commit v6 on v5

--- a/solution.py
+++ b/solution.py
@@ -233,12 +233,6 @@
     )(me[None], blocks, grads)
 
 
-def acts_part(factor, weight, index, parts):
-    rows = weight.shape[0] // parts
-    some = weight[index * rows : (index + 1) * rows]
-    return dot_nt(factor, some)
-
-
 def contrib_part(both, weight, index, parts):
     cols = weight.shape[1] // parts
     some = weight[:, index * cols : (index + 1) * cols]
@@ -302,10 +296,16 @@
     factor = initial_right_factor[0]
     weight = mlp_weight[0]
 
+    near = jnp.concatenate([keys[0], values[0]], axis=-1)
     chips = count // 2
-    packed = pack(inputs[0], chips)
-    near = jnp.concatenate([keys[0], values[0]], axis=-1)
-    near, packed = lax.optimization_barrier((near, packed))
+    beside = [pack(inputs[0], chips), head_delta(out_grad[0], outputs[0], heads), factor]
+    for index, bit in enumerate(bits):
+        if bit == 1:
+            break
+        far = swap(near, "seq", bit, True if index == 0 else None)
+        near, far, beside = lax.optimization_barrier((near, far, beside))
+        near = jnp.concatenate([near, far], axis=0)
+    packed, delta, factor = beside
     blocks = lax.all_to_all(
         packed,
         "seq",
@@ -314,23 +314,12 @@
         tiled=True,
         axis_index_groups=[list(range(core, count, 2)) for core in range(2)],
     )
-
-    acts_parts = []
-    for index, bit in enumerate(bits):
-        far = swap(near, "seq", bit, True if index == 0 else None)
-        if index < PARTS:
-            acts_parts.append(acts_part(factor, weight, index, PARTS))
-        factor, near, far, acts_parts = lax.optimization_barrier(
-            (factor, near, far, acts_parts)
-        )
-        if bit > 1:
-            near = jnp.concatenate([near, far], axis=0)
-    acts = jnp.concatenate(acts_parts, axis=1)
+    far = swap(near, "seq", 1)
+    acts = dot_nt(factor, weight)
+    near, far, acts = lax.optimization_barrier((near, far, acts))
     lower_acts = from_cycle(acts, "rep", 1)
     higher_acts = from_cycle(acts, "rep", -1)
 
-    delta = head_delta(out_grad[0], outputs[0], heads)
-    delta, near, far = lax.optimization_barrier((delta, near, far))
     query_grad, grads, sent = attend(me, queries[0], out_grad[0], log_norm[0], delta, near, far)
     lower_acts, higher_acts, sent = lax.optimization_barrier((lower_acts, higher_acts, sent))
 
@@ -344,22 +333,23 @@
             contrib_parts += [
                 contrib_part(both, weight, index + i, PARTS) for i in range(share)
             ]
-        both, grads, arrived, contrib_parts, blocks = lax.optimization_barrier(
-            (both, grads, arrived, contrib_parts, blocks)
-        ) if bit * 2 == last else (
-            *lax.optimization_barrier((both, grads, arrived, contrib_parts)), blocks
+        both, grads, arrived, contrib_parts = lax.optimization_barrier(
+            (both, grads, arrived, contrib_parts)
         )
         grads = grads + arrived.astype(F32)
         keep = grads.shape[0] // 2
         if bit * 2 < last:
             sent = grads[keep:].astype(BF16)
             grads = grads[:keep]
+    blocks, grads = lax.optimization_barrier((blocks, grads))
     contrib = jnp.concatenate(contrib_parts, axis=2)
     lower_half = from_cycle(contrib[1], "rep", 1)
     higher_half = from_cycle(contrib[0], "rep", -1)
 
     upper = (me & last) != 0
-    arrived = swap(grads.astype(BF16), "seq", last).astype(F32)
+    arrived = swap(grads.astype(BF16), "seq", last)
+    arrived, lower_half, higher_half = lax.optimization_barrier((arrived, lower_half, higher_half))
+    arrived = arrived.astype(F32)
     mine, theirs = grads[:keep], grads[keep:]
     own = jnp.where(upper, mine, mine + arrived[keep:])
     other = jnp.where(upper, theirs + arrived[:keep], arrived[:keep])

time: 107 us -> 85.6 us (0.80)
  waiting for transfers between devices: 27.1 us -> 14.8 us
  starting transfers between devices: 32.9 us -> 22.1 us
  local copies, waits for them, and re-layouts: 3.89 us -> 7.47 us
  matrix products: 22.5 us -> 19 us
  other arithmetic: 3.38 us -> 4.51 us
    ppermute x8, waiting for transfers between devices: 24.9 us -> 9.3 us  [swap(): return lax.ppermute(block, axis, route)]
    ppermute x8, starting transfers between devices: 21.1 us -> 13.1 us  [swap(): return lax.ppermute(block, axis, route)]
    dot_general x2 -> x1, matrix products: 12.4 us -> 8.91 us  [dot_nt(): lax.dot_general(a, b, (((1,), (1,)), ((), ())), preferred_element_type=F32)]
    ppermute x4, waiting for transfers between devices: 2.25 us -> 5.52 us  [from_cycle(): lax.ppermute(block, axis, [(i, (i + distance) % count) for i in range(cou...]
    all_to_all x1, starting transfers between devices: 6.32 us -> 3.56 us  [on_device(): lax.all_to_all(packed, 'seq', split_axis=0, concat_axis=0, tiled=True, ax...]
    unnamed x32 -> x29, local copies, waits for them, and re-layouts: 3.74 us -> 6.42 us
  transfers between devices with their start and end apart: 13 -> 13, of which waited for: 7 -> 5; matrix products, arithmetic and copies ran while one was open for 22% -> 27% of each run, Pallas kernels for 13% -> 18%
where the time goes in v6:
time: 85.6 us; the launch traced here: 85.1 us
  starting transfers between devices  22.1 us (26%)
  matrix products  19 us (22%)
  Pallas kernels  16.3 us (19%)
  waiting for transfers between devices  14.8 us (17%)
  local copies, waits for them, and re-layouts  7.47 us (9%)
  other arithmetic  4.51 us (5%)
  between operations  0.92 us (1%)
    ppermute x8, starting transfers between devices, swap(): return lax.ppermute(block, axis, route)  13.1 us
    pallas_call x1, Pallas kernels, attend(): pl.pallas_call(functools.partial(attention_kernel, order, group, join, hd...  11.8 us
    dot_general x2, matrix products, contrib_part(): part = jnp.dot(both, some, preferred_element_type=F32)  10 us
    ppermute x8, waiting for transfers between devices, swap(): return lax.ppermute(block, axis, route)  9.3 us
    dot_general x1, matrix products, dot_nt(): lax.dot_general(a, b, (((1,), (1,)), ((), ())), preferred_element_type=F32)  8.91 us
    unnamed x29, local copies, waits for them, and re-layouts  6.42 us
    ppermute x4, waiting for transfers between devices, from_cycle(): lax.ppermute(block, axis, [(i, (i + distance) % count) for i in range(cou...  5.52 us
    ppermute x4, starting transfers between devices, from_cycle(): lax.ppermute(block, axis, [(i, (i + distance) % count) for i in range(cou...  5.45 us
  transfers between devices with their start and end apart: 13, of which 5 were waited for; matrix products, arithmetic and copies ran while one was open for 27% of the time, Pallas kernels for 18%

profile of v6, /device:TPU:0, one launch (start us, length us, event | category | flops | bytes accessed | tf_op | source)
XLA Modules:
  0.0 85.1 jit_solution(16653977339667635675)
XLA Ops:
  0.6 0.0 copy-start
  0.6 0.0 copy-start.2
  0.7 0.9 %pad_maximum_fusion.2 = bf16[128,256]{1,0:T(8,128)(2,1)S(1)} fusion(bf16[128,128]{1,0:T(8,128)(2,1)} %bitcast.44, bf16[128,128]{1,0:T(8,128)(2,1)} %bitcast.45), kind=kLoop, calls=%fused_computation.17 | loop fusion | flops 131072 | bytes 131072 | tf_op jit(solution)/shard_map/concatenate | solution.py:299
  1.5 5.9 %collective-permute-start = (bf16[128,256]{1,0:T(8,128)(2,1)S(1)}, bf16[128,256]{1,0:T(8,128)(2,1)S(1)}, u32[]{:S(2)}, u32[]{:S(2)}) collective-permute-start(bf16[128,256]{1,0:T(8,128)(2,1)S(1)} %pad_maximum_fusion.2), channel_id=1, source_target_pairs={{0,4},{1,5},{2,6},{3,7},{8,12},{9,13},{10,14},{11,15},{16,20},{17,... | collective-permute-start | bytes 196616 | tf_op jit(solution)/shard_map/ppermute | solution.py:79
  7.5 0.0 copy-start.3
  7.5 1.4 %copy-done.3 = bf16[1,128,6144]{2,1,0:T(8,128)(2,1)S(1)} copy-done((bf16[1,128,6144]{2,1,0:T(8,128)(2,1)S(1)}, bf16[1,128,6144]{2,1,0:T(8,128)(2,1)}, u32[]{:S(2)}) %copy-start.3) | copy-done | bytes 1572888
  8.9 0.0 copy-start.5
  8.9 0.0 copy-start.7
  8.9 1.3 %shard_map.128 = bf16[4,128,1536]{2,1,0:T(8,128)(2,1)} custom-call(bf16[128,6144]{1,0:T(8,128)(2,1)S(1)} %bitcast.38), custom_call_target="tpu_custom_call" | custom-call | flops 1 | bytes 1 | tf_op jit(solution)/shard_map/pallas_call | solution.py:202
  10.2 0.0 copy-start.1
  10.2 1.1 %copy-done.1 = bf16[1,128,3072]{2,1,0:T(8,128)(2,1)S(1)} copy-done((bf16[1,128,3072]{2,1,0:T(8,128)(2,1)S(1)}, bf16[1,128,3072]{2,1,0:T(8,128)(2,1)}, u32[]{:S(2)}) %copy-start.1) | copy-done | bytes 786456
  11.3 0.0 copy-start.4
  11.3 1.1 %copy-done.4 = bf16[1,128,3072]{2,1,0:T(8,128)(2,1)S(1)} copy-done((bf16[1,128,3072]{2,1,0:T(8,128)(2,1)S(1)}, bf16[1,128,3072]{2,1,0:T(8,128)(2,1)}, u32[]{:S(2)}) %copy-start.4) | copy-done | bytes 786456
  12.4 0.5 shard_map.129.delta_ref
  12.9 0.0 collective-permute-done
  12.9 0.0 copy-done
  13.0 0.0 copy-start.8
  13.0 1.6 %collective-permute-start.1 = (bf16[256,256]{1,0:T(8,128)(2,1)S(1)}, bf16[256,256]{1,0:T(8,128)(2,1)S(1)}, u32[]{:S(2)}, u32[]{:S(2)}) collective-permute-start(bf16[256,256]{1,0:T(8,128)(2,1)S(1)} %constant_dynamic-update-slice_fusion), channel_id=1, source_target_pairs={{0,2},{1,3},{2,0},{3,1},{4,6},{5,7},{6,4},{7,5},{8,10},{9,11},{10,... | collective-permute-start | bytes 393224 | tf_op jit(solution)/shard_map/ppermute | solution.py:79
  14.6 3.4 %collective-permute-done.1 = bf16[256,256]{1,0:T(8,128)(2,1)S(1)} collective-permute-done((bf16[256,256]{1,0:T(8,128)(2,1)S(1)}, bf16[256,256]{1,0:T(8,128)(2,1)S(1)}, u32[]{:S(2)}, u32[]{:S(2)}) %collective-permute-start.1) | collective-permute-done | bytes 131104 | tf_op jit(solution)/shard_map/ppermute | solution.py:79
  18.0 0.0 copy-done.8
  18.0 0.7 copy-done.9
  18.7 3.6 %all-to-all-start = ((bf16[4,128,1536]{2,1,0:T(8,128)(2,1)}), bf16[4,128,1536]{2,1,0:T(8,128)(2,1)S(1)}, u32[]{:S(2)}, u32[]{:S(2)}) async-start(bf16[4,128,1536]{2,1,0:T(8,128)(2,1)} %shard_map.128), calls=%async_computation | async-start | bytes 3145728 | tf_op jit(solution)/shard_map/all_to_all | solution.py:309
  22.2 0.9 %constant_dynamic-update-slice_fusion.3 = bf16[512,256]{1,0:T(8,128)(2,1)S(1)} fusion(bf16[256,256]{1,0:T(8,128)(2,1)} %copy-done.8), kind=kLoop, calls=%fused_computation.23 | loop fusion | bytes 262144
  23.2 0.9 %constant_dynamic-update-slice_fusion.2.near_ref = bf16[512,256]{1,0:T(8,128)(2,1)S(1)} fusion(bf16[512,256]{1,0:T(8,128)(2,1)S(1)} %constant_dynamic-update-slice_fusion.3, bf16[256,256]{1,0:T(8,128)(2,1)} %copy-done.9), kind=kLoop, calls=%fused_computation.22 | loop fusion | bytes 262144 | tf_op jit(solution)/shard_map/concatenate | solution.py:307
  24.1 0.1 collective-permute-start.2
  24.2 8.9 %fusion.7.acts_ref = f32[4,1536]{1,0:T(4,128)S(1)} fusion(bf16[4,6144]{1,0:T(4,128)(2,1)S(1)} %bitcast.35, bf16[1,1536,6144]{2,1,0:T(8,128)(2,1)} %param.16), kind=kOutput, calls=%fused_computation.26 | convolution fusion | flops 75497472 | bytes 18948096 | tf_op jit(solution)/shard_map/dot_general | solution.py:25
  33.1 0.0 collective-permute-done.2.far_ref
  33.1 2.5 %collective-permute-start.4 = (f32[4,1536]{1,0:T(4,128)S(1)}, f32[4,1536]{1,0:T(4,128)S(1)}, u32[]{:S(2)}, u32[]{:S(2)}) collective-permute-start(f32[4,1536]{1,0:T(4,128)S(1)} %fusion.7.acts_ref), channel_id=1, source_target_pairs={{0,24},{8,0},{16,8},{24,16},{1,25},{9,1},{17,9},{25,17},{2,26},{10... | collective-permute-start | bytes 73736 | tf_op jit(solution)/shard_map/ppermute | solution.py:285
  35.6 0.0 collective-permute-start.3
  35.6 0.0 copy-done.2
  35.6 0.0 copy-done.5
  35.6 0.0 copy-done.7
  35.6 11.8 %shard_map.130 = (f32[128,3072]{1,0:T(8,128)}, f32[512,256]{1,0:T(8,128)S(1)}, f32[512,256]{1,0:T(8,128)}) custom-call(s32[1]{0:T(128)} %bitcast.me_ref, bf16[128,3072]{1,0:T(8,128)(2,1)S(1)} %bitcast.40, bf16[128,3072]{1,0:T(8,128)(2,1)S(1)} %bitcast.37, f32[24,128]{1,0:T(8,128)S(1)} %bitcast.41, f32[24,128]{1,0:T(8,128)S(1)} %shard_map.129.delta_ref, ...), custom_call_target="tpu_custom_call" | custom-call | flops 1 | bytes 1 | tf_op jit(solution)/shard_map/pallas_call | solution.py:175
  47.4 0.8 copy-done.6
  48.2 0.0 collective-permute-done.4.higher_ref
  48.2 0.0 collective-permute-done.3.lower_ref
  48.2 0.0 copy-start.12
  48.3 0.3 collective-permute-start.5
  48.5 0.0 copy-done.10
  48.5 0.3 copy-done.11
  48.8 0.0 copy-done.12
  48.9 2.1 %shard_map.131 = (f32[2,4,1536]{2,1,0:T(4,128)}, bf16[8,1536]{1,0:T(8,128)(2,1)}) custom-call(f32[4,1536]{1,0:T(4,128)} %copy-done.10, f32[4,1536]{1,0:T(4,128)} %copy-done.12, f32[4,1536]{1,0:T(4,128)} %copy-done.11), custom_call_target="tpu_custom_call" | custom-call | flops 1 | bytes 1 | tf_op jit(solution)/shard_map/pallas_call | solution.py:271
  50.9 5.0 %fusion.2 = f32[8,3072]{1,0:T(8,128)S(1)} fusion(bf16[8,1536]{1,0:T(8,128)(2,1)} %get-tuple-element.61, bf16[1536,6144]{1,0:T(8,128)(2,1)} %bitcast.42), kind=kOutput, calls=%fused_computation.2 | convolution fusion | flops 75497472 | bytes 9560064 | tf_op jit(solution)/shard_map/dot_general | solution.py:239
  56.0 0.0 collective-permute-done.5
  56.0 1.1 %add.21 = f32[512,256]{1,0:T(8,128)S(1)} add(f32[512,256]{1,0:T(8,128)} %copy-done.6, f32[512,256]{1,0:T(8,128)S(1)} %collective-permute-done.5) | non-fusion elementwise | flops 131072 | bytes 1572864 | tf_op jit(solution)/shard_map/add | solution.py:339
  57.1 2.0 %collective-permute-start.6 = (bf16[256,256]{1,0:T(8,128)(2,1)S(1)}, bf16[256,256]{1,0:T(8,128)(2,1)S(1)}, u32[]{:S(2)}, u32[]{:S(2)}) collective-permute-start(bf16[256,256]{1,0:T(8,128)(2,1)S(1)} %slice.75), channel_id=1, source_target_pairs={{0,2},{1,3},{2,0},{3,1},{4,6},{5,7},{6,4},{7,5},{8,10},{9,11},{10,... | collective-permute-start | bytes 393224 | tf_op jit(solution)/shard_map/ppermute | solution.py:79
  59.2 5.0 %fusion = f32[8,3072]{1,0:T(8,128)S(1)} fusion(bf16[8,1536]{1,0:T(8,128)(2,1)} %get-tuple-element.61, bf16[1536,6144]{1,0:T(8,128)(2,1)} %bitcast.43), kind=kOutput, calls=%fused_computation | convolution fusion | flops 75497472 | bytes 9560064 | tf_op jit(solution)/shard_map/dot_general | solution.py:239
  64.3 0.0 collective-permute-done.6
  64.4 0.0 all-to-all-done.x_ref
  64.4 2.4 %collective-permute-start.7 = (bf16[256,256]{1,0:T(8,128)(2,1)S(1)}, bf16[256,256]{1,0:T(8,128)(2,1)S(1)}, u32[]{:S(2)}, u32[]{:S(2)}) collective-permute-start(bf16[256,256]{1,0:T(8,128)(2,1)S(1)} %convert_element_type.12), channel_id=1, source_target_pairs={{0,4},{1,5},{2,6},{3,7},{4,0},{5,1},{6,2},{7,3},{8,12},{9,13},{10,... | collective-permute-start | bytes 393224 | tf_op jit(solution)/shard_map/ppermute | solution.py:79
  66.8 2.9 %collective-permute-start.9 = (f32[4,6144]{1,0:T(4,128)S(1)}, f32[4,6144]{1,0:T(4,128)S(1)}, u32[]{:S(2)}, u32[]{:S(2)}) collective-permute-start(f32[4,6144]{1,0:T(4,128)S(1)} %get-tuple-element.82), channel_id=1, source_target_pairs={{0,24},{8,0},{16,8},{24,16},{1,25},{9,1},{17,9},{25,17},{2,26},{10... | collective-permute-start | bytes 294920 | tf_op jit(solution)/shard_map/ppermute | solution.py:285
  69.8 0.0 collective-permute-start.8
  69.8 2.7 %collective-permute-done.9 = f32[4,6144]{1,0:T(4,128)S(1)} collective-permute-done((f32[4,6144]{1,0:T(4,128)S(1)}, f32[4,6144]{1,0:T(4,128)S(1)}, u32[]{:S(2)}, u32[]{:S(2)}) %collective-permute-start.9) | collective-permute-done | bytes 98336 | tf_op jit(solution)/shard_map/ppermute | solution.py:285
  72.5 2.8 %collective-permute-done.8 = f32[4,6144]{1,0:T(4,128)S(1)} collective-permute-done((f32[4,6144]{1,0:T(4,128)S(1)}, f32[4,6144]{1,0:T(4,128)S(1)}, u32[]{:S(2)}, u32[]{:S(2)}) %collective-permute-start.8) | collective-permute-done | bytes 98336 | tf_op jit(solution)/shard_map/ppermute | solution.py:285
  75.3 0.0 collective-permute-done.7
  75.3 0.7 fusion.5
  76.0 0.6 collective-permute-start.10
  76.7 4.4 %collective-permute-done.10 = bf16[256,256]{1,0:T(8,128)(2,1)S(1)} collective-permute-done((bf16[256,256]{1,0:T(8,128)(2,1)S(1)}, bf16[256,256]{1,0:T(8,128)(2,1)S(1)}, u32[]{:S(2)}, u32[]{:S(2)}) %collective-permute-start.10) | collective-permute-done | bytes 131104 | tf_op jit(solution)/shard_map/ppermute | solution.py:79
  81.1 0.6 shard_map.132
  81.7 0.1 collective-permute-start.11
  81.8 0.1 add_bitcast_fusion.2
  81.9 0.7 maximum_bitcast_fusion
  82.6 1.5 %collective-permute-done.11 = f32[768,256]{1,0:T(8,128)S(1)} collective-permute-done((f32[768,256]{1,0:T(8,128)S(1)}, f32[768,256]{1,0:T(8,128)S(1)}, u32[]{:S(2)}, u32[]{:S(2)}) %collective-permute-start.11) | collective-permute-done | bytes 786464 | tf_op jit(solution)/shard_map/ppermute | solution.py:79
  84.1 1.0 %add_bitcast_fusion = f32[1,768,256]{2,1,0:T(8,128)} fusion(f32[768,256]{1,0:T(8,128)S(1)} %get-tuple-element.72, f32[768,256]{1,0:T(8,128)S(1)} %collective-permute-done.11), kind=kLoop, calls=%fused_computation.4 | loop fusion | flops 196608 | bytes 2359296 | tf_op jit(solution)/shard_map/broadcast_in_dim | solution.py:366
  (18 shorter events, 0.2 us)
Async XLA Ops:
  0.6 12.3 %copy-start = (bf16[1,4,6144]{2,1,0:T(4,128)(2,1)S(1)}, bf16[1,4,6144]{2,1,0:T(4,128)(2,1)}, u32[]{:S(2)}) copy-start(bf16[1,4,6144]{2,1,0:T(4,128)(2,1)} %param.17) | copy-start | bytes 147460
  0.6 34.9 %copy-start.2 = (bf16[1,128,3072]{2,1,0:T(8,128)(2,1)S(1)}, bf16[1,128,3072]{2,1,0:T(8,128)(2,1)}, u32[]{:S(2)}) copy-start(bf16[1,128,3072]{2,1,0:T(8,128)(2,1)} %param.13) | copy-start | bytes 2359300
  1.5 11.4 %collective-permute-start = (bf16[128,256]{1,0:T(8,128)(2,1)S(1)}, bf16[128,256]{1,0:T(8,128)(2,1)S(1)}, u32[]{:S(2)}, u32[]{:S(2)}) collective-permute-start(bf16[128,256]{1,0:T(8,128)(2,1)S(1)} %pad_maximum_fusion.2), channel_id=1, source_target_pairs={{0,4},{1,5},{2,6},{3,7},{8,12},{9,13},{10,14},{11,15},{16,20},{17,... | collective-permute-start | bytes 196616 | tf_op jit(solution)/shard_map/ppermute | solution.py:79
  7.5 1.4 %copy-start.3 = (bf16[1,128,6144]{2,1,0:T(8,128)(2,1)S(1)}, bf16[1,128,6144]{2,1,0:T(8,128)(2,1)}, u32[]{:S(2)}) copy-start(bf16[1,128,6144]{2,1,0:T(8,128)(2,1)} %param.15) | copy-start | bytes 4718596
  8.9 26.7 %copy-start.5 = (bf16[1,128,3072]{2,1,0:T(8,128)(2,1)S(1)}, bf16[1,128,3072]{2,1,0:T(8,128)(2,1)}, u32[]{:S(2)}) copy-start(bf16[1,128,3072]{2,1,0:T(8,128)(2,1)} %param.9) | copy-start | bytes 2359300
  8.9 26.7 %copy-start.7 = (f32[1,24,128]{2,1,0:T(8,128)S(1)}, f32[1,24,128]{2,1,0:T(8,128)}, u32[]{:S(2)}) copy-start(f32[1,24,128]{2,1,0:T(8,128)} %param.14) | copy-start | bytes 36868
  10.2 1.1 %copy-start.1 = (bf16[1,128,3072]{2,1,0:T(8,128)(2,1)S(1)}, bf16[1,128,3072]{2,1,0:T(8,128)(2,1)}, u32[]{:S(2)}) copy-start(bf16[1,128,3072]{2,1,0:T(8,128)(2,1)} %param.13) | copy-start | bytes 2359300
  11.3 1.1 %copy-start.4 = (bf16[1,128,3072]{2,1,0:T(8,128)(2,1)S(1)}, bf16[1,128,3072]{2,1,0:T(8,128)(2,1)}, u32[]{:S(2)}) copy-start(bf16[1,128,3072]{2,1,0:T(8,128)(2,1)} %param.12) | copy-start | bytes 2359300
  13.0 5.0 %copy-start.8 = (bf16[256,256]{1,0:T(8,128)(2,1)}, bf16[256,256]{1,0:T(8,128)(2,1)S(1)}, u32[]{:S(2)}) copy-start(bf16[256,256]{1,0:T(8,128)(2,1)S(1)} %constant_dynamic-update-slice_fusion) | copy-start | bytes 393220
  13.0 5.0 %collective-permute-start.1 = (bf16[256,256]{1,0:T(8,128)(2,1)S(1)}, bf16[256,256]{1,0:T(8,128)(2,1)S(1)}, u32[]{:S(2)}, u32[]{:S(2)}) collective-permute-start(bf16[256,256]{1,0:T(8,128)(2,1)S(1)} %constant_dynamic-update-slice_fusion), channel_id=1, source_target_pairs={{0,2},{1,3},{2,0},{3,1},{4,6},{5,7},{6,4},{7,5},{8,10},{9,11},{10,... | collective-permute-start | bytes 393224 | tf_op jit(solution)/shard_map/ppermute | solution.py:79
  18.0 0.7 copy-start.9
  18.7 45.7 %all-to-all-start = ((bf16[4,128,1536]{2,1,0:T(8,128)(2,1)}), bf16[4,128,1536]{2,1,0:T(8,128)(2,1)S(1)}, u32[]{:S(2)}, u32[]{:S(2)}) async-start(bf16[4,128,1536]{2,1,0:T(8,128)(2,1)} %shard_map.128), calls=%async_computation | async-start | bytes 3145728 | tf_op jit(solution)/shard_map/all_to_all | solution.py:309
  24.1 9.0 %collective-permute-start.2 = (bf16[512,256]{1,0:T(8,128)(2,1)S(1)}, bf16[512,256]{1,0:T(8,128)(2,1)}, u32[]{:S(2)}, u32[]{:S(2)}) collective-permute-start(bf16[512,256]{1,0:T(8,128)(2,1)S(1)} %constant_dynamic-update-slice_fusion.2.near_ref), channel_id=1, source_target_pairs={{0,1},{1,0},{2,3},{3,2},{4,5},{5,4},{6,7},{7,6},{8,9},{9,8},{10,11... | collective-permute-start | bytes 786440 | tf_op jit(solution)/shard_map/ppermute | solution.py:79
  33.1 15.5 %copy-start.10 = (f32[4,1536]{1,0:T(4,128)}, f32[4,1536]{1,0:T(4,128)S(1)}, u32[]{:S(2)}) copy-start(f32[4,1536]{1,0:T(4,128)S(1)} %fusion.7.acts_ref) | copy-start | bytes 73732
  33.1 15.2 %collective-permute-start.4 = (f32[4,1536]{1,0:T(4,128)S(1)}, f32[4,1536]{1,0:T(4,128)S(1)}, u32[]{:S(2)}, u32[]{:S(2)}) collective-permute-start(f32[4,1536]{1,0:T(4,128)S(1)} %fusion.7.acts_ref), channel_id=1, source_target_pairs={{0,24},{8,0},{16,8},{24,16},{1,25},{9,1},{17,9},{25,17},{2,26},{10... | collective-permute-start | bytes 73736 | tf_op jit(solution)/shard_map/ppermute | solution.py:285
  35.6 12.7 %collective-permute-start.3 = (f32[4,1536]{1,0:T(4,128)S(1)}, f32[4,1536]{1,0:T(4,128)S(1)}, u32[]{:S(2)}, u32[]{:S(2)}) collective-permute-start(f32[4,1536]{1,0:T(4,128)S(1)} %fusion.7.acts_ref), channel_id=1, source_target_pairs={{0,8},{8,16},{16,24},{24,0},{1,9},{9,17},{17,25},{25,1},{2,10},{10... | collective-permute-start | bytes 73736 | tf_op jit(solution)/shard_map/ppermute | solution.py:285
  47.4 0.8 copy-start.6
  48.2 0.6 copy-start.11
  48.2 0.6 copy-start.12
  48.3 7.7 %collective-permute-start.5 = (f32[512,256]{1,0:T(8,128)}, f32[512,256]{1,0:T(8,128)S(1)}, u32[]{:S(2)}, u32[]{:S(2)}) collective-permute-start(f32[512,256]{1,0:T(8,128)} %get-tuple-element.60), channel_id=1, source_target_pairs={{0,1},{1,0},{2,3},{3,2},{4,5},{5,4},{6,7},{7,6},{8,9},{9,8},{10,11... | collective-permute-start | bytes 1572872 | tf_op jit(solution)/shard_map/ppermute | solution.py:79
  57.1 7.1 %collective-permute-start.6 = (bf16[256,256]{1,0:T(8,128)(2,1)S(1)}, bf16[256,256]{1,0:T(8,128)(2,1)S(1)}, u32[]{:S(2)}, u32[]{:S(2)}) collective-permute-start(bf16[256,256]{1,0:T(8,128)(2,1)S(1)} %slice.75), channel_id=1, source_target_pairs={{0,2},{1,3},{2,0},{3,1},{4,6},{5,7},{6,4},{7,5},{8,10},{9,11},{10,... | collective-permute-start | bytes 393224 | tf_op jit(solution)/shard_map/ppermute | solution.py:79
  64.4 10.9 %collective-permute-start.7 = (bf16[256,256]{1,0:T(8,128)(2,1)S(1)}, bf16[256,256]{1,0:T(8,128)(2,1)S(1)}, u32[]{:S(2)}, u32[]{:S(2)}) collective-permute-start(bf16[256,256]{1,0:T(8,128)(2,1)S(1)} %convert_element_type.12), channel_id=1, source_target_pairs={{0,4},{1,5},{2,6},{3,7},{4,0},{5,1},{6,2},{7,3},{8,12},{9,13},{10,... | collective-permute-start | bytes 393224 | tf_op jit(solution)/shard_map/ppermute | solution.py:79
  66.8 5.6 %collective-permute-start.9 = (f32[4,6144]{1,0:T(4,128)S(1)}, f32[4,6144]{1,0:T(4,128)S(1)}, u32[]{:S(2)}, u32[]{:S(2)}) collective-permute-start(f32[4,6144]{1,0:T(4,128)S(1)} %get-tuple-element.82), channel_id=1, source_target_pairs={{0,24},{8,0},{16,8},{24,16},{1,25},{9,1},{17,9},{25,17},{2,26},{10... | collective-permute-start | bytes 294920 | tf_op jit(solution)/shard_map/ppermute | solution.py:285
  69.8 5.5 %collective-permute-start.8 = (f32[4,6144]{1,0:T(4,128)S(1)}, f32[4,6144]{1,0:T(4,128)S(1)}, u32[]{:S(2)}, u32[]{:S(2)}) collective-permute-start(f32[4,6144]{1,0:T(4,128)S(1)} %get-tuple-element.83), channel_id=1, source_target_pairs={{0,8},{8,16},{16,24},{24,0},{1,9},{9,17},{17,25},{25,1},{2,10},{10... | collective-permute-start | bytes 294920 | tf_op jit(solution)/shard_map/ppermute | solution.py:285
  76.0 5.0 %collective-permute-start.10 = (bf16[256,256]{1,0:T(8,128)(2,1)S(1)}, bf16[256,256]{1,0:T(8,128)(2,1)S(1)}, u32[]{:S(2)}, u32[]{:S(2)}) collective-permute-start(bf16[256,256]{1,0:T(8,128)(2,1)S(1)} %pad_maximum_fusion.1), channel_id=1, source_target_pairs={{0,2},{1,3},{2,0},{3,1},{4,6},{5,7},{6,4},{7,5},{8,10},{9,11},{10,... | collective-permute-start | bytes 393224 | tf_op jit(solution)/shard_map/ppermute | solution.py:79
  81.7 2.4 %collective-permute-start.11 = (f32[768,256]{1,0:T(8,128)S(1)}, f32[768,256]{1,0:T(8,128)S(1)}, u32[]{:S(2)}, u32[]{:S(2)}) collective-permute-start(f32[768,256]{1,0:T(8,128)S(1)} %get-tuple-element.73), channel_id=1, source_target_pairs={{0,1},{1,0},{2,3},{3,2},{4,5},{5,4},{6,7},{7,6},{8,9},{9,8},{10,11... | collective-permute-start | bytes 2359304 | tf_op jit(solution)/shard_map/ppermute | solution.py:79

commit v7 on v6

--- a/solution.py
+++ b/solution.py
@@ -14,11 +14,9 @@
 F32 = jnp.float32
 BF16 = jnp.bfloat16
 VMEM_LIMIT = 48 * 1024 * 1024
-PARTS = 2
-COST = pl.CostEstimate(flops=1, bytes_accessed=1, transcendentals=0)
-PARTS = 2
 COST = pl.CostEstimate(flops=1, bytes_accessed=1, transcendentals=0)
 COST = pl.CostEstimate(flops=1, bytes_accessed=1, transcendentals=0)
+COST = pl.CostEstimate(flops=1, bytes_accessed=1, transcendentals=0)
 
 
 def dot_nt(a, b):
@@ -31,6 +29,63 @@
 
 def vmem_specs(count):
     return [pl.BlockSpec(memory_space=pltpu.VMEM)] * count
+
+
+def local_call(kernel, outs, *args):
+    return pl.pallas_call(
+        kernel,
+        out_shape=outs,
+        in_specs=vmem_specs(len(args)),
+        out_specs=jax.tree.map(lambda _: pl.BlockSpec(memory_space=pltpu.VMEM), outs),
+        cost_estimate=COST,
+    )(*args)
+
+
+def join_kernel(axis, a_ref, b_ref, out_ref):
+    cut = a_ref.shape[axis]
+    if axis:
+        out_ref[:, :cut] = a_ref[...]
+        out_ref[:, cut:] = b_ref[...]
+    else:
+        out_ref[:cut] = a_ref[...]
+        out_ref[cut:] = b_ref[...]
+
+
+def join(a, b, axis=0):
+    shape = list(a.shape)
+    shape[axis] += b.shape[axis]
+    out = jax.ShapeDtypeStruct(shape, a.dtype)
+    return local_call(functools.partial(join_kernel, axis), out, a, b)
+
+
+def add_kernel(kept_ref, arrived_ref, stay_ref, sent_ref):
+    total = kept_ref[...] + arrived_ref[...].astype(F32)
+    rows = total.shape[0] - sent_ref.shape[0]
+    stay_ref[...] = total[: stay_ref.shape[0]]
+    sent_ref[...] = total[rows:].astype(BF16)
+
+
+def add_split(kept, arrived, stay, sent):
+    cols = kept.shape[1]
+    outs = [jax.ShapeDtypeStruct((stay, cols), F32), jax.ShapeDtypeStruct((sent, cols), BF16)]
+    return local_call(add_kernel, outs, kept, arrived)
+
+
+def merge_kernel(upper_ref, here_ref, there_ref, own_ref, both_ref):
+    rows = own_ref.shape[0]
+    upper = upper_ref[...] > 0.5
+    there = there_ref[...].astype(F32)
+    own = jnp.where(upper, here_ref[:rows], here_ref[:rows] + there[rows:])
+    other = jnp.where(upper, here_ref[rows:] + there[:rows], there[:rows])
+    own_ref[...] = own
+    both_ref[:rows] = own.astype(BF16)
+    both_ref[rows:] = other.astype(BF16)
+
+
+def merge(upper, here, there):
+    rows, cols = here.shape
+    outs = [jax.ShapeDtypeStruct((rows // 2, cols), F32), jax.ShapeDtypeStruct(here.shape, BF16)]
+    return local_call(merge_kernel, outs, jnp.full((1, cols), upper, F32), here, there)
 
 
 def delta_kernel(head_dim, grad_ref, out_ref, delta_ref):
@@ -171,7 +226,7 @@
     half = near.shape[0]
     order = gather_order(2 * half // tok)
     group = next(g for g in (4, 3, 2, 1) if heads % g == 0)
-    join = 2 if half % (2 * tok) == 0 else 1
+    join = next(j for j in (4, 2, 1) if half % (j * tok) == 0)
     return pl.pallas_call(
         functools.partial(attention_kernel, order, group, join, hd ** (-0.5)),
         out_shape=[
@@ -233,13 +288,6 @@
     )(me[None], blocks, grads)
 
 
-def contrib_part(both, weight, index, parts):
-    cols = weight.shape[1] // parts
-    some = weight[:, index * cols : (index + 1) * cols]
-    part = jnp.dot(both, some, preferred_element_type=F32)
-    return part.reshape(2, both.shape[0] // 2, cols)
-
-
 def orthonormal(rows):
     columns = []
     for source in rows:
@@ -296,16 +344,21 @@
     factor = initial_right_factor[0]
     weight = mlp_weight[0]
 
-    near = jnp.concatenate([keys[0], values[0]], axis=-1)
+    near = join(keys[0], values[0], axis=1)
     chips = count // 2
-    beside = [pack(inputs[0], chips), head_delta(out_grad[0], outputs[0], heads), factor]
-    for index, bit in enumerate(bits):
-        if bit == 1:
-            break
+    packed = pack(inputs[0], chips)
+    for index, bit in enumerate(bits[:-1]):
         far = swap(near, "seq", bit, True if index == 0 else None)
-        near, far, beside = lax.optimization_barrier((near, far, beside))
-        near = jnp.concatenate([near, far], axis=0)
-    packed, delta, factor = beside
+        if index == 1:
+            delta = head_delta(grad_rows, out_rows, heads)
+            near, far, delta, packed, factor = lax.optimization_barrier(
+                (near, far, delta, packed, factor)
+            )
+        else:
+            near, far, packed, grad_rows, out_rows = lax.optimization_barrier(
+                (near, far, packed, out_grad[0], outputs[0])
+            )
+        near = join(near, far)
     blocks = lax.all_to_all(
         packed,
         "seq",
@@ -323,39 +376,26 @@
     query_grad, grads, sent = attend(me, queries[0], out_grad[0], log_norm[0], delta, near, far)
     lower_acts, higher_acts, sent = lax.optimization_barrier((lower_acts, higher_acts, sent))
 
+    last = bits[0]
+    upper = (me & last) != 0
+    arrived = swap(sent, "seq", 1)
     basis, both = make_basis(acts, lower_acts, higher_acts)
-    contrib_parts = []
-    last = bits[0]
-    for index, bit in enumerate(b for b in reversed(bits) if b != last):
+    contrib = jnp.dot(both, weight, preferred_element_type=F32)
+    arrived, contrib, blocks = lax.optimization_barrier((arrived, contrib, blocks))
+    contrib = contrib.reshape(2, contrib.shape[0] // 2, contrib.shape[1])
+    lower_half = from_cycle(contrib[1], "rep", 1)
+    for bit in reversed(bits[1:-1]):
+        keep = grads.shape[0] // 2
+        grads, sent = add_split(grads, arrived, keep, keep)
         arrived = swap(sent, "seq", bit)
-        share = PARTS - index if bit * 2 == last else 1
-        if index < PARTS:
-            contrib_parts += [
-                contrib_part(both, weight, index + i, PARTS) for i in range(share)
-            ]
-        both, grads, arrived, contrib_parts = lax.optimization_barrier(
-            (both, grads, arrived, contrib_parts)
-        )
-        grads = grads + arrived.astype(F32)
-        keep = grads.shape[0] // 2
-        if bit * 2 < last:
-            sent = grads[keep:].astype(BF16)
-            grads = grads[:keep]
-    blocks, grads = lax.optimization_barrier((blocks, grads))
-    contrib = jnp.concatenate(contrib_parts, axis=2)
-    lower_half = from_cycle(contrib[1], "rep", 1)
+    arrived, lower_half = lax.optimization_barrier((arrived, lower_half))
     higher_half = from_cycle(contrib[0], "rep", -1)
 
-    upper = (me & last) != 0
-    arrived = swap(grads.astype(BF16), "seq", last)
-    arrived, lower_half, higher_half = lax.optimization_barrier((arrived, lower_half, higher_half))
-    arrived = arrived.astype(F32)
-    mine, theirs = grads[:keep], grads[keep:]
-    own = jnp.where(upper, mine, mine + arrived[keep:])
-    other = jnp.where(upper, theirs + arrived[:keep], arrived[:keep])
-    near_b = jnp.concatenate([own, other], axis=0).astype(BF16)
+    grads, sent = add_split(grads, arrived, grads.shape[0], grads.shape[0])
+    arrived, higher_half = lax.optimization_barrier((swap(sent, "seq", last), higher_half))
+    own, near_b = merge(upper.astype(F32), grads, arrived)
     for bit in bits[1:-1]:
-        near_b = jnp.concatenate([near_b, swap(near_b, "seq", bit)], axis=0)
+        near_b = join(near_b, swap(near_b, "seq", bit))
     order = [x // 2 for x in gather_order(count)[: count // 2]]
     proj_mine, proj_theirs = project(me, blocks, near_b, order)
     proj_grad = proj_mine + swap(proj_theirs, "seq", 1)

time: 85.6 us -> 97.5 us (1.14)
  Pallas kernels: 16.3 us -> 28.2 us
  other arithmetic: 4.51 us -> 1.75 us
  starting transfers between devices: 22.1 us -> 24.8 us
  matrix products: 19 us -> 16.6 us
  local copies, waits for them, and re-layouts: 7.47 us -> 9.22 us
    pallas_call x0 -> x7, Pallas kernels: none -> 11.8 us  [local_call(): pl.pallas_call(kernel, out_shape=outs, in_specs=vmem_specs(len(args)), ou...]
    dot_general x2 -> x1, matrix products: 10 us -> 7.71 us  [on_device(): contrib = jnp.dot(both, weight, preferred_element_type=F32)]
    all_to_all x1, starting transfers between devices: 3.56 us -> 5.87 us  [on_device(): lax.all_to_all(packed, 'seq', split_axis=0, concat_axis=0, tiled=True, ax...]
    unnamed x29 -> x38, local copies, waits for them, and re-layouts: 6.42 us -> 8.6 us
    add x2 -> x0, other arithmetic: 1.14 us -> none  [on_device(): grads = grads + arrived.astype(F32)]
    ppermute x4, starting transfers between devices: 5.45 us -> 6.46 us  [from_cycle(): lax.ppermute(block, axis, [(i, (i + distance) % count) for i in range(cou...]
  transfers between devices with their start and end apart: 13 -> 13, of which waited for: 5 -> 6; matrix products, arithmetic and copies ran while one was open for 27% -> 18% of each run, Pallas kernels for 18% -> 18%
where the time goes in v7:
time: 97.5 us; the launch traced here: 96.9 us
  Pallas kernels  28.2 us (29%)
  starting transfers between devices  24.8 us (25%)
  matrix products  16.6 us (17%)
  waiting for transfers between devices  15.5 us (16%)
  local copies, waits for them, and re-layouts  9.22 us (9%)
  other arithmetic  1.75 us (2%)
    ppermute x8, starting transfers between devices, swap(): return lax.ppermute(block, axis, route)  12.5 us
    pallas_call x1, Pallas kernels, attend(): pl.pallas_call(functools.partial(attention_kernel, order, group, join, hd...  11.9 us
    pallas_call x7, Pallas kernels, local_call(): pl.pallas_call(kernel, out_shape=outs, in_specs=vmem_specs(len(args)), ou...  11.8 us
    ppermute x8, waiting for transfers between devices, swap(): return lax.ppermute(block, axis, route)  9.17 us
    dot_general x1, matrix products, dot_nt(): lax.dot_general(a, b, (((1,), (1,)), ((), ())), preferred_element_type=F32)  8.94 us
    unnamed x38, local copies, waits for them, and re-layouts  8.6 us
    dot_general x1, matrix products, on_device(): contrib = jnp.dot(both, weight, preferred_element_type=F32)  7.71 us
    ppermute x4, starting transfers between devices, from_cycle(): lax.ppermute(block, axis, [(i, (i + distance) % count) for i in range(cou...  6.46 us
  transfers between devices with their start and end apart: 13, of which 6 were waited for; matrix products, arithmetic and copies ran while one was open for 18% of the time, Pallas kernels for 18%

profile of v7, /device:TPU:0, one launch (start us, length us, event | category | flops | bytes accessed | tf_op | source)
XLA Modules:
  0.0 96.9 jit_solution(5032655690166173158)
XLA Ops:
  0.6 0.0 copy-start
  0.6 0.0 copy-start.2
  0.7 1.5 %shard_map.128.a_ref = bf16[128,256]{1,0:T(8,128)(2,1)} custom-call(bf16[128,128]{1,0:T(8,128)(2,1)} %bitcast.34, bf16[128,128]{1,0:T(8,128)(2,1)} %bitcast.35), custom_call_target="tpu_custom_call" | custom-call | flops 1 | bytes 1 | tf_op jit(solution)/shard_map/pallas_call | solution.py:35
  2.1 5.9 %collective-permute-start = (bf16[128,256]{1,0:T(8,128)(2,1)}, bf16[128,256]{1,0:T(8,128)(2,1)S(1)}, u32[]{:S(2)}, u32[]{:S(2)}) collective-permute-start(bf16[128,256]{1,0:T(8,128)(2,1)} %shard_map.128.a_ref), channel_id=1, source_target_pairs={{0,4},{1,5},{2,6},{3,7},{8,12},{9,13},{10,14},{11,15},{16,20},{17,... | collective-permute-start | bytes 196616 | tf_op jit(solution)/shard_map/ppermute | solution.py:134
  8.1 0.0 copy-start.3
  8.1 1.4 %copy-done.3 = bf16[1,128,6144]{2,1,0:T(8,128)(2,1)S(1)} copy-done((bf16[1,128,6144]{2,1,0:T(8,128)(2,1)S(1)}, bf16[1,128,6144]{2,1,0:T(8,128)(2,1)}, u32[]{:S(2)}) %copy-start.3) | copy-done | bytes 1572888
  9.5 1.3 %shard_map.129 = bf16[4,128,1536]{2,1,0:T(8,128)(2,1)} custom-call(bf16[128,6144]{1,0:T(8,128)(2,1)S(1)} %bitcast.30), custom_call_target="tpu_custom_call" | custom-call | flops 1 | bytes 1 | tf_op jit(solution)/shard_map/pallas_call | solution.py:257
  10.8 0.0 collective-permute-done.b_ref
  10.8 0.6 copy-done.16
  11.4 1.5 %shard_map.130.a_ref = bf16[256,256]{1,0:T(8,128)(2,1)} custom-call(bf16[128,256]{1,0:T(8,128)(2,1)} %shard_map.128.a_ref, bf16[128,256]{1,0:T(8,128)(2,1)} %copy-done.16), custom_call_target="tpu_custom_call" | custom-call | flops 1 | bytes 1 | tf_op jit(solution)/shard_map/pallas_call | solution.py:35
  13.0 1.8 %collective-permute-start.1 = (bf16[256,256]{1,0:T(8,128)(2,1)}, bf16[256,256]{1,0:T(8,128)(2,1)S(1)}, u32[]{:S(2)}, u32[]{:S(2)}) collective-permute-start(bf16[256,256]{1,0:T(8,128)(2,1)} %shard_map.130.a_ref), channel_id=1, source_target_pairs={{0,2},{1,3},{2,0},{3,1},{4,6},{5,7},{6,4},{7,5},{8,10},{9,11},{10,... | collective-permute-start | bytes 393224 | tf_op jit(solution)/shard_map/ppermute | solution.py:134
  14.8 1.1 %copy-done.1 = bf16[1,128,3072]{2,1,0:T(8,128)(2,1)S(1)} copy-done((bf16[1,128,3072]{2,1,0:T(8,128)(2,1)S(1)}, bf16[1,128,3072]{2,1,0:T(8,128)(2,1)}, u32[]{:S(2)}) %copy-start.1) | copy-done | bytes 786456
  15.9 1.1 %copy-done.6 = bf16[1,128,3072]{2,1,0:T(8,128)(2,1)S(1)} copy-done((bf16[1,128,3072]{2,1,0:T(8,128)(2,1)S(1)}, bf16[1,128,3072]{2,1,0:T(8,128)(2,1)}, u32[]{:S(2)}) %copy-start.6) | copy-done | bytes 786456
  17.0 0.5 shard_map.131.delta_ref
  17.5 0.6 collective-permute-done.1.b_ref
  18.2 0.0 copy-done
  18.2 5.9 %all-to-all-start = ((bf16[4,128,1536]{2,1,0:T(8,128)(2,1)}), bf16[4,128,1536]{2,1,0:T(8,128)(2,1)S(1)}, u32[]{:S(2)}, u32[]{:S(2)}) async-start(bf16[4,128,1536]{2,1,0:T(8,128)(2,1)} %shard_map.129), calls=%async_computation | async-start | bytes 3145728 | tf_op jit(solution)/shard_map/all_to_all | solution.py:362
  24.0 0.0 copy-done.13
  24.0 1.7 %shard_map.132.near_ref = bf16[512,256]{1,0:T(8,128)(2,1)} custom-call(bf16[256,256]{1,0:T(8,128)(2,1)} %shard_map.130.a_ref, bf16[256,256]{1,0:T(8,128)(2,1)} %copy-done.13), custom_call_target="tpu_custom_call" | custom-call | flops 1 | bytes 1 | tf_op jit(solution)/shard_map/pallas_call | solution.py:35
  25.7 0.0 collective-permute-start.2
  25.7 8.9 %fusion.2.acts_ref = f32[4,1536]{1,0:T(4,128)S(1)} fusion(bf16[4,6144]{1,0:T(4,128)(2,1)S(1)} %bitcast.27, bf16[1,1536,6144]{2,1,0:T(8,128)(2,1)} %param.16), kind=kOutput, calls=%fused_computation.2 | convolution fusion | flops 75497472 | bytes 18948096 | tf_op jit(solution)/shard_map/dot_general | solution.py:23
  34.7 0.0 collective-permute-done.2.far_ref
  34.7 2.5 %collective-permute-start.4 = (f32[4,1536]{1,0:T(4,128)S(1)}, f32[4,1536]{1,0:T(4,128)S(1)}, u32[]{:S(2)}, u32[]{:S(2)}) collective-permute-start(f32[4,1536]{1,0:T(4,128)S(1)} %fusion.2.acts_ref), channel_id=1, source_target_pairs={{0,24},{8,0},{16,8},{24,16},{1,25},{9,1},{17,9},{25,17},{2,26},{10... | collective-permute-start | bytes 73736 | tf_op jit(solution)/shard_map/ppermute | solution.py:333
  37.2 0.0 collective-permute-start.3
  37.2 0.0 copy-done.2
  37.2 0.0 copy-done.7
  37.2 11.9 %shard_map.133 = (f32[128,3072]{1,0:T(8,128)}, f32[512,256]{1,0:T(8,128)S(1)}, f32[512,256]{1,0:T(8,128)}) custom-call(s32[1]{0:T(128)} %bitcast.me_ref, bf16[128,3072]{1,0:T(8,128)(2,1)S(1)} %bitcast.32, bf16[128,3072]{1,0:T(8,128)(2,1)S(1)} %bitcast.29, f32[24,128]{1,0:T(8,128)S(1)} %bitcast.33, f32[24,128]{1,0:T(8,128)S(1)} %shard_map.131.delta_ref, ...), custom_call_target="tpu_custom_call" | custom-call | flops 1 | bytes 1 | tf_op jit(solution)/shard_map/pallas_call | solution.py:230
  49.1 0.8 copy-done.8
  49.9 0.0 collective-permute-done.4.higher_ref
  50.0 0.0 collective-permute-done.3.lower_ref
  50.0 0.0 copy-start.18
  50.0 0.3 collective-permute-start.5
  50.2 0.3 copy-done.17
  50.6 0.0 copy-done.18
  50.6 2.1 %shard_map.134 = (f32[2,4,1536]{2,1,0:T(4,128)}, bf16[8,1536]{1,0:T(8,128)(2,1)}) custom-call(f32[4,1536]{1,0:T(4,128)} %copy-done.15, f32[4,1536]{1,0:T(4,128)} %copy-done.18, f32[4,1536]{1,0:T(4,128)} %copy-done.17), custom_call_target="tpu_custom_call" | custom-call | flops 1 | bytes 1 | tf_op jit(solution)/shard_map/pallas_call | solution.py:319
  52.7 7.7 %fusion = f32[8,6144]{1,0:T(8,128)S(1)} fusion(bf16[8,1536]{1,0:T(8,128)(2,1)} %get-tuple-element.59, bf16[1,1536,6144]{2,1,0:T(8,128)(2,1)} %param.16), kind=kOutput, calls=%fused_computation | convolution fusion | flops 150994944 | bytes 19095552 | tf_op jit(solution)/shard_map/dot_general | solution.py:383
  60.4 0.0 collective-permute-done.5.arrived_ref
  60.4 0.0 all-to-all-done.x_ref
  60.4 0.8 copy-done.10
  61.2 2.0 %shard_map.135 = (f32[256,256]{1,0:T(8,128)}, bf16[256,256]{1,0:T(8,128)(2,1)}) custom-call(f32[512,256]{1,0:T(8,128)} %copy-done.8, f32[512,256]{1,0:T(8,128)} %copy-done.10), custom_call_target="tpu_custom_call" | custom-call | flops 1 | bytes 1 | tf_op jit(solution)/shard_map/pallas_call | solution.py:35
  63.1 2.0 %collective-permute-start.6 = (bf16[256,256]{1,0:T(8,128)(2,1)}, bf16[256,256]{1,0:T(8,128)(2,1)S(1)}, u32[]{:S(2)}, u32[]{:S(2)}) collective-permute-start(bf16[256,256]{1,0:T(8,128)(2,1)} %get-tuple-element.63), channel_id=1, source_target_pairs={{0,2},{1,3},{2,0},{3,1},{4,6},{5,7},{6,4},{7,5},{8,10},{9,11},{10,... | collective-permute-start | bytes 393224 | tf_op jit(solution)/shard_map/ppermute | solution.py:134
  65.2 2.0 %collective-permute-start.7 = (f32[4,6144]{1,0:T(4,128)S(1)}, f32[4,6144]{1,0:T(4,128)S(1)}, u32[]{:S(2)}, u32[]{:S(2)}) collective-permute-start(f32[4,6144]{1,0:T(4,128)S(1)} %get-tuple-element.80), channel_id=1, source_target_pairs={{0,8},{8,16},{16,24},{24,0},{1,9},{9,17},{17,25},{25,1},{2,10},{10... | collective-permute-start | bytes 294920 | tf_op jit(solution)/shard_map/ppermute | solution.py:333
  67.2 3.6 %collective-permute-done.7 = f32[4,6144]{1,0:T(4,128)S(1)} collective-permute-done((f32[4,6144]{1,0:T(4,128)S(1)}, f32[4,6144]{1,0:T(4,128)S(1)}, u32[]{:S(2)}, u32[]{:S(2)}) %collective-permute-start.7) | collective-permute-done | bytes 98336 | tf_op jit(solution)/shard_map/ppermute | solution.py:333
  70.8 0.0 collective-permute-done.6.arrived_ref
  70.8 0.7 copy-done.12
  71.5 1.8 %shard_map.136 = (f32[256,256]{1,0:T(8,128)}, bf16[256,256]{1,0:T(8,128)(2,1)}) custom-call(f32[256,256]{1,0:T(8,128)} %get-tuple-element.62.kept_ref, bf16[256,256]{1,0:T(8,128)(2,1)} %copy-done.12), custom_call_target="tpu_custom_call" | custom-call | flops 1 | bytes 1 | tf_op jit(solution)/shard_map/pallas_call | solution.py:35
  73.2 2.4 %collective-permute-start.8 = (bf16[256,256]{1,0:T(8,128)(2,1)}, bf16[256,256]{1,0:T(8,128)(2,1)S(1)}, u32[]{:S(2)}, u32[]{:S(2)}) collective-permute-start(bf16[256,256]{1,0:T(8,128)(2,1)} %get-tuple-element.67), channel_id=1, source_target_pairs={{0,4},{1,5},{2,6},{3,7},{4,0},{5,1},{6,2},{7,3},{8,12},{9,13},{10,... | collective-permute-start | bytes 393224 | tf_op jit(solution)/shard_map/ppermute | solution.py:134
  75.6 2.0 %collective-permute-start.9 = (f32[4,6144]{1,0:T(4,128)S(1)}, f32[4,6144]{1,0:T(4,128)S(1)}, u32[]{:S(2)}, u32[]{:S(2)}) collective-permute-start(f32[4,6144]{1,0:T(4,128)S(1)} %get-tuple-element.79), channel_id=1, source_target_pairs={{0,24},{8,0},{16,8},{24,16},{1,25},{9,1},{17,9},{25,17},{2,26},{10... | collective-permute-start | bytes 294920 | tf_op jit(solution)/shard_map/ppermute | solution.py:333
  77.5 2.7 %collective-permute-done.9 = f32[4,6144]{1,0:T(4,128)S(1)} collective-permute-done((f32[4,6144]{1,0:T(4,128)S(1)}, f32[4,6144]{1,0:T(4,128)S(1)}, u32[]{:S(2)}, u32[]{:S(2)}) %collective-permute-start.9) | collective-permute-done | bytes 98336 | tf_op jit(solution)/shard_map/ppermute | solution.py:333
  80.2 1.5 %collective-permute-done.8.there_ref = bf16[256,256]{1,0:T(8,128)(2,1)S(1)} collective-permute-done((bf16[256,256]{1,0:T(8,128)(2,1)}, bf16[256,256]{1,0:T(8,128)(2,1)S(1)}, u32[]{:S(2)}, u32[]{:S(2)}) %collective-permute-start.8) | collective-permute-done | bytes 131104 | tf_op jit(solution)/shard_map/ppermute | solution.py:134
  81.7 0.6 broadcast_in_dim.24.upper_ref
  82.3 0.1 copy-done.11
  82.3 1.7 %shard_map.137 = (f32[128,256]{1,0:T(8,128)}, bf16[256,256]{1,0:T(8,128)(2,1)}) custom-call(f32[1,256]{1,0:T(1,128)} %broadcast_in_dim.24.upper_ref, f32[256,256]{1,0:T(8,128)} %get-tuple-element.66.here_ref, bf16[256,256]{1,0:T(8,128)(2,1)} %copy-done.11), custom_call_target="tpu_custom_call" | custom-call | flops 1 | bytes 1 | tf_op jit(solution)/shard_map/pallas_call | solution.py:35
  84.0 0.0 collective-permute-start.10
  84.0 5.6 %collective-permute-done.10.b_ref = bf16[256,256]{1,0:T(8,128)(2,1)S(1)} collective-permute-done((bf16[256,256]{1,0:T(8,128)(2,1)}, bf16[256,256]{1,0:T(8,128)(2,1)S(1)}, u32[]{:S(2)}, u32[]{:S(2)}) %collective-permute-start.10) | collective-permute-done | bytes 131104 | tf_op jit(solution)/shard_map/ppermute | solution.py:134
  89.6 0.7 copy-done.14
  90.2 1.7 %shard_map.138.grads_ref = bf16[512,256]{1,0:T(8,128)(2,1)} custom-call(bf16[256,256]{1,0:T(8,128)(2,1)} %get-tuple-element.71.a_ref, bf16[256,256]{1,0:T(8,128)(2,1)} %copy-done.14), custom_call_target="tpu_custom_call" | custom-call | flops 1 | bytes 1 | tf_op jit(solution)/shard_map/pallas_call | solution.py:35
  91.9 0.9 copy-done.5
  92.9 0.6 shard_map.139
  93.5 0.1 collective-permute-start.11
  93.6 0.1 add_bitcast_fusion.2
  93.7 0.7 maximum_bitcast_fusion
  94.4 1.5 %collective-permute-done.11 = f32[768,256]{1,0:T(8,128)S(1)} collective-permute-done((f32[768,256]{1,0:T(8,128)S(1)}, f32[768,256]{1,0:T(8,128)S(1)}, u32[]{:S(2)}, u32[]{:S(2)}) %collective-permute-start.11) | collective-permute-done | bytes 786464 | tf_op jit(solution)/shard_map/ppermute | solution.py:134
  95.9 1.0 %add_bitcast_fusion = f32[1,768,256]{2,1,0:T(8,128)} fusion(f32[768,256]{1,0:T(8,128)S(1)} %get-tuple-element.72, f32[768,256]{1,0:T(8,128)S(1)} %collective-permute-done.11), kind=kLoop, calls=%fused_computation.4 | loop fusion | flops 196608 | bytes 2359296 | tf_op jit(solution)/shard_map/broadcast_in_dim | solution.py:406
  (19 shorter events, 0.1 us)
Async XLA Ops:
  0.6 17.5 %copy-start = (bf16[1,4,6144]{2,1,0:T(4,128)(2,1)S(1)}, bf16[1,4,6144]{2,1,0:T(4,128)(2,1)}, u32[]{:S(2)}) copy-start(bf16[1,4,6144]{2,1,0:T(4,128)(2,1)} %param.17) | copy-start | bytes 147460
  0.6 36.5 %copy-start.2 = (bf16[1,128,3072]{2,1,0:T(8,128)(2,1)S(1)}, bf16[1,128,3072]{2,1,0:T(8,128)(2,1)}, u32[]{:S(2)}) copy-start(bf16[1,128,3072]{2,1,0:T(8,128)(2,1)} %param.13) | copy-start | bytes 2359300
  2.1 8.6 %collective-permute-start = (bf16[128,256]{1,0:T(8,128)(2,1)}, bf16[128,256]{1,0:T(8,128)(2,1)S(1)}, u32[]{:S(2)}, u32[]{:S(2)}) collective-permute-start(bf16[128,256]{1,0:T(8,128)(2,1)} %shard_map.128.a_ref), channel_id=1, source_target_pairs={{0,4},{1,5},{2,6},{3,7},{8,12},{9,13},{10,14},{11,15},{16,20},{17,... | collective-permute-start | bytes 196616 | tf_op jit(solution)/shard_map/ppermute | solution.py:134
  8.1 1.4 %copy-start.3 = (bf16[1,128,6144]{2,1,0:T(8,128)(2,1)S(1)}, bf16[1,128,6144]{2,1,0:T(8,128)(2,1)}, u32[]{:S(2)}) copy-start(bf16[1,128,6144]{2,1,0:T(8,128)(2,1)} %param.15) | copy-start | bytes 4718596
  9.5 27.7 %copy-start.7 = (bf16[1,128,3072]{2,1,0:T(8,128)(2,1)S(1)}, bf16[1,128,3072]{2,1,0:T(8,128)(2,1)}, u32[]{:S(2)}) copy-start(bf16[1,128,3072]{2,1,0:T(8,128)(2,1)} %param.9) | copy-start | bytes 2359300
  9.5 27.7 %copy-start.9 = (f32[1,24,128]{2,1,0:T(8,128)S(1)}, f32[1,24,128]{2,1,0:T(8,128)}, u32[]{:S(2)}) copy-start(f32[1,24,128]{2,1,0:T(8,128)} %param.14) | copy-start | bytes 36868
  10.8 0.6 copy-start.16
  13.0 5.2 %collective-permute-start.1 = (bf16[256,256]{1,0:T(8,128)(2,1)}, bf16[256,256]{1,0:T(8,128)(2,1)S(1)}, u32[]{:S(2)}, u32[]{:S(2)}) collective-permute-start(bf16[256,256]{1,0:T(8,128)(2,1)} %shard_map.130.a_ref), channel_id=1, source_target_pairs={{0,2},{1,3},{2,0},{3,1},{4,6},{5,7},{6,4},{7,5},{8,10},{9,11},{10,... | collective-permute-start | bytes 393224 | tf_op jit(solution)/shard_map/ppermute | solution.py:134
  14.8 1.1 %copy-start.1 = (bf16[1,128,3072]{2,1,0:T(8,128)(2,1)S(1)}, bf16[1,128,3072]{2,1,0:T(8,128)(2,1)}, u32[]{:S(2)}) copy-start(bf16[1,128,3072]{2,1,0:T(8,128)(2,1)} %param.13) | copy-start | bytes 2359300
  15.9 1.1 %copy-start.6 = (bf16[1,128,3072]{2,1,0:T(8,128)(2,1)S(1)}, bf16[1,128,3072]{2,1,0:T(8,128)(2,1)}, u32[]{:S(2)}) copy-start(bf16[1,128,3072]{2,1,0:T(8,128)(2,1)} %param.12) | copy-start | bytes 2359300
  18.2 5.9 %copy-start.13 = (bf16[256,256]{1,0:T(8,128)(2,1)}, bf16[256,256]{1,0:T(8,128)(2,1)S(1)}, u32[]{:S(2)}) copy-start(bf16[256,256]{1,0:T(8,128)(2,1)S(1)} %collective-permute-done.1.b_ref) | copy-start | bytes 393220
  18.2 42.2 %all-to-all-start = ((bf16[4,128,1536]{2,1,0:T(8,128)(2,1)}), bf16[4,128,1536]{2,1,0:T(8,128)(2,1)S(1)}, u32[]{:S(2)}, u32[]{:S(2)}) async-start(bf16[4,128,1536]{2,1,0:T(8,128)(2,1)} %shard_map.129), calls=%async_computation | async-start | bytes 3145728 | tf_op jit(solution)/shard_map/all_to_all | solution.py:362
  25.7 11.5 %copy-start.4 = (bf16[512,256]{1,0:T(8,128)(2,1)S(1)}, bf16[512,256]{1,0:T(8,128)(2,1)}, u32[]{:S(2)}) copy-start(bf16[512,256]{1,0:T(8,128)(2,1)} %shard_map.132.near_ref) | copy-start | bytes 786436
  25.7 9.0 %collective-permute-start.2 = (bf16[512,256]{1,0:T(8,128)(2,1)}, bf16[512,256]{1,0:T(8,128)(2,1)}, u32[]{:S(2)}, u32[]{:S(2)}) collective-permute-start(bf16[512,256]{1,0:T(8,128)(2,1)} %shard_map.132.near_ref), channel_id=1, source_target_pairs={{0,1},{1,0},{2,3},{3,2},{4,5},{5,4},{6,7},{7,6},{8,9},{9,8},{10,11... | collective-permute-start | bytes 786440 | tf_op jit(solution)/shard_map/ppermute | solution.py:134
  34.7 15.6 %copy-start.15 = (f32[4,1536]{1,0:T(4,128)}, f32[4,1536]{1,0:T(4,128)S(1)}, u32[]{:S(2)}) copy-start(f32[4,1536]{1,0:T(4,128)S(1)} %fusion.2.acts_ref) | copy-start | bytes 73732
  34.7 15.3 %collective-permute-start.4 = (f32[4,1536]{1,0:T(4,128)S(1)}, f32[4,1536]{1,0:T(4,128)S(1)}, u32[]{:S(2)}, u32[]{:S(2)}) collective-permute-start(f32[4,1536]{1,0:T(4,128)S(1)} %fusion.2.acts_ref), channel_id=1, source_target_pairs={{0,24},{8,0},{16,8},{24,16},{1,25},{9,1},{17,9},{25,17},{2,26},{10... | collective-permute-start | bytes 73736 | tf_op jit(solution)/shard_map/ppermute | solution.py:333
  37.2 12.8 %collective-permute-start.3 = (f32[4,1536]{1,0:T(4,128)S(1)}, f32[4,1536]{1,0:T(4,128)S(1)}, u32[]{:S(2)}, u32[]{:S(2)}) collective-permute-start(f32[4,1536]{1,0:T(4,128)S(1)} %fusion.2.acts_ref), channel_id=1, source_target_pairs={{0,8},{8,16},{16,24},{24,0},{1,9},{9,17},{17,25},{25,1},{2,10},{10... | collective-permute-start | bytes 73736 | tf_op jit(solution)/shard_map/ppermute | solution.py:333
  49.1 0.8 copy-start.8
  50.0 0.6 copy-start.17
  50.0 0.6 copy-start.18
  50.0 10.4 %collective-permute-start.5 = (f32[512,256]{1,0:T(8,128)}, f32[512,256]{1,0:T(8,128)S(1)}, u32[]{:S(2)}, u32[]{:S(2)}) collective-permute-start(f32[512,256]{1,0:T(8,128)} %get-tuple-element.56), channel_id=1, source_target_pairs={{0,1},{1,0},{2,3},{3,2},{4,5},{5,4},{6,7},{7,6},{8,9},{9,8},{10,11... | collective-permute-start | bytes 1572872 | tf_op jit(solution)/shard_map/ppermute | solution.py:134
  60.4 0.8 copy-start.10
  63.1 7.7 %collective-permute-start.6 = (bf16[256,256]{1,0:T(8,128)(2,1)}, bf16[256,256]{1,0:T(8,128)(2,1)S(1)}, u32[]{:S(2)}, u32[]{:S(2)}) collective-permute-start(bf16[256,256]{1,0:T(8,128)(2,1)} %get-tuple-element.63), channel_id=1, source_target_pairs={{0,2},{1,3},{2,0},{3,1},{4,6},{5,7},{6,4},{7,5},{8,10},{9,11},{10,... | collective-permute-start | bytes 393224 | tf_op jit(solution)/shard_map/ppermute | solution.py:134
  65.2 5.6 %collective-permute-start.7 = (f32[4,6144]{1,0:T(4,128)S(1)}, f32[4,6144]{1,0:T(4,128)S(1)}, u32[]{:S(2)}, u32[]{:S(2)}) collective-permute-start(f32[4,6144]{1,0:T(4,128)S(1)} %get-tuple-element.80), channel_id=1, source_target_pairs={{0,8},{8,16},{16,24},{24,0},{1,9},{9,17},{17,25},{25,1},{2,10},{10... | collective-permute-start | bytes 294920 | tf_op jit(solution)/shard_map/ppermute | solution.py:333
  70.8 0.7 copy-start.12
  73.2 8.4 %collective-permute-start.8 = (bf16[256,256]{1,0:T(8,128)(2,1)}, bf16[256,256]{1,0:T(8,128)(2,1)S(1)}, u32[]{:S(2)}, u32[]{:S(2)}) collective-permute-start(bf16[256,256]{1,0:T(8,128)(2,1)} %get-tuple-element.67), channel_id=1, source_target_pairs={{0,4},{1,5},{2,6},{3,7},{4,0},{5,1},{6,2},{7,3},{8,12},{9,13},{10,... | collective-permute-start | bytes 393224 | tf_op jit(solution)/shard_map/ppermute | solution.py:134
  75.6 4.6 %collective-permute-start.9 = (f32[4,6144]{1,0:T(4,128)S(1)}, f32[4,6144]{1,0:T(4,128)S(1)}, u32[]{:S(2)}, u32[]{:S(2)}) collective-permute-start(f32[4,6144]{1,0:T(4,128)S(1)} %get-tuple-element.79), channel_id=1, source_target_pairs={{0,24},{8,0},{16,8},{24,16},{1,25},{9,1},{17,9},{25,17},{2,26},{10... | collective-permute-start | bytes 294920 | tf_op jit(solution)/shard_map/ppermute | solution.py:333
  81.7 0.7 copy-start.11
  84.0 5.6 %collective-permute-start.10 = (bf16[256,256]{1,0:T(8,128)(2,1)}, bf16[256,256]{1,0:T(8,128)(2,1)S(1)}, u32[]{:S(2)}, u32[]{:S(2)}) collective-permute-start(bf16[256,256]{1,0:T(8,128)(2,1)} %get-tuple-element.71.a_ref), channel_id=1, source_target_pairs={{0,2},{1,3},{2,0},{3,1},{4,6},{5,7},{6,4},{7,5},{8,10},{9,11},{10,... | collective-permute-start | bytes 393224 | tf_op jit(solution)/shard_map/ppermute | solution.py:134
  89.6 0.7 copy-start.14
  91.9 0.9 copy-start.5
  93.5 2.4 %collective-permute-start.11 = (f32[768,256]{1,0:T(8,128)S(1)}, f32[768,256]{1,0:T(8,128)S(1)}, u32[]{:S(2)}, u32[]{:S(2)}) collective-permute-start(f32[768,256]{1,0:T(8,128)S(1)} %get-tuple-element.73), channel_id=1, source_target_pairs={{0,1},{1,0},{2,3},{3,2},{4,5},{5,4},{6,7},{7,6},{8,9},{9,8},{10,11... | collective-permute-start | bytes 2359304 | tf_op jit(solution)/shard_map/ppermute | solution.py:134

commit v8 on v7

--- a/solution.py
+++ b/solution.py
@@ -13,7 +13,8 @@
 LOG2E = math.log2(math.e)
 F32 = jnp.float32
 BF16 = jnp.bfloat16
-VMEM_LIMIT = 48 * 1024 * 1024
+SMALL = pltpu.CompilerParams(vmem_limit_bytes=8 * 1024 * 1024)
+LARGE = pltpu.CompilerParams(vmem_limit_bytes=28 * 1024 * 1024)
 COST = pl.CostEstimate(flops=1, bytes_accessed=1, transcendentals=0)
 COST = pl.CostEstimate(flops=1, bytes_accessed=1, transcendentals=0)
 COST = pl.CostEstimate(flops=1, bytes_accessed=1, transcendentals=0)
@@ -37,6 +38,7 @@
         out_shape=outs,
         in_specs=vmem_specs(len(args)),
         out_specs=jax.tree.map(lambda _: pl.BlockSpec(memory_space=pltpu.VMEM), outs),
+        compiler_params=SMALL,
         cost_estimate=COST,
     )(*args)
 
@@ -71,9 +73,9 @@
     return local_call(add_kernel, outs, kept, arrived)
 
 
-def merge_kernel(upper_ref, here_ref, there_ref, own_ref, both_ref):
+def merge_kernel(bit, me_ref, here_ref, there_ref, own_ref, both_ref):
     rows = own_ref.shape[0]
-    upper = upper_ref[...] > 0.5
+    upper = (me_ref[0] & bit) != 0
     there = there_ref[...].astype(F32)
     own = jnp.where(upper, here_ref[:rows], here_ref[:rows] + there[rows:])
     other = jnp.where(upper, here_ref[rows:] + there[:rows], there[:rows])
@@ -82,10 +84,17 @@
     both_ref[rows:] = other.astype(BF16)
 
 
-def merge(upper, here, there):
+def merge(me, bit, here, there):
     rows, cols = here.shape
     outs = [jax.ShapeDtypeStruct((rows // 2, cols), F32), jax.ShapeDtypeStruct(here.shape, BF16)]
-    return local_call(merge_kernel, outs, jnp.full((1, cols), upper, F32), here, there)
+    return pl.pallas_call(
+        functools.partial(merge_kernel, bit),
+        out_shape=outs,
+        in_specs=[pl.BlockSpec(memory_space=pltpu.SMEM)] + vmem_specs(2),
+        out_specs=vmem_specs(2),
+        compiler_params=SMALL,
+        cost_estimate=COST,
+    )(me[None], here, there)
 
 
 def delta_kernel(head_dim, grad_ref, out_ref, delta_ref):
@@ -102,7 +111,7 @@
         out_shape=jax.ShapeDtypeStruct((heads, rows), F32),
         in_specs=vmem_specs(2),
         out_specs=pl.BlockSpec(memory_space=pltpu.VMEM),
-        compiler_params=pltpu.CompilerParams(vmem_limit_bytes=VMEM_LIMIT),
+        compiler_params=SMALL,
         cost_estimate=COST,
     )(out_grad, outputs)
 
@@ -241,7 +250,7 @@
             pltpu.VMEM((hd, half), BF16),
             pltpu.VMEM((hd, group * tok), F32),
         ],
-        compiler_params=pltpu.CompilerParams(vmem_limit_bytes=VMEM_LIMIT),
+        compiler_params=LARGE,
         cost_estimate=COST,
     )(me[None], queries, out_grad, norm, delta, near, far)
 
@@ -259,7 +268,7 @@
         out_shape=jax.ShapeDtypeStruct((chips, tok, cols // chips), inputs.dtype),
         in_specs=vmem_specs(1),
         out_specs=pl.BlockSpec(memory_space=pltpu.VMEM),
-        compiler_params=pltpu.CompilerParams(vmem_limit_bytes=VMEM_LIMIT),
+        compiler_params=SMALL,
         cost_estimate=COST,
     )(inputs)
 
@@ -283,7 +292,7 @@
         out_shape=[jax.ShapeDtypeStruct((width, grads.shape[1]), F32)] * 2,
         in_specs=[pl.BlockSpec(memory_space=pltpu.SMEM)] + vmem_specs(2),
         out_specs=vmem_specs(2),
-        compiler_params=pltpu.CompilerParams(vmem_limit_bytes=VMEM_LIMIT),
+        compiler_params=LARGE,
         cost_estimate=COST,
     )(me[None], blocks, grads)
 
@@ -324,6 +333,7 @@
         ],
         in_specs=vmem_specs(3),
         out_specs=vmem_specs(2),
+        compiler_params=SMALL,
         cost_estimate=COST,
     )(acts, lower, higher)
 
@@ -377,7 +387,6 @@
     lower_acts, higher_acts, sent = lax.optimization_barrier((lower_acts, higher_acts, sent))
 
     last = bits[0]
-    upper = (me & last) != 0
     arrived = swap(sent, "seq", 1)
     basis, both = make_basis(acts, lower_acts, higher_acts)
     contrib = jnp.dot(both, weight, preferred_element_type=F32)
@@ -388,12 +397,11 @@
         keep = grads.shape[0] // 2
         grads, sent = add_split(grads, arrived, keep, keep)
         arrived = swap(sent, "seq", bit)
-    arrived, lower_half = lax.optimization_barrier((arrived, lower_half))
     higher_half = from_cycle(contrib[0], "rep", -1)
 
     grads, sent = add_split(grads, arrived, grads.shape[0], grads.shape[0])
-    arrived, higher_half = lax.optimization_barrier((swap(sent, "seq", last), higher_half))
-    own, near_b = merge(upper.astype(F32), grads, arrived)
+    arrived = swap(sent, "seq", last)
+    own, near_b = merge(me, last, grads, arrived)
     for bit in bits[1:-1]:
         near_b = join(near_b, swap(near_b, "seq", bit))
     order = [x // 2 for x in gather_order(count)[: count // 2]]

time: 97.5 us -> 83.8 us (0.86)
  Pallas kernels: 28.2 us -> 16.5 us
    pallas_call x7 -> x6, Pallas kernels: 11.8 us -> 0.14 us  [local_call(): pl.pallas_call(kernel, out_shape=outs, in_specs=vmem_specs(len(args)), ou...]
    ppermute x4, waiting for transfers between devices: 6.29 us -> 2.49 us  [from_cycle(): lax.ppermute(block, axis, [(i, (i + distance) % count) for i in range(cou...]
    ppermute x8, waiting for transfers between devices: 9.17 us -> 11.6 us  [swap(): return lax.ppermute(block, axis, route)]
    unnamed x38 -> x30, local copies, waits for them, and re-layouts: 8.6 us -> 8.54 us
  transfers between devices with their start and end apart: 13 -> 13, of which waited for: 6 -> 7; matrix products, arithmetic and copies ran while one was open for 18% -> 21% of each run, Pallas kernels for 18% -> 19%
where the time goes in v8:
time: 83.8 us; the launch traced here: 83.2 us
  starting transfers between devices  24.5 us (29%)
  matrix products  16.6 us (20%)
  Pallas kernels  16.5 us (20%)
  waiting for transfers between devices  14.6 us (17%)
  local copies, waits for them, and re-layouts  8.57 us (10%)
  other arithmetic  1.76 us (2%)
    ppermute x8, starting transfers between devices, swap(): return lax.ppermute(block, axis, route)  13 us
    pallas_call x1, Pallas kernels, attend(): pl.pallas_call(functools.partial(attention_kernel, order, group, join, hd...  12 us
    ppermute x8, waiting for transfers between devices, swap(): return lax.ppermute(block, axis, route)  11.6 us
    dot_general x1, matrix products, dot_nt(): lax.dot_general(a, b, (((1,), (1,)), ((), ())), preferred_element_type=F32)  8.91 us
    unnamed x30, local copies, waits for them, and re-layouts  8.54 us
    dot_general x1, matrix products, on_device(): contrib = jnp.dot(both, weight, preferred_element_type=F32)  7.69 us
    ppermute x4, starting transfers between devices, from_cycle(): lax.ppermute(block, axis, [(i, (i + distance) % count) for i in range(cou...  5.75 us
    all_to_all x1, starting transfers between devices, on_device(): lax.all_to_all(packed, 'seq', split_axis=0, concat_axis=0, tiled=True, ax...  5.69 us
  transfers between devices with their start and end apart: 13, of which 7 were waited for; matrix products, arithmetic and copies ran while one was open for 21% of the time, Pallas kernels for 19%

profile of v8, /device:TPU:0, one launch (start us, length us, event | category | flops | bytes accessed | tf_op | source)
XLA Modules:
  0.0 83.2 jit_solution(14931859316348575339)
XLA Ops:
  0.6 0.0 copy-start
  0.6 0.0 copy-start.2
  0.7 0.0 copy-start.12
  0.7 0.8 copy-done.12
  1.5 0.0 copy-start.13
  1.5 0.8 copy-done.13
  2.3 5.9 %collective-permute-start = (bf16[128,256]{1,0:T(8,128)(2,1)S(1)}, bf16[128,256]{1,0:T(8,128)(2,1)S(1)}, u32[]{:S(2)}, u32[]{:S(2)}) collective-permute-start(bf16[128,256]{1,0:T(8,128)(2,1)S(1)} %shard_map.128.a_ref), channel_id=1, source_target_pairs={{0,4},{1,5},{2,6},{3,7},{8,12},{9,13},{10,14},{11,15},{16,20},{17,... | collective-permute-start | bytes 196616 | tf_op jit(solution)/shard_map/ppermute | solution.py:143
  8.2 0.0 copy-start.3
  8.2 1.4 %copy-done.3 = bf16[1,128,6144]{2,1,0:T(8,128)(2,1)S(1)} copy-done((bf16[1,128,6144]{2,1,0:T(8,128)(2,1)S(1)}, bf16[1,128,6144]{2,1,0:T(8,128)(2,1)}, u32[]{:S(2)}) %copy-start.3) | copy-done | bytes 1572888
  9.6 0.0 copy-start.5
  9.6 0.0 copy-start.14
  9.6 1.3 %shard_map.129 = bf16[4,128,1536]{2,1,0:T(8,128)(2,1)} custom-call(bf16[128,6144]{1,0:T(8,128)(2,1)S(1)} %bitcast.30), custom_call_target="tpu_custom_call" | custom-call | flops 1 | bytes 1 | tf_op jit(solution)/shard_map/pallas_call | solution.py:266
  10.9 0.0 collective-permute-done.b_ref
  10.9 0.0 copy-start.8
  10.9 1.6 %collective-permute-start.1 = (bf16[256,256]{1,0:T(8,128)(2,1)S(1)}, bf16[256,256]{1,0:T(8,128)(2,1)S(1)}, u32[]{:S(2)}, u32[]{:S(2)}) collective-permute-start(bf16[256,256]{1,0:T(8,128)(2,1)S(1)} %shard_map.130.a_ref), channel_id=1, source_target_pairs={{0,2},{1,3},{2,0},{3,1},{4,6},{5,7},{6,4},{7,5},{8,10},{9,11},{10,... | collective-permute-start | bytes 393224 | tf_op jit(solution)/shard_map/ppermute | solution.py:143
  12.6 0.0 copy-start.1
  12.6 1.1 %copy-done.1 = bf16[1,128,3072]{2,1,0:T(8,128)(2,1)S(1)} copy-done((bf16[1,128,3072]{2,1,0:T(8,128)(2,1)S(1)}, bf16[1,128,3072]{2,1,0:T(8,128)(2,1)}, u32[]{:S(2)}) %copy-start.1) | copy-done | bytes 786456
  13.7 0.0 copy-start.4
  13.7 1.1 %copy-done.4 = bf16[1,128,3072]{2,1,0:T(8,128)(2,1)S(1)} copy-done((bf16[1,128,3072]{2,1,0:T(8,128)(2,1)S(1)}, bf16[1,128,3072]{2,1,0:T(8,128)(2,1)}, u32[]{:S(2)}) %copy-start.4) | copy-done | bytes 786456
  14.8 0.5 shard_map.131.delta_ref
  15.3 0.6 collective-permute-done.1.b_ref
  16.0 0.0 copy-done
  16.0 0.0 copy-start.10
  16.0 0.0 copy-done.8
  16.0 0.7 copy-done.10
  16.6 5.7 %all-to-all-start = ((bf16[4,128,1536]{2,1,0:T(8,128)(2,1)}), bf16[4,128,1536]{2,1,0:T(8,128)(2,1)S(1)}, u32[]{:S(2)}, u32[]{:S(2)}) async-start(bf16[4,128,1536]{2,1,0:T(8,128)(2,1)} %shard_map.129), calls=%async_computation | async-start | bytes 3145728 | tf_op jit(solution)/shard_map/all_to_all | solution.py:372
  22.3 0.9 %copy-done.9 = bf16[256,256]{1,0:T(8,128)(2,1)S(1)} copy-done((bf16[256,256]{1,0:T(8,128)(2,1)S(1)}, bf16[256,256]{1,0:T(8,128)(2,1)}, u32[]{:S(2)}) %copy-start.9) | copy-done | bytes 131096
  23.2 0.9 %copy-done.11 = bf16[256,256]{1,0:T(8,128)(2,1)S(1)} copy-done((bf16[256,256]{1,0:T(8,128)(2,1)S(1)}, bf16[256,256]{1,0:T(8,128)(2,1)}, u32[]{:S(2)}) %copy-start.11) | copy-done | bytes 131096
  24.1 0.1 collective-permute-start.2
  24.2 8.9 %fusion.2.acts_ref = f32[4,1536]{1,0:T(4,128)S(1)} fusion(bf16[4,6144]{1,0:T(4,128)(2,1)S(1)} %bitcast.27, bf16[1,1536,6144]{2,1,0:T(8,128)(2,1)} %param.16), kind=kOutput, calls=%fused_computation.2 | convolution fusion | flops 75497472 | bytes 18948096 | tf_op jit(solution)/shard_map/dot_general | solution.py:24
  33.1 0.0 collective-permute-done.2.far_ref
  33.2 2.5 %collective-permute-start.4 = (f32[4,1536]{1,0:T(4,128)S(1)}, f32[4,1536]{1,0:T(4,128)S(1)}, u32[]{:S(2)}, u32[]{:S(2)}) collective-permute-start(f32[4,1536]{1,0:T(4,128)S(1)} %fusion.2.acts_ref), channel_id=1, source_target_pairs={{0,24},{8,0},{16,8},{24,16},{1,25},{9,1},{17,9},{25,17},{2,26},{10... | collective-permute-start | bytes 73736 | tf_op jit(solution)/shard_map/ppermute | solution.py:343
  35.7 0.0 collective-permute-start.3
  35.7 0.0 copy-done.2
  35.7 0.0 copy-done.5
  35.7 0.0 copy-done.14
  35.7 12.0 %shard_map.133 = (f32[128,3072]{1,0:T(8,128)}, f32[512,256]{1,0:T(8,128)S(1)}, f32[512,256]{1,0:T(8,128)S(1)}) custom-call(s32[1]{0:T(128)} %bitcast.me_ref, bf16[128,3072]{1,0:T(8,128)(2,1)S(1)} %bitcast.32, bf16[128,3072]{1,0:T(8,128)(2,1)S(1)} %bitcast.29, f32[24,128]{1,0:T(8,128)S(1)} %bitcast.35, f32[24,128]{1,0:T(8,128)S(1)} %shard_map.131.delta_ref, ...), custom_call_target="tpu_custom_call" | custom-call | flops 1 | bytes 1 | tf_op jit(solution)/shard_map/pallas_call | solution.py:239
  47.6 0.8 copy-done.6
  48.4 0.0 collective-permute-done.4.higher_ref
  48.4 0.0 collective-permute-done.3.lower_ref
  48.4 0.3 collective-permute-start.5
  48.7 1.3 %shard_map.134 = (f32[2,4,1536]{2,1,0:T(4,128)}, bf16[8,1536]{1,0:T(8,128)(2,1)S(1)}) custom-call(f32[4,1536]{1,0:T(4,128)S(1)} %fusion.2.acts_ref, f32[4,1536]{1,0:T(4,128)S(1)} %collective-permute-done.3.lower_ref, f32[4,1536]{1,0:T(4,128)S(1)} %collective-permute-done.4.higher_ref), custom_call_target="tpu_custom_call" | custom-call | flops 1 | bytes 1 | tf_op jit(solution)/shard_map/pallas_call | solution.py:328
  50.0 7.7 %fusion = f32[8,6144]{1,0:T(8,128)S(1)} fusion(bf16[8,1536]{1,0:T(8,128)(2,1)S(1)} %get-tuple-element.55, bf16[1,1536,6144]{2,1,0:T(8,128)(2,1)} %param.16), kind=kOutput, calls=%fused_computation | convolution fusion | flops 150994944 | bytes 19095552 | tf_op jit(solution)/shard_map/dot_general | solution.py:392
  57.7 0.0 collective-permute-done.5.arrived_ref
  57.7 0.5 all-to-all-done.x_ref
  58.2 0.0 copy-done.7
  58.2 0.1 shard_map.135
  58.3 1.6 %collective-permute-start.6 = (bf16[256,256]{1,0:T(8,128)(2,1)S(1)}, bf16[256,256]{1,0:T(8,128)(2,1)S(1)}, u32[]{:S(2)}, u32[]{:S(2)}) collective-permute-start(bf16[256,256]{1,0:T(8,128)(2,1)S(1)} %get-tuple-element.59), channel_id=1, source_target_pairs={{0,2},{1,3},{2,0},{3,1},{4,6},{5,7},{6,4},{7,5},{8,10},{9,11},{10,... | collective-permute-start | bytes 393224 | tf_op jit(solution)/shard_map/ppermute | solution.py:143
  59.9 4.0 %collective-permute-done.6.arrived_ref = bf16[256,256]{1,0:T(8,128)(2,1)S(1)} collective-permute-done((bf16[256,256]{1,0:T(8,128)(2,1)S(1)}, bf16[256,256]{1,0:T(8,128)(2,1)S(1)}, u32[]{:S(2)}, u32[]{:S(2)}) %collective-permute-start.6) | collective-permute-done | bytes 131104 | tf_op jit(solution)/shard_map/ppermute | solution.py:143
  63.9 2.7 %collective-permute-start.7 = (bf16[256,256]{1,0:T(8,128)(2,1)S(1)}, bf16[256,256]{1,0:T(8,128)(2,1)S(1)}, u32[]{:S(2)}, u32[]{:S(2)}) collective-permute-start(bf16[256,256]{1,0:T(8,128)(2,1)S(1)} %get-tuple-element.61), channel_id=1, source_target_pairs={{0,4},{1,5},{2,6},{3,7},{4,0},{5,1},{6,2},{7,3},{8,12},{9,13},{10,... | collective-permute-start | bytes 393224 | tf_op jit(solution)/shard_map/ppermute | solution.py:143
  66.6 6.0 %collective-permute-done.7.there_ref = bf16[256,256]{1,0:T(8,128)(2,1)S(1)} collective-permute-done((bf16[256,256]{1,0:T(8,128)(2,1)S(1)}, bf16[256,256]{1,0:T(8,128)(2,1)S(1)}, u32[]{:S(2)}, u32[]{:S(2)}) %collective-permute-start.7) | collective-permute-done | bytes 131104 | tf_op jit(solution)/shard_map/ppermute | solution.py:143
  72.6 0.7 shard_map.137
  73.2 0.7 collective-permute-start.8
  74.0 2.2 %collective-permute-start.10 = (f32[4,6144]{1,0:T(4,128)S(1)}, f32[4,6144]{1,0:T(4,128)S(1)}, u32[]{:S(2)}, u32[]{:S(2)}) collective-permute-start(f32[4,6144]{1,0:T(4,128)S(1)} %get-tuple-element.71), channel_id=1, source_target_pairs={{0,8},{8,16},{16,24},{24,0},{1,9},{9,17},{17,25},{25,1},{2,10},{10... | collective-permute-start | bytes 294920 | tf_op jit(solution)/shard_map/ppermute | solution.py:343
  76.2 1.0 %collective-permute-start.11 = (f32[4,6144]{1,0:T(4,128)S(1)}, f32[4,6144]{1,0:T(4,128)S(1)}, u32[]{:S(2)}, u32[]{:S(2)}) collective-permute-start(f32[4,6144]{1,0:T(4,128)S(1)} %get-tuple-element.72), channel_id=1, source_target_pairs={{0,24},{8,0},{16,8},{24,16},{1,25},{9,1},{17,9},{25,17},{2,26},{10... | collective-permute-start | bytes 294920 | tf_op jit(solution)/shard_map/ppermute | solution.py:343
  77.2 1.0 %collective-permute-done.8.b_ref = bf16[256,256]{1,0:T(8,128)(2,1)S(1)} collective-permute-done((bf16[256,256]{1,0:T(8,128)(2,1)S(1)}, bf16[256,256]{1,0:T(8,128)(2,1)S(1)}, u32[]{:S(2)}, u32[]{:S(2)}) %collective-permute-start.8) | collective-permute-done | bytes 131104 | tf_op jit(solution)/shard_map/ppermute | solution.py:143
  78.2 0.6 shard_map.139
  78.9 0.1 collective-permute-start.9
  78.9 1.6 %collective-permute-done.10 = f32[4,6144]{1,0:T(4,128)S(1)} collective-permute-done((f32[4,6144]{1,0:T(4,128)S(1)}, f32[4,6144]{1,0:T(4,128)S(1)}, u32[]{:S(2)}, u32[]{:S(2)}) %collective-permute-start.10) | collective-permute-done | bytes 98336 | tf_op jit(solution)/shard_map/ppermute | solution.py:343
  80.6 0.8 %collective-permute-done.11 = f32[4,6144]{1,0:T(4,128)S(1)} collective-permute-done((f32[4,6144]{1,0:T(4,128)S(1)}, f32[4,6144]{1,0:T(4,128)S(1)}, u32[]{:S(2)}, u32[]{:S(2)}) %collective-permute-start.11) | collective-permute-done | bytes 98336 | tf_op jit(solution)/shard_map/ppermute | solution.py:343
  81.4 0.1 add_bitcast_fusion.2
  81.5 0.7 maximum_bitcast_fusion
  82.2 0.0 collective-permute-done.9
  82.2 1.0 %add_bitcast_fusion = f32[1,768,256]{2,1,0:T(8,128)} fusion(f32[768,256]{1,0:T(8,128)S(1)} %get-tuple-element.65, f32[768,256]{1,0:T(8,128)S(1)} %collective-permute-done.9), kind=kLoop, calls=%fused_computation.4 | loop fusion | flops 196608 | bytes 2359296 | tf_op jit(solution)/shard_map/broadcast_in_dim | solution.py:414
  (10 shorter events, 0.1 us)
Async XLA Ops:
  0.6 15.3 %copy-start = (bf16[1,4,6144]{2,1,0:T(4,128)(2,1)S(1)}, bf16[1,4,6144]{2,1,0:T(4,128)(2,1)}, u32[]{:S(2)}) copy-start(bf16[1,4,6144]{2,1,0:T(4,128)(2,1)} %param.17) | copy-start | bytes 147460
  0.6 35.0 %copy-start.2 = (bf16[1,128,3072]{2,1,0:T(8,128)(2,1)S(1)}, bf16[1,128,3072]{2,1,0:T(8,128)(2,1)}, u32[]{:S(2)}) copy-start(bf16[1,128,3072]{2,1,0:T(8,128)(2,1)} %param.13) | copy-start | bytes 2359300
  0.7 0.8 %copy-start.12 = (bf16[1,128,128]{2,1,0:T(8,128)(2,1)S(1)}, bf16[1,128,128]{2,1,0:T(8,128)(2,1)}, u32[]{:S(2)}) copy-start(bf16[1,128,128]{2,1,0:T(8,128)(2,1)} %param.10) | copy-start | bytes 98308
  1.5 0.8 copy-start.13
  2.3 8.6 %collective-permute-start = (bf16[128,256]{1,0:T(8,128)(2,1)S(1)}, bf16[128,256]{1,0:T(8,128)(2,1)S(1)}, u32[]{:S(2)}, u32[]{:S(2)}) collective-permute-start(bf16[128,256]{1,0:T(8,128)(2,1)S(1)} %shard_map.128.a_ref), channel_id=1, source_target_pairs={{0,4},{1,5},{2,6},{3,7},{8,12},{9,13},{10,14},{11,15},{16,20},{17,... | collective-permute-start | bytes 196616 | tf_op jit(solution)/shard_map/ppermute | solution.py:143
  8.2 1.4 %copy-start.3 = (bf16[1,128,6144]{2,1,0:T(8,128)(2,1)S(1)}, bf16[1,128,6144]{2,1,0:T(8,128)(2,1)}, u32[]{:S(2)}) copy-start(bf16[1,128,6144]{2,1,0:T(8,128)(2,1)} %param.15) | copy-start | bytes 4718596
  9.6 26.0 %copy-start.5 = (bf16[1,128,3072]{2,1,0:T(8,128)(2,1)S(1)}, bf16[1,128,3072]{2,1,0:T(8,128)(2,1)}, u32[]{:S(2)}) copy-start(bf16[1,128,3072]{2,1,0:T(8,128)(2,1)} %param.9) | copy-start | bytes 2359300
  9.6 26.0 %copy-start.14 = (f32[1,24,128]{2,1,0:T(8,128)S(1)}, f32[1,24,128]{2,1,0:T(8,128)}, u32[]{:S(2)}) copy-start(f32[1,24,128]{2,1,0:T(8,128)} %param.14) | copy-start | bytes 36868
  10.9 5.1 %copy-start.8 = (bf16[256,256]{1,0:T(8,128)(2,1)}, bf16[256,256]{1,0:T(8,128)(2,1)S(1)}, u32[]{:S(2)}) copy-start(bf16[256,256]{1,0:T(8,128)(2,1)S(1)} %shard_map.130.a_ref) | copy-start | bytes 393220
  10.9 5.0 %collective-permute-start.1 = (bf16[256,256]{1,0:T(8,128)(2,1)S(1)}, bf16[256,256]{1,0:T(8,128)(2,1)S(1)}, u32[]{:S(2)}, u32[]{:S(2)}) collective-permute-start(bf16[256,256]{1,0:T(8,128)(2,1)S(1)} %shard_map.130.a_ref), channel_id=1, source_target_pairs={{0,2},{1,3},{2,0},{3,1},{4,6},{5,7},{6,4},{7,5},{8,10},{9,11},{10,... | collective-permute-start | bytes 393224 | tf_op jit(solution)/shard_map/ppermute | solution.py:143
  12.6 1.1 %copy-start.1 = (bf16[1,128,3072]{2,1,0:T(8,128)(2,1)S(1)}, bf16[1,128,3072]{2,1,0:T(8,128)(2,1)}, u32[]{:S(2)}) copy-start(bf16[1,128,3072]{2,1,0:T(8,128)(2,1)} %param.13) | copy-start | bytes 2359300
  13.7 1.1 %copy-start.4 = (bf16[1,128,3072]{2,1,0:T(8,128)(2,1)S(1)}, bf16[1,128,3072]{2,1,0:T(8,128)(2,1)}, u32[]{:S(2)}) copy-start(bf16[1,128,3072]{2,1,0:T(8,128)(2,1)} %param.12) | copy-start | bytes 2359300
  16.0 0.7 copy-start.10
  16.6 41.6 %all-to-all-start = ((bf16[4,128,1536]{2,1,0:T(8,128)(2,1)}), bf16[4,128,1536]{2,1,0:T(8,128)(2,1)S(1)}, u32[]{:S(2)}, u32[]{:S(2)}) async-start(bf16[4,128,1536]{2,1,0:T(8,128)(2,1)} %shard_map.129), calls=%async_computation | async-start | bytes 3145728 | tf_op jit(solution)/shard_map/all_to_all | solution.py:372
  22.3 0.9 %copy-start.9 = (bf16[256,256]{1,0:T(8,128)(2,1)S(1)}, bf16[256,256]{1,0:T(8,128)(2,1)}, u32[]{:S(2)}) copy-start(bf16[256,256]{1,0:T(8,128)(2,1)} %copy-done.8) | copy-start | bytes 393220
  23.2 0.9 %copy-start.11 = (bf16[256,256]{1,0:T(8,128)(2,1)S(1)}, bf16[256,256]{1,0:T(8,128)(2,1)}, u32[]{:S(2)}) copy-start(bf16[256,256]{1,0:T(8,128)(2,1)} %copy-done.10) | copy-start | bytes 393220
  24.1 9.0 %collective-permute-start.2 = (bf16[512,256]{1,0:T(8,128)(2,1)S(1)}, bf16[512,256]{1,0:T(8,128)(2,1)}, u32[]{:S(2)}, u32[]{:S(2)}) collective-permute-start(bf16[512,256]{1,0:T(8,128)(2,1)S(1)} %shard_map.132.near_ref), channel_id=1, source_target_pairs={{0,1},{1,0},{2,3},{3,2},{4,5},{5,4},{6,7},{7,6},{8,9},{9,8},{10,11... | collective-permute-start | bytes 786440 | tf_op jit(solution)/shard_map/ppermute | solution.py:143
  33.2 15.3 %collective-permute-start.4 = (f32[4,1536]{1,0:T(4,128)S(1)}, f32[4,1536]{1,0:T(4,128)S(1)}, u32[]{:S(2)}, u32[]{:S(2)}) collective-permute-start(f32[4,1536]{1,0:T(4,128)S(1)} %fusion.2.acts_ref), channel_id=1, source_target_pairs={{0,24},{8,0},{16,8},{24,16},{1,25},{9,1},{17,9},{25,17},{2,26},{10... | collective-permute-start | bytes 73736 | tf_op jit(solution)/shard_map/ppermute | solution.py:343
  35.7 12.8 %collective-permute-start.3 = (f32[4,1536]{1,0:T(4,128)S(1)}, f32[4,1536]{1,0:T(4,128)S(1)}, u32[]{:S(2)}, u32[]{:S(2)}) collective-permute-start(f32[4,1536]{1,0:T(4,128)S(1)} %fusion.2.acts_ref), channel_id=1, source_target_pairs={{0,8},{8,16},{16,24},{24,0},{1,9},{9,17},{17,25},{25,1},{2,10},{10... | collective-permute-start | bytes 73736 | tf_op jit(solution)/shard_map/ppermute | solution.py:343
  47.6 0.8 copy-start.6
  48.4 9.8 %copy-start.7 = (f32[512,256]{1,0:T(8,128)S(1)}, f32[512,256]{1,0:T(8,128)}, u32[]{:S(2)}) copy-start(f32[512,256]{1,0:T(8,128)} %copy-done.6) | copy-start | bytes 1572868
  48.4 9.3 %collective-permute-start.5 = (f32[512,256]{1,0:T(8,128)S(1)}, f32[512,256]{1,0:T(8,128)S(1)}, u32[]{:S(2)}, u32[]{:S(2)}) collective-permute-start(f32[512,256]{1,0:T(8,128)S(1)} %get-tuple-element.52), channel_id=1, source_target_pairs={{0,1},{1,0},{2,3},{3,2},{4,5},{5,4},{6,7},{7,6},{8,9},{9,8},{10,11... | collective-permute-start | bytes 1572872 | tf_op jit(solution)/shard_map/ppermute | solution.py:143
  58.3 5.6 %collective-permute-start.6 = (bf16[256,256]{1,0:T(8,128)(2,1)S(1)}, bf16[256,256]{1,0:T(8,128)(2,1)S(1)}, u32[]{:S(2)}, u32[]{:S(2)}) collective-permute-start(bf16[256,256]{1,0:T(8,128)(2,1)S(1)} %get-tuple-element.59), channel_id=1, source_target_pairs={{0,2},{1,3},{2,0},{3,1},{4,6},{5,7},{6,4},{7,5},{8,10},{9,11},{10,... | collective-permute-start | bytes 393224 | tf_op jit(solution)/shard_map/ppermute | solution.py:143
  63.9 8.7 %collective-permute-start.7 = (bf16[256,256]{1,0:T(8,128)(2,1)S(1)}, bf16[256,256]{1,0:T(8,128)(2,1)S(1)}, u32[]{:S(2)}, u32[]{:S(2)}) collective-permute-start(bf16[256,256]{1,0:T(8,128)(2,1)S(1)} %get-tuple-element.61), channel_id=1, source_target_pairs={{0,4},{1,5},{2,6},{3,7},{4,0},{5,1},{6,2},{7,3},{8,12},{9,13},{10,... | collective-permute-start | bytes 393224 | tf_op jit(solution)/shard_map/ppermute | solution.py:143
  73.2 5.0 %collective-permute-start.8 = (bf16[256,256]{1,0:T(8,128)(2,1)S(1)}, bf16[256,256]{1,0:T(8,128)(2,1)S(1)}, u32[]{:S(2)}, u32[]{:S(2)}) collective-permute-start(bf16[256,256]{1,0:T(8,128)(2,1)S(1)} %get-tuple-element.64.a_ref), channel_id=1, source_target_pairs={{0,2},{1,3},{2,0},{3,1},{4,6},{5,7},{6,4},{7,5},{8,10},{9,11},{10,... | collective-permute-start | bytes 393224 | tf_op jit(solution)/shard_map/ppermute | solution.py:143
  74.0 6.6 %collective-permute-start.10 = (f32[4,6144]{1,0:T(4,128)S(1)}, f32[4,6144]{1,0:T(4,128)S(1)}, u32[]{:S(2)}, u32[]{:S(2)}) collective-permute-start(f32[4,6144]{1,0:T(4,128)S(1)} %get-tuple-element.71), channel_id=1, source_target_pairs={{0,8},{8,16},{16,24},{24,0},{1,9},{9,17},{17,25},{25,1},{2,10},{10... | collective-permute-start | bytes 294920 | tf_op jit(solution)/shard_map/ppermute | solution.py:343
  76.2 5.2 %collective-permute-start.11 = (f32[4,6144]{1,0:T(4,128)S(1)}, f32[4,6144]{1,0:T(4,128)S(1)}, u32[]{:S(2)}, u32[]{:S(2)}) collective-permute-start(f32[4,6144]{1,0:T(4,128)S(1)} %get-tuple-element.72), channel_id=1, source_target_pairs={{0,24},{8,0},{16,8},{24,16},{1,25},{9,1},{17,9},{25,17},{2,26},{10... | collective-permute-start | bytes 294920 | tf_op jit(solution)/shard_map/ppermute | solution.py:343
  78.9 3.3 %collective-permute-start.9 = (f32[768,256]{1,0:T(8,128)S(1)}, f32[768,256]{1,0:T(8,128)S(1)}, u32[]{:S(2)}, u32[]{:S(2)}) collective-permute-start(f32[768,256]{1,0:T(8,128)S(1)} %get-tuple-element.66), channel_id=1, source_target_pairs={{0,1},{1,0},{2,3},{3,2},{4,5},{5,4},{6,7},{7,6},{8,9},{9,8},{10,11... | collective-permute-start | bytes 2359304 | tf_op jit(solution)/shard_map/ppermute | solution.py:143

commit v9 on v8

--- a/solution.py
+++ b/solution.py
@@ -43,21 +43,15 @@
     )(*args)
 
 
-def join_kernel(axis, a_ref, b_ref, out_ref):
-    cut = a_ref.shape[axis]
-    if axis:
-        out_ref[:, :cut] = a_ref[...]
-        out_ref[:, cut:] = b_ref[...]
-    else:
-        out_ref[:cut] = a_ref[...]
-        out_ref[cut:] = b_ref[...]
-
-
-def join(a, b, axis=0):
-    shape = list(a.shape)
-    shape[axis] += b.shape[axis]
-    out = jax.ShapeDtypeStruct(shape, a.dtype)
-    return local_call(functools.partial(join_kernel, axis), out, a, b)
+def join_kernel(a_ref, b_ref, out_ref):
+    rows = a_ref.shape[0]
+    out_ref[:rows] = a_ref[...]
+    out_ref[rows:] = b_ref[...]
+
+
+def join(a, b):
+    out = jax.ShapeDtypeStruct((a.shape[0] + b.shape[0], a.shape[1]), a.dtype)
+    return local_call(join_kernel, out, a, b)
 
 
 def add_kernel(kept_ref, arrived_ref, stay_ref, sent_ref):
@@ -354,7 +348,7 @@
     factor = initial_right_factor[0]
     weight = mlp_weight[0]
 
-    near = join(keys[0], values[0], axis=1)
+    near = jnp.concatenate([keys[0], values[0]], axis=-1)
     chips = count // 2
     packed = pack(inputs[0], chips)
     for index, bit in enumerate(bits[:-1]):
@@ -368,7 +362,7 @@
             near, far, packed, grad_rows, out_rows = lax.optimization_barrier(
                 (near, far, packed, out_grad[0], outputs[0])
             )
-        near = join(near, far)
+        near, packed = lax.optimization_barrier((join(near, far), packed))
     blocks = lax.all_to_all(
         packed,
         "seq",
@@ -387,20 +381,31 @@
     lower_acts, higher_acts, sent = lax.optimization_barrier((lower_acts, higher_acts, sent))
 
     last = bits[0]
+    half = weight.shape[1] // 2
     arrived = swap(sent, "seq", 1)
     basis, both = make_basis(acts, lower_acts, higher_acts)
-    contrib = jnp.dot(both, weight, preferred_element_type=F32)
-    arrived, contrib, blocks = lax.optimization_barrier((arrived, contrib, blocks))
-    contrib = contrib.reshape(2, contrib.shape[0] // 2, contrib.shape[1])
-    lower_half = from_cycle(contrib[1], "rep", 1)
+    arrived, basis, both = lax.optimization_barrier((arrived, basis, both))
+    contrib = None
     for bit in reversed(bits[1:-1]):
         keep = grads.shape[0] // 2
         grads, sent = add_split(grads, arrived, keep, keep)
         arrived = swap(sent, "seq", bit)
-    higher_half = from_cycle(contrib[0], "rep", -1)
+        if contrib is None:
+            contrib = jnp.dot(both, weight[:, :half], preferred_element_type=F32)
+            arrived, contrib, both, blocks = lax.optimization_barrier(
+                (arrived, contrib, both, blocks)
+            )
 
     grads, sent = add_split(grads, arrived, grads.shape[0], grads.shape[0])
     arrived = swap(sent, "seq", last)
+    if contrib is None:
+        contrib = jnp.dot(both, weight[:, :half], preferred_element_type=F32)
+    rest = jnp.dot(both, weight[:, half:], preferred_element_type=F32)
+    arrived, rest = lax.optimization_barrier((arrived, rest))
+    contrib = jnp.concatenate([contrib, rest], axis=1)
+    contrib = contrib.reshape(2, contrib.shape[0] // 2, contrib.shape[1])
+    lower_half = from_cycle(contrib[1], "rep", 1)
+    higher_half = from_cycle(contrib[0], "rep", -1)
     own, near_b = merge(me, last, grads, arrived)
     for bit in bits[1:-1]:
         near_b = join(near_b, swap(near_b, "seq", bit))

time: 83.8 us -> 83.5 us (level)
  local copies, waits for them, and re-layouts: 8.57 us -> 3.74 us
  waiting for transfers between devices: 14.6 us -> 19.3 us
  starting transfers between devices: 24.5 us -> 21.2 us
  matrix products: 16.6 us -> 18.9 us
  other arithmetic: 1.76 us -> 2.61 us
    ppermute x8, waiting for transfers between devices: 11.6 us -> 17.7 us  [swap(): return lax.ppermute(block, axis, route)]
    unnamed x30 -> x15, local copies, waits for them, and re-layouts: 8.54 us -> 3.7 us
    ppermute x8, starting transfers between devices: 13 us -> 10 us  [swap(): return lax.ppermute(block, axis, route)]
    dot_general x1 -> x2, matrix products: 7.69 us -> 10 us  [the longest x1 5.01 us: on_device(): rest = jnp.dot(both, weight[:, half:], preferred_element_type=F32)]
    ppermute x4, waiting for transfers between devices: 2.49 us -> 1.52 us  [from_cycle(): lax.ppermute(block, axis, [(i, (i + distance) % count) for i in range(cou...]
    concatenate x0 -> x1, other arithmetic: none -> 0.86 us  [on_device(): near = jnp.concatenate([keys[0], values[0]], axis=-1)]
  transfers between devices with their start and end apart: 13 -> 13, of which waited for: 7 -> 7; matrix products, arithmetic and copies ran while one was open for 21% -> 18% of each run, Pallas kernels for 19% -> 19%
where the time goes in v9:
time: 83.5 us; the launch traced here: 83 us
  starting transfers between devices  21.2 us (25%)
  waiting for transfers between devices  19.3 us (23%)
  matrix products  18.9 us (23%)
  Pallas kernels  16.5 us (20%)
  local copies, waits for them, and re-layouts  3.74 us (4%)
  other arithmetic  2.61 us (3%)
    ppermute x8, waiting for transfers between devices, swap(): return lax.ppermute(block, axis, route)  17.7 us
    pallas_call x1, Pallas kernels, attend(): pl.pallas_call(functools.partial(attention_kernel, order, group, join, hd...  12 us
    ppermute x8, starting transfers between devices, swap(): return lax.ppermute(block, axis, route)  10 us
    dot_general x1, matrix products, dot_nt(): lax.dot_general(a, b, (((1,), (1,)), ((), ())), preferred_element_type=F32)  8.9 us
    all_to_all x1, starting transfers between devices, on_device(): lax.all_to_all(packed, 'seq', split_axis=0, concat_axis=0, tiled=True, ax...  5.7 us
    ppermute x4, starting transfers between devices, from_cycle(): lax.ppermute(block, axis, [(i, (i + distance) % count) for i in range(cou...  5.48 us
    dot_general x1, matrix products, on_device(): rest = jnp.dot(both, weight[:, half:], preferred_element_type=F32)  5.01 us
    dot_general x1, matrix products, on_device(): contrib = jnp.dot(both, weight[:, :half], preferred_element_type=F32)  5 us
  transfers between devices with their start and end apart: 13, of which 7 were waited for; matrix products, arithmetic and copies ran while one was open for 18% of the time, Pallas kernels for 19%

profile of v9, /device:TPU:0, one launch (start us, length us, event | category | flops | bytes accessed | tf_op | source)
XLA Modules:
  0.0 83.0 jit_solution(3272744557162441192)
XLA Ops:
  0.6 0.0 copy-start
  0.6 0.0 copy-start.2
  0.7 0.9 %pad_maximum_fusion.a_ref = bf16[128,256]{1,0:T(8,128)(2,1)S(1)} fusion(bf16[128,128]{1,0:T(8,128)(2,1)} %bitcast.35, bf16[128,128]{1,0:T(8,128)(2,1)} %bitcast.36), kind=kLoop, calls=%fused_computation.8 | loop fusion | flops 131072 | bytes 131072 | tf_op jit(solution)/shard_map/concatenate | solution.py:351
  1.5 5.9 %collective-permute-start = (bf16[128,256]{1,0:T(8,128)(2,1)S(1)}, bf16[128,256]{1,0:T(8,128)(2,1)S(1)}, u32[]{:S(2)}, u32[]{:S(2)}) collective-permute-start(bf16[128,256]{1,0:T(8,128)(2,1)S(1)} %pad_maximum_fusion.a_ref), channel_id=1, source_target_pairs={{0,4},{1,5},{2,6},{3,7},{8,12},{9,13},{10,14},{11,15},{16,20},{17,... | collective-permute-start | bytes 196616 | tf_op jit(solution)/shard_map/ppermute | solution.py:137
  7.5 0.0 copy-start.3
  7.5 1.4 %copy-done.3 = bf16[1,128,6144]{2,1,0:T(8,128)(2,1)S(1)} copy-done((bf16[1,128,6144]{2,1,0:T(8,128)(2,1)S(1)}, bf16[1,128,6144]{2,1,0:T(8,128)(2,1)}, u32[]{:S(2)}) %copy-start.3) | copy-done | bytes 1572888
  8.9 0.0 copy-start.5
  8.9 0.0 copy-start.6
  8.9 1.3 %shard_map.128 = bf16[4,128,1536]{2,1,0:T(8,128)(2,1)} custom-call(bf16[128,6144]{1,0:T(8,128)(2,1)S(1)} %bitcast.29), custom_call_target="tpu_custom_call" | custom-call | flops 1 | bytes 1 | tf_op jit(solution)/shard_map/pallas_call | solution.py:260
  10.2 0.0 collective-permute-done.b_ref
  10.2 1.6 %collective-permute-start.1 = (bf16[256,256]{1,0:T(8,128)(2,1)S(1)}, bf16[256,256]{1,0:T(8,128)(2,1)S(1)}, u32[]{:S(2)}, u32[]{:S(2)}) collective-permute-start(bf16[256,256]{1,0:T(8,128)(2,1)S(1)} %shard_map.129.a_ref), channel_id=1, source_target_pairs={{0,2},{1,3},{2,0},{3,1},{4,6},{5,7},{6,4},{7,5},{8,10},{9,11},{10,... | collective-permute-start | bytes 393224 | tf_op jit(solution)/shard_map/ppermute | solution.py:137
  11.8 0.0 copy-start.1
  11.8 1.1 %copy-done.1 = bf16[1,128,3072]{2,1,0:T(8,128)(2,1)S(1)} copy-done((bf16[1,128,3072]{2,1,0:T(8,128)(2,1)S(1)}, bf16[1,128,3072]{2,1,0:T(8,128)(2,1)}, u32[]{:S(2)}) %copy-start.1) | copy-done | bytes 786456
  12.9 0.0 copy-start.4
  13.0 1.1 %copy-done.4 = bf16[1,128,3072]{2,1,0:T(8,128)(2,1)S(1)} copy-done((bf16[1,128,3072]{2,1,0:T(8,128)(2,1)S(1)}, bf16[1,128,3072]{2,1,0:T(8,128)(2,1)}, u32[]{:S(2)}) %copy-start.4) | copy-done | bytes 786456
  14.1 0.5 shard_map.130.delta_ref
  14.6 0.6 collective-permute-done.1.b_ref
  15.2 0.0 copy-done
  15.2 5.7 %all-to-all-start = ((bf16[4,128,1536]{2,1,0:T(8,128)(2,1)}), bf16[4,128,1536]{2,1,0:T(8,128)(2,1)S(1)}, u32[]{:S(2)}, u32[]{:S(2)}) async-start(bf16[4,128,1536]{2,1,0:T(8,128)(2,1)} %shard_map.128), calls=%async_computation | async-start | bytes 3145728 | tf_op jit(solution)/shard_map/all_to_all | solution.py:366
  20.9 0.0 collective-permute-start.2
  20.9 8.9 %fusion.4.acts_ref = f32[4,1536]{1,0:T(4,128)S(1)} fusion(bf16[4,6144]{1,0:T(4,128)(2,1)S(1)} %bitcast.26, bf16[1,1536,6144]{2,1,0:T(8,128)(2,1)} %param.16), kind=kOutput, calls=%fused_computation.11 | convolution fusion | flops 75497472 | bytes 18948096 | tf_op jit(solution)/shard_map/dot_general | solution.py:24
  29.8 0.0 collective-permute-done.2.far_ref
  29.9 2.5 %collective-permute-start.4 = (f32[4,1536]{1,0:T(4,128)S(1)}, f32[4,1536]{1,0:T(4,128)S(1)}, u32[]{:S(2)}, u32[]{:S(2)}) collective-permute-start(f32[4,1536]{1,0:T(4,128)S(1)} %fusion.4.acts_ref), channel_id=1, source_target_pairs={{0,24},{8,0},{16,8},{24,16},{1,25},{9,1},{17,9},{25,17},{2,26},{10... | collective-permute-start | bytes 73736 | tf_op jit(solution)/shard_map/ppermute | solution.py:337
  32.4 0.0 collective-permute-start.3
  32.4 0.0 copy-done.2
  32.4 0.0 copy-done.5
  32.4 0.0 copy-done.6
  32.4 12.0 %shard_map.132 = (f32[128,3072]{1,0:T(8,128)}, f32[512,256]{1,0:T(8,128)S(1)}, f32[512,256]{1,0:T(8,128)S(1)}) custom-call(s32[1]{0:T(128)} %bitcast.me_ref, bf16[128,3072]{1,0:T(8,128)(2,1)S(1)} %bitcast.31, bf16[128,3072]{1,0:T(8,128)(2,1)S(1)} %bitcast.28, f32[24,128]{1,0:T(8,128)S(1)} %bitcast.32, f32[24,128]{1,0:T(8,128)S(1)} %shard_map.130.delta_ref, ...), custom_call_target="tpu_custom_call" | custom-call | flops 1 | bytes 1 | tf_op jit(solution)/shard_map/pallas_call | solution.py:233
  44.4 0.0 collective-permute-done.4.higher_ref
  44.4 0.0 collective-permute-done.3.lower_ref
  44.4 0.2 collective-permute-start.5
  44.6 1.3 %shard_map.133 = (f32[2,4,1536]{2,1,0:T(4,128)}, bf16[8,1536]{1,0:T(8,128)(2,1)S(1)}) custom-call(f32[4,1536]{1,0:T(4,128)S(1)} %fusion.4.acts_ref, f32[4,1536]{1,0:T(4,128)S(1)} %collective-permute-done.3.lower_ref, f32[4,1536]{1,0:T(4,128)S(1)} %collective-permute-done.4.higher_ref), custom_call_target="tpu_custom_call" | custom-call | flops 1 | bytes 1 | tf_op jit(solution)/shard_map/pallas_call | solution.py:322
  45.9 0.4 collective-permute-done.5.arrived_ref
  46.3 0.1 shard_map.134
  46.4 2.1 %collective-permute-start.6 = (bf16[256,256]{1,0:T(8,128)(2,1)S(1)}, bf16[256,256]{1,0:T(8,128)(2,1)S(1)}, u32[]{:S(2)}, u32[]{:S(2)}) collective-permute-start(bf16[256,256]{1,0:T(8,128)(2,1)S(1)} %get-tuple-element.73), channel_id=1, source_target_pairs={{0,2},{1,3},{2,0},{3,1},{4,6},{5,7},{6,4},{7,5},{8,10},{9,11},{10,... | collective-permute-start | bytes 393224 | tf_op jit(solution)/shard_map/ppermute | solution.py:137
  48.5 5.0 %fusion.2 = f32[8,3072]{1,0:T(8,128)S(1)} fusion(bf16[8,1536]{1,0:T(8,128)(2,1)S(1)} %get-tuple-element.79, bf16[1536,6144]{1,0:T(8,128)(2,1)} %bitcast.33), kind=kOutput, calls=%fused_computation.2 | convolution fusion | flops 75497472 | bytes 9560064 | tf_op jit(solution)/shard_map/dot_general | solution.py:394
  53.5 6.2 %collective-permute-done.6.arrived_ref = bf16[256,256]{1,0:T(8,128)(2,1)S(1)} collective-permute-done((bf16[256,256]{1,0:T(8,128)(2,1)S(1)}, bf16[256,256]{1,0:T(8,128)(2,1)S(1)}, u32[]{:S(2)}, u32[]{:S(2)}) %collective-permute-start.6) | collective-permute-done | bytes 131104 | tf_op jit(solution)/shard_map/ppermute | solution.py:137
  59.6 0.0 all-to-all-done.x_ref
  59.6 5.0 %fusion = f32[8,3072]{1,0:T(8,128)S(1)} fusion(bf16[8,1536]{1,0:T(8,128)(2,1)S(1)} %get-tuple-element.79, bf16[1536,6144]{1,0:T(8,128)(2,1)} %bitcast.34), kind=kOutput, calls=%fused_computation | convolution fusion | flops 75497472 | bytes 9560064 | tf_op jit(solution)/shard_map/dot_general | solution.py:403
  64.7 0.1 collective-permute-start.7
  64.8 8.1 %collective-permute-done.7.there_ref = bf16[256,256]{1,0:T(8,128)(2,1)S(1)} collective-permute-done((bf16[256,256]{1,0:T(8,128)(2,1)S(1)}, bf16[256,256]{1,0:T(8,128)(2,1)S(1)}, u32[]{:S(2)}, u32[]{:S(2)}) %collective-permute-start.7) | collective-permute-done | bytes 131104 | tf_op jit(solution)/shard_map/ppermute | solution.py:137
  72.9 0.7 shard_map.136
  73.6 0.0 collective-permute-start.8
  73.7 1.5 %collective-permute-start.10 = (f32[4,6144]{1,0:T(4,128)S(1)}, f32[4,6144]{1,0:T(4,128)S(1)}, u32[]{:S(2)}, u32[]{:S(2)}) collective-permute-start(f32[4,6144]{1,0:T(4,128)S(1)} %get-tuple-element.91), channel_id=1, source_target_pairs={{0,8},{8,16},{16,24},{24,0},{1,9},{9,17},{17,25},{25,1},{2,10},{10... | collective-permute-start | bytes 294920 | tf_op jit(solution)/shard_map/ppermute | solution.py:337
  75.2 1.4 %collective-permute-start.11 = (f32[4,6144]{1,0:T(4,128)S(1)}, f32[4,6144]{1,0:T(4,128)S(1)}, u32[]{:S(2)}, u32[]{:S(2)}) collective-permute-start(f32[4,6144]{1,0:T(4,128)S(1)} %get-tuple-element.92), channel_id=1, source_target_pairs={{0,24},{8,0},{16,8},{24,16},{1,25},{9,1},{17,9},{25,17},{2,26},{10... | collective-permute-start | bytes 294920 | tf_op jit(solution)/shard_map/ppermute | solution.py:337
  76.6 2.4 %collective-permute-done.8.b_ref = bf16[256,256]{1,0:T(8,128)(2,1)S(1)} collective-permute-done((bf16[256,256]{1,0:T(8,128)(2,1)S(1)}, bf16[256,256]{1,0:T(8,128)(2,1)S(1)}, u32[]{:S(2)}, u32[]{:S(2)}) %collective-permute-start.8) | collective-permute-done | bytes 131104 | tf_op jit(solution)/shard_map/ppermute | solution.py:137
  79.0 0.6 shard_map.138
  79.7 0.1 collective-permute-start.9
  79.8 0.4 collective-permute-done.10
  80.2 1.1 %collective-permute-done.11 = f32[4,6144]{1,0:T(4,128)S(1)} collective-permute-done((f32[4,6144]{1,0:T(4,128)S(1)}, f32[4,6144]{1,0:T(4,128)S(1)}, u32[]{:S(2)}, u32[]{:S(2)}) %collective-permute-start.11) | collective-permute-done | bytes 98336 | tf_op jit(solution)/shard_map/ppermute | solution.py:337
  81.3 0.7 maximum_bitcast_fusion
  82.1 0.0 collective-permute-done.9
  82.1 1.0 %add_bitcast_fusion = f32[1,768,256]{2,1,0:T(8,128)} fusion(f32[768,256]{1,0:T(8,128)S(1)} %get-tuple-element.84, f32[768,256]{1,0:T(8,128)S(1)} %collective-permute-done.9), kind=kLoop, calls=%fused_computation.4 | loop fusion | flops 196608 | bytes 2359296 | tf_op jit(solution)/shard_map/broadcast_in_dim | solution.py:419
  (8 shorter events, 0.2 us)
Async XLA Ops:
  0.6 14.6 %copy-start = (bf16[1,4,6144]{2,1,0:T(4,128)(2,1)S(1)}, bf16[1,4,6144]{2,1,0:T(4,128)(2,1)}, u32[]{:S(2)}) copy-start(bf16[1,4,6144]{2,1,0:T(4,128)(2,1)} %param.17) | copy-start | bytes 147460
  0.6 31.7 %copy-start.2 = (bf16[1,128,3072]{2,1,0:T(8,128)(2,1)S(1)}, bf16[1,128,3072]{2,1,0:T(8,128)(2,1)}, u32[]{:S(2)}) copy-start(bf16[1,128,3072]{2,1,0:T(8,128)(2,1)} %param.13) | copy-start | bytes 2359300
  1.5 8.6 %collective-permute-start = (bf16[128,256]{1,0:T(8,128)(2,1)S(1)}, bf16[128,256]{1,0:T(8,128)(2,1)S(1)}, u32[]{:S(2)}, u32[]{:S(2)}) collective-permute-start(bf16[128,256]{1,0:T(8,128)(2,1)S(1)} %pad_maximum_fusion.a_ref), channel_id=1, source_target_pairs={{0,4},{1,5},{2,6},{3,7},{8,12},{9,13},{10,14},{11,15},{16,20},{17,... | collective-permute-start | bytes 196616 | tf_op jit(solution)/shard_map/ppermute | solution.py:137
  7.5 1.4 %copy-start.3 = (bf16[1,128,6144]{2,1,0:T(8,128)(2,1)S(1)}, bf16[1,128,6144]{2,1,0:T(8,128)(2,1)}, u32[]{:S(2)}) copy-start(bf16[1,128,6144]{2,1,0:T(8,128)(2,1)} %param.15) | copy-start | bytes 4718596
  8.9 23.5 %copy-start.5 = (bf16[1,128,3072]{2,1,0:T(8,128)(2,1)S(1)}, bf16[1,128,3072]{2,1,0:T(8,128)(2,1)}, u32[]{:S(2)}) copy-start(bf16[1,128,3072]{2,1,0:T(8,128)(2,1)} %param.9) | copy-start | bytes 2359300
  8.9 23.5 %copy-start.6 = (f32[1,24,128]{2,1,0:T(8,128)S(1)}, f32[1,24,128]{2,1,0:T(8,128)}, u32[]{:S(2)}) copy-start(f32[1,24,128]{2,1,0:T(8,128)} %param.14) | copy-start | bytes 36868
  10.2 5.0 %collective-permute-start.1 = (bf16[256,256]{1,0:T(8,128)(2,1)S(1)}, bf16[256,256]{1,0:T(8,128)(2,1)S(1)}, u32[]{:S(2)}, u32[]{:S(2)}) collective-permute-start(bf16[256,256]{1,0:T(8,128)(2,1)S(1)} %shard_map.129.a_ref), channel_id=1, source_target_pairs={{0,2},{1,3},{2,0},{3,1},{4,6},{5,7},{6,4},{7,5},{8,10},{9,11},{10,... | collective-permute-start | bytes 393224 | tf_op jit(solution)/shard_map/ppermute | solution.py:137
  11.8 1.1 %copy-start.1 = (bf16[1,128,3072]{2,1,0:T(8,128)(2,1)S(1)}, bf16[1,128,3072]{2,1,0:T(8,128)(2,1)}, u32[]{:S(2)}) copy-start(bf16[1,128,3072]{2,1,0:T(8,128)(2,1)} %param.13) | copy-start | bytes 2359300
  12.9 1.1 %copy-start.4 = (bf16[1,128,3072]{2,1,0:T(8,128)(2,1)S(1)}, bf16[1,128,3072]{2,1,0:T(8,128)(2,1)}, u32[]{:S(2)}) copy-start(bf16[1,128,3072]{2,1,0:T(8,128)(2,1)} %param.12) | copy-start | bytes 2359300
  15.2 44.4 %all-to-all-start = ((bf16[4,128,1536]{2,1,0:T(8,128)(2,1)}), bf16[4,128,1536]{2,1,0:T(8,128)(2,1)S(1)}, u32[]{:S(2)}, u32[]{:S(2)}) async-start(bf16[4,128,1536]{2,1,0:T(8,128)(2,1)} %shard_map.128), calls=%async_computation | async-start | bytes 3145728 | tf_op jit(solution)/shard_map/all_to_all | solution.py:366
  20.9 8.9 %collective-permute-start.2 = (bf16[512,256]{1,0:T(8,128)(2,1)S(1)}, bf16[512,256]{1,0:T(8,128)(2,1)}, u32[]{:S(2)}, u32[]{:S(2)}) collective-permute-start(bf16[512,256]{1,0:T(8,128)(2,1)S(1)} %shard_map.131.near_ref), channel_id=1, source_target_pairs={{0,1},{1,0},{2,3},{3,2},{4,5},{5,4},{6,7},{7,6},{8,9},{9,8},{10,11... | collective-permute-start | bytes 786440 | tf_op jit(solution)/shard_map/ppermute | solution.py:137
  29.9 14.5 %collective-permute-start.4 = (f32[4,1536]{1,0:T(4,128)S(1)}, f32[4,1536]{1,0:T(4,128)S(1)}, u32[]{:S(2)}, u32[]{:S(2)}) collective-permute-start(f32[4,1536]{1,0:T(4,128)S(1)} %fusion.4.acts_ref), channel_id=1, source_target_pairs={{0,24},{8,0},{16,8},{24,16},{1,25},{9,1},{17,9},{25,17},{2,26},{10... | collective-permute-start | bytes 73736 | tf_op jit(solution)/shard_map/ppermute | solution.py:337
  32.4 12.0 %collective-permute-start.3 = (f32[4,1536]{1,0:T(4,128)S(1)}, f32[4,1536]{1,0:T(4,128)S(1)}, u32[]{:S(2)}, u32[]{:S(2)}) collective-permute-start(f32[4,1536]{1,0:T(4,128)S(1)} %fusion.4.acts_ref), channel_id=1, source_target_pairs={{0,8},{8,16},{16,24},{24,0},{1,9},{9,17},{17,25},{25,1},{2,10},{10... | collective-permute-start | bytes 73736 | tf_op jit(solution)/shard_map/ppermute | solution.py:337
  44.4 1.9 %collective-permute-start.5 = (f32[512,256]{1,0:T(8,128)S(1)}, f32[512,256]{1,0:T(8,128)S(1)}, u32[]{:S(2)}, u32[]{:S(2)}) collective-permute-start(f32[512,256]{1,0:T(8,128)S(1)} %get-tuple-element.66), channel_id=1, source_target_pairs={{0,1},{1,0},{2,3},{3,2},{4,5},{5,4},{6,7},{7,6},{8,9},{9,8},{10,11... | collective-permute-start | bytes 1572872 | tf_op jit(solution)/shard_map/ppermute | solution.py:137
  46.4 13.2 %collective-permute-start.6 = (bf16[256,256]{1,0:T(8,128)(2,1)S(1)}, bf16[256,256]{1,0:T(8,128)(2,1)S(1)}, u32[]{:S(2)}, u32[]{:S(2)}) collective-permute-start(bf16[256,256]{1,0:T(8,128)(2,1)S(1)} %get-tuple-element.73), channel_id=1, source_target_pairs={{0,2},{1,3},{2,0},{3,1},{4,6},{5,7},{6,4},{7,5},{8,10},{9,11},{10,... | collective-permute-start | bytes 393224 | tf_op jit(solution)/shard_map/ppermute | solution.py:137
  64.7 8.2 %collective-permute-start.7 = (bf16[256,256]{1,0:T(8,128)(2,1)S(1)}, bf16[256,256]{1,0:T(8,128)(2,1)S(1)}, u32[]{:S(2)}, u32[]{:S(2)}) collective-permute-start(bf16[256,256]{1,0:T(8,128)(2,1)S(1)} %get-tuple-element.78), channel_id=1, source_target_pairs={{0,4},{1,5},{2,6},{3,7},{4,0},{5,1},{6,2},{7,3},{8,12},{9,13},{10,... | collective-permute-start | bytes 393224 | tf_op jit(solution)/shard_map/ppermute | solution.py:137
  73.6 5.4 %collective-permute-start.8 = (bf16[256,256]{1,0:T(8,128)(2,1)S(1)}, bf16[256,256]{1,0:T(8,128)(2,1)S(1)}, u32[]{:S(2)}, u32[]{:S(2)}) collective-permute-start(bf16[256,256]{1,0:T(8,128)(2,1)S(1)} %get-tuple-element.83.a_ref), channel_id=1, source_target_pairs={{0,2},{1,3},{2,0},{3,1},{4,6},{5,7},{6,4},{7,5},{8,10},{9,11},{10,... | collective-permute-start | bytes 393224 | tf_op jit(solution)/shard_map/ppermute | solution.py:137
  73.7 6.5 %collective-permute-start.10 = (f32[4,6144]{1,0:T(4,128)S(1)}, f32[4,6144]{1,0:T(4,128)S(1)}, u32[]{:S(2)}, u32[]{:S(2)}) collective-permute-start(f32[4,6144]{1,0:T(4,128)S(1)} %get-tuple-element.91), channel_id=1, source_target_pairs={{0,8},{8,16},{16,24},{24,0},{1,9},{9,17},{17,25},{25,1},{2,10},{10... | collective-permute-start | bytes 294920 | tf_op jit(solution)/shard_map/ppermute | solution.py:337
  75.2 6.1 %collective-permute-start.11 = (f32[4,6144]{1,0:T(4,128)S(1)}, f32[4,6144]{1,0:T(4,128)S(1)}, u32[]{:S(2)}, u32[]{:S(2)}) collective-permute-start(f32[4,6144]{1,0:T(4,128)S(1)} %get-tuple-element.92), channel_id=1, source_target_pairs={{0,24},{8,0},{16,8},{24,16},{1,25},{9,1},{17,9},{25,17},{2,26},{10... | collective-permute-start | bytes 294920 | tf_op jit(solution)/shard_map/ppermute | solution.py:337
  79.7 2.4 %collective-permute-start.9 = (f32[768,256]{1,0:T(8,128)S(1)}, f32[768,256]{1,0:T(8,128)S(1)}, u32[]{:S(2)}, u32[]{:S(2)}) collective-permute-start(f32[768,256]{1,0:T(8,128)S(1)} %get-tuple-element.85), channel_id=1, source_target_pairs={{0,1},{1,0},{2,3},{3,2},{4,5},{5,4},{6,7},{7,6},{8,9},{9,8},{10,11... | collective-permute-start | bytes 2359304 | tf_op jit(solution)/shard_map/ppermute | solution.py:137

commit v10 on v9

--- a/solution.py
+++ b/solution.py
@@ -381,7 +381,6 @@
     lower_acts, higher_acts, sent = lax.optimization_barrier((lower_acts, higher_acts, sent))
 
     last = bits[0]
-    half = weight.shape[1] // 2
     arrived = swap(sent, "seq", 1)
     basis, both = make_basis(acts, lower_acts, higher_acts)
     arrived, basis, both = lax.optimization_barrier((arrived, basis, both))
@@ -391,18 +390,13 @@
         grads, sent = add_split(grads, arrived, keep, keep)
         arrived = swap(sent, "seq", bit)
         if contrib is None:
-            contrib = jnp.dot(both, weight[:, :half], preferred_element_type=F32)
-            arrived, contrib, both, blocks = lax.optimization_barrier(
-                (arrived, contrib, both, blocks)
-            )
+            contrib = jnp.dot(both, weight, preferred_element_type=F32)
+            arrived, contrib, blocks = lax.optimization_barrier((arrived, contrib, blocks))
 
     grads, sent = add_split(grads, arrived, grads.shape[0], grads.shape[0])
     arrived = swap(sent, "seq", last)
     if contrib is None:
-        contrib = jnp.dot(both, weight[:, :half], preferred_element_type=F32)
-    rest = jnp.dot(both, weight[:, half:], preferred_element_type=F32)
-    arrived, rest = lax.optimization_barrier((arrived, rest))
-    contrib = jnp.concatenate([contrib, rest], axis=1)
+        contrib = jnp.dot(both, weight, preferred_element_type=F32)
     contrib = contrib.reshape(2, contrib.shape[0] // 2, contrib.shape[1])
     lower_half = from_cycle(contrib[1], "rep", 1)
     higher_half = from_cycle(contrib[0], "rep", -1)

time: 83.5 us -> 78.4 us (0.939)
  waiting for transfers between devices: 19.3 us -> 16.7 us
  matrix products: 18.9 us -> 16.6 us
    ppermute x8, waiting for transfers between devices: 17.7 us -> 15.1 us  [swap(): return lax.ppermute(block, axis, route)]
    dot_general x2 -> x1, matrix products: 10 us -> 7.69 us  [on_device(): contrib = jnp.dot(both, weight, preferred_element_type=F32)]
    unnamed x15 -> x14, local copies, waits for them, and re-layouts: 3.7 us -> 3.69 us
  transfers between devices with their start and end apart: 13 -> 13, of which waited for: 7 -> 7; matrix products, arithmetic and copies ran while one was open for 18% -> 22% of each run, Pallas kernels for 19% -> 20%
where the time goes in v10:
time: 78.4 us; the launch traced here: 78 us
  starting transfers between devices  21.2 us (27%)
  waiting for transfers between devices  16.7 us (21%)
  matrix products  16.6 us (21%)
  Pallas kernels  16.4 us (21%)
  local copies, waits for them, and re-layouts  3.72 us (5%)
  other arithmetic  2.62 us (3%)
    ppermute x8, waiting for transfers between devices, swap(): return lax.ppermute(block, axis, route)  15.1 us
    pallas_call x1, Pallas kernels, attend(): pl.pallas_call(functools.partial(attention_kernel, order, group, join, hd...  11.9 us
    ppermute x8, starting transfers between devices, swap(): return lax.ppermute(block, axis, route)  10 us
    dot_general x1, matrix products, dot_nt(): lax.dot_general(a, b, (((1,), (1,)), ((), ())), preferred_element_type=F32)  8.9 us
    dot_general x1, matrix products, on_device(): contrib = jnp.dot(both, weight, preferred_element_type=F32)  7.69 us
    all_to_all x1, starting transfers between devices, on_device(): lax.all_to_all(packed, 'seq', split_axis=0, concat_axis=0, tiled=True, ax...  5.7 us
    ppermute x4, starting transfers between devices, from_cycle(): lax.ppermute(block, axis, [(i, (i + distance) % count) for i in range(cou...  5.48 us
    unnamed x14, local copies, waits for them, and re-layouts  3.69 us
  transfers between devices with their start and end apart: 13, of which 7 were waited for; matrix products, arithmetic and copies ran while one was open for 22% of the time, Pallas kernels for 20%

profile of v10, /device:TPU:0, one launch (start us, length us, event | category | flops | bytes accessed | tf_op | source)
XLA Modules:
  0.0 78.0 jit_solution(14157534252951060599)
XLA Ops:
  0.6 0.0 copy-start
  0.6 0.0 copy-start.2
  0.7 0.9 %pad_maximum_fusion.a_ref = bf16[128,256]{1,0:T(8,128)(2,1)S(1)} fusion(bf16[128,128]{1,0:T(8,128)(2,1)} %bitcast.34, bf16[128,128]{1,0:T(8,128)(2,1)} %bitcast.35), kind=kLoop, calls=%fused_computation.8 | loop fusion | flops 131072 | bytes 131072 | tf_op jit(solution)/shard_map/concatenate | solution.py:351
  1.5 5.9 %collective-permute-start = (bf16[128,256]{1,0:T(8,128)(2,1)S(1)}, bf16[128,256]{1,0:T(8,128)(2,1)S(1)}, u32[]{:S(2)}, u32[]{:S(2)}) collective-permute-start(bf16[128,256]{1,0:T(8,128)(2,1)S(1)} %pad_maximum_fusion.a_ref), channel_id=1, source_target_pairs={{0,4},{1,5},{2,6},{3,7},{8,12},{9,13},{10,14},{11,15},{16,20},{17,... | collective-permute-start | bytes 196616 | tf_op jit(solution)/shard_map/ppermute | solution.py:137
  7.5 0.0 copy-start.3
  7.5 1.4 %copy-done.3 = bf16[1,128,6144]{2,1,0:T(8,128)(2,1)S(1)} copy-done((bf16[1,128,6144]{2,1,0:T(8,128)(2,1)S(1)}, bf16[1,128,6144]{2,1,0:T(8,128)(2,1)}, u32[]{:S(2)}) %copy-start.3) | copy-done | bytes 1572888
  8.9 0.0 copy-start.5
  8.9 0.0 copy-start.6
  8.9 1.3 %shard_map.128 = bf16[4,128,1536]{2,1,0:T(8,128)(2,1)} custom-call(bf16[128,6144]{1,0:T(8,128)(2,1)S(1)} %bitcast.30), custom_call_target="tpu_custom_call" | custom-call | flops 1 | bytes 1 | tf_op jit(solution)/shard_map/pallas_call | solution.py:260
  10.2 0.0 collective-permute-done.b_ref
  10.2 1.6 %collective-permute-start.1 = (bf16[256,256]{1,0:T(8,128)(2,1)S(1)}, bf16[256,256]{1,0:T(8,128)(2,1)S(1)}, u32[]{:S(2)}, u32[]{:S(2)}) collective-permute-start(bf16[256,256]{1,0:T(8,128)(2,1)S(1)} %shard_map.129.a_ref), channel_id=1, source_target_pairs={{0,2},{1,3},{2,0},{3,1},{4,6},{5,7},{6,4},{7,5},{8,10},{9,11},{10,... | collective-permute-start | bytes 393224 | tf_op jit(solution)/shard_map/ppermute | solution.py:137
  11.8 0.0 copy-start.1
  11.8 1.1 %copy-done.1 = bf16[1,128,3072]{2,1,0:T(8,128)(2,1)S(1)} copy-done((bf16[1,128,3072]{2,1,0:T(8,128)(2,1)S(1)}, bf16[1,128,3072]{2,1,0:T(8,128)(2,1)}, u32[]{:S(2)}) %copy-start.1) | copy-done | bytes 786456
  12.9 0.0 copy-start.4
  13.0 1.1 %copy-done.4 = bf16[1,128,3072]{2,1,0:T(8,128)(2,1)S(1)} copy-done((bf16[1,128,3072]{2,1,0:T(8,128)(2,1)S(1)}, bf16[1,128,3072]{2,1,0:T(8,128)(2,1)}, u32[]{:S(2)}) %copy-start.4) | copy-done | bytes 786456
  14.1 0.5 shard_map.130.delta_ref
  14.6 0.6 collective-permute-done.1.b_ref
  15.2 0.0 copy-done
  15.2 5.7 %all-to-all-start = ((bf16[4,128,1536]{2,1,0:T(8,128)(2,1)}), bf16[4,128,1536]{2,1,0:T(8,128)(2,1)S(1)}, u32[]{:S(2)}, u32[]{:S(2)}) async-start(bf16[4,128,1536]{2,1,0:T(8,128)(2,1)} %shard_map.128), calls=%async_computation | async-start | bytes 3145728 | tf_op jit(solution)/shard_map/all_to_all | solution.py:366
  20.9 0.0 collective-permute-start.2
  20.9 8.9 %fusion.2.acts_ref = f32[4,1536]{1,0:T(4,128)S(1)} fusion(bf16[4,6144]{1,0:T(4,128)(2,1)S(1)} %bitcast.27, bf16[1,1536,6144]{2,1,0:T(8,128)(2,1)} %param.16), kind=kOutput, calls=%fused_computation.2 | convolution fusion | flops 75497472 | bytes 18948096 | tf_op jit(solution)/shard_map/dot_general | solution.py:24
  29.8 0.0 collective-permute-done.2.far_ref
  29.9 2.5 %collective-permute-start.4 = (f32[4,1536]{1,0:T(4,128)S(1)}, f32[4,1536]{1,0:T(4,128)S(1)}, u32[]{:S(2)}, u32[]{:S(2)}) collective-permute-start(f32[4,1536]{1,0:T(4,128)S(1)} %fusion.2.acts_ref), channel_id=1, source_target_pairs={{0,24},{8,0},{16,8},{24,16},{1,25},{9,1},{17,9},{25,17},{2,26},{10... | collective-permute-start | bytes 73736 | tf_op jit(solution)/shard_map/ppermute | solution.py:337
  32.4 0.0 collective-permute-start.3
  32.4 0.0 copy-done.2
  32.4 0.0 copy-done.5
  32.4 0.0 copy-done.6
  32.4 11.9 %shard_map.132 = (f32[128,3072]{1,0:T(8,128)}, f32[512,256]{1,0:T(8,128)S(1)}, f32[512,256]{1,0:T(8,128)S(1)}) custom-call(s32[1]{0:T(128)} %bitcast.me_ref, bf16[128,3072]{1,0:T(8,128)(2,1)S(1)} %bitcast.32, bf16[128,3072]{1,0:T(8,128)(2,1)S(1)} %bitcast.29, f32[24,128]{1,0:T(8,128)S(1)} %bitcast.33, f32[24,128]{1,0:T(8,128)S(1)} %shard_map.130.delta_ref, ...), custom_call_target="tpu_custom_call" | custom-call | flops 1 | bytes 1 | tf_op jit(solution)/shard_map/pallas_call | solution.py:233
  44.3 0.0 collective-permute-done.4.higher_ref
  44.3 0.0 collective-permute-done.3.lower_ref
  44.3 0.2 collective-permute-start.5
  44.5 1.3 %shard_map.133 = (f32[2,4,1536]{2,1,0:T(4,128)}, bf16[8,1536]{1,0:T(8,128)(2,1)S(1)}) custom-call(f32[4,1536]{1,0:T(4,128)S(1)} %fusion.2.acts_ref, f32[4,1536]{1,0:T(4,128)S(1)} %collective-permute-done.3.lower_ref, f32[4,1536]{1,0:T(4,128)S(1)} %collective-permute-done.4.higher_ref), custom_call_target="tpu_custom_call" | custom-call | flops 1 | bytes 1 | tf_op jit(solution)/shard_map/pallas_call | solution.py:322
  45.8 0.4 collective-permute-done.5.arrived_ref
  46.2 0.1 shard_map.134
  46.3 2.1 %collective-permute-start.6 = (bf16[256,256]{1,0:T(8,128)(2,1)S(1)}, bf16[256,256]{1,0:T(8,128)(2,1)S(1)}, u32[]{:S(2)}, u32[]{:S(2)}) collective-permute-start(bf16[256,256]{1,0:T(8,128)(2,1)S(1)} %get-tuple-element.70), channel_id=1, source_target_pairs={{0,2},{1,3},{2,0},{3,1},{4,6},{5,7},{6,4},{7,5},{8,10},{9,11},{10,... | collective-permute-start | bytes 393224 | tf_op jit(solution)/shard_map/ppermute | solution.py:137
  48.4 7.7 %fusion = f32[8,6144]{1,0:T(8,128)S(1)} fusion(bf16[8,1536]{1,0:T(8,128)(2,1)S(1)} %get-tuple-element.71, bf16[1,1536,6144]{2,1,0:T(8,128)(2,1)} %param.16), kind=kOutput, calls=%fused_computation | convolution fusion | flops 150994944 | bytes 19095552 | tf_op jit(solution)/shard_map/dot_general | solution.py:393
  56.0 3.6 %collective-permute-done.6.arrived_ref = bf16[256,256]{1,0:T(8,128)(2,1)S(1)} collective-permute-done((bf16[256,256]{1,0:T(8,128)(2,1)S(1)}, bf16[256,256]{1,0:T(8,128)(2,1)S(1)}, u32[]{:S(2)}, u32[]{:S(2)}) %collective-permute-start.6) | collective-permute-done | bytes 131104 | tf_op jit(solution)/shard_map/ppermute | solution.py:137
  59.6 0.0 all-to-all-done.x_ref
  59.7 0.1 collective-permute-start.7
  59.7 8.1 %collective-permute-done.7.there_ref = bf16[256,256]{1,0:T(8,128)(2,1)S(1)} collective-permute-done((bf16[256,256]{1,0:T(8,128)(2,1)S(1)}, bf16[256,256]{1,0:T(8,128)(2,1)S(1)}, u32[]{:S(2)}, u32[]{:S(2)}) %collective-permute-start.7) | collective-permute-done | bytes 131104 | tf_op jit(solution)/shard_map/ppermute | solution.py:137
  67.8 0.7 shard_map.136
  68.5 0.0 collective-permute-start.8
  68.5 1.6 %collective-permute-start.10 = (f32[4,6144]{1,0:T(4,128)S(1)}, f32[4,6144]{1,0:T(4,128)S(1)}, u32[]{:S(2)}, u32[]{:S(2)}) collective-permute-start(f32[4,6144]{1,0:T(4,128)S(1)} %get-tuple-element.85), channel_id=1, source_target_pairs={{0,8},{8,16},{16,24},{24,0},{1,9},{9,17},{17,25},{25,1},{2,10},{10... | collective-permute-start | bytes 294920 | tf_op jit(solution)/shard_map/ppermute | solution.py:337
  70.2 1.3 %collective-permute-start.11 = (f32[4,6144]{1,0:T(4,128)S(1)}, f32[4,6144]{1,0:T(4,128)S(1)}, u32[]{:S(2)}, u32[]{:S(2)}) collective-permute-start(f32[4,6144]{1,0:T(4,128)S(1)} %get-tuple-element.86), channel_id=1, source_target_pairs={{0,24},{8,0},{16,8},{24,16},{1,25},{9,1},{17,9},{25,17},{2,26},{10... | collective-permute-start | bytes 294920 | tf_op jit(solution)/shard_map/ppermute | solution.py:337
  71.5 2.4 %collective-permute-done.8.b_ref = bf16[256,256]{1,0:T(8,128)(2,1)S(1)} collective-permute-done((bf16[256,256]{1,0:T(8,128)(2,1)S(1)}, bf16[256,256]{1,0:T(8,128)(2,1)S(1)}, u32[]{:S(2)}, u32[]{:S(2)}) %collective-permute-start.8) | collective-permute-done | bytes 131104 | tf_op jit(solution)/shard_map/ppermute | solution.py:137
  73.9 0.6 shard_map.138
  74.6 0.1 collective-permute-start.9
  74.7 0.3 collective-permute-done.10
  74.9 1.3 %collective-permute-done.11 = f32[4,6144]{1,0:T(4,128)S(1)} collective-permute-done((f32[4,6144]{1,0:T(4,128)S(1)}, f32[4,6144]{1,0:T(4,128)S(1)}, u32[]{:S(2)}, u32[]{:S(2)}) %collective-permute-start.11) | collective-permute-done | bytes 98336 | tf_op jit(solution)/shard_map/ppermute | solution.py:337
  76.3 0.1 add_bitcast_fusion.2
  76.3 0.7 maximum_bitcast_fusion
  77.0 0.0 collective-permute-done.9
  77.0 1.0 %add_bitcast_fusion = f32[1,768,256]{2,1,0:T(8,128)} fusion(f32[768,256]{1,0:T(8,128)S(1)} %get-tuple-element.79, f32[768,256]{1,0:T(8,128)S(1)} %collective-permute-done.9), kind=kLoop, calls=%fused_computation.4 | loop fusion | flops 196608 | bytes 2359296 | tf_op jit(solution)/shard_map/broadcast_in_dim | solution.py:413
  (5 shorter events, 0.1 us)
Async XLA Ops:
  0.6 14.6 %copy-start = (bf16[1,4,6144]{2,1,0:T(4,128)(2,1)S(1)}, bf16[1,4,6144]{2,1,0:T(4,128)(2,1)}, u32[]{:S(2)}) copy-start(bf16[1,4,6144]{2,1,0:T(4,128)(2,1)} %param.17) | copy-start | bytes 147460
  0.6 31.7 %copy-start.2 = (bf16[1,128,3072]{2,1,0:T(8,128)(2,1)S(1)}, bf16[1,128,3072]{2,1,0:T(8,128)(2,1)}, u32[]{:S(2)}) copy-start(bf16[1,128,3072]{2,1,0:T(8,128)(2,1)} %param.13) | copy-start | bytes 2359300
  1.5 8.6 %collective-permute-start = (bf16[128,256]{1,0:T(8,128)(2,1)S(1)}, bf16[128,256]{1,0:T(8,128)(2,1)S(1)}, u32[]{:S(2)}, u32[]{:S(2)}) collective-permute-start(bf16[128,256]{1,0:T(8,128)(2,1)S(1)} %pad_maximum_fusion.a_ref), channel_id=1, source_target_pairs={{0,4},{1,5},{2,6},{3,7},{8,12},{9,13},{10,14},{11,15},{16,20},{17,... | collective-permute-start | bytes 196616 | tf_op jit(solution)/shard_map/ppermute | solution.py:137
  7.5 1.4 %copy-start.3 = (bf16[1,128,6144]{2,1,0:T(8,128)(2,1)S(1)}, bf16[1,128,6144]{2,1,0:T(8,128)(2,1)}, u32[]{:S(2)}) copy-start(bf16[1,128,6144]{2,1,0:T(8,128)(2,1)} %param.15) | copy-start | bytes 4718596
  8.9 23.5 %copy-start.5 = (bf16[1,128,3072]{2,1,0:T(8,128)(2,1)S(1)}, bf16[1,128,3072]{2,1,0:T(8,128)(2,1)}, u32[]{:S(2)}) copy-start(bf16[1,128,3072]{2,1,0:T(8,128)(2,1)} %param.9) | copy-start | bytes 2359300
  8.9 23.5 %copy-start.6 = (f32[1,24,128]{2,1,0:T(8,128)S(1)}, f32[1,24,128]{2,1,0:T(8,128)}, u32[]{:S(2)}) copy-start(f32[1,24,128]{2,1,0:T(8,128)} %param.14) | copy-start | bytes 36868
  10.2 5.0 %collective-permute-start.1 = (bf16[256,256]{1,0:T(8,128)(2,1)S(1)}, bf16[256,256]{1,0:T(8,128)(2,1)S(1)}, u32[]{:S(2)}, u32[]{:S(2)}) collective-permute-start(bf16[256,256]{1,0:T(8,128)(2,1)S(1)} %shard_map.129.a_ref), channel_id=1, source_target_pairs={{0,2},{1,3},{2,0},{3,1},{4,6},{5,7},{6,4},{7,5},{8,10},{9,11},{10,... | collective-permute-start | bytes 393224 | tf_op jit(solution)/shard_map/ppermute | solution.py:137
  11.8 1.1 %copy-start.1 = (bf16[1,128,3072]{2,1,0:T(8,128)(2,1)S(1)}, bf16[1,128,3072]{2,1,0:T(8,128)(2,1)}, u32[]{:S(2)}) copy-start(bf16[1,128,3072]{2,1,0:T(8,128)(2,1)} %param.13) | copy-start | bytes 2359300
  12.9 1.1 %copy-start.4 = (bf16[1,128,3072]{2,1,0:T(8,128)(2,1)S(1)}, bf16[1,128,3072]{2,1,0:T(8,128)(2,1)}, u32[]{:S(2)}) copy-start(bf16[1,128,3072]{2,1,0:T(8,128)(2,1)} %param.12) | copy-start | bytes 2359300
  15.2 44.4 %all-to-all-start = ((bf16[4,128,1536]{2,1,0:T(8,128)(2,1)}), bf16[4,128,1536]{2,1,0:T(8,128)(2,1)S(1)}, u32[]{:S(2)}, u32[]{:S(2)}) async-start(bf16[4,128,1536]{2,1,0:T(8,128)(2,1)} %shard_map.128), calls=%async_computation | async-start | bytes 3145728 | tf_op jit(solution)/shard_map/all_to_all | solution.py:366
  20.9 8.9 %collective-permute-start.2 = (bf16[512,256]{1,0:T(8,128)(2,1)S(1)}, bf16[512,256]{1,0:T(8,128)(2,1)}, u32[]{:S(2)}, u32[]{:S(2)}) collective-permute-start(bf16[512,256]{1,0:T(8,128)(2,1)S(1)} %shard_map.131.near_ref), channel_id=1, source_target_pairs={{0,1},{1,0},{2,3},{3,2},{4,5},{5,4},{6,7},{7,6},{8,9},{9,8},{10,11... | collective-permute-start | bytes 786440 | tf_op jit(solution)/shard_map/ppermute | solution.py:137
  29.9 14.4 %collective-permute-start.4 = (f32[4,1536]{1,0:T(4,128)S(1)}, f32[4,1536]{1,0:T(4,128)S(1)}, u32[]{:S(2)}, u32[]{:S(2)}) collective-permute-start(f32[4,1536]{1,0:T(4,128)S(1)} %fusion.2.acts_ref), channel_id=1, source_target_pairs={{0,24},{8,0},{16,8},{24,16},{1,25},{9,1},{17,9},{25,17},{2,26},{10... | collective-permute-start | bytes 73736 | tf_op jit(solution)/shard_map/ppermute | solution.py:337
  32.4 11.9 %collective-permute-start.3 = (f32[4,1536]{1,0:T(4,128)S(1)}, f32[4,1536]{1,0:T(4,128)S(1)}, u32[]{:S(2)}, u32[]{:S(2)}) collective-permute-start(f32[4,1536]{1,0:T(4,128)S(1)} %fusion.2.acts_ref), channel_id=1, source_target_pairs={{0,8},{8,16},{16,24},{24,0},{1,9},{9,17},{17,25},{25,1},{2,10},{10... | collective-permute-start | bytes 73736 | tf_op jit(solution)/shard_map/ppermute | solution.py:337
  44.3 1.9 %collective-permute-start.5 = (f32[512,256]{1,0:T(8,128)S(1)}, f32[512,256]{1,0:T(8,128)S(1)}, u32[]{:S(2)}, u32[]{:S(2)}) collective-permute-start(f32[512,256]{1,0:T(8,128)S(1)} %get-tuple-element.63), channel_id=1, source_target_pairs={{0,1},{1,0},{2,3},{3,2},{4,5},{5,4},{6,7},{7,6},{8,9},{9,8},{10,11... | collective-permute-start | bytes 1572872 | tf_op jit(solution)/shard_map/ppermute | solution.py:137
  46.3 13.3 %collective-permute-start.6 = (bf16[256,256]{1,0:T(8,128)(2,1)S(1)}, bf16[256,256]{1,0:T(8,128)(2,1)S(1)}, u32[]{:S(2)}, u32[]{:S(2)}) collective-permute-start(bf16[256,256]{1,0:T(8,128)(2,1)S(1)} %get-tuple-element.70), channel_id=1, source_target_pairs={{0,2},{1,3},{2,0},{3,1},{4,6},{5,7},{6,4},{7,5},{8,10},{9,11},{10,... | collective-permute-start | bytes 393224 | tf_op jit(solution)/shard_map/ppermute | solution.py:137
  59.7 8.2 %collective-permute-start.7 = (bf16[256,256]{1,0:T(8,128)(2,1)S(1)}, bf16[256,256]{1,0:T(8,128)(2,1)S(1)}, u32[]{:S(2)}, u32[]{:S(2)}) collective-permute-start(bf16[256,256]{1,0:T(8,128)(2,1)S(1)} %get-tuple-element.75), channel_id=1, source_target_pairs={{0,4},{1,5},{2,6},{3,7},{4,0},{5,1},{6,2},{7,3},{8,12},{9,13},{10,... | collective-permute-start | bytes 393224 | tf_op jit(solution)/shard_map/ppermute | solution.py:137
  68.5 5.4 %collective-permute-start.8 = (bf16[256,256]{1,0:T(8,128)(2,1)S(1)}, bf16[256,256]{1,0:T(8,128)(2,1)S(1)}, u32[]{:S(2)}, u32[]{:S(2)}) collective-permute-start(bf16[256,256]{1,0:T(8,128)(2,1)S(1)} %get-tuple-element.78.a_ref), channel_id=1, source_target_pairs={{0,2},{1,3},{2,0},{3,1},{4,6},{5,7},{6,4},{7,5},{8,10},{9,11},{10,... | collective-permute-start | bytes 393224 | tf_op jit(solution)/shard_map/ppermute | solution.py:137
  68.5 6.4 %collective-permute-start.10 = (f32[4,6144]{1,0:T(4,128)S(1)}, f32[4,6144]{1,0:T(4,128)S(1)}, u32[]{:S(2)}, u32[]{:S(2)}) collective-permute-start(f32[4,6144]{1,0:T(4,128)S(1)} %get-tuple-element.85), channel_id=1, source_target_pairs={{0,8},{8,16},{16,24},{24,0},{1,9},{9,17},{17,25},{25,1},{2,10},{10... | collective-permute-start | bytes 294920 | tf_op jit(solution)/shard_map/ppermute | solution.py:337
  70.2 6.1 %collective-permute-start.11 = (f32[4,6144]{1,0:T(4,128)S(1)}, f32[4,6144]{1,0:T(4,128)S(1)}, u32[]{:S(2)}, u32[]{:S(2)}) collective-permute-start(f32[4,6144]{1,0:T(4,128)S(1)} %get-tuple-element.86), channel_id=1, source_target_pairs={{0,24},{8,0},{16,8},{24,16},{1,25},{9,1},{17,9},{25,17},{2,26},{10... | collective-permute-start | bytes 294920 | tf_op jit(solution)/shard_map/ppermute | solution.py:337
  74.6 2.5 %collective-permute-start.9 = (f32[768,256]{1,0:T(8,128)S(1)}, f32[768,256]{1,0:T(8,128)S(1)}, u32[]{:S(2)}, u32[]{:S(2)}) collective-permute-start(f32[768,256]{1,0:T(8,128)S(1)} %get-tuple-element.80), channel_id=1, source_target_pairs={{0,1},{1,0},{2,3},{3,2},{4,5},{5,4},{6,7},{7,6},{8,9},{9,8},{10,11... | collective-permute-start | bytes 2359304 | tf_op jit(solution)/shard_map/ppermute | solution.py:137

commit v11 on v10

--- a/solution.py
+++ b/solution.py
@@ -393,13 +393,15 @@
             contrib = jnp.dot(both, weight, preferred_element_type=F32)
             arrived, contrib, blocks = lax.optimization_barrier((arrived, contrib, blocks))
 
-    grads, sent = add_split(grads, arrived, grads.shape[0], grads.shape[0])
-    arrived = swap(sent, "seq", last)
     if contrib is None:
         contrib = jnp.dot(both, weight, preferred_element_type=F32)
     contrib = contrib.reshape(2, contrib.shape[0] // 2, contrib.shape[1])
     lower_half = from_cycle(contrib[1], "rep", 1)
     higher_half = from_cycle(contrib[0], "rep", -1)
+
+    grads, sent = add_split(grads, arrived, grads.shape[0], grads.shape[0])
+    arrived = swap(sent, "seq", last)
+    arrived, lower_half, higher_half = lax.optimization_barrier((arrived, lower_half, higher_half))
     own, near_b = merge(me, last, grads, arrived)
     for bit in bits[1:-1]:
         near_b = join(near_b, swap(near_b, "seq", bit))

time: 78.4 us -> 78.3 us (level)
  waiting for transfers between devices: 16.7 us -> 15 us
  starting transfers between devices: 21.2 us -> 22.8 us
    ppermute x8, waiting for transfers between devices: 15.1 us -> 9.52 us  [swap(): return lax.ppermute(block, axis, route)]
    ppermute x4, waiting for transfers between devices: 1.61 us -> 5.52 us  [from_cycle(): lax.ppermute(block, axis, [(i, (i + distance) % count) for i in range(cou...]
    ppermute x8, starting transfers between devices: 10 us -> 12 us  [swap(): return lax.ppermute(block, axis, route)]
  transfers between devices with their start and end apart: 13 -> 13, of which waited for: 7 -> 7; matrix products, arithmetic and copies ran while one was open for 22% -> 22% of each run, Pallas kernels for 20% -> 19%
where the time goes in v11:
time: 78.3 us; the launch traced here: 77.9 us
  starting transfers between devices  22.8 us (29%)
  matrix products  16.6 us (21%)
  Pallas kernels  16.4 us (21%)
  waiting for transfers between devices  15 us (19%)
  local copies, waits for them, and re-layouts  3.72 us (5%)
  other arithmetic  2.62 us (3%)
    ppermute x8, starting transfers between devices, swap(): return lax.ppermute(block, axis, route)  12 us
    pallas_call x1, Pallas kernels, attend(): pl.pallas_call(functools.partial(attention_kernel, order, group, join, hd...  11.9 us
    ppermute x8, waiting for transfers between devices, swap(): return lax.ppermute(block, axis, route)  9.52 us
    dot_general x1, matrix products, dot_nt(): lax.dot_general(a, b, (((1,), (1,)), ((), ())), preferred_element_type=F32)  8.9 us
    dot_general x1, matrix products, on_device(): contrib = jnp.dot(both, weight, preferred_element_type=F32)  7.69 us
    all_to_all x1, starting transfers between devices, on_device(): lax.all_to_all(packed, 'seq', split_axis=0, concat_axis=0, tiled=True, ax...  5.7 us
    ppermute x4, waiting for transfers between devices, from_cycle(): lax.ppermute(block, axis, [(i, (i + distance) % count) for i in range(cou...  5.52 us
    ppermute x4, starting transfers between devices, from_cycle(): lax.ppermute(block, axis, [(i, (i + distance) % count) for i in range(cou...  5.02 us
  transfers between devices with their start and end apart: 13, of which 7 were waited for; matrix products, arithmetic and copies ran while one was open for 22% of the time, Pallas kernels for 19%

profile of v11, /device:TPU:0, one launch (start us, length us, event | category | flops | bytes accessed | tf_op | source)
XLA Modules:
  0.0 77.9 jit_solution(13385664158380068214)
XLA Ops:
  0.6 0.0 copy-start
  0.6 0.0 copy-start.2
  0.7 0.9 %pad_maximum_fusion.a_ref = bf16[128,256]{1,0:T(8,128)(2,1)S(1)} fusion(bf16[128,128]{1,0:T(8,128)(2,1)} %bitcast.34, bf16[128,128]{1,0:T(8,128)(2,1)} %bitcast.35), kind=kLoop, calls=%fused_computation.8 | loop fusion | flops 131072 | bytes 131072 | tf_op jit(solution)/shard_map/concatenate | solution.py:351
  1.5 5.9 %collective-permute-start = (bf16[128,256]{1,0:T(8,128)(2,1)S(1)}, bf16[128,256]{1,0:T(8,128)(2,1)S(1)}, u32[]{:S(2)}, u32[]{:S(2)}) collective-permute-start(bf16[128,256]{1,0:T(8,128)(2,1)S(1)} %pad_maximum_fusion.a_ref), channel_id=1, source_target_pairs={{0,4},{1,5},{2,6},{3,7},{8,12},{9,13},{10,14},{11,15},{16,20},{17,... | collective-permute-start | bytes 196616 | tf_op jit(solution)/shard_map/ppermute | solution.py:137
  7.5 0.0 copy-start.3
  7.5 1.4 %copy-done.3 = bf16[1,128,6144]{2,1,0:T(8,128)(2,1)S(1)} copy-done((bf16[1,128,6144]{2,1,0:T(8,128)(2,1)S(1)}, bf16[1,128,6144]{2,1,0:T(8,128)(2,1)}, u32[]{:S(2)}) %copy-start.3) | copy-done | bytes 1572888
  8.9 0.0 copy-start.5
  8.9 0.0 copy-start.6
  8.9 1.3 %shard_map.128 = bf16[4,128,1536]{2,1,0:T(8,128)(2,1)} custom-call(bf16[128,6144]{1,0:T(8,128)(2,1)S(1)} %bitcast.30), custom_call_target="tpu_custom_call" | custom-call | flops 1 | bytes 1 | tf_op jit(solution)/shard_map/pallas_call | solution.py:260
  10.2 0.0 collective-permute-done.b_ref
  10.2 1.6 %collective-permute-start.1 = (bf16[256,256]{1,0:T(8,128)(2,1)S(1)}, bf16[256,256]{1,0:T(8,128)(2,1)S(1)}, u32[]{:S(2)}, u32[]{:S(2)}) collective-permute-start(bf16[256,256]{1,0:T(8,128)(2,1)S(1)} %shard_map.129.a_ref), channel_id=1, source_target_pairs={{0,2},{1,3},{2,0},{3,1},{4,6},{5,7},{6,4},{7,5},{8,10},{9,11},{10,... | collective-permute-start | bytes 393224 | tf_op jit(solution)/shard_map/ppermute | solution.py:137
  11.8 0.0 copy-start.1
  11.8 1.1 %copy-done.1 = bf16[1,128,3072]{2,1,0:T(8,128)(2,1)S(1)} copy-done((bf16[1,128,3072]{2,1,0:T(8,128)(2,1)S(1)}, bf16[1,128,3072]{2,1,0:T(8,128)(2,1)}, u32[]{:S(2)}) %copy-start.1) | copy-done | bytes 786456
  12.9 0.0 copy-start.4
  13.0 1.1 %copy-done.4 = bf16[1,128,3072]{2,1,0:T(8,128)(2,1)S(1)} copy-done((bf16[1,128,3072]{2,1,0:T(8,128)(2,1)S(1)}, bf16[1,128,3072]{2,1,0:T(8,128)(2,1)}, u32[]{:S(2)}) %copy-start.4) | copy-done | bytes 786456
  14.1 0.5 shard_map.130.delta_ref
  14.6 0.6 collective-permute-done.1.b_ref
  15.2 0.0 copy-done
  15.2 5.7 %all-to-all-start = ((bf16[4,128,1536]{2,1,0:T(8,128)(2,1)}), bf16[4,128,1536]{2,1,0:T(8,128)(2,1)S(1)}, u32[]{:S(2)}, u32[]{:S(2)}) async-start(bf16[4,128,1536]{2,1,0:T(8,128)(2,1)} %shard_map.128), calls=%async_computation | async-start | bytes 3145728 | tf_op jit(solution)/shard_map/all_to_all | solution.py:366
  20.9 0.0 collective-permute-start.2
  20.9 8.9 %fusion.2.acts_ref = f32[4,1536]{1,0:T(4,128)S(1)} fusion(bf16[4,6144]{1,0:T(4,128)(2,1)S(1)} %bitcast.27, bf16[1,1536,6144]{2,1,0:T(8,128)(2,1)} %param.16), kind=kOutput, calls=%fused_computation.2 | convolution fusion | flops 75497472 | bytes 18948096 | tf_op jit(solution)/shard_map/dot_general | solution.py:24
  29.8 0.0 collective-permute-done.2.far_ref
  29.9 2.5 %collective-permute-start.4 = (f32[4,1536]{1,0:T(4,128)S(1)}, f32[4,1536]{1,0:T(4,128)S(1)}, u32[]{:S(2)}, u32[]{:S(2)}) collective-permute-start(f32[4,1536]{1,0:T(4,128)S(1)} %fusion.2.acts_ref), channel_id=1, source_target_pairs={{0,24},{8,0},{16,8},{24,16},{1,25},{9,1},{17,9},{25,17},{2,26},{10... | collective-permute-start | bytes 73736 | tf_op jit(solution)/shard_map/ppermute | solution.py:337
  32.4 0.0 collective-permute-start.3
  32.4 0.0 copy-done.2
  32.4 0.0 copy-done.5
  32.4 0.0 copy-done.6
  32.4 11.9 %shard_map.132 = (f32[128,3072]{1,0:T(8,128)}, f32[512,256]{1,0:T(8,128)S(1)}, f32[512,256]{1,0:T(8,128)S(1)}) custom-call(s32[1]{0:T(128)} %bitcast.me_ref, bf16[128,3072]{1,0:T(8,128)(2,1)S(1)} %bitcast.32, bf16[128,3072]{1,0:T(8,128)(2,1)S(1)} %bitcast.29, f32[24,128]{1,0:T(8,128)S(1)} %bitcast.33, f32[24,128]{1,0:T(8,128)S(1)} %shard_map.130.delta_ref, ...), custom_call_target="tpu_custom_call" | custom-call | flops 1 | bytes 1 | tf_op jit(solution)/shard_map/pallas_call | solution.py:233
  44.3 0.0 collective-permute-done.4.higher_ref
  44.3 0.0 collective-permute-done.3.lower_ref
  44.3 0.2 collective-permute-start.5
  44.5 1.3 %shard_map.133 = (f32[2,4,1536]{2,1,0:T(4,128)}, bf16[8,1536]{1,0:T(8,128)(2,1)S(1)}) custom-call(f32[4,1536]{1,0:T(4,128)S(1)} %fusion.2.acts_ref, f32[4,1536]{1,0:T(4,128)S(1)} %collective-permute-done.3.lower_ref, f32[4,1536]{1,0:T(4,128)S(1)} %collective-permute-done.4.higher_ref), custom_call_target="tpu_custom_call" | custom-call | flops 1 | bytes 1 | tf_op jit(solution)/shard_map/pallas_call | solution.py:322
  45.8 0.4 collective-permute-done.5.arrived_ref
  46.2 0.1 shard_map.134
  46.3 2.1 %collective-permute-start.6 = (bf16[256,256]{1,0:T(8,128)(2,1)S(1)}, bf16[256,256]{1,0:T(8,128)(2,1)S(1)}, u32[]{:S(2)}, u32[]{:S(2)}) collective-permute-start(bf16[256,256]{1,0:T(8,128)(2,1)S(1)} %get-tuple-element.73), channel_id=1, source_target_pairs={{0,2},{1,3},{2,0},{3,1},{4,6},{5,7},{6,4},{7,5},{8,10},{9,11},{10,... | collective-permute-start | bytes 393224 | tf_op jit(solution)/shard_map/ppermute | solution.py:137
  48.4 7.7 %fusion = f32[8,6144]{1,0:T(8,128)S(1)} fusion(bf16[8,1536]{1,0:T(8,128)(2,1)S(1)} %get-tuple-element.74, bf16[1,1536,6144]{2,1,0:T(8,128)(2,1)} %param.16), kind=kOutput, calls=%fused_computation | convolution fusion | flops 150994944 | bytes 19095552 | tf_op jit(solution)/shard_map/dot_general | solution.py:393
  56.0 3.6 %collective-permute-done.6.arrived_ref = bf16[256,256]{1,0:T(8,128)(2,1)S(1)} collective-permute-done((bf16[256,256]{1,0:T(8,128)(2,1)S(1)}, bf16[256,256]{1,0:T(8,128)(2,1)S(1)}, u32[]{:S(2)}, u32[]{:S(2)}) %collective-permute-start.6) | collective-permute-done | bytes 131104 | tf_op jit(solution)/shard_map/ppermute | solution.py:137
  59.6 0.0 all-to-all-done.x_ref
  59.7 0.1 collective-permute-start.7
  59.8 2.5 %collective-permute-start.9 = (f32[4,6144]{1,0:T(4,128)S(1)}, f32[4,6144]{1,0:T(4,128)S(1)}, u32[]{:S(2)}, u32[]{:S(2)}) collective-permute-start(f32[4,6144]{1,0:T(4,128)S(1)} %get-tuple-element.91), channel_id=1, source_target_pairs={{0,24},{8,0},{16,8},{24,16},{1,25},{9,1},{17,9},{25,17},{2,26},{10... | collective-permute-start | bytes 294920 | tf_op jit(solution)/shard_map/ppermute | solution.py:337
  62.3 0.0 collective-permute-start.8
  62.3 3.2 %collective-permute-done.9 = f32[4,6144]{1,0:T(4,128)S(1)} collective-permute-done((f32[4,6144]{1,0:T(4,128)S(1)}, f32[4,6144]{1,0:T(4,128)S(1)}, u32[]{:S(2)}, u32[]{:S(2)}) %collective-permute-start.9) | collective-permute-done | bytes 98336 | tf_op jit(solution)/shard_map/ppermute | solution.py:337
  65.5 2.3 %collective-permute-done.8 = f32[4,6144]{1,0:T(4,128)S(1)} collective-permute-done((f32[4,6144]{1,0:T(4,128)S(1)}, f32[4,6144]{1,0:T(4,128)S(1)}, u32[]{:S(2)}, u32[]{:S(2)}) %collective-permute-start.8) | collective-permute-done | bytes 98336 | tf_op jit(solution)/shard_map/ppermute | solution.py:337
  67.8 0.0 collective-permute-done.7.there_ref
  67.8 0.7 shard_map.136
  68.5 2.0 %collective-permute-start.10 = (bf16[256,256]{1,0:T(8,128)(2,1)S(1)}, bf16[256,256]{1,0:T(8,128)(2,1)S(1)}, u32[]{:S(2)}, u32[]{:S(2)}) collective-permute-start(bf16[256,256]{1,0:T(8,128)(2,1)S(1)} %get-tuple-element.83.a_ref), channel_id=1, source_target_pairs={{0,2},{1,3},{2,0},{3,1},{4,6},{5,7},{6,4},{7,5},{8,10},{9,11},{10,... | collective-permute-start | bytes 393224 | tf_op jit(solution)/shard_map/ppermute | solution.py:137
  70.5 3.4 %collective-permute-done.10.b_ref = bf16[256,256]{1,0:T(8,128)(2,1)S(1)} collective-permute-done((bf16[256,256]{1,0:T(8,128)(2,1)S(1)}, bf16[256,256]{1,0:T(8,128)(2,1)S(1)}, u32[]{:S(2)}, u32[]{:S(2)}) %collective-permute-start.10) | collective-permute-done | bytes 131104 | tf_op jit(solution)/shard_map/ppermute | solution.py:137
  73.9 0.6 shard_map.138
  74.6 0.1 collective-permute-start.11
  74.7 0.1 add_bitcast_fusion.2
  74.7 0.7 maximum_bitcast_fusion
  75.4 1.5 %collective-permute-done.11 = f32[768,256]{1,0:T(8,128)S(1)} collective-permute-done((f32[768,256]{1,0:T(8,128)S(1)}, f32[768,256]{1,0:T(8,128)S(1)}, u32[]{:S(2)}, u32[]{:S(2)}) %collective-permute-start.11) | collective-permute-done | bytes 786464 | tf_op jit(solution)/shard_map/ppermute | solution.py:137
  76.9 1.0 %add_bitcast_fusion = f32[1,768,256]{2,1,0:T(8,128)} fusion(f32[768,256]{1,0:T(8,128)S(1)} %get-tuple-element.84, f32[768,256]{1,0:T(8,128)S(1)} %collective-permute-done.11), kind=kLoop, calls=%fused_computation.4 | loop fusion | flops 196608 | bytes 2359296 | tf_op jit(solution)/shard_map/broadcast_in_dim | solution.py:415
  (5 shorter events, 0.1 us)
Async XLA Ops:
  0.6 14.6 %copy-start = (bf16[1,4,6144]{2,1,0:T(4,128)(2,1)S(1)}, bf16[1,4,6144]{2,1,0:T(4,128)(2,1)}, u32[]{:S(2)}) copy-start(bf16[1,4,6144]{2,1,0:T(4,128)(2,1)} %param.17) | copy-start | bytes 147460
  0.6 31.7 %copy-start.2 = (bf16[1,128,3072]{2,1,0:T(8,128)(2,1)S(1)}, bf16[1,128,3072]{2,1,0:T(8,128)(2,1)}, u32[]{:S(2)}) copy-start(bf16[1,128,3072]{2,1,0:T(8,128)(2,1)} %param.13) | copy-start | bytes 2359300
  1.5 8.6 %collective-permute-start = (bf16[128,256]{1,0:T(8,128)(2,1)S(1)}, bf16[128,256]{1,0:T(8,128)(2,1)S(1)}, u32[]{:S(2)}, u32[]{:S(2)}) collective-permute-start(bf16[128,256]{1,0:T(8,128)(2,1)S(1)} %pad_maximum_fusion.a_ref), channel_id=1, source_target_pairs={{0,4},{1,5},{2,6},{3,7},{8,12},{9,13},{10,14},{11,15},{16,20},{17,... | collective-permute-start | bytes 196616 | tf_op jit(solution)/shard_map/ppermute | solution.py:137
  7.5 1.4 %copy-start.3 = (bf16[1,128,6144]{2,1,0:T(8,128)(2,1)S(1)}, bf16[1,128,6144]{2,1,0:T(8,128)(2,1)}, u32[]{:S(2)}) copy-start(bf16[1,128,6144]{2,1,0:T(8,128)(2,1)} %param.15) | copy-start | bytes 4718596
  8.9 23.5 %copy-start.5 = (bf16[1,128,3072]{2,1,0:T(8,128)(2,1)S(1)}, bf16[1,128,3072]{2,1,0:T(8,128)(2,1)}, u32[]{:S(2)}) copy-start(bf16[1,128,3072]{2,1,0:T(8,128)(2,1)} %param.9) | copy-start | bytes 2359300
  8.9 23.5 %copy-start.6 = (f32[1,24,128]{2,1,0:T(8,128)S(1)}, f32[1,24,128]{2,1,0:T(8,128)}, u32[]{:S(2)}) copy-start(f32[1,24,128]{2,1,0:T(8,128)} %param.14) | copy-start | bytes 36868
  10.2 5.0 %collective-permute-start.1 = (bf16[256,256]{1,0:T(8,128)(2,1)S(1)}, bf16[256,256]{1,0:T(8,128)(2,1)S(1)}, u32[]{:S(2)}, u32[]{:S(2)}) collective-permute-start(bf16[256,256]{1,0:T(8,128)(2,1)S(1)} %shard_map.129.a_ref), channel_id=1, source_target_pairs={{0,2},{1,3},{2,0},{3,1},{4,6},{5,7},{6,4},{7,5},{8,10},{9,11},{10,... | collective-permute-start | bytes 393224 | tf_op jit(solution)/shard_map/ppermute | solution.py:137
  11.8 1.1 %copy-start.1 = (bf16[1,128,3072]{2,1,0:T(8,128)(2,1)S(1)}, bf16[1,128,3072]{2,1,0:T(8,128)(2,1)}, u32[]{:S(2)}) copy-start(bf16[1,128,3072]{2,1,0:T(8,128)(2,1)} %param.13) | copy-start | bytes 2359300
  12.9 1.1 %copy-start.4 = (bf16[1,128,3072]{2,1,0:T(8,128)(2,1)S(1)}, bf16[1,128,3072]{2,1,0:T(8,128)(2,1)}, u32[]{:S(2)}) copy-start(bf16[1,128,3072]{2,1,0:T(8,128)(2,1)} %param.12) | copy-start | bytes 2359300
  15.2 44.4 %all-to-all-start = ((bf16[4,128,1536]{2,1,0:T(8,128)(2,1)}), bf16[4,128,1536]{2,1,0:T(8,128)(2,1)S(1)}, u32[]{:S(2)}, u32[]{:S(2)}) async-start(bf16[4,128,1536]{2,1,0:T(8,128)(2,1)} %shard_map.128), calls=%async_computation | async-start | bytes 3145728 | tf_op jit(solution)/shard_map/all_to_all | solution.py:366
  20.9 8.9 %collective-permute-start.2 = (bf16[512,256]{1,0:T(8,128)(2,1)S(1)}, bf16[512,256]{1,0:T(8,128)(2,1)}, u32[]{:S(2)}, u32[]{:S(2)}) collective-permute-start(bf16[512,256]{1,0:T(8,128)(2,1)S(1)} %shard_map.131.near_ref), channel_id=1, source_target_pairs={{0,1},{1,0},{2,3},{3,2},{4,5},{5,4},{6,7},{7,6},{8,9},{9,8},{10,11... | collective-permute-start | bytes 786440 | tf_op jit(solution)/shard_map/ppermute | solution.py:137
  29.9 14.4 %collective-permute-start.4 = (f32[4,1536]{1,0:T(4,128)S(1)}, f32[4,1536]{1,0:T(4,128)S(1)}, u32[]{:S(2)}, u32[]{:S(2)}) collective-permute-start(f32[4,1536]{1,0:T(4,128)S(1)} %fusion.2.acts_ref), channel_id=1, source_target_pairs={{0,24},{8,0},{16,8},{24,16},{1,25},{9,1},{17,9},{25,17},{2,26},{10... | collective-permute-start | bytes 73736 | tf_op jit(solution)/shard_map/ppermute | solution.py:337
  32.4 11.9 %collective-permute-start.3 = (f32[4,1536]{1,0:T(4,128)S(1)}, f32[4,1536]{1,0:T(4,128)S(1)}, u32[]{:S(2)}, u32[]{:S(2)}) collective-permute-start(f32[4,1536]{1,0:T(4,128)S(1)} %fusion.2.acts_ref), channel_id=1, source_target_pairs={{0,8},{8,16},{16,24},{24,0},{1,9},{9,17},{17,25},{25,1},{2,10},{10... | collective-permute-start | bytes 73736 | tf_op jit(solution)/shard_map/ppermute | solution.py:337
  44.3 1.9 %collective-permute-start.5 = (f32[512,256]{1,0:T(8,128)S(1)}, f32[512,256]{1,0:T(8,128)S(1)}, u32[]{:S(2)}, u32[]{:S(2)}) collective-permute-start(f32[512,256]{1,0:T(8,128)S(1)} %get-tuple-element.66), channel_id=1, source_target_pairs={{0,1},{1,0},{2,3},{3,2},{4,5},{5,4},{6,7},{7,6},{8,9},{9,8},{10,11... | collective-permute-start | bytes 1572872 | tf_op jit(solution)/shard_map/ppermute | solution.py:137
  46.3 13.3 %collective-permute-start.6 = (bf16[256,256]{1,0:T(8,128)(2,1)S(1)}, bf16[256,256]{1,0:T(8,128)(2,1)S(1)}, u32[]{:S(2)}, u32[]{:S(2)}) collective-permute-start(bf16[256,256]{1,0:T(8,128)(2,1)S(1)} %get-tuple-element.73), channel_id=1, source_target_pairs={{0,2},{1,3},{2,0},{3,1},{4,6},{5,7},{6,4},{7,5},{8,10},{9,11},{10,... | collective-permute-start | bytes 393224 | tf_op jit(solution)/shard_map/ppermute | solution.py:137
  59.7 8.2 %collective-permute-start.7 = (bf16[256,256]{1,0:T(8,128)(2,1)S(1)}, bf16[256,256]{1,0:T(8,128)(2,1)S(1)}, u32[]{:S(2)}, u32[]{:S(2)}) collective-permute-start(bf16[256,256]{1,0:T(8,128)(2,1)S(1)} %get-tuple-element.78), channel_id=1, source_target_pairs={{0,4},{1,5},{2,6},{3,7},{4,0},{5,1},{6,2},{7,3},{8,12},{9,13},{10,... | collective-permute-start | bytes 393224 | tf_op jit(solution)/shard_map/ppermute | solution.py:137
  59.8 5.7 %collective-permute-start.9 = (f32[4,6144]{1,0:T(4,128)S(1)}, f32[4,6144]{1,0:T(4,128)S(1)}, u32[]{:S(2)}, u32[]{:S(2)}) collective-permute-start(f32[4,6144]{1,0:T(4,128)S(1)} %get-tuple-element.91), channel_id=1, source_target_pairs={{0,24},{8,0},{16,8},{24,16},{1,25},{9,1},{17,9},{25,17},{2,26},{10... | collective-permute-start | bytes 294920 | tf_op jit(solution)/shard_map/ppermute | solution.py:337
  62.3 5.5 %collective-permute-start.8 = (f32[4,6144]{1,0:T(4,128)S(1)}, f32[4,6144]{1,0:T(4,128)S(1)}, u32[]{:S(2)}, u32[]{:S(2)}) collective-permute-start(f32[4,6144]{1,0:T(4,128)S(1)} %get-tuple-element.92), channel_id=1, source_target_pairs={{0,8},{8,16},{16,24},{24,0},{1,9},{9,17},{17,25},{25,1},{2,10},{10... | collective-permute-start | bytes 294920 | tf_op jit(solution)/shard_map/ppermute | solution.py:337
  68.5 5.4 %collective-permute-start.10 = (bf16[256,256]{1,0:T(8,128)(2,1)S(1)}, bf16[256,256]{1,0:T(8,128)(2,1)S(1)}, u32[]{:S(2)}, u32[]{:S(2)}) collective-permute-start(bf16[256,256]{1,0:T(8,128)(2,1)S(1)} %get-tuple-element.83.a_ref), channel_id=1, source_target_pairs={{0,2},{1,3},{2,0},{3,1},{4,6},{5,7},{6,4},{7,5},{8,10},{9,11},{10,... | collective-permute-start | bytes 393224 | tf_op jit(solution)/shard_map/ppermute | solution.py:137
  74.6 2.4 %collective-permute-start.11 = (f32[768,256]{1,0:T(8,128)S(1)}, f32[768,256]{1,0:T(8,128)S(1)}, u32[]{:S(2)}, u32[]{:S(2)}) collective-permute-start(f32[768,256]{1,0:T(8,128)S(1)} %get-tuple-element.85), channel_id=1, source_target_pairs={{0,1},{1,0},{2,3},{3,2},{4,5},{5,4},{6,7},{7,6},{8,9},{9,8},{10,11... | collective-permute-start | bytes 2359304 | tf_op jit(solution)/shard_map/ppermute | solution.py:137
